TPU v7x, 512 devices: a whole 4x8x8 slice. The times are simulated.
512 devices in a mesh: blk: 8 (over z_hi, core), dp: 64 (over z_lo, x, y).
Axes of the slice: x: 4, y: 8, z: 8 (z_hi: 4, z_lo: 2; z = z_hi * 2 + z_lo), core: 2. Of those that a mesh axis runs over, the one named last changes fastest.
Arguments:
- audio_features: bfloat16 [131072, 1024], P(('blk', 'dp'))
- proj_weight: bfloat16 [1024, 512], replicated
- text_raw: bfloat16 [131072, 512], P(('blk', 'dp'))
- positive: int32 [131072], P(('blk', 'dp')), may hold values from 0 to 2047
Outputs:
- grad_weight: float32 [1024, 512], replicated
- grad_features: bfloat16 [131072, 1024], P(('blk', 'dp'))
- grad_text: float32 [131072, 512], P(('blk', 'dp'))
Inputs may be any that keep to these rules, and one draw needn't show every extreme that they name: Any text row of a group may be the positive of several audio rows of that group or of none.
All inputs are finite; a program needn't handle non-finite values.
Results may differ from a plain program's by a relative error of at most 0.015.
Values may be sent and summed in bfloat16 or wider, within the bound.
No kernel may reach another device: no remote copies, remote signals or barrier semaphores. Data moves between devices by JAX's collectives and lax.ppermute only.
A program may use at most 64 MiB of HBM per device.

v0:
```python
import jax
import jax.numpy as jnp
from jax import lax
from jax.sharding import PartitionSpec as P

SCALE = 100.0
EPS = 1e-06


def shifted(block, axis, distance):
    devices = range(lax.axis_size(axis))
    route = [((i - distance) % len(devices), i) for i in devices]
    return lax.ppermute(block, axis, route)


def scores_for(audio_b, piece):
    return SCALE * lax.dot_general(
        audio_b, piece, (((1,), (1,)), ((), ())), preferred_element_type=jnp.float32
    )


def grad_tile(audio_b, piece, ids, positive, lse):
    scores = scores_for(audio_b, piece)
    match = jnp.where(positive[:, None] == ids[None, :], 1.0, 0.0)
    return (jnp.exp(scores - lse[:, None]) - match).astype(jnp.bfloat16)


def tile_product(tile, audio_b):
    return SCALE * lax.dot_general(
        tile, audio_b, (((0,), (0,)), ((), ())), preferred_element_type=jnp.float32
    )


def finish_audio(audio_features, proj_weight, audio, audio_scale, audio_grad):
    along = jnp.sum(audio * audio_grad, axis=1, keepdims=True)
    proj_grad = ((audio_grad - audio * along) * audio_scale).astype(jnp.bfloat16)
    grad_features = lax.dot_general(
        proj_grad, proj_weight, (((1,), (1,)), ((), ())), preferred_element_type=jnp.float32
    ).astype(jnp.bfloat16)
    weight_part = lax.dot_general(
        audio_features, proj_grad, (((0,), (0,)), ((), ())), preferred_element_type=jnp.float32
    )
    grad_weight = lax.psum(weight_part, ("blk", "dp"))
    return (grad_weight, grad_features)


def body(audio_features, proj_weight, text_raw, positive):
    rows = audio_features.shape[0]
    width = text_raw.shape[1]
    blocks = lax.axis_size("blk")
    me_blk = lax.axis_index("blk")
    proj = jnp.dot(audio_features, proj_weight, preferred_element_type=jnp.float32)
    audio_scale = lax.rsqrt(jnp.sum(proj * proj, axis=1, keepdims=True) + EPS)
    audio = proj * audio_scale
    audio_b = audio.astype(jnp.bfloat16)
    text_f = text_raw.astype(jnp.float32)
    text_scale = lax.rsqrt(jnp.sum(text_f * text_f, axis=1, keepdims=True) + EPS)
    text = text_f * text_scale
    text_b = text.astype(jnp.bfloat16)
    offsets = jnp.arange(rows, dtype=jnp.int32)
    peak = jnp.full((rows,), -jnp.inf, jnp.float32)
    total = jnp.zeros((rows,), jnp.float32)
    stored = []
    current = text_b
    for step in range(blocks):
        ids = (me_blk - step) % blocks * rows + 0 + offsets
        stored.append((current, ids))
        accumulate_total = total
        scores = scores_for(audio_b, current)
        new_peak = jnp.maximum(peak, jnp.max(scores, axis=1))
        accumulate_total = accumulate_total * jnp.exp(peak - new_peak) + jnp.sum(
            jnp.exp(scores - new_peak[:, None]), axis=1
        )
        peak = new_peak
        total = accumulate_total
        if step + 1 < blocks:
            current = shifted(current, "blk", 1)
    lse = peak + jnp.log(total)
    tiles = []
    audio_grad = jnp.zeros((rows, width), jnp.float32)
    for step in range(blocks):
        piece, ids = stored[step]
        grads = grad_tile(audio_b, piece, ids, positive, lse)
        tiles.append(grads)
        audio_grad = audio_grad + SCALE * jnp.dot(grads, piece, preferred_element_type=jnp.float32)
    text_acc = jnp.zeros((rows, width), jnp.float32)
    for step in range(blocks):
        text_part = tile_product(tiles[step], audio_b)
        text_acc = text_acc + text_part
        text_acc = shifted(text_acc.astype(jnp.bfloat16), "blk", 1).astype(text_acc.dtype)
    grad_weight, grad_features = finish_audio(
        audio_features, proj_weight, audio, audio_scale, audio_grad
    )
    text_along = jnp.sum(text * text_acc, axis=1, keepdims=True)
    grad_text = (text_acc - text * text_along) * text_scale
    return (grad_weight, grad_features, grad_text)


def solution(mesh):
    placed = (P(("blk", "dp"), None), P(), P(("blk", "dp"), None), P(("blk", "dp")))
    return jax.shard_map(
        body,
        mesh=mesh,
        in_specs=placed,
        out_specs=(P(), P(("blk", "dp"), None), P(("blk", "dp"), None)),
        check_vma=False,
    )
```

profile of v0, /device:TPU:1, one launch (start us, length us, event | category | flops | bytes accessed | tf_op | source)
XLA Modules:
  0.0 438.0 jit_solution(10961548759670314348)
XLA Ops:
  9.5 7.2 %collective-permute-start = (bf16[256,512]{1,0:T(8,128)(2,1)S(1)}, bf16[256,512]{1,0:T(8,128)(2,1)S(1)}, u32[]{:S(2)}, u32[]{:S(2)}) collective-permute-start(bf16[256,512]{1,0:T(8,128)(2,1)S(1)} %fusion.3), channel_id=1, source_target_pairs={{448,0},{0,64},{64,128},{128,192},{192,256},{256,320},{320,384},{3... | collective-permute-start | bytes 786440 | tf_op jit(solution)/shard_map/ppermute | solution.py:13
  18.4 1.6 collective-permute-done
  20.0 5.4 %collective-permute-start.1 = (bf16[256,512]{1,0:T(8,128)(2,1)S(1)}, bf16[256,512]{1,0:T(8,128)(2,1)S(1)}, u32[]{:S(2)}, u32[]{:S(2)}) collective-permute-start(bf16[256,512]{1,0:T(8,128)(2,1)S(1)} %collective-permute-done), channel_id=1, source_target_pairs={{448,0},{0,64},{64,128},{128,192},{192,256},{256,320},{320,384},{3... | collective-permute-start | bytes 786440 | tf_op jit(solution)/shard_map/ppermute | solution.py:13
  25.5 4.1 collective-permute-done.1
  29.6 5.4 %collective-permute-start.2 = (bf16[256,512]{1,0:T(8,128)(2,1)S(1)}, bf16[256,512]{1,0:T(8,128)(2,1)S(1)}, u32[]{:S(2)}, u32[]{:S(2)}) collective-permute-start(bf16[256,512]{1,0:T(8,128)(2,1)S(1)} %collective-permute-done.1), channel_id=1, source_target_pairs={{448,0},{0,64},{64,128},{128,192},{192,256},{256,320},{320,384},{3... | collective-permute-start | bytes 786440 | tf_op jit(solution)/shard_map/ppermute | solution.py:13
  35.3 5.0 %collective-permute-done.2 = bf16[256,512]{1,0:T(8,128)(2,1)S(1)} collective-permute-done((bf16[256,512]{1,0:T(8,128)(2,1)S(1)}, bf16[256,512]{1,0:T(8,128)(2,1)S(1)}, u32[]{:S(2)}, u32[]{:S(2)}) %collective-permute-start.2) | collective-permute-done | bytes 262176 | tf_op jit(solution)/shard_map/ppermute | solution.py:13
  40.3 5.3 %collective-permute-start.3 = (bf16[256,512]{1,0:T(8,128)(2,1)S(1)}, bf16[256,512]{1,0:T(8,128)(2,1)S(1)}, u32[]{:S(2)}, u32[]{:S(2)}) collective-permute-start(bf16[256,512]{1,0:T(8,128)(2,1)S(1)} %collective-permute-done.2), channel_id=1, source_target_pairs={{448,0},{0,64},{64,128},{128,192},{192,256},{256,320},{320,384},{3... | collective-permute-start | bytes 786440 | tf_op jit(solution)/shard_map/ppermute | solution.py:13
  45.8 4.4 %collective-permute-done.3 = bf16[256,512]{1,0:T(8,128)(2,1)S(1)} collective-permute-done((bf16[256,512]{1,0:T(8,128)(2,1)S(1)}, bf16[256,512]{1,0:T(8,128)(2,1)S(1)}, u32[]{:S(2)}, u32[]{:S(2)}) %collective-permute-start.3) | collective-permute-done | bytes 262176 | tf_op jit(solution)/shard_map/ppermute | solution.py:13
  50.2 5.4 %collective-permute-start.4 = (bf16[256,512]{1,0:T(8,128)(2,1)S(1)}, bf16[256,512]{1,0:T(8,128)(2,1)S(1)}, u32[]{:S(2)}, u32[]{:S(2)}) collective-permute-start(bf16[256,512]{1,0:T(8,128)(2,1)S(1)} %collective-permute-done.3), channel_id=1, source_target_pairs={{448,0},{0,64},{64,128},{128,192},{192,256},{256,320},{320,384},{3... | collective-permute-start | bytes 786440 | tf_op jit(solution)/shard_map/ppermute | solution.py:13
  56.1 4.0 collective-permute-done.4
  60.1 5.4 %collective-permute-start.5 = (bf16[256,512]{1,0:T(8,128)(2,1)S(1)}, bf16[256,512]{1,0:T(8,128)(2,1)S(1)}, u32[]{:S(2)}, u32[]{:S(2)}) collective-permute-start(bf16[256,512]{1,0:T(8,128)(2,1)S(1)} %collective-permute-done.4), channel_id=1, source_target_pairs={{448,0},{0,64},{64,128},{128,192},{192,256},{256,320},{320,384},{3... | collective-permute-start | bytes 786440 | tf_op jit(solution)/shard_map/ppermute | solution.py:13
  66.0 3.9 collective-permute-done.5
  70.0 5.4 %collective-permute-start.6 = (bf16[256,512]{1,0:T(8,128)(2,1)S(1)}, bf16[256,512]{1,0:T(8,128)(2,1)S(1)}, u32[]{:S(2)}, u32[]{:S(2)}) collective-permute-start(bf16[256,512]{1,0:T(8,128)(2,1)S(1)} %collective-permute-done.5), channel_id=1, source_target_pairs={{448,0},{0,64},{64,128},{128,192},{192,256},{256,320},{320,384},{3... | collective-permute-start | bytes 786440 | tf_op jit(solution)/shard_map/ppermute | solution.py:13
  75.9 3.9 collective-permute-done.6
  81.7 5.5 %collective-permute-start.7 = (bf16[256,512]{1,0:T(8,128)(2,1)S(1)}, bf16[256,512]{1,0:T(8,128)(2,1)S(1)}, u32[]{:S(2)}, u32[]{:S(2)}) collective-permute-start(bf16[256,512]{1,0:T(8,128)(2,1)S(1)} %fusion.1), channel_id=1, source_target_pairs={{448,0},{0,64},{64,128},{128,192},{192,256},{256,320},{320,384},{3... | collective-permute-start | bytes 786440 | tf_op jit(solution)/shard_map/ppermute | solution.py:13
  88.7 1.9 collective-permute-done.7
  90.8 5.3 %collective-permute-start.8 = (bf16[256,512]{1,0:T(8,128)(2,1)S(1)}, bf16[256,512]{1,0:T(8,128)(2,1)S(1)}, u32[]{:S(2)}, u32[]{:S(2)}) collective-permute-start(bf16[256,512]{1,0:T(8,128)(2,1)S(1)} %add_convert_fusion.6), channel_id=1, source_target_pairs={{448,0},{0,64},{64,128},{128,192},{192,256},{256,320},{320,384},{3... | collective-permute-start | bytes 786440 | tf_op jit(solution)/shard_map/ppermute | solution.py:13
  96.5 5.1 %collective-permute-done.8 = bf16[256,512]{1,0:T(8,128)(2,1)S(1)} collective-permute-done((bf16[256,512]{1,0:T(8,128)(2,1)S(1)}, bf16[256,512]{1,0:T(8,128)(2,1)S(1)}, u32[]{:S(2)}, u32[]{:S(2)}) %collective-permute-start.8) | collective-permute-done | bytes 262176 | tf_op jit(solution)/shard_map/ppermute | solution.py:13
  101.7 5.3 %collective-permute-start.9 = (bf16[256,512]{1,0:T(8,128)(2,1)S(1)}, bf16[256,512]{1,0:T(8,128)(2,1)S(1)}, u32[]{:S(2)}, u32[]{:S(2)}) collective-permute-start(bf16[256,512]{1,0:T(8,128)(2,1)S(1)} %add_convert_fusion.5), channel_id=1, source_target_pairs={{448,0},{0,64},{64,128},{128,192},{192,256},{256,320},{320,384},{3... | collective-permute-start | bytes 786440 | tf_op jit(solution)/shard_map/ppermute | solution.py:13
  107.4 4.3 collective-permute-done.9
  111.8 5.4 %collective-permute-start.10 = (bf16[256,512]{1,0:T(8,128)(2,1)S(1)}, bf16[256,512]{1,0:T(8,128)(2,1)S(1)}, u32[]{:S(2)}, u32[]{:S(2)}) collective-permute-start(bf16[256,512]{1,0:T(8,128)(2,1)S(1)} %add_convert_fusion.4), channel_id=1, source_target_pairs={{448,0},{0,64},{64,128},{128,192},{192,256},{256,320},{320,384},{3... | collective-permute-start | bytes 786440 | tf_op jit(solution)/shard_map/ppermute | solution.py:13
  117.9 3.8 collective-permute-done.10
  121.8 5.4 %collective-permute-start.11 = (bf16[256,512]{1,0:T(8,128)(2,1)S(1)}, bf16[256,512]{1,0:T(8,128)(2,1)S(1)}, u32[]{:S(2)}, u32[]{:S(2)}) collective-permute-start(bf16[256,512]{1,0:T(8,128)(2,1)S(1)} %add_convert_fusion.3), channel_id=1, source_target_pairs={{448,0},{0,64},{64,128},{128,192},{192,256},{256,320},{320,384},{3... | collective-permute-start | bytes 786440 | tf_op jit(solution)/shard_map/ppermute | solution.py:13
  127.6 4.1 collective-permute-done.11
  131.8 5.4 %collective-permute-start.12 = (bf16[256,512]{1,0:T(8,128)(2,1)S(1)}, bf16[256,512]{1,0:T(8,128)(2,1)S(1)}, u32[]{:S(2)}, u32[]{:S(2)}) collective-permute-start(bf16[256,512]{1,0:T(8,128)(2,1)S(1)} %add_convert_fusion.2), channel_id=1, source_target_pairs={{448,0},{0,64},{64,128},{128,192},{192,256},{256,320},{320,384},{3... | collective-permute-start | bytes 786440 | tf_op jit(solution)/shard_map/ppermute | solution.py:13
  137.2 1.8 convolution_bitcast_fusion
  139.2 2.4 collective-permute-done.12
  141.7 5.4 %collective-permute-start.13 = (bf16[256,512]{1,0:T(8,128)(2,1)S(1)}, bf16[256,512]{1,0:T(8,128)(2,1)S(1)}, u32[]{:S(2)}, u32[]{:S(2)}) collective-permute-start(bf16[256,512]{1,0:T(8,128)(2,1)S(1)} %add_convert_fusion.1), channel_id=1, source_target_pairs={{448,0},{0,64},{64,128},{128,192},{192,256},{256,320},{320,384},{3... | collective-permute-start | bytes 786440 | tf_op jit(solution)/shard_map/ppermute | solution.py:13
  147.4 4.2 collective-permute-done.13
  151.7 5.4 %collective-permute-start.14 = (bf16[256,512]{1,0:T(8,128)(2,1)S(1)}, bf16[256,512]{1,0:T(8,128)(2,1)S(1)}, u32[]{:S(2)}, u32[]{:S(2)}) collective-permute-start(bf16[256,512]{1,0:T(8,128)(2,1)S(1)} %add_convert_fusion), channel_id=1, source_target_pairs={{448,0},{0,64},{64,128},{128,192},{192,256},{256,320},{320,384},{3... | collective-permute-start | bytes 786440 | tf_op jit(solution)/shard_map/ppermute | solution.py:13
  158.4 268.6 %all-reduce.2.cloned.1.call-done = f32[1024,512]{0,1:T(8,128)} async-done(((f32[1024,512]{0,1:T(8,128)}), f32[1024,512]{0,1:T(8,128)}) %all-reduce.2.cloned.1.call-update) | async-done | bytes 2097168 | tf_op jit(solution)/shard_map/psum | solution.py:43
  427.0 2.9 copy.7
  (74 shorter events, 14.7 us)
Async XLA Ops:
  7.2 9.6 %copy-start = (bf16[1024,512]{1,0:T(8,128)(2,1)S(1)}, bf16[1024,512]{1,0:T(8,128)(2,1)}, u32[]{:S(2)}) copy-start(bf16[1024,512]{1,0:T(8,128)(2,1)} %param.5) | copy-start | bytes 3145732
  7.2 419.9 %all-reduce.2.cloned.1.call-start = ((), (), s32[]{:S(2)}) async-start(), calls=%async_computation | async-start | bytes 4194304 | tf_op jit(solution)/shard_map/psum | solution.py:43
  9.5 10.5 %collective-permute-start = (bf16[256,512]{1,0:T(8,128)(2,1)S(1)}, bf16[256,512]{1,0:T(8,128)(2,1)S(1)}, u32[]{:S(2)}, u32[]{:S(2)}) collective-permute-start(bf16[256,512]{1,0:T(8,128)(2,1)S(1)} %fusion.3), channel_id=1, source_target_pairs={{448,0},{0,64},{64,128},{128,192},{192,256},{256,320},{320,384},{3... | collective-permute-start | bytes 786440 | tf_op jit(solution)/shard_map/ppermute | solution.py:13
  20.0 9.6 %collective-permute-start.1 = (bf16[256,512]{1,0:T(8,128)(2,1)S(1)}, bf16[256,512]{1,0:T(8,128)(2,1)S(1)}, u32[]{:S(2)}, u32[]{:S(2)}) collective-permute-start(bf16[256,512]{1,0:T(8,128)(2,1)S(1)} %collective-permute-done), channel_id=1, source_target_pairs={{448,0},{0,64},{64,128},{128,192},{192,256},{256,320},{320,384},{3... | collective-permute-start | bytes 786440 | tf_op jit(solution)/shard_map/ppermute | solution.py:13
  29.6 10.7 %collective-permute-start.2 = (bf16[256,512]{1,0:T(8,128)(2,1)S(1)}, bf16[256,512]{1,0:T(8,128)(2,1)S(1)}, u32[]{:S(2)}, u32[]{:S(2)}) collective-permute-start(bf16[256,512]{1,0:T(8,128)(2,1)S(1)} %collective-permute-done.1), channel_id=1, source_target_pairs={{448,0},{0,64},{64,128},{128,192},{192,256},{256,320},{320,384},{3... | collective-permute-start | bytes 786440 | tf_op jit(solution)/shard_map/ppermute | solution.py:13
  40.3 35.3 %copy-start.3 = (bf16[256,512]{1,0:T(8,128)(2,1)}, bf16[256,512]{1,0:T(8,128)(2,1)S(1)}, u32[]{:S(2)}) copy-start(bf16[256,512]{1,0:T(8,128)(2,1)S(1)} %collective-permute-done.2) | copy-start | bytes 786436
  40.3 9.8 %collective-permute-start.3 = (bf16[256,512]{1,0:T(8,128)(2,1)S(1)}, bf16[256,512]{1,0:T(8,128)(2,1)S(1)}, u32[]{:S(2)}, u32[]{:S(2)}) collective-permute-start(bf16[256,512]{1,0:T(8,128)(2,1)S(1)} %collective-permute-done.2), channel_id=1, source_target_pairs={{448,0},{0,64},{64,128},{128,192},{192,256},{256,320},{320,384},{3... | collective-permute-start | bytes 786440 | tf_op jit(solution)/shard_map/ppermute | solution.py:13
  50.2 25.2 %copy-start.5 = (bf16[256,512]{1,0:T(8,128)(2,1)}, bf16[256,512]{1,0:T(8,128)(2,1)S(1)}, u32[]{:S(2)}) copy-start(bf16[256,512]{1,0:T(8,128)(2,1)S(1)} %collective-permute-done.3) | copy-start | bytes 786436
  50.2 9.9 %collective-permute-start.4 = (bf16[256,512]{1,0:T(8,128)(2,1)S(1)}, bf16[256,512]{1,0:T(8,128)(2,1)S(1)}, u32[]{:S(2)}, u32[]{:S(2)}) collective-permute-start(bf16[256,512]{1,0:T(8,128)(2,1)S(1)} %collective-permute-done.3), channel_id=1, source_target_pairs={{448,0},{0,64},{64,128},{128,192},{192,256},{256,320},{320,384},{3... | collective-permute-start | bytes 786440 | tf_op jit(solution)/shard_map/ppermute | solution.py:13
  60.1 9.9 %collective-permute-start.5 = (bf16[256,512]{1,0:T(8,128)(2,1)S(1)}, bf16[256,512]{1,0:T(8,128)(2,1)S(1)}, u32[]{:S(2)}, u32[]{:S(2)}) collective-permute-start(bf16[256,512]{1,0:T(8,128)(2,1)S(1)} %collective-permute-done.4), channel_id=1, source_target_pairs={{448,0},{0,64},{64,128},{128,192},{192,256},{256,320},{320,384},{3... | collective-permute-start | bytes 786440 | tf_op jit(solution)/shard_map/ppermute | solution.py:13
  66.0 14.5 %copy-start.7 = (s32[256]{0:T(256)S(1)}, s32[256]{0:T(256)}, u32[]{:S(2)}) copy-start(s32[256]{0:T(256)} %param.7) | copy-start | bytes 3076
  70.0 9.9 %collective-permute-start.6 = (bf16[256,512]{1,0:T(8,128)(2,1)S(1)}, bf16[256,512]{1,0:T(8,128)(2,1)S(1)}, u32[]{:S(2)}, u32[]{:S(2)}) collective-permute-start(bf16[256,512]{1,0:T(8,128)(2,1)S(1)} %collective-permute-done.5), channel_id=1, source_target_pairs={{448,0},{0,64},{64,128},{128,192},{192,256},{256,320},{320,384},{3... | collective-permute-start | bytes 786440 | tf_op jit(solution)/shard_map/ppermute | solution.py:13
  81.4 6.5 %copy-start.4 = (bf16[256,512]{1,0:T(8,128)(2,1)S(1)}, bf16[256,512]{1,0:T(8,128)(2,1)}, u32[]{:S(2)}) copy-start(bf16[256,512]{1,0:T(8,128)(2,1)} %copy-done.3) | copy-start | bytes 786436
  81.7 6.6 %copy-start.6 = (bf16[256,512]{1,0:T(8,128)(2,1)S(1)}, bf16[256,512]{1,0:T(8,128)(2,1)}, u32[]{:S(2)}) copy-start(bf16[256,512]{1,0:T(8,128)(2,1)} %copy-done.5) | copy-start | bytes 786436
  81.7 8.8 %collective-permute-start.7 = (bf16[256,512]{1,0:T(8,128)(2,1)S(1)}, bf16[256,512]{1,0:T(8,128)(2,1)S(1)}, u32[]{:S(2)}, u32[]{:S(2)}) collective-permute-start(bf16[256,512]{1,0:T(8,128)(2,1)S(1)} %fusion.1), channel_id=1, source_target_pairs={{448,0},{0,64},{64,128},{128,192},{192,256},{256,320},{320,384},{3... | collective-permute-start | bytes 786440 | tf_op jit(solution)/shard_map/ppermute | solution.py:13
  90.8 10.8 %collective-permute-start.8 = (bf16[256,512]{1,0:T(8,128)(2,1)S(1)}, bf16[256,512]{1,0:T(8,128)(2,1)S(1)}, u32[]{:S(2)}, u32[]{:S(2)}) collective-permute-start(bf16[256,512]{1,0:T(8,128)(2,1)S(1)} %add_convert_fusion.6), channel_id=1, source_target_pairs={{448,0},{0,64},{64,128},{128,192},{192,256},{256,320},{320,384},{3... | collective-permute-start | bytes 786440 | tf_op jit(solution)/shard_map/ppermute | solution.py:13
  101.7 10.0 %collective-permute-start.9 = (bf16[256,512]{1,0:T(8,128)(2,1)S(1)}, bf16[256,512]{1,0:T(8,128)(2,1)S(1)}, u32[]{:S(2)}, u32[]{:S(2)}) collective-permute-start(bf16[256,512]{1,0:T(8,128)(2,1)S(1)} %add_convert_fusion.5), channel_id=1, source_target_pairs={{448,0},{0,64},{64,128},{128,192},{192,256},{256,320},{320,384},{3... | collective-permute-start | bytes 786440 | tf_op jit(solution)/shard_map/ppermute | solution.py:13
  111.8 9.9 %collective-permute-start.10 = (bf16[256,512]{1,0:T(8,128)(2,1)S(1)}, bf16[256,512]{1,0:T(8,128)(2,1)S(1)}, u32[]{:S(2)}, u32[]{:S(2)}) collective-permute-start(bf16[256,512]{1,0:T(8,128)(2,1)S(1)} %add_convert_fusion.4), channel_id=1, source_target_pairs={{448,0},{0,64},{64,128},{128,192},{192,256},{256,320},{320,384},{3... | collective-permute-start | bytes 786440 | tf_op jit(solution)/shard_map/ppermute | solution.py:13
  117.9 19.2 %copy-start.2 = (bf16[256,1024]{1,0:T(8,128)(2,1)S(1)}, bf16[256,1024]{1,0:T(8,128)(2,1)}, u32[]{:S(2)}) copy-start(bf16[256,1024]{1,0:T(8,128)(2,1)} %param.4) | copy-start | bytes 1572868
  121.8 9.9 %collective-permute-start.11 = (bf16[256,512]{1,0:T(8,128)(2,1)S(1)}, bf16[256,512]{1,0:T(8,128)(2,1)S(1)}, u32[]{:S(2)}, u32[]{:S(2)}) collective-permute-start(bf16[256,512]{1,0:T(8,128)(2,1)S(1)} %add_convert_fusion.3), channel_id=1, source_target_pairs={{448,0},{0,64},{64,128},{128,192},{192,256},{256,320},{320,384},{3... | collective-permute-start | bytes 786440 | tf_op jit(solution)/shard_map/ppermute | solution.py:13
  131.8 9.9 %collective-permute-start.12 = (bf16[256,512]{1,0:T(8,128)(2,1)S(1)}, bf16[256,512]{1,0:T(8,128)(2,1)S(1)}, u32[]{:S(2)}, u32[]{:S(2)}) collective-permute-start(bf16[256,512]{1,0:T(8,128)(2,1)S(1)} %add_convert_fusion.2), channel_id=1, source_target_pairs={{448,0},{0,64},{64,128},{128,192},{192,256},{256,320},{320,384},{3... | collective-permute-start | bytes 786440 | tf_op jit(solution)/shard_map/ppermute | solution.py:13
  141.7 9.9 %collective-permute-start.13 = (bf16[256,512]{1,0:T(8,128)(2,1)S(1)}, bf16[256,512]{1,0:T(8,128)(2,1)S(1)}, u32[]{:S(2)}, u32[]{:S(2)}) collective-permute-start(bf16[256,512]{1,0:T(8,128)(2,1)S(1)} %add_convert_fusion.1), channel_id=1, source_target_pairs={{448,0},{0,64},{64,128},{128,192},{192,256},{256,320},{320,384},{3... | collective-permute-start | bytes 786440 | tf_op jit(solution)/shard_map/ppermute | solution.py:13
  151.7 278.2 %collective-permute-start.14 = (bf16[256,512]{1,0:T(8,128)(2,1)S(1)}, bf16[256,512]{1,0:T(8,128)(2,1)S(1)}, u32[]{:S(2)}, u32[]{:S(2)}) collective-permute-start(bf16[256,512]{1,0:T(8,128)(2,1)S(1)} %add_convert_fusion), channel_id=1, source_target_pairs={{448,0},{0,64},{64,128},{128,192},{192,256},{256,320},{320,384},{3... | collective-permute-start | bytes 786440 | tf_op jit(solution)/shard_map/ppermute | solution.py:13
  158.4 271.5 %copy-start.1 = (bf16[256,512]{1,0:T(8,128)(2,1)S(1)}, bf16[256,512]{1,0:T(8,128)(2,1)}, u32[]{:S(2)}) copy-start(bf16[256,512]{1,0:T(8,128)(2,1)} %param.6) | copy-start | bytes 786436
Sparse Core Ops, SparseCore 0:
  139.1 287.9 all-reduce.1
where the time goes:
time: 439 us; the launch traced here: 438 us
  waiting for transfers between devices  321 us (73%)
  starting transfers between devices  82.5 us (19%)
  between operations  14.7 us (3%)
  matrix products  11.7 us (3%)
  other arithmetic  4.69 us (1%)
    psum x1, waiting for transfers between devices, finish_audio(): grad_weight = lax.psum(weight_part, ('blk', 'dp'))  269 us
    ppermute x15, starting transfers between devices, shifted(): return lax.ppermute(block, axis, route)  82.5 us
    ppermute x15, waiting for transfers between devices, shifted(): return lax.ppermute(block, axis, route)  52.8 us
  transfers between devices with their start and end apart: 16, of which 15 were waited for; matrix products, arithmetic and copies ran while one was open for 3% of the time, Pallas kernels for 0%

commit v1 on v0

v1 whole, which is shorter than its diff:
```python
import jax
import jax.numpy as jnp
from jax import lax
from jax.sharding import Mesh, PartitionSpec as P

SCALE = 100.0
EPS = 1e-06
FINE = ("zh", "core", "zl", "x", "y")
PLANE = ("x", "y")
COLUMN = ("zh", "zl")


def shifted(block, axis, distance):
    count = lax.axis_size(axis)
    return lax.ppermute(block, axis, [(i, (i + distance) % count) for i in range(count)])


def exchanged(block, axes):
    return lax.all_to_all(block, axes, split_axis=0, concat_axis=0, tiled=True)


def copies(block, count):
    return jnp.broadcast_to(block[None], (count,) + block.shape).reshape(
        (count * block.shape[0],) + block.shape[1:]
    )


def folded(block, count):
    parts = block.reshape((count, block.shape[0] // count) + block.shape[1:])
    return jnp.sum(parts.astype(jnp.float32), axis=0)


def dot(a, b, da, db):
    return lax.dot_general(a, b, (((da,), (db,)), ((), ())), preferred_element_type=jnp.float32)


def summed_everywhere(own, other):
    core = lax.axis_index("core")
    plane = lax.axis_size(PLANE)
    column = lax.axis_size(COLUMN)
    half = (own + shifted(other.astype(jnp.bfloat16), "core", 1)).astype(jnp.bfloat16)
    part = folded(exchanged(half, PLANE), plane).astype(jnp.bfloat16)
    part = folded(exchanged(copies(part, column), COLUMN), column).astype(jnp.bfloat16)
    half = exchanged(copies(part, plane), PLANE)
    there = shifted(half, "core", 1)
    low = jnp.where(core == 0, half, there)
    high = jnp.where(core == 0, there, half)
    return jnp.concatenate([low, high]).astype(jnp.float32)


def body(audio_features, proj_weight, text_raw, positive):
    rows = audio_features.shape[0]
    width = text_raw.shape[1]
    channels = audio_features.shape[1]
    chips = lax.axis_size("zh")
    cores = lax.axis_size("core")
    core = lax.axis_index("core")
    chip = lax.axis_index("zh")
    text_f = text_raw.astype(jnp.float32)
    text_scale = lax.rsqrt(jnp.sum(text_f * text_f, axis=1, keepdims=True) + EPS)
    text = text_f * text_scale
    text_b = text.astype(jnp.bfloat16)
    mine = [text_b] + [shifted(text_b, "zh", k) for k in range(1, chips)]
    beside = [shifted(piece, "core", 1) for piece in mine]
    proj = dot(audio_features, proj_weight, 1, 0)
    audio_scale = lax.rsqrt(jnp.sum(proj * proj, axis=1, keepdims=True) + EPS)
    audio = proj * audio_scale
    audio_b = audio.astype(jnp.bfloat16)
    pieces = mine + beside
    offsets = jnp.arange(rows, dtype=jnp.int32)
    scores = [SCALE * dot(audio_b, piece, 1, 1) for piece in pieces]
    peak = jnp.max(jnp.stack([jnp.max(s, axis=1) for s in scores]), axis=0)
    total = sum(jnp.sum(jnp.exp(s - peak[:, None]), axis=1) for s in scores)
    lse = peak + jnp.log(total)
    tiles = []
    for n, s in enumerate(scores):
        column = core if n < chips else 1 - core
        block = (chip - n % chips + chips) % chips * cores + column
        ids = block * rows + offsets
        match = jnp.where(positive[:, None] == ids[None, :], 1.0, 0.0)
        tiles.append((jnp.exp(s - lse[:, None]) - match).astype(jnp.bfloat16))
    audio_grad = SCALE * sum(dot(tile, piece, 1, 0) for tile, piece in zip(tiles, pieces))
    along = jnp.sum(audio * audio_grad, axis=1, keepdims=True)
    proj_grad = ((audio_grad - audio * along) * audio_scale).astype(jnp.bfloat16)
    half = channels // cores
    own_features = lax.dynamic_slice_in_dim(audio_features, core * half, half, 1)
    other_features = lax.dynamic_slice_in_dim(audio_features, (1 - core) * half, half, 1)
    grad_weight = summed_everywhere(
        dot(own_features, proj_grad, 0, 0), dot(other_features, proj_grad, 0, 0)
    )
    grad_features = dot(proj_grad, proj_weight, 1, 1).astype(jnp.bfloat16)
    sums = []
    for n in range(chips):
        over = SCALE * dot(tiles[chips + n], audio_b, 0, 0)
        kept = SCALE * dot(tiles[n], audio_b, 0, 0)
        sums.append(kept + shifted(over.astype(jnp.bfloat16), "core", 1))
    text_grad = sums[0]
    for n in range(1, chips):
        text_grad = text_grad + shifted(sums[n].astype(jnp.bfloat16), "zh", -n)
    text_along = jnp.sum(text * text_grad, axis=1, keepdims=True)
    grad_text = (text_grad - text * text_along) * text_scale
    return (grad_weight, grad_features, grad_text)


def solution(mesh):
    split = (4, 2, 2, 4, 8)
    fine = Mesh(mesh.devices.reshape(split), FINE)
    rows = P(FINE, None)
    return jax.shard_map(
        body,
        mesh=fine,
        in_specs=(rows, P(), rows, P(FINE)),
        out_specs=(P(), rows, rows),
        check_vma=False,
    )
```

time: 439 us -> 153 us (0.35)
  waiting for transfers between devices: 321 us -> 34.5 us
  between operations: 14.7 us -> 1.34 us
  matrix products: 11.7 us -> 24.5 us
    psum x1 -> x0, waiting for transfers between devices: 269 us -> none  [finish_audio(): grad_weight = lax.psum(weight_part, ('blk', 'dp'))]
    ppermute x15 -> x16, waiting for transfers between devices: 52.8 us -> 26.4 us  [shifted(): lax.ppermute(block, axis, [(i, (i + distance) % count) for i in range(cou...]
    ppermute x15 -> x16, starting transfers between devices: 82.5 us -> 58.4 us  [shifted(): lax.ppermute(block, axis, [(i, (i + distance) % count) for i in range(cou...]
    all_to_all x0 -> x3, starting transfers between devices: none -> 22.7 us  [exchanged(): return lax.all_to_all(block, axes, split_axis=0, concat_axis=0, tiled=True)]
    dot_general x27 -> x28, matrix products: 11.7 us -> 24.5 us  [dot(): lax.dot_general(a, b, (((da,), (db,)), ((), ())), preferred_element_type=...]
    all_to_all x0 -> x3, waiting for transfers between devices: none -> 8.08 us  [exchanged(): return lax.all_to_all(block, axes, split_axis=0, concat_axis=0, tiled=True)]
  transfers between devices with their start and end apart: 16 -> 19, of which waited for: 15 -> 6; matrix products, arithmetic and copies ran while one was open for 3% -> 13% of each run, Pallas kernels for 0% -> 0%
where the time goes in v1:
time: 153 us; the launch traced here: 152 us
  starting transfers between devices  81.2 us (53%)
  waiting for transfers between devices  34.5 us (23%)
  matrix products  24.5 us (16%)
  other arithmetic  7.79 us (5%)
  local copies, waits for them, and re-layouts  2.43 us (2%)
    ppermute x16, starting transfers between devices, shifted(): lax.ppermute(block, axis, [(i, (i + distance) % count) for i in range(cou...  58.4 us
    ppermute x16, waiting for transfers between devices, shifted(): lax.ppermute(block, axis, [(i, (i + distance) % count) for i in range(cou...  26.4 us
    dot_general x28, matrix products, dot(): lax.dot_general(a, b, (((da,), (db,)), ((), ())), preferred_element_type=...  24.5 us
    all_to_all x3, starting transfers between devices, exchanged(): return lax.all_to_all(block, axes, split_axis=0, concat_axis=0, tiled=True)  22.7 us
    all_to_all x3, waiting for transfers between devices, exchanged(): return lax.all_to_all(block, axes, split_axis=0, concat_axis=0, tiled=True)  8.08 us
  transfers between devices with their start and end apart: 19, of which 6 were waited for; matrix products, arithmetic and copies ran while one was open for 13% of the time, Pallas kernels for 0%

profile of v1, /device:TPU:1, one launch (start us, length us, event | category | flops | bytes accessed | tf_op | source)
XLA Modules:
  0.0 151.7 jit_solution(760887117572952788)
XLA Ops:
  2.9 11.5 %collective-permute-start.2 = (bf16[256,512]{1,0:T(8,128)(2,1)S(1)}, bf16[256,512]{1,0:T(8,128)(2,1)S(1)}, u32[]{:S(2)}, u32[]{:S(2)}) collective-permute-start(bf16[256,512]{1,0:T(8,128)(2,1)S(1)} %fusion.11), channel_id=1, source_target_pairs={{0,384},{128,0},{256,128},{384,256},{1,385},{129,1},{257,129},{385... | collective-permute-start | bytes 786440 | tf_op jit(solution)/shard_map/ppermute | solution.py:15
  14.4 1.9 %collective-permute-start.1 = (bf16[256,512]{1,0:T(8,128)(2,1)S(1)}, bf16[256,512]{1,0:T(8,128)(2,1)}, u32[]{:S(2)}, u32[]{:S(2)}) collective-permute-start(bf16[256,512]{1,0:T(8,128)(2,1)S(1)} %fusion.11), channel_id=1, source_target_pairs={{0,256},{128,384},{256,0},{384,128},{1,257},{129,385},{257,1},{385... | collective-permute-start | bytes 786440 | tf_op jit(solution)/shard_map/ppermute | solution.py:15
  16.3 4.2 %collective-permute-start = (bf16[256,512]{1,0:T(8,128)(2,1)S(1)}, bf16[256,512]{1,0:T(8,128)(2,1)}, u32[]{:S(2)}, u32[]{:S(2)}) collective-permute-start(bf16[256,512]{1,0:T(8,128)(2,1)S(1)} %fusion.11), channel_id=1, source_target_pairs={{0,128},{128,256},{256,384},{384,0},{1,129},{129,257},{257,385},{3... | collective-permute-start | bytes 786440 | tf_op jit(solution)/shard_map/ppermute | solution.py:15
  20.6 3.4 %collective-permute-start.3 = (bf16[256,512]{1,0:T(8,128)(2,1)S(1)}, bf16[256,512]{1,0:T(8,128)(2,1)S(1)}, u32[]{:S(2)}, u32[]{:S(2)}) collective-permute-start(bf16[256,512]{1,0:T(8,128)(2,1)S(1)} %fusion.11), channel_id=1, source_target_pairs={{0,64},{64,0},{1,65},{65,1},{2,66},{66,2},{3,67},{67,3},{4,68},{68... | collective-permute-start | bytes 786440 | tf_op jit(solution)/shard_map/ppermute | solution.py:15
  24.1 1.6 %multiply_reduce_fusion.1 = (f32[256]{0:T(256)S(1)}, f32[256,512]{1,0:T(8,128)S(1)}) fusion(bf16[256,1024]{1,0:T(8,128)(2,1)} %param.4, bf16[1024,512]{1,0:T(8,128)(2,1)S(1)} %copy-done), kind=kOutput, calls=%fused_computation.47 | convolution fusion | flops 268697344 | bytes 2098176 | tf_op jit(solution)/shard_map/dot_general | solution.py:34
  26.2 10.0 %collective-permute-done.2 = bf16[256,512]{1,0:T(8,128)(2,1)S(1)} collective-permute-done((bf16[256,512]{1,0:T(8,128)(2,1)S(1)}, bf16[256,512]{1,0:T(8,128)(2,1)S(1)}, u32[]{:S(2)}, u32[]{:S(2)}) %collective-permute-start.2) | collective-permute-done | bytes 262176 | tf_op jit(solution)/shard_map/ppermute | solution.py:15
  36.2 3.5 %collective-permute-start.6 = (bf16[256,512]{1,0:T(8,128)(2,1)S(1)}, bf16[256,512]{1,0:T(8,128)(2,1)S(1)}, u32[]{:S(2)}, u32[]{:S(2)}) collective-permute-start(bf16[256,512]{1,0:T(8,128)(2,1)S(1)} %collective-permute-done.2), channel_id=1, source_target_pairs={{0,64},{64,0},{1,65},{65,1},{2,66},{66,2},{3,67},{67,3},{4,68},{68... | collective-permute-start | bytes 786440 | tf_op jit(solution)/shard_map/ppermute | solution.py:15
  39.9 1.9 %collective-permute-start.5 = (bf16[256,512]{1,0:T(8,128)(2,1)}, bf16[256,512]{1,0:T(8,128)(2,1)S(1)}, u32[]{:S(2)}, u32[]{:S(2)}) collective-permute-start(bf16[256,512]{1,0:T(8,128)(2,1)} %collective-permute-done.1), channel_id=1, source_target_pairs={{0,64},{64,0},{1,65},{65,1},{2,66},{66,2},{3,67},{67,3},{4,68},{68... | collective-permute-start | bytes 786440 | tf_op jit(solution)/shard_map/ppermute | solution.py:15
  43.1 2.4 %collective-permute-start.4 = (bf16[256,512]{1,0:T(8,128)(2,1)}, bf16[256,512]{1,0:T(8,128)(2,1)S(1)}, u32[]{:S(2)}, u32[]{:S(2)}) collective-permute-start(bf16[256,512]{1,0:T(8,128)(2,1)} %collective-permute-done), channel_id=1, source_target_pairs={{0,64},{64,0},{1,65},{65,1},{2,66},{66,2},{3,67},{67,3},{4,68},{68... | collective-permute-start | bytes 786440 | tf_op jit(solution)/shard_map/ppermute | solution.py:15
  50.5 1.3 convolution_add_fusion.2
  51.8 1.3 fusion.4
  55.3 1.9 %collective-permute-start.7 = (bf16[512,512]{1,0:T(8,128)(2,1)}, bf16[512,512]{1,0:T(8,128)(2,1)}, u32[]{:S(2)}, u32[]{:S(2)}) collective-permute-start(bf16[512,512]{1,0:T(8,128)(2,1)} %convolution_convert_fusion.1), channel_id=1, source_target_pairs={{0,64},{64,0},{1,65},{65,1},{2,66},{66,2},{3,67},{67,3},{4,68},{68... | collective-permute-start | bytes 1572872 | tf_op jit(solution)/shard_map/ppermute | solution.py:15
  57.2 2.2 %collective-permute-done.7 = bf16[512,512]{1,0:T(8,128)(2,1)} collective-permute-done((bf16[512,512]{1,0:T(8,128)(2,1)}, bf16[512,512]{1,0:T(8,128)(2,1)}, u32[]{:S(2)}, u32[]{:S(2)}) %collective-permute-start.7) | collective-permute-done | bytes 524320 | tf_op jit(solution)/shard_map/ppermute | solution.py:15
  59.4 2.2 %add_convert_fusion = bf16[512,512]{1,0:T(8,128)(2,1)} fusion(bf16[512,512]{1,0:T(8,128)(2,1)} %collective-permute-done.7, bf16[256,512]{1,0:T(8,128)(2,1)S(1)} %multiply_convert_fusion, bf16[256,1024]{1,0:T(8,128)(2,1)} %param.4, s32[]{:T(128)S(6)} %select_n.71), kind=kOutput, calls=%fused_computation.31 | convolution fusion | flops 135004160 | bytes 1572868 | tf_op jit(solution)/shard_map/dot_general | solution.py:34
  61.7 9.8 %all-to-all-start = ((bf16[32,16,512]{2,1,0:T(8,128)(2,1)}), bf16[32,16,512]{2,1,0:T(8,128)(2,1)}, u32[]{:S(2)}, u32[]{:S(2)}) async-start(bf16[32,16,512]{2,1,0:T(8,128)(2,1)} %bitcast.42), calls=%async_computation | async-start | bytes 1048576 | tf_op jit(solution)/shard_map/all_to_all | solution.py:19
  72.5 2.3 %collective-permute-start.14 = (bf16[256,512]{1,0:T(8,128)(2,1)}, bf16[256,512]{1,0:T(8,128)(2,1)}, u32[]{:S(2)}, u32[]{:S(2)}) collective-permute-start(bf16[256,512]{1,0:T(8,128)(2,1)} %fusion.8), channel_id=1, source_target_pairs={{0,64},{64,0},{1,65},{65,1},{2,66},{66,2},{3,67},{67,3},{4,68},{68... | collective-permute-start | bytes 786440 | tf_op jit(solution)/shard_map/ppermute | solution.py:15
  76.8 2.0 %collective-permute-start.12 = (bf16[256,512]{1,0:T(8,128)(2,1)}, bf16[256,512]{1,0:T(8,128)(2,1)}, u32[]{:S(2)}, u32[]{:S(2)}) collective-permute-start(bf16[256,512]{1,0:T(8,128)(2,1)} %fusion.7), channel_id=1, source_target_pairs={{0,64},{64,0},{1,65},{65,1},{2,66},{66,2},{3,67},{67,3},{4,68},{68... | collective-permute-start | bytes 786440 | tf_op jit(solution)/shard_map/ppermute | solution.py:15
  78.8 7.5 %all-to-all-done = bf16[32,16,512]{2,1,0:T(8,128)(2,1)} async-done(((bf16[32,16,512]{2,1,0:T(8,128)(2,1)}), bf16[32,16,512]{2,1,0:T(8,128)(2,1)}, u32[]{:S(2)}, u32[]{:S(2)}) %all-to-all-start) | async-done | bytes 524320 | tf_op jit(solution)/shard_map/all_to_all | solution.py:19
  88.0 5.6 %all-to-all-start.1 = ((bf16[8,16,512]{2,1,0:T(8,128)(2,1)}), bf16[8,16,512]{2,1,0:T(8,128)(2,1)S(1)}, u32[]{:S(2)}, u32[]{:S(2)}) async-start(bf16[8,16,512]{2,1,0:T(8,128)(2,1)} %broadcast_in_dim.28), calls=%async_computation.1 | async-start | bytes 262144 | tf_op jit(solution)/shard_map/all_to_all | solution.py:19
  93.9 5.2 %collective-permute-start.10 = (bf16[256,512]{1,0:T(8,128)(2,1)}, bf16[256,512]{1,0:T(8,128)(2,1)}, u32[]{:S(2)}, u32[]{:S(2)}) collective-permute-start(bf16[256,512]{1,0:T(8,128)(2,1)} %fusion.6), channel_id=1, source_target_pairs={{0,64},{64,0},{1,65},{65,1},{2,66},{66,2},{3,67},{67,3},{4,68},{68... | collective-permute-start | bytes 786440 | tf_op jit(solution)/shard_map/ppermute | solution.py:15
  99.1 1.9 %collective-permute-start.9 = (bf16[256,512]{1,0:T(8,128)(2,1)S(1)}, bf16[256,512]{1,0:T(8,128)(2,1)S(1)}, u32[]{:S(2)}, u32[]{:S(2)}) collective-permute-start(bf16[256,512]{1,0:T(8,128)(2,1)S(1)} %fusion.5), channel_id=1, source_target_pairs={{0,64},{64,0},{1,65},{65,1},{2,66},{66,2},{3,67},{67,3},{4,68},{68... | collective-permute-start | bytes 786440 | tf_op jit(solution)/shard_map/ppermute | solution.py:15
  102.5 7.3 %all-to-all-start.2 = ((bf16[32,16,512]{2,1,0:T(8,128)(2,1)}), bf16[32,16,512]{2,1,0:T(8,128)(2,1)}, u32[]{:S(2)}, u32[]{:S(2)}) async-start(bf16[32,16,512]{2,1,0:T(8,128)(2,1)} %broadcast_in_dim.29), calls=%async_computation.2 | async-start | bytes 1048576 | tf_op jit(solution)/shard_map/all_to_all | solution.py:19
  109.9 1.9 %add_convert_fusion.1 = bf16[256,512]{1,0:T(8,128)(2,1)} fusion(bf16[256,512]{1,0:T(8,128)(2,1)} %collective-permute-done.14, bf16[256,512]{1,0:T(8,128)(2,1)S(1)} %multiply_convert_fusion.1, f32[256,256]{0,1:T(8,128)S(1)} %get-tuple-element.24, s32[256]{0:T(256)S(1)} %copy-done.13, f32[256]{0:T(256)S(1)} %log_add_fusion, s32[256]{0:T(256)S(1)} %iota_add_fusion.4), kind=kOutput, calls=%fused_computation.42 | convolution fusion | flops 67960832 | bytes 1051648 | tf_op jit(solution)/shard_map/dot_general | solution.py:34
  111.8 2.3 %collective-permute-start.15 = (bf16[256,512]{1,0:T(8,128)(2,1)}, bf16[256,512]{1,0:T(8,128)(2,1)S(1)}, u32[]{:S(2)}, u32[]{:S(2)}) collective-permute-start(bf16[256,512]{1,0:T(8,128)(2,1)} %add_convert_fusion.1), channel_id=1, source_target_pairs={{0,128},{128,256},{256,384},{384,0},{1,129},{129,257},{257,385},{3... | collective-permute-start | bytes 786440 | tf_op jit(solution)/shard_map/ppermute | solution.py:15
  114.2 1.9 %add_convert_fusion.2 = bf16[256,512]{1,0:T(8,128)(2,1)} fusion(bf16[256,512]{1,0:T(8,128)(2,1)} %collective-permute-done.12, bf16[256,512]{1,0:T(8,128)(2,1)S(1)} %multiply_convert_fusion.1, f32[256,256]{0,1:T(8,128)S(1)} %copy-done.7, s32[256]{0:T(256)S(1)} %copy-done.13, f32[256]{0:T(256)S(1)} %log_add_fusion, s32[256]{0:T(256)S(1)} %iota_add_fusion.5), kind=kOutput, calls=%fused_computation.43 | convolution fusion | flops 67960832 | bytes 1051648 | tf_op jit(solution)/shard_map/dot_general | solution.py:34
  116.1 5.2 %collective-permute-start.13 = (bf16[256,512]{1,0:T(8,128)(2,1)}, bf16[256,512]{1,0:T(8,128)(2,1)S(1)}, u32[]{:S(2)}, u32[]{:S(2)}) collective-permute-start(bf16[256,512]{1,0:T(8,128)(2,1)} %add_convert_fusion.2), channel_id=1, source_target_pairs={{0,256},{128,384},{256,0},{384,128},{1,257},{129,385},{257,1},{385... | collective-permute-start | bytes 786440 | tf_op jit(solution)/shard_map/ppermute | solution.py:15
  121.3 1.9 %add_convert_fusion.3 = bf16[256,512]{1,0:T(8,128)(2,1)} fusion(bf16[256,512]{1,0:T(8,128)(2,1)} %collective-permute-done.10, bf16[256,512]{1,0:T(8,128)(2,1)S(1)} %multiply_convert_fusion.1, f32[256,256]{0,1:T(8,128)S(1)} %copy-done.5, s32[256]{0:T(256)S(1)} %copy-done.13, f32[256]{0:T(256)S(1)} %log_add_fusion, s32[256]{0:T(256)S(1)} %iota_add_fusion.6), kind=kOutput, calls=%fused_computation.44 | convolution fusion | flops 67960832 | bytes 1051648 | tf_op jit(solution)/shard_map/dot_general | solution.py:34
  123.3 5.2 %collective-permute-start.11 = (bf16[256,512]{1,0:T(8,128)(2,1)}, bf16[256,512]{1,0:T(8,128)(2,1)S(1)}, u32[]{:S(2)}, u32[]{:S(2)}) collective-permute-start(bf16[256,512]{1,0:T(8,128)(2,1)} %add_convert_fusion.3), channel_id=1, source_target_pairs={{0,384},{128,0},{256,128},{384,256},{1,385},{129,1},{257,129},{385... | collective-permute-start | bytes 786440 | tf_op jit(solution)/shard_map/ppermute | solution.py:15
  129.7 3.5 %collective-permute-start.8 = (bf16[512,512]{1,0:T(8,128)(2,1)}, bf16[512,512]{1,0:T(8,128)(2,1)S(1)}, u32[]{:S(2)}, u32[]{:S(2)}) collective-permute-start(bf16[512,512]{1,0:T(8,128)(2,1)} %bitcast.1), channel_id=1, source_target_pairs={{0,64},{64,0},{1,65},{65,1},{2,66},{66,2},{3,67},{67,3},{4,68},{68... | collective-permute-start | bytes 1572872 | tf_op jit(solution)/shard_map/ppermute | solution.py:15
  133.3 1.4 collective-permute-done.13
  134.7 12.8 %collective-permute-done.11 = bf16[256,512]{1,0:T(8,128)(2,1)S(1)} collective-permute-done((bf16[256,512]{1,0:T(8,128)(2,1)}, bf16[256,512]{1,0:T(8,128)(2,1)S(1)}, u32[]{:S(2)}, u32[]{:S(2)}) %collective-permute-start.11) | collective-permute-done | bytes 262176 | tf_op jit(solution)/shard_map/ppermute | solution.py:15
  150.1 1.6 %maximum_convert_fusion = f32[1024,512]{1,0:T(8,128)} fusion(bf16[512,512]{1,0:T(8,128)(2,1)S(1)} %get-tuple-element.12, bf16[512,512]{1,0:T(8,128)(2,1)S(1)} %get-tuple-element.11), kind=kLoop, calls=%fused_computation.30 | loop fusion | flops 2097152 | bytes 3145728 | tf_op jit(solution)/shard_map/convert_element_type | solution.py:48
  (86 shorter events, 21.6 us)
Async XLA Ops:
  0.6 23.4 %copy-start = (bf16[1024,512]{1,0:T(8,128)(2,1)S(1)}, bf16[1024,512]{1,0:T(8,128)(2,1)}, u32[]{:S(2)}) copy-start(bf16[1024,512]{1,0:T(8,128)(2,1)} %param.5) | copy-start | bytes 3145732
  2.9 33.3 %collective-permute-start.2 = (bf16[256,512]{1,0:T(8,128)(2,1)S(1)}, bf16[256,512]{1,0:T(8,128)(2,1)S(1)}, u32[]{:S(2)}, u32[]{:S(2)}) collective-permute-start(bf16[256,512]{1,0:T(8,128)(2,1)S(1)} %fusion.11), channel_id=1, source_target_pairs={{0,384},{128,0},{256,128},{384,256},{1,385},{129,1},{257,129},{385... | collective-permute-start | bytes 786440 | tf_op jit(solution)/shard_map/ppermute | solution.py:15
  14.4 25.5 %collective-permute-start.1 = (bf16[256,512]{1,0:T(8,128)(2,1)S(1)}, bf16[256,512]{1,0:T(8,128)(2,1)}, u32[]{:S(2)}, u32[]{:S(2)}) collective-permute-start(bf16[256,512]{1,0:T(8,128)(2,1)S(1)} %fusion.11), channel_id=1, source_target_pairs={{0,256},{128,384},{256,0},{384,128},{1,257},{129,385},{257,1},{385... | collective-permute-start | bytes 786440 | tf_op jit(solution)/shard_map/ppermute | solution.py:15
  16.3 26.8 %collective-permute-start = (bf16[256,512]{1,0:T(8,128)(2,1)S(1)}, bf16[256,512]{1,0:T(8,128)(2,1)}, u32[]{:S(2)}, u32[]{:S(2)}) collective-permute-start(bf16[256,512]{1,0:T(8,128)(2,1)S(1)} %fusion.11), channel_id=1, source_target_pairs={{0,128},{128,256},{256,384},{384,0},{1,129},{129,257},{257,385},{3... | collective-permute-start | bytes 786440 | tf_op jit(solution)/shard_map/ppermute | solution.py:15
  20.6 26.2 %collective-permute-start.3 = (bf16[256,512]{1,0:T(8,128)(2,1)S(1)}, bf16[256,512]{1,0:T(8,128)(2,1)S(1)}, u32[]{:S(2)}, u32[]{:S(2)}) collective-permute-start(bf16[256,512]{1,0:T(8,128)(2,1)S(1)} %fusion.11), channel_id=1, source_target_pairs={{0,64},{64,0},{1,65},{65,1},{2,66},{66,2},{3,67},{67,3},{4,68},{68... | collective-permute-start | bytes 786440 | tf_op jit(solution)/shard_map/ppermute | solution.py:15
  36.2 11.7 %copy-start.9 = (bf16[256,512]{1,0:T(8,128)(2,1)}, bf16[256,512]{1,0:T(8,128)(2,1)S(1)}, u32[]{:S(2)}) copy-start(bf16[256,512]{1,0:T(8,128)(2,1)S(1)} %collective-permute-done.2) | copy-start | bytes 786436
  36.2 11.4 %collective-permute-start.6 = (bf16[256,512]{1,0:T(8,128)(2,1)S(1)}, bf16[256,512]{1,0:T(8,128)(2,1)S(1)}, u32[]{:S(2)}, u32[]{:S(2)}) collective-permute-start(bf16[256,512]{1,0:T(8,128)(2,1)S(1)} %collective-permute-done.2), channel_id=1, source_target_pairs={{0,64},{64,0},{1,65},{65,1},{2,66},{66,2},{3,67},{67,3},{4,68},{68... | collective-permute-start | bytes 786440 | tf_op jit(solution)/shard_map/ppermute | solution.py:15
  39.9 7.9 %collective-permute-start.5 = (bf16[256,512]{1,0:T(8,128)(2,1)}, bf16[256,512]{1,0:T(8,128)(2,1)S(1)}, u32[]{:S(2)}, u32[]{:S(2)}) collective-permute-start(bf16[256,512]{1,0:T(8,128)(2,1)} %collective-permute-done.1), channel_id=1, source_target_pairs={{0,64},{64,0},{1,65},{65,1},{2,66},{66,2},{3,67},{67,3},{4,68},{68... | collective-permute-start | bytes 786440 | tf_op jit(solution)/shard_map/ppermute | solution.py:15
  43.1 8.7 %copy-start.6 = (f32[256,256]{0,1:T(8,128)}, f32[256,256]{0,1:T(8,128)S(1)}, u32[]{:S(2)}) copy-start(f32[256,256]{0,1:T(8,128)S(1)} %get-tuple-element.26) | copy-start | bytes 786436
  43.1 5.0 %collective-permute-start.4 = (bf16[256,512]{1,0:T(8,128)(2,1)}, bf16[256,512]{1,0:T(8,128)(2,1)S(1)}, u32[]{:S(2)}, u32[]{:S(2)}) collective-permute-start(bf16[256,512]{1,0:T(8,128)(2,1)} %collective-permute-done), channel_id=1, source_target_pairs={{0,64},{64,0},{1,65},{65,1},{2,66},{66,2},{3,67},{67,3},{4,68},{68... | collective-permute-start | bytes 786440 | tf_op jit(solution)/shard_map/ppermute | solution.py:15
  46.8 3.7 %copy-start.4 = (f32[256,256]{0,1:T(8,128)}, f32[256,256]{0,1:T(8,128)S(1)}, u32[]{:S(2)}) copy-start(f32[256,256]{0,1:T(8,128)S(1)} %get-tuple-element.30) | copy-start | bytes 786436
  47.5 1.2 copy-start.13
  48.4 4.7 %copy-start.2 = (f32[256,256]{0,1:T(8,128)}, f32[256,256]{0,1:T(8,128)S(1)}, u32[]{:S(2)}) copy-start(f32[256,256]{0,1:T(8,128)S(1)} %get-tuple-element.20) | copy-start | bytes 786436
  48.7 1.1 copy-start.12
  48.8 1.4 copy-start.10
  53.1 1.0 copy-start.8
  55.3 4.1 %collective-permute-start.7 = (bf16[512,512]{1,0:T(8,128)(2,1)}, bf16[512,512]{1,0:T(8,128)(2,1)}, u32[]{:S(2)}, u32[]{:S(2)}) collective-permute-start(bf16[512,512]{1,0:T(8,128)(2,1)} %convolution_convert_fusion.1), channel_id=1, source_target_pairs={{0,64},{64,0},{1,65},{65,1},{2,66},{66,2},{3,67},{67,3},{4,68},{68... | collective-permute-start | bytes 1572872 | tf_op jit(solution)/shard_map/ppermute | solution.py:15
  57.2 18.6 %copy-start.3 = (f32[256,256]{0,1:T(8,128)S(1)}, f32[256,256]{0,1:T(8,128)}, u32[]{:S(2)}) copy-start(f32[256,256]{0,1:T(8,128)} %copy-done.2) | copy-start | bytes 786436
  61.7 24.6 %all-to-all-start = ((bf16[32,16,512]{2,1,0:T(8,128)(2,1)}), bf16[32,16,512]{2,1,0:T(8,128)(2,1)}, u32[]{:S(2)}, u32[]{:S(2)}) async-start(bf16[32,16,512]{2,1,0:T(8,128)(2,1)} %bitcast.42), calls=%async_computation | async-start | bytes 1048576 | tf_op jit(solution)/shard_map/all_to_all | solution.py:19
  72.5 37.4 %collective-permute-start.14 = (bf16[256,512]{1,0:T(8,128)(2,1)}, bf16[256,512]{1,0:T(8,128)(2,1)}, u32[]{:S(2)}, u32[]{:S(2)}) collective-permute-start(bf16[256,512]{1,0:T(8,128)(2,1)} %fusion.8), channel_id=1, source_target_pairs={{0,64},{64,0},{1,65},{65,1},{2,66},{66,2},{3,67},{67,3},{4,68},{68... | collective-permute-start | bytes 786440 | tf_op jit(solution)/shard_map/ppermute | solution.py:15
  76.8 37.4 %collective-permute-start.12 = (bf16[256,512]{1,0:T(8,128)(2,1)}, bf16[256,512]{1,0:T(8,128)(2,1)}, u32[]{:S(2)}, u32[]{:S(2)}) collective-permute-start(bf16[256,512]{1,0:T(8,128)(2,1)} %fusion.7), channel_id=1, source_target_pairs={{0,64},{64,0},{1,65},{65,1},{2,66},{66,2},{3,67},{67,3},{4,68},{68... | collective-permute-start | bytes 786440 | tf_op jit(solution)/shard_map/ppermute | solution.py:15
  87.4 26.8 %copy-start.7 = (f32[256,256]{0,1:T(8,128)S(1)}, f32[256,256]{0,1:T(8,128)}, u32[]{:S(2)}) copy-start(f32[256,256]{0,1:T(8,128)} %copy-done.6) | copy-start | bytes 786436
  88.0 13.6 %all-to-all-start.1 = ((bf16[8,16,512]{2,1,0:T(8,128)(2,1)}), bf16[8,16,512]{2,1,0:T(8,128)(2,1)S(1)}, u32[]{:S(2)}, u32[]{:S(2)}) async-start(bf16[8,16,512]{2,1,0:T(8,128)(2,1)} %broadcast_in_dim.28), calls=%async_computation.1 | async-start | bytes 262144 | tf_op jit(solution)/shard_map/all_to_all | solution.py:19
  93.9 27.4 %copy-start.5 = (f32[256,256]{0,1:T(8,128)S(1)}, f32[256,256]{0,1:T(8,128)}, u32[]{:S(2)}) copy-start(f32[256,256]{0,1:T(8,128)} %copy-done.4) | copy-start | bytes 786436
  93.9 27.4 %collective-permute-start.10 = (bf16[256,512]{1,0:T(8,128)(2,1)}, bf16[256,512]{1,0:T(8,128)(2,1)}, u32[]{:S(2)}, u32[]{:S(2)}) collective-permute-start(bf16[256,512]{1,0:T(8,128)(2,1)} %fusion.6), channel_id=1, source_target_pairs={{0,64},{64,0},{1,65},{65,1},{2,66},{66,2},{3,67},{67,3},{4,68},{68... | collective-permute-start | bytes 786440 | tf_op jit(solution)/shard_map/ppermute | solution.py:15
  99.1 34.1 %collective-permute-start.9 = (bf16[256,512]{1,0:T(8,128)(2,1)S(1)}, bf16[256,512]{1,0:T(8,128)(2,1)S(1)}, u32[]{:S(2)}, u32[]{:S(2)}) collective-permute-start(bf16[256,512]{1,0:T(8,128)(2,1)S(1)} %fusion.5), channel_id=1, source_target_pairs={{0,64},{64,0},{1,65},{65,1},{2,66},{66,2},{3,67},{67,3},{4,68},{68... | collective-permute-start | bytes 786440 | tf_op jit(solution)/shard_map/ppermute | solution.py:15
  102.5 27.2 %all-to-all-start.2 = ((bf16[32,16,512]{2,1,0:T(8,128)(2,1)}), bf16[32,16,512]{2,1,0:T(8,128)(2,1)}, u32[]{:S(2)}, u32[]{:S(2)}) async-start(bf16[32,16,512]{2,1,0:T(8,128)(2,1)} %broadcast_in_dim.29), calls=%async_computation.2 | async-start | bytes 1048576 | tf_op jit(solution)/shard_map/all_to_all | solution.py:19
  111.8 35.6 %copy-start.1 = (bf16[256,512]{1,0:T(8,128)(2,1)S(1)}, bf16[256,512]{1,0:T(8,128)(2,1)}, u32[]{:S(2)}) copy-start(bf16[256,512]{1,0:T(8,128)(2,1)} %param.6) | copy-start | bytes 786436
  111.8 21.4 %collective-permute-start.15 = (bf16[256,512]{1,0:T(8,128)(2,1)}, bf16[256,512]{1,0:T(8,128)(2,1)S(1)}, u32[]{:S(2)}, u32[]{:S(2)}) collective-permute-start(bf16[256,512]{1,0:T(8,128)(2,1)} %add_convert_fusion.1), channel_id=1, source_target_pairs={{0,128},{128,256},{256,384},{384,0},{1,129},{129,257},{257,385},{3... | collective-permute-start | bytes 786440 | tf_op jit(solution)/shard_map/ppermute | solution.py:15
  116.1 18.5 %collective-permute-start.13 = (bf16[256,512]{1,0:T(8,128)(2,1)}, bf16[256,512]{1,0:T(8,128)(2,1)S(1)}, u32[]{:S(2)}, u32[]{:S(2)}) collective-permute-start(bf16[256,512]{1,0:T(8,128)(2,1)} %add_convert_fusion.2), channel_id=1, source_target_pairs={{0,256},{128,384},{256,0},{384,128},{1,257},{129,385},{257,1},{385... | collective-permute-start | bytes 786440 | tf_op jit(solution)/shard_map/ppermute | solution.py:15
  123.3 24.2 %collective-permute-start.11 = (bf16[256,512]{1,0:T(8,128)(2,1)}, bf16[256,512]{1,0:T(8,128)(2,1)S(1)}, u32[]{:S(2)}, u32[]{:S(2)}) collective-permute-start(bf16[256,512]{1,0:T(8,128)(2,1)} %add_convert_fusion.3), channel_id=1, source_target_pairs={{0,384},{128,0},{256,128},{384,256},{1,385},{129,1},{257,129},{385... | collective-permute-start | bytes 786440 | tf_op jit(solution)/shard_map/ppermute | solution.py:15
  129.7 19.3 %collective-permute-start.8 = (bf16[512,512]{1,0:T(8,128)(2,1)}, bf16[512,512]{1,0:T(8,128)(2,1)S(1)}, u32[]{:S(2)}, u32[]{:S(2)}) collective-permute-start(bf16[512,512]{1,0:T(8,128)(2,1)} %bitcast.1), channel_id=1, source_target_pairs={{0,64},{64,0},{1,65},{65,1},{2,66},{66,2},{3,67},{67,3},{4,68},{68... | collective-permute-start | bytes 1572872 | tf_op jit(solution)/shard_map/ppermute | solution.py:15
  (1 other events, 0.8 us)

commit v2 on v1

v2 whole, which is shorter than its diff:
```python
import jax
import jax.numpy as jnp
from jax import lax
from jax.experimental import pallas as pl
from jax.experimental.pallas import tpu as pltpu
from jax.sharding import Mesh, PartitionSpec as P

SCALE = 100.0
EPS = 1e-06
FINE = ("zh", "core", "zl", "x", "y")
SPLIT = (4, 2, 2, 4, 8)
PLANE = ("x", "y")
COLUMN = ("zh", "zl")
REST = 16
MIB = 1 << 20


def shifted(block, axis, distance):
    count = lax.axis_size(axis)
    return lax.ppermute(block, axis, [(i, (i + distance) % count) for i in range(count)])


def exchanged(block, axes):
    return lax.all_to_all(block, axes, split_axis=0, concat_axis=0, tiled=True)


def copies(block, count):
    return jnp.broadcast_to(block[None], (count,) + block.shape).reshape(
        (count * block.shape[0],) + block.shape[1:]
    )


def folded(block, count):
    parts = block.reshape((count, block.shape[0] // count) + block.shape[1:])
    return jnp.sum(parts.astype(jnp.float32), axis=0)


def dot(a, b, da, db):
    return lax.dot_general(a, b, (((da,), (db,)), ((), ())), preferred_element_type=jnp.float32)


def call(kernel, outs, *args, scratch=(), flops=0, limit=16):
    whole = pl.BlockSpec(memory_space=pltpu.VMEM)
    scalars = pl.BlockSpec(memory_space=pltpu.SMEM)
    size = sum(a.size * a.dtype.itemsize for a in (*args, *outs))
    return pl.pallas_call(
        kernel,
        out_shape=outs,
        in_specs=[scalars if a.shape == (2,) else whole for a in args],
        out_specs=[whole] * len(outs),
        scratch_shapes=scratch,
        compiler_params=pltpu.CompilerParams(vmem_limit_bytes=limit * MIB),
        cost_estimate=pl.CostEstimate(flops=flops, bytes_accessed=size, transcendentals=0),
    )(*args)


def shape(dims, dtype):
    return jax.ShapeDtypeStruct(dims, dtype)


def text_kernel(text_ref, main_ref, rest_ref):
    main = main_ref.shape[0]
    text = text_ref[...].astype(jnp.float32)
    scale = lax.rsqrt(jnp.sum(text * text, axis=1, keepdims=True) + EPS)
    text = (text * scale).astype(jnp.bfloat16)
    main_ref[...] = text[:main]
    rest_ref[...] = text[main:]


def audio_kernel(features_ref, weight_ref, audio_ref, audio_b_ref, scale_ref):
    proj = dot(features_ref[...], weight_ref[...], 1, 0)
    scale = lax.rsqrt(jnp.sum(proj * proj, axis=1, keepdims=True) + EPS)
    audio = proj * scale
    audio_ref[...] = audio
    audio_b_ref[...] = audio.astype(jnp.bfloat16)
    scale_ref[...] = scale


def score_kernel(
    place_ref, audio_ref, audio_b_ref, scale_ref, positive_ref, own_ref, other_ref,
    grad_ref, tiles_ref, text_ref, scores_ref,
):
    chip, core = place_ref[0], place_ref[1]
    blocks, rows, _ = tiles_ref.shape
    chips = blocks // 2
    main = rows - REST
    audio_b = audio_b_ref[...]
    for n in range(blocks):
        held = own_ref if n < chips else other_ref
        back = lax.rem(chip - n % chips + chips, chips)
        start = pl.multiple_of(chips * main + back * REST, REST)
        lane = pl.ds(n * rows, main)
        text_ref[lane, :] = held[pl.ds((n % chips) * main, main), :]
        text_ref[pl.ds(n * rows + main, REST), :] = held[pl.ds(start, REST), :]
        scores_ref[:, pl.ds(n * rows, rows)] = SCALE * dot(
            audio_b, text_ref[pl.ds(n * rows, rows), :], 1, 1
        )
    step = 16
    ids = lax.broadcasted_iota(jnp.int32, (step, rows), 1)
    for r in range(0, rows, step):
        scores = scores_ref[r : r + step, :]
        weights = jnp.exp(scores - jnp.max(scores, axis=1, keepdims=True))
        weights = weights * (1.0 / jnp.sum(weights, axis=1, keepdims=True))
        positive = positive_ref[r : r + step, :]
        for n in range(blocks):
            column = core if n < chips else 1 - core
            first = ((n % chips) * 2 + column) * rows
            match = jnp.where(positive - first == ids, 1.0, 0.0)
            part = weights[:, n * rows : (n + 1) * rows] - match
            tiles_ref[n, r : r + step, :] = part.astype(jnp.bfloat16)
    total = jnp.zeros(audio_ref.shape, jnp.float32)
    for n in range(blocks):
        total = total + dot(tiles_ref[n], text_ref[pl.ds(n * rows, rows), :], 1, 0)
    total = SCALE * total
    audio = audio_ref[...]
    along = jnp.sum(audio * total, axis=1, keepdims=True)
    grad_ref[...] = ((total - audio * along) * scale_ref[...]).astype(jnp.bfloat16)


def over_kernel(tiles_ref, audio_b_ref, over_ref):
    blocks = tiles_ref.shape[0] // 2
    for n in range(blocks):
        part = SCALE * dot(tiles_ref[blocks + n], audio_b_ref[...], 0, 0)
        over_ref[n] = part.astype(jnp.bfloat16)


def kept_kernel(place_ref, tiles_ref, audio_b_ref, over_ref, home_ref, *away_refs):
    chips = len(away_refs) + 1
    for n in range(chips):
        to = lax.rem(place_ref[0] + n, chips)
        part = SCALE * dot(tiles_ref[to], audio_b_ref[...], 0, 0)
        part = part + over_ref[to].astype(jnp.float32)
        if n == 0:
            home_ref[...] = part
        else:
            away_refs[n - 1][...] = part.astype(jnp.bfloat16)


def weight_kernel(features_ref, grad_ref, part_ref, half_ref):
    part = part_ref[...] + dot(features_ref[...], grad_ref[...], 0, 0)
    half_ref[...] = part.astype(jnp.bfloat16)


def summed_everywhere(half):
    core = lax.axis_index("core")
    plane = lax.axis_size(PLANE)
    column = lax.axis_size(COLUMN)
    part = folded(exchanged(half, PLANE), plane).astype(jnp.bfloat16)
    part = folded(exchanged(copies(part, column), COLUMN), column).astype(jnp.bfloat16)
    half = exchanged(copies(part, plane), PLANE)
    there = shifted(half, "core", 1)
    low, high = jnp.concatenate([half, there]), jnp.concatenate([there, half])
    return jnp.where(core == 0, low, high).astype(jnp.float32)


def body(audio_features, proj_weight, text_raw, positive):
    rows, channels = audio_features.shape
    width = text_raw.shape[1]
    chips = lax.axis_size("zh")
    blocks = chips * lax.axis_size("core")
    core = lax.axis_index("core")
    place = jnp.stack([lax.axis_index("zh"), core]).astype(jnp.int32)
    bf16, f32 = jnp.bfloat16, jnp.float32
    pair_flops = 2 * rows * rows * blocks * width

    main, rest = call(
        text_kernel, (shape((rows - REST, width), bf16), shape((REST, width), bf16)), text_raw
    )
    rests = [rest] + [shifted(rest, "zh", k) for k in range(1, chips)]
    main = lax.all_gather(main, "zh", axis=0, tiled=True)
    own = jnp.concatenate([main] + rests)
    own, audio_features = lax.optimization_barrier((own, audio_features))
    other = shifted(own, "core", 1)
    half = channels // 2
    features = lax.dynamic_slice_in_dim(audio_features, core * half, half, 1)
    beside = lax.dynamic_slice_in_dim(audio_features, (1 - core) * half, half, 1)
    beside = shifted(beside, "core", 1)
    audio, audio_b, scale = call(
        audio_kernel,
        (shape((rows, width), f32), shape((rows, width), bf16), shape((rows, 1), f32)),
        audio_features,
        proj_weight,
        flops=2 * rows * channels * width,
    )
    proj_grad, tiles = call(
        score_kernel,
        (shape((rows, width), bf16), shape((blocks, rows, rows), bf16)),
        place,
        audio,
        audio_b,
        scale,
        positive.reshape(rows, 1),
        own,
        other,
        scratch=[pltpu.VMEM((blocks * rows, width), bf16), pltpu.VMEM((rows, blocks * rows), f32)],
        flops=2 * pair_flops,
    )
    grad_beside = shifted(proj_grad, "core", 1)
    (weight_half,) = call(
        weight_kernel,
        (shape((half, width), bf16),),
        beside,
        grad_beside,
        dot(features, proj_grad, 0, 0),
        flops=2 * half * rows * width,
    )
    grad_weight = summed_everywhere(weight_half)
    grad_features = dot(proj_grad, proj_weight, 1, 1).astype(bf16)
    (over,) = call(
        over_kernel, (shape((chips, rows, width), bf16),), tiles, audio_b, flops=pair_flops // 2
    )
    over = shifted(over, "core", 1)
    home, *away = call(
        kept_kernel,
        (shape((rows, width), f32),) + (shape((rows, width), bf16),) * (chips - 1),
        place,
        tiles,
        audio_b,
        over,
        flops=pair_flops // 2,
    )
    text_grad = home
    for n, block in enumerate(away):
        text_grad = text_grad + shifted(block, "zh", n + 1)
    text_f = text_raw.astype(f32)
    text_scale = lax.rsqrt(jnp.sum(text_f * text_f, axis=1, keepdims=True) + EPS)
    text = text_f * text_scale
    text_along = jnp.sum(text * text_grad, axis=1, keepdims=True)
    grad_text = (text_grad - text * text_along) * text_scale
    return (grad_weight, grad_features, grad_text)


def solution(mesh):
    fine = Mesh(mesh.devices.reshape(SPLIT), FINE)
    rows = P(FINE, None)
    return jax.shard_map(
        body,
        mesh=fine,
        in_specs=(rows, P(), rows, P(FINE)),
        out_specs=(P(), rows, rows),
        check_vma=False,
    )
```

time: 153 us -> 140 us (0.915); the launches traced: 152 us -> 137 us
  blocking collectives: 0 us -> 42.1 us
  waiting for transfers between devices: 34.5 us -> 10.8 us
  matrix products: 24.5 us -> 1.6 us
  starting transfers between devices: 81.2 us -> 63.4 us
  Pallas kernels: 0 us -> 9.2 us
  other arithmetic: 7.79 us -> 4.47 us
  local copies, waits for them, and re-layouts: 2.43 us -> 4.64 us
    all_to_all x0 -> x1, blocking collectives: none -> 23.6 us  [exchanged(): return lax.all_to_all(block, axes, split_axis=0, concat_axis=0, tiled=True)]
    dot_general x28 -> x2, matrix products: 24.5 us -> 1.6 us  [dot(): lax.dot_general(a, b, (((da,), (db,)), ((), ())), preferred_element_type=...]
    all_gather x0 -> x1, blocking collectives: none -> 18.5 us  [body(): main = lax.all_gather(main, 'zh', axis=0, tiled=True)]
    ppermute x16 -> x11, waiting for transfers between devices: 26.4 us -> 9.94 us  [shifted(): lax.ppermute(block, axis, [(i, (i + distance) % count) for i in range(cou...]
    all_to_all x3 -> x2, starting transfers between devices: 22.7 us -> 11.5 us  [exchanged(): return lax.all_to_all(block, axes, split_axis=0, concat_axis=0, tiled=True)]
    pallas_call x0 -> x6, Pallas kernels: none -> 9.2 us  [call(): pl.pallas_call(kernel, out_shape=outs, in_specs=[scalars if a.shape == (2...]
    all_to_all x3 -> x2, waiting for transfers between devices: 8.08 us -> 0.89 us  [exchanged(): return lax.all_to_all(block, axes, split_axis=0, concat_axis=0, tiled=True)]
    ppermute x16 -> x11, starting transfers between devices: 58.4 us -> 51.9 us  [shifted(): lax.ppermute(block, axis, [(i, (i + distance) % count) for i in range(cou...]
  transfers between devices with their start and end apart: 19 -> 13, of which waited for: 6 -> 3; matrix products, arithmetic and copies ran while one was open for 13% -> 4% of each run, Pallas kernels for 0% -> 6%
where the time goes in v2:
time: 140 us; the launch traced here: 137 us
  starting transfers between devices  63.4 us (45%)
  blocking collectives  42.1 us (30%)
  waiting for transfers between devices  10.8 us (8%)
  Pallas kernels  9.2 us (7%)
  local copies, waits for them, and re-layouts  4.64 us (3%)
  other arithmetic  4.47 us (3%)
  matrix products  1.6 us (1%)
    ppermute x11, starting transfers between devices, shifted(): lax.ppermute(block, axis, [(i, (i + distance) % count) for i in range(cou...  51.9 us
    all_to_all x1, blocking collectives, exchanged(): return lax.all_to_all(block, axes, split_axis=0, concat_axis=0, tiled=True)  23.6 us
    all_gather x1, blocking collectives, body(): main = lax.all_gather(main, 'zh', axis=0, tiled=True)  18.5 us
    all_to_all x2, starting transfers between devices, exchanged(): return lax.all_to_all(block, axes, split_axis=0, concat_axis=0, tiled=True)  11.5 us
    ppermute x11, waiting for transfers between devices, shifted(): lax.ppermute(block, axis, [(i, (i + distance) % count) for i in range(cou...  9.94 us
    pallas_call x6, Pallas kernels, call(): pl.pallas_call(kernel, out_shape=outs, in_specs=[scalars if a.shape == (2...  9.2 us
    convert_element_type x1, other arithmetic, summed_everywhere(): return jnp.where(core == 0, low, high).astype(jnp.float32)  2.88 us
  transfers between devices with their start and end apart: 13, of which 3 were waited for; matrix products, arithmetic and copies ran while one was open for 4% of the time, Pallas kernels for 6%

profile of v2, /device:TPU:1, one launch (start us, length us, event | category | flops | bytes accessed | tf_op | source)
XLA Modules:
  0.0 137.2 jit_solution(6357039472526590023)
XLA Ops:
  0.6 0.9 copy-done.1
  1.7 6.8 %collective-permute-start = (bf16[16,512]{1,0:T(8,128)(2,1)S(1)}, bf16[16,512]{1,0:T(8,128)(2,1)S(1)}, u32[]{:S(2)}, u32[]{:S(2)}) collective-permute-start(bf16[16,512]{1,0:T(8,128)(2,1)S(1)} %get-tuple-element.17), channel_id=1, source_target_pairs={{0,128},{128,256},{256,384},{384,0},{1,129},{129,257},{257,385},{3... | collective-permute-start | bytes 49160 | tf_op jit(solution)/shard_map/ppermute | solution.py:20
  8.5 8.8 %collective-permute-start.1 = (bf16[16,512]{1,0:T(8,128)(2,1)S(1)}, bf16[16,512]{1,0:T(8,128)(2,1)S(1)}, u32[]{:S(2)}, u32[]{:S(2)}) collective-permute-start(bf16[16,512]{1,0:T(8,128)(2,1)S(1)} %get-tuple-element.17), channel_id=1, source_target_pairs={{0,256},{128,384},{256,0},{384,128},{1,257},{129,385},{257,1},{385... | collective-permute-start | bytes 49160 | tf_op jit(solution)/shard_map/ppermute | solution.py:20
  17.4 3.4 %collective-permute-start.2 = (bf16[16,512]{1,0:T(8,128)(2,1)S(1)}, bf16[16,512]{1,0:T(8,128)(2,1)S(1)}, u32[]{:S(2)}, u32[]{:S(2)}) collective-permute-start(bf16[16,512]{1,0:T(8,128)(2,1)S(1)} %get-tuple-element.17), channel_id=1, source_target_pairs={{0,384},{128,0},{256,128},{384,256},{1,385},{129,1},{257,129},{385... | collective-permute-start | bytes 49160 | tf_op jit(solution)/shard_map/ppermute | solution.py:20
  20.7 18.5 %all_gather.3 = bf16[960,512]{1,0:T(8,128)(2,1)S(1)} all-gather(bf16[240,512]{1,0:T(8,128)(2,1)S(1)} %get-tuple-element.16), channel_id=1, replica_groups=mesh['zh'=4,'core'=2,'zl'=2,'x'=4,'y'=8] {'zh'}, dimensions={0}, use_global_device_ids=true | all-gather | bytes 1228800 | tf_op jit(solution)/shard_map/all_gather | solution.py:170
  39.4 6.3 %collective-permute-start.4 = (bf16[1024,512]{1,0:T(8,128)(2,1)S(1)}, bf16[1024,512]{1,0:T(8,128)(2,1)}, u32[]{:S(2)}, u32[]{:S(2)}) collective-permute-start(bf16[1024,512]{1,0:T(8,128)(2,1)S(1)} %constant_dynamic-update-slice_fusion.own_ref), channel_id=1, source_target_pairs={{0,64},{64,0},{1,65},{65,1},{2,66},{66,2},{3,67},{67,3},{4,68},{68... | collective-permute-start | bytes 3145736 | tf_op jit(solution)/shard_map/ppermute | solution.py:20
  45.9 0.7 constant_dynamic-slice_fusion
  46.6 1.9 %collective-permute-start.3 = (bf16[256,512]{1,0:T(8,128)(2,1)}, bf16[256,512]{1,0:T(8,128)(2,1)S(1)}, u32[]{:S(2)}, u32[]{:S(2)}) collective-permute-start(bf16[256,512]{1,0:T(8,128)(2,1)} %constant_dynamic-slice_fusion), channel_id=1, source_target_pairs={{0,64},{64,0},{1,65},{65,1},{2,66},{66,2},{3,67},{67,3},{4,68},{68... | collective-permute-start | bytes 786440 | tf_op jit(solution)/shard_map/ppermute | solution.py:20
  48.6 0.5 shard_map.68
  49.1 1.2 copy-done.5
  50.3 3.4 %shard_map.69 = (bf16[256,512]{1,0:T(8,128)(2,1)S(1)}, bf16[8,256,256]{2,1,0:T(8,128)(2,1)S(1)}) custom-call(s32[2]{0:T(128)S(1)} %pad_add_fusion.place_ref, f32[256,512]{1,0:T(8,128)S(1)} %get-tuple-element.19.audio_ref, bf16[256,512]{1,0:T(8,128)(2,1)S(1)} %get-tuple-element.20.audio_b_ref, f32[256,1]{1,0:T(8,128)S(1)} %get-tuple-element.21.scale_ref, ...), custom_call_target="tpu_custom_call" | custom-call | flops 1073741824 | bytes 4196360 | tf_op jit(solution)/shard_map/pallas_call | solution.py:46
  53.7 2.4 %collective-permute-start.5 = (bf16[256,512]{1,0:T(8,128)(2,1)S(1)}, bf16[256,512]{1,0:T(8,128)(2,1)}, u32[]{:S(2)}, u32[]{:S(2)}) collective-permute-start(bf16[256,512]{1,0:T(8,128)(2,1)S(1)} %get-tuple-element.23), channel_id=1, source_target_pairs={{0,64},{64,0},{1,65},{65,1},{2,66},{66,2},{3,67},{67,3},{4,68},{68... | collective-permute-start | bytes 786440 | tf_op jit(solution)/shard_map/ppermute | solution.py:20
  56.1 0.3 fusion.7.part_ref
  56.5 0.9 collective-permute-done.5.grad_ref
  57.4 1.3 shard_map.70
  58.7 23.6 %all_to_all.24 = bf16[32,16,512]{2,1,0:T(8,128)(2,1)S(1)} all-to-all(bf16[32,16,512]{2,1,0:T(8,128)(2,1)S(1)} %bitcast.8), channel_id=1, replica_groups=mesh['zh'=4,'core'=2,'zl'=2,'x'=4,'y'=8] {'x','y'}, dimensions={0} | all-to-all | bytes 1048576 | tf_op jit(solution)/shard_map/all_to_all | solution.py:24
  82.4 0.7 broadcast_in_dim.4
  83.0 3.4 %all-to-all-start.1 = ((bf16[8,16,512]{2,1,0:T(8,128)(2,1)}), bf16[8,16,512]{2,1,0:T(8,128)(2,1)S(1)}, u32[]{:S(2)}, u32[]{:S(2)}) async-start(bf16[8,16,512]{2,1,0:T(8,128)(2,1)} %broadcast_in_dim.4), calls=%async_computation.1 | async-start | bytes 262144 | tf_op jit(solution)/shard_map/all_to_all | solution.py:24
  86.4 1.4 %shard_map.71 = bf16[4,256,512]{2,1,0:T(8,128)(2,1)} custom-call(bf16[8,256,256]{2,1,0:T(8,128)(2,1)S(1)} %get-tuple-element.24.tiles_ref, bf16[256,512]{1,0:T(8,128)(2,1)S(1)} %get-tuple-element.20.audio_b_ref), custom_call_target="tpu_custom_call" | custom-call | flops 268435456 | bytes 2359296 | tf_op jit(solution)/shard_map/pallas_call | solution.py:46
  87.9 5.5 %collective-permute-start.7 = (bf16[4,256,512]{2,1,0:T(8,128)(2,1)}, bf16[4,256,512]{2,1,0:T(8,128)(2,1)}, u32[]{:S(2)}, u32[]{:S(2)}) collective-permute-start(bf16[4,256,512]{2,1,0:T(8,128)(2,1)} %shard_map.71), channel_id=1, source_target_pairs={{0,64},{64,0},{1,65},{65,1},{2,66},{66,2},{3,67},{67,3},{4,68},{68... | collective-permute-start | bytes 3145736 | tf_op jit(solution)/shard_map/ppermute | solution.py:20
  93.4 0.9 all-to-all-done.1
  94.3 0.9 broadcast_in_dim.5
  95.1 8.1 %all-to-all-start.2 = ((bf16[32,16,512]{2,1,0:T(8,128)(2,1)}), bf16[32,16,512]{2,1,0:T(8,128)(2,1)}, u32[]{:S(2)}, u32[]{:S(2)}) async-start(bf16[32,16,512]{2,1,0:T(8,128)(2,1)} %broadcast_in_dim.5), calls=%async_computation.2 | async-start | bytes 1048576 | tf_op jit(solution)/shard_map/all_to_all | solution.py:24
  103.4 2.5 %shard_map.72 = (f32[256,512]{1,0:T(8,128)S(1)}, bf16[256,512]{1,0:T(8,128)(2,1)}, bf16[256,512]{1,0:T(8,128)(2,1)}, bf16[256,512]{1,0:T(8,128)(2,1)}) custom-call(s32[2]{0:T(128)S(1)} %pad_add_fusion.place_ref, bf16[8,256,256]{2,1,0:T(8,128)(2,1)S(1)} %get-tuple-element.24.tiles_ref, bf16[256,512]{1,0:T(8,128)(2,1)S(1)} %get-tuple-element.20.audio_b_ref, ...), custom_call_target="tpu_custom_call" | custom-call | flops 268435456 | bytes 3670024 | tf_op jit(solution)/shard_map/pallas_call | solution.py:46
  105.9 3.1 %collective-permute-start.10 = (bf16[256,512]{1,0:T(8,128)(2,1)}, bf16[256,512]{1,0:T(8,128)(2,1)S(1)}, u32[]{:S(2)}, u32[]{:S(2)}) collective-permute-start(bf16[256,512]{1,0:T(8,128)(2,1)} %get-tuple-element.28), channel_id=1, source_target_pairs={{0,384},{128,0},{256,128},{384,256},{1,385},{129,1},{257,129},{385... | collective-permute-start | bytes 786440 | tf_op jit(solution)/shard_map/ppermute | solution.py:20
  109.0 3.0 %collective-permute-start.8 = (bf16[256,512]{1,0:T(8,128)(2,1)}, bf16[256,512]{1,0:T(8,128)(2,1)S(1)}, u32[]{:S(2)}, u32[]{:S(2)}) collective-permute-start(bf16[256,512]{1,0:T(8,128)(2,1)} %get-tuple-element.26), channel_id=1, source_target_pairs={{0,128},{128,256},{256,384},{384,0},{1,129},{129,257},{257,385},{3... | collective-permute-start | bytes 786440 | tf_op jit(solution)/shard_map/ppermute | solution.py:20
  112.1 4.2 %collective-permute-start.9 = (bf16[256,512]{1,0:T(8,128)(2,1)}, bf16[256,512]{1,0:T(8,128)(2,1)S(1)}, u32[]{:S(2)}, u32[]{:S(2)}) collective-permute-start(bf16[256,512]{1,0:T(8,128)(2,1)} %get-tuple-element.27), channel_id=1, source_target_pairs={{0,256},{128,384},{256,0},{384,128},{1,257},{129,385},{257,1},{385... | collective-permute-start | bytes 786440 | tf_op jit(solution)/shard_map/ppermute | solution.py:20
  116.3 6.5 %collective-permute-start.6 = (bf16[512,512]{1,0:T(8,128)(2,1)}, bf16[512,512]{1,0:T(8,128)(2,1)S(1)}, u32[]{:S(2)}, u32[]{:S(2)}) collective-permute-start(bf16[512,512]{1,0:T(8,128)(2,1)} %bitcast.4), channel_id=1, source_target_pairs={{0,64},{64,0},{1,65},{65,1},{2,66},{66,2},{3,67},{67,3},{4,68},{68... | collective-permute-start | bytes 1572872 | tf_op jit(solution)/shard_map/ppermute | solution.py:20
  122.8 1.3 convolution_convert_fusion
  124.0 9.0 %collective-permute-done.9 = bf16[256,512]{1,0:T(8,128)(2,1)S(1)} collective-permute-done((bf16[256,512]{1,0:T(8,128)(2,1)}, bf16[256,512]{1,0:T(8,128)(2,1)S(1)}, u32[]{:S(2)}, u32[]{:S(2)}) %collective-permute-start.9) | collective-permute-done | bytes 262176 | tf_op jit(solution)/shard_map/ppermute | solution.py:20
  133.3 1.0 fusion.5
  134.3 2.9 %fusion = f32[1024,512]{1,0:T(8,128)} fusion(bf16[512,512]{1,0:T(8,128)(2,1)S(1)} %collective-permute-done.6, bf16[512,512]{1,0:T(8,128)(2,1)} %bitcast.4, pred[]{:T(512)S(6)} %eq.3), kind=kLoop, calls=%fused_computation.2 | loop fusion | flops 5242880 | bytes 3145729 | tf_op jit(solution)/shard_map/convert_element_type | solution.py:153
  (35 shorter events, 1.0 us)
Async XLA Ops:
  0.6 1.0 copy-start.1
  1.6 44.1 %copy-start.6 = (s32[256]{0:T(256)S(1)}, s32[256]{0:T(256)}, u32[]{:S(2)}) copy-start(s32[256]{0:T(256)} %param.7) | copy-start | bytes 3076
  1.6 44.3 %copy-start.3 = (bf16[256,1024]{1,0:T(8,128)(2,1)S(1)}, bf16[256,1024]{1,0:T(8,128)(2,1)}, u32[]{:S(2)}) copy-start(bf16[256,1024]{1,0:T(8,128)(2,1)} %features_ref) | copy-start | bytes 1572868
  1.6 47.0 %copy-start = (bf16[1024,512]{1,0:T(8,128)(2,1)S(1)}, bf16[1024,512]{1,0:T(8,128)(2,1)}, u32[]{:S(2)}) copy-start(bf16[1024,512]{1,0:T(8,128)(2,1)} %weight_ref.1) | copy-start | bytes 3145732
  1.7 37.6 %collective-permute-start = (bf16[16,512]{1,0:T(8,128)(2,1)S(1)}, bf16[16,512]{1,0:T(8,128)(2,1)S(1)}, u32[]{:S(2)}, u32[]{:S(2)}) collective-permute-start(bf16[16,512]{1,0:T(8,128)(2,1)S(1)} %get-tuple-element.17), channel_id=1, source_target_pairs={{0,128},{128,256},{256,384},{384,0},{1,129},{129,257},{257,385},{3... | collective-permute-start | bytes 49160 | tf_op jit(solution)/shard_map/ppermute | solution.py:20
  8.5 30.8 %collective-permute-start.1 = (bf16[16,512]{1,0:T(8,128)(2,1)S(1)}, bf16[16,512]{1,0:T(8,128)(2,1)S(1)}, u32[]{:S(2)}, u32[]{:S(2)}) collective-permute-start(bf16[16,512]{1,0:T(8,128)(2,1)S(1)} %get-tuple-element.17), channel_id=1, source_target_pairs={{0,256},{128,384},{256,0},{384,128},{1,257},{129,385},{257,1},{385... | collective-permute-start | bytes 49160 | tf_op jit(solution)/shard_map/ppermute | solution.py:20
  17.4 22.0 %collective-permute-start.2 = (bf16[16,512]{1,0:T(8,128)(2,1)S(1)}, bf16[16,512]{1,0:T(8,128)(2,1)S(1)}, u32[]{:S(2)}, u32[]{:S(2)}) collective-permute-start(bf16[16,512]{1,0:T(8,128)(2,1)S(1)} %get-tuple-element.17), channel_id=1, source_target_pairs={{0,384},{128,0},{256,128},{384,256},{1,385},{129,1},{257,129},{385... | collective-permute-start | bytes 49160 | tf_op jit(solution)/shard_map/ppermute | solution.py:20
  39.4 9.7 %copy-start.4 = (bf16[1024,512]{1,0:T(8,128)(2,1)}, bf16[1024,512]{1,0:T(8,128)(2,1)S(1)}, u32[]{:S(2)}) copy-start(bf16[1024,512]{1,0:T(8,128)(2,1)S(1)} %constant_dynamic-update-slice_fusion.own_ref) | copy-start | bytes 3145732
  39.4 9.7 %collective-permute-start.4 = (bf16[1024,512]{1,0:T(8,128)(2,1)S(1)}, bf16[1024,512]{1,0:T(8,128)(2,1)}, u32[]{:S(2)}, u32[]{:S(2)}) collective-permute-start(bf16[1024,512]{1,0:T(8,128)(2,1)S(1)} %constant_dynamic-update-slice_fusion.own_ref), channel_id=1, source_target_pairs={{0,64},{64,0},{1,65},{65,1},{2,66},{66,2},{3,67},{67,3},{4,68},{68... | collective-permute-start | bytes 3145736 | tf_op jit(solution)/shard_map/ppermute | solution.py:20
  46.6 9.8 %collective-permute-start.3 = (bf16[256,512]{1,0:T(8,128)(2,1)}, bf16[256,512]{1,0:T(8,128)(2,1)S(1)}, u32[]{:S(2)}, u32[]{:S(2)}) collective-permute-start(bf16[256,512]{1,0:T(8,128)(2,1)} %constant_dynamic-slice_fusion), channel_id=1, source_target_pairs={{0,64},{64,0},{1,65},{65,1},{2,66},{66,2},{3,67},{67,3},{4,68},{68... | collective-permute-start | bytes 786440 | tf_op jit(solution)/shard_map/ppermute | solution.py:20
  49.1 1.2 copy-start.5
  53.7 3.7 %collective-permute-start.5 = (bf16[256,512]{1,0:T(8,128)(2,1)S(1)}, bf16[256,512]{1,0:T(8,128)(2,1)}, u32[]{:S(2)}, u32[]{:S(2)}) collective-permute-start(bf16[256,512]{1,0:T(8,128)(2,1)S(1)} %get-tuple-element.23), channel_id=1, source_target_pairs={{0,64},{64,0},{1,65},{65,1},{2,66},{66,2},{3,67},{67,3},{4,68},{68... | collective-permute-start | bytes 786440 | tf_op jit(solution)/shard_map/ppermute | solution.py:20
  83.0 11.2 %all-to-all-start.1 = ((bf16[8,16,512]{2,1,0:T(8,128)(2,1)}), bf16[8,16,512]{2,1,0:T(8,128)(2,1)S(1)}, u32[]{:S(2)}, u32[]{:S(2)}) async-start(bf16[8,16,512]{2,1,0:T(8,128)(2,1)} %broadcast_in_dim.4), calls=%async_computation.1 | async-start | bytes 262144 | tf_op jit(solution)/shard_map/all_to_all | solution.py:24
  86.4 16.8 %copy-start.2 = (bf16[256,512]{1,0:T(8,128)(2,1)S(1)}, bf16[256,512]{1,0:T(8,128)(2,1)}, u32[]{:S(2)}) copy-start(bf16[256,512]{1,0:T(8,128)(2,1)} %text_ref.1) | copy-start | bytes 786436
  87.9 15.5 %collective-permute-start.7 = (bf16[4,256,512]{2,1,0:T(8,128)(2,1)}, bf16[4,256,512]{2,1,0:T(8,128)(2,1)}, u32[]{:S(2)}, u32[]{:S(2)}) collective-permute-start(bf16[4,256,512]{2,1,0:T(8,128)(2,1)} %shard_map.71), channel_id=1, source_target_pairs={{0,64},{64,0},{1,65},{65,1},{2,66},{66,2},{3,67},{67,3},{4,68},{68... | collective-permute-start | bytes 3145736 | tf_op jit(solution)/shard_map/ppermute | solution.py:20
  95.1 21.1 %all-to-all-start.2 = ((bf16[32,16,512]{2,1,0:T(8,128)(2,1)}), bf16[32,16,512]{2,1,0:T(8,128)(2,1)}, u32[]{:S(2)}, u32[]{:S(2)}) async-start(bf16[32,16,512]{2,1,0:T(8,128)(2,1)} %broadcast_in_dim.5), calls=%async_computation.2 | async-start | bytes 1048576 | tf_op jit(solution)/shard_map/all_to_all | solution.py:24
  105.9 18.2 %collective-permute-start.10 = (bf16[256,512]{1,0:T(8,128)(2,1)}, bf16[256,512]{1,0:T(8,128)(2,1)S(1)}, u32[]{:S(2)}, u32[]{:S(2)}) collective-permute-start(bf16[256,512]{1,0:T(8,128)(2,1)} %get-tuple-element.28), channel_id=1, source_target_pairs={{0,384},{128,0},{256,128},{384,256},{1,385},{129,1},{257,129},{385... | collective-permute-start | bytes 786440 | tf_op jit(solution)/shard_map/ppermute | solution.py:20
  109.0 15.0 %collective-permute-start.8 = (bf16[256,512]{1,0:T(8,128)(2,1)}, bf16[256,512]{1,0:T(8,128)(2,1)S(1)}, u32[]{:S(2)}, u32[]{:S(2)}) collective-permute-start(bf16[256,512]{1,0:T(8,128)(2,1)} %get-tuple-element.26), channel_id=1, source_target_pairs={{0,128},{128,256},{256,384},{384,0},{1,129},{129,257},{257,385},{3... | collective-permute-start | bytes 786440 | tf_op jit(solution)/shard_map/ppermute | solution.py:20
  112.1 21.0 %collective-permute-start.9 = (bf16[256,512]{1,0:T(8,128)(2,1)}, bf16[256,512]{1,0:T(8,128)(2,1)S(1)}, u32[]{:S(2)}, u32[]{:S(2)}) collective-permute-start(bf16[256,512]{1,0:T(8,128)(2,1)} %get-tuple-element.27), channel_id=1, source_target_pairs={{0,256},{128,384},{256,0},{384,128},{1,257},{129,385},{257,1},{385... | collective-permute-start | bytes 786440 | tf_op jit(solution)/shard_map/ppermute | solution.py:20
  116.3 18.1 %collective-permute-start.6 = (bf16[512,512]{1,0:T(8,128)(2,1)}, bf16[512,512]{1,0:T(8,128)(2,1)S(1)}, u32[]{:S(2)}, u32[]{:S(2)}) collective-permute-start(bf16[512,512]{1,0:T(8,128)(2,1)} %bitcast.4), channel_id=1, source_target_pairs={{0,64},{64,0},{1,65},{65,1},{2,66},{66,2},{3,67},{67,3},{4,68},{68... | collective-permute-start | bytes 1572872 | tf_op jit(solution)/shard_map/ppermute | solution.py:20

commit v3 on v2

--- a/solution.py
+++ b/solution.py
@@ -11,7 +11,6 @@
 SPLIT = (4, 2, 2, 4, 8)
 PLANE = ("x", "y")
 COLUMN = ("zh", "zl")
-REST = 16
 MIB = 1 << 20
 
 
@@ -24,25 +23,14 @@
     return lax.all_to_all(block, axes, split_axis=0, concat_axis=0, tiled=True)
 
 
-def copies(block, count):
-    return jnp.broadcast_to(block[None], (count,) + block.shape).reshape(
-        (count * block.shape[0],) + block.shape[1:]
-    )
-
-
-def folded(block, count):
-    parts = block.reshape((count, block.shape[0] // count) + block.shape[1:])
-    return jnp.sum(parts.astype(jnp.float32), axis=0)
-
-
 def dot(a, b, da, db):
     return lax.dot_general(a, b, (((da,), (db,)), ((), ())), preferred_element_type=jnp.float32)
 
 
-def call(kernel, outs, *args, scratch=(), flops=0, limit=16):
+def call(kernel, outs, *args, scratch=(), flops=0, limit=16, light=False):
     whole = pl.BlockSpec(memory_space=pltpu.VMEM)
     scalars = pl.BlockSpec(memory_space=pltpu.SMEM)
-    size = sum(a.size * a.dtype.itemsize for a in (*args, *outs))
+    size = 0 if light else sum(a.size * a.dtype.itemsize for a in (*args, *outs))
     return pl.pallas_call(
         kernel,
         out_shape=outs,
@@ -58,13 +46,12 @@
     return jax.ShapeDtypeStruct(dims, dtype)
 
 
-def text_kernel(text_ref, main_ref, rest_ref):
-    main = main_ref.shape[0]
+def text_kernel(text_ref, copies_ref):
     text = text_ref[...].astype(jnp.float32)
     scale = lax.rsqrt(jnp.sum(text * text, axis=1, keepdims=True) + EPS)
     text = (text * scale).astype(jnp.bfloat16)
-    main_ref[...] = text[:main]
-    rest_ref[...] = text[main:]
+    for n in range(copies_ref.shape[0]):
+        copies_ref[n] = text
 
 
 def audio_kernel(features_ref, weight_ref, audio_ref, audio_b_ref, scale_ref):
@@ -78,23 +65,15 @@
 
 def score_kernel(
     place_ref, audio_ref, audio_b_ref, scale_ref, positive_ref, own_ref, other_ref,
-    grad_ref, tiles_ref, text_ref, scores_ref,
+    grad_ref, tiles_ref, scores_ref,
 ):
-    chip, core = place_ref[0], place_ref[1]
+    core = place_ref[1]
     blocks, rows, _ = tiles_ref.shape
     chips = blocks // 2
-    main = rows - REST
     audio_b = audio_b_ref[...]
     for n in range(blocks):
-        held = own_ref if n < chips else other_ref
-        back = lax.rem(chip - n % chips + chips, chips)
-        start = pl.multiple_of(chips * main + back * REST, REST)
-        lane = pl.ds(n * rows, main)
-        text_ref[lane, :] = held[pl.ds((n % chips) * main, main), :]
-        text_ref[pl.ds(n * rows + main, REST), :] = held[pl.ds(start, REST), :]
-        scores_ref[:, pl.ds(n * rows, rows)] = SCALE * dot(
-            audio_b, text_ref[pl.ds(n * rows, rows), :], 1, 1
-        )
+        text = (own_ref if n < chips else other_ref)[n % chips]
+        scores_ref[:, pl.ds(n * rows, rows)] = SCALE * dot(audio_b, text, 1, 1)
     step = 16
     ids = lax.broadcasted_iota(jnp.int32, (step, rows), 1)
     for r in range(0, rows, step):
@@ -110,7 +89,8 @@
             tiles_ref[n, r : r + step, :] = part.astype(jnp.bfloat16)
     total = jnp.zeros(audio_ref.shape, jnp.float32)
     for n in range(blocks):
-        total = total + dot(tiles_ref[n], text_ref[pl.ds(n * rows, rows), :], 1, 0)
+        text = (own_ref if n < chips else other_ref)[n % chips]
+        total = total + dot(tiles_ref[n], text, 1, 0)
     total = SCALE * total
     audio = audio_ref[...]
     along = jnp.sum(audio * total, axis=1, keepdims=True)
@@ -136,21 +116,56 @@
             away_refs[n - 1][...] = part.astype(jnp.bfloat16)
 
 
+def features_kernel(grad_ref, weight_ref, out_ref):
+    out_ref[...] = dot(grad_ref[...], weight_ref[...], 1, 1).astype(jnp.bfloat16)
+
+
 def weight_kernel(features_ref, grad_ref, part_ref, half_ref):
     part = part_ref[...] + dot(features_ref[...], grad_ref[...], 0, 0)
     half_ref[...] = part.astype(jnp.bfloat16)
 
 
-def summed_everywhere(half):
-    core = lax.axis_index("core")
-    plane = lax.axis_size(PLANE)
-    column = lax.axis_size(COLUMN)
-    part = folded(exchanged(half, PLANE), plane).astype(jnp.bfloat16)
-    part = folded(exchanged(copies(part, column), COLUMN), column).astype(jnp.bfloat16)
-    half = exchanged(copies(part, plane), PLANE)
-    there = shifted(half, "core", 1)
-    low, high = jnp.concatenate([half, there]), jnp.concatenate([there, half])
-    return jnp.where(core == 0, low, high).astype(jnp.float32)
+def fold_kernel(parts_ref, copies_ref):
+    total = jnp.sum(parts_ref[...].astype(jnp.float32), axis=0).astype(jnp.bfloat16)
+    for n in range(copies_ref.shape[0]):
+        copies_ref[n] = total
+
+
+def place_kernel(place_ref, half_ref, *refs):
+    refs[-1][...] = half_ref[...].astype(jnp.float32)
+
+
+def placed(place, half, side, whole):
+    steps, (rows, width) = 4, half.shape
+    tile = (rows // steps, width)
+    given = [] if whole is None else [whole]
+    return pl.pallas_call(
+        place_kernel,
+        out_shape=shape((2 * rows, width), jnp.float32),
+        grid_spec=pltpu.PrefetchScalarGridSpec(
+            num_scalar_prefetch=1,
+            grid=(steps,),
+            in_specs=[pl.BlockSpec(tile, lambda i, at: (i, 0))]
+            + [pl.BlockSpec(memory_space=pl.ANY)] * len(given),
+            out_specs=pl.BlockSpec(tile, lambda i, at: ((at[1] + side) % 2 * steps + i, 0)),
+        ),
+        input_output_aliases={2: 0} if given else {},
+        compiler_params=pltpu.CompilerParams(vmem_limit_bytes=8 * MIB),
+        cost_estimate=pl.CostEstimate(
+            flops=0, bytes_accessed=6 * rows * width, transcendentals=0
+        ),
+    )(place, half, *given)
+
+
+def text_grad_kernel(text_ref, home_ref, *refs):
+    grad = home_ref[...]
+    for ref in refs[:-1]:
+        grad = grad + ref[...].astype(jnp.float32)
+    text = text_ref[...].astype(jnp.float32)
+    scale = lax.rsqrt(jnp.sum(text * text, axis=1, keepdims=True) + EPS)
+    text = text * scale
+    along = jnp.sum(text * grad, axis=1, keepdims=True)
+    refs[-1][...] = (grad - text * along) * scale
 
 
 def body(audio_features, proj_weight, text_raw, positive):
@@ -163,13 +178,8 @@
     bf16, f32 = jnp.bfloat16, jnp.float32
     pair_flops = 2 * rows * rows * blocks * width
 
-    main, rest = call(
-        text_kernel, (shape((rows - REST, width), bf16), shape((REST, width), bf16)), text_raw
-    )
-    rests = [rest] + [shifted(rest, "zh", k) for k in range(1, chips)]
-    main = lax.all_gather(main, "zh", axis=0, tiled=True)
-    own = jnp.concatenate([main] + rests)
-    own, audio_features = lax.optimization_barrier((own, audio_features))
+    (text_b,) = call(text_kernel, (shape((chips, rows, width), bf16),), text_raw)
+    own = exchanged(text_b, "zh")
     other = shifted(own, "core", 1)
     half = channels // 2
     features = lax.dynamic_slice_in_dim(audio_features, core * half, half, 1)
@@ -192,7 +202,7 @@
         positive.reshape(rows, 1),
         own,
         other,
-        scratch=[pltpu.VMEM((blocks * rows, width), bf16), pltpu.VMEM((rows, blocks * rows), f32)],
+        scratch=[pltpu.VMEM((rows, blocks * rows), f32)],
         flops=2 * pair_flops,
     )
     grad_beside = shifted(proj_grad, "core", 1)
@@ -204,10 +214,21 @@
         dot(features, proj_grad, 0, 0),
         flops=2 * half * rows * width,
     )
-    grad_weight = summed_everywhere(weight_half)
-    grad_features = dot(proj_grad, proj_weight, 1, 1).astype(bf16)
+    weight_half, tiles = lax.optimization_barrier((weight_half, tiles))
+    plane = lax.axis_size(PLANE)
+    column = lax.axis_size(COLUMN)
+    part = half // plane
+    parts = exchanged(weight_half.reshape(plane, part, width), PLANE)
+    (grad_features,) = call(
+        features_kernel,
+        (shape((rows, channels), bf16),),
+        proj_grad,
+        proj_weight,
+        flops=40 * rows * channels * width,
+    )
+    grad_features, tiles = lax.optimization_barrier((grad_features, tiles))
     (over,) = call(
-        over_kernel, (shape((chips, rows, width), bf16),), tiles, audio_b, flops=pair_flops // 2
+        over_kernel, (shape((chips, rows, width), bf16),), tiles, audio_b, light=True
     )
     over = shifted(over, "core", 1)
     home, *away = call(
@@ -217,16 +238,21 @@
         tiles,
         audio_b,
         over,
-        flops=pair_flops // 2,
-    )
-    text_grad = home
-    for n, block in enumerate(away):
-        text_grad = text_grad + shifted(block, "zh", n + 1)
-    text_f = text_raw.astype(f32)
-    text_scale = lax.rsqrt(jnp.sum(text_f * text_f, axis=1, keepdims=True) + EPS)
-    text = text_f * text_scale
-    text_along = jnp.sum(text * text_grad, axis=1, keepdims=True)
-    grad_text = (text_grad - text * text_along) * text_scale
+        light=True,
+    )
+    parts, home, away, grad_features = lax.optimization_barrier(
+        (parts, home, away, grad_features)
+    )
+    (parts,) = call(fold_kernel, (shape((column, part, width), bf16),), parts)
+    parts = exchanged(parts, COLUMN)
+    away = [shifted(block, "zh", n + 1) for n, block in enumerate(away)]
+    (parts,) = call(fold_kernel, (shape((plane, part, width), bf16),), parts)
+    weight_half = exchanged(parts, PLANE).reshape(half, width)
+    weight_half, away = lax.optimization_barrier((weight_half, away))
+    there = shifted(weight_half, "core", 1)
+    grad_weight = placed(place, weight_half, 0, None)
+    grad_weight = placed(place, there, 1, grad_weight)
+    (grad_text,) = call(text_grad_kernel, (shape((rows, width), f32),), text_raw, home, *away)
     return (grad_weight, grad_features, grad_text)
 
 

time: 140 us -> 144 us (1.029); the launches traced: 137 us -> 143 us
  waiting for transfers between devices: 10.8 us -> 34.1 us
  starting transfers between devices: 63.4 us -> 42.7 us
  Pallas kernels: 9.2 us -> 15.1 us
  other arithmetic: 4.47 us -> 0.08 us
  blocking collectives: 42.1 us -> 44.9 us
    ppermute x11 -> x8, starting transfers between devices: 51.9 us -> 25.2 us  [shifted(): lax.ppermute(block, axis, [(i, (i + distance) % count) for i in range(cou...]
    all_to_all x1 -> x2, blocking collectives: 23.6 us -> 44.9 us  [exchanged(): return lax.all_to_all(block, axes, split_axis=0, concat_axis=0, tiled=True)]
    all_gather x1 -> x0, blocking collectives: 18.5 us -> none  [body(): main = lax.all_gather(main, 'zh', axis=0, tiled=True)]
    ppermute x11 -> x8, waiting for transfers between devices: 9.94 us -> 23.1 us  [shifted(): lax.ppermute(block, axis, [(i, (i + distance) % count) for i in range(cou...]
    all_to_all x2, waiting for transfers between devices: 0.89 us -> 11 us  [exchanged(): return lax.all_to_all(block, axes, split_axis=0, concat_axis=0, tiled=True)]
    all_to_all x2, starting transfers between devices: 11.5 us -> 17.5 us  [exchanged(): return lax.all_to_all(block, axes, split_axis=0, concat_axis=0, tiled=True)]
    pallas_call x0 -> x2, Pallas kernels: none -> 4.2 us  [placed(): pl.pallas_call(place_kernel, out_shape=shape((2 * rows, width), jnp.float...]
    convert_element_type x1 -> x0, other arithmetic: 2.88 us -> none  [summed_everywhere(): return jnp.where(core == 0, low, high).astype(jnp.float32)]
  transfers between devices with their start and end apart: 13 -> 10, of which waited for: 3 -> 4; matrix products, arithmetic and copies ran while one was open for 4% -> 1% of each run, Pallas kernels for 6% -> 7%
where the time goes in v3:
time: 144 us; the launch traced here: 143 us
  blocking collectives  44.9 us (31%)
  starting transfers between devices  42.7 us (30%)
  waiting for transfers between devices  34.1 us (24%)
  Pallas kernels  15.1 us (10%)
  local copies, waits for them, and re-layouts  5.21 us (4%)
    all_to_all x2, blocking collectives, exchanged(): return lax.all_to_all(block, axes, split_axis=0, concat_axis=0, tiled=True)  44.9 us
    ppermute x8, starting transfers between devices, shifted(): lax.ppermute(block, axis, [(i, (i + distance) % count) for i in range(cou...  25.2 us
    ppermute x8, waiting for transfers between devices, shifted(): lax.ppermute(block, axis, [(i, (i + distance) % count) for i in range(cou...  23.1 us
    all_to_all x2, starting transfers between devices, exchanged(): return lax.all_to_all(block, axes, split_axis=0, concat_axis=0, tiled=True)  17.5 us
    all_to_all x2, waiting for transfers between devices, exchanged(): return lax.all_to_all(block, axes, split_axis=0, concat_axis=0, tiled=True)  11 us
    pallas_call x10, Pallas kernels, call(): pl.pallas_call(kernel, out_shape=outs, in_specs=[scalars if a.shape == (2...  10.9 us
    unnamed x26, local copies, waits for them, and re-layouts  4.35 us
    pallas_call x2, Pallas kernels, placed(): pl.pallas_call(place_kernel, out_shape=shape((2 * rows, width), jnp.float...  4.2 us
  transfers between devices with their start and end apart: 10, of which 4 were waited for; matrix products, arithmetic and copies ran while one was open for 1% of the time, Pallas kernels for 7%

profile of v3, /device:TPU:1, one launch (start us, length us, event | category | flops | bytes accessed | tf_op | source)
XLA Modules:
  0.0 143.3 jit_solution(18204032972793145537)
XLA Ops:
  0.7 1.0 copy-done.4
  1.8 32.3 %all_to_all.20.own_ref = bf16[4,256,512]{2,1,0:T(8,128)(2,1)S(1)} all-to-all(bf16[4,256,512]{2,1,0:T(8,128)(2,1)S(1)} %shard_map.68), channel_id=1, replica_groups=mesh['zh'=4,'core'=2,'zl'=2,'x'=4,'y'=8] {'zh'}, dimensions={0} | all-to-all | bytes 2097152 | tf_op jit(solution)/shard_map/all_to_all | solution.py:23
  34.1 6.8 %collective-permute-start.1 = (bf16[4,256,512]{2,1,0:T(8,128)(2,1)S(1)}, bf16[4,256,512]{2,1,0:T(8,128)(2,1)}, u32[]{:S(2)}, u32[]{:S(2)}) collective-permute-start(bf16[4,256,512]{2,1,0:T(8,128)(2,1)S(1)} %all_to_all.20.own_ref), channel_id=1, source_target_pairs={{0,64},{64,0},{1,65},{65,1},{2,66},{66,2},{3,67},{67,3},{4,68},{68... | collective-permute-start | bytes 3145736 | tf_op jit(solution)/shard_map/ppermute | solution.py:19
  41.0 0.7 constant_dynamic-slice_fusion
  41.7 1.9 %collective-permute-start = (bf16[256,512]{1,0:T(8,128)(2,1)}, bf16[256,512]{1,0:T(8,128)(2,1)S(1)}, u32[]{:S(2)}, u32[]{:S(2)}) collective-permute-start(bf16[256,512]{1,0:T(8,128)(2,1)} %constant_dynamic-slice_fusion), channel_id=1, source_target_pairs={{0,64},{64,0},{1,65},{65,1},{2,66},{66,2},{3,67},{67,3},{4,68},{68... | collective-permute-start | bytes 786440 | tf_op jit(solution)/shard_map/ppermute | solution.py:19
  43.8 0.5 shard_map.67
  44.4 1.2 copy-done.3
  45.7 3.3 %shard_map.69 = (bf16[256,512]{1,0:T(8,128)(2,1)S(1)}, bf16[8,256,256]{2,1,0:T(8,128)(2,1)S(1)}) custom-call(s32[2]{0:T(128)S(1)} %pad_add_fusion.place_ref, f32[256,512]{1,0:T(8,128)S(1)} %get-tuple-element.26.audio_ref, bf16[256,512]{1,0:T(8,128)(2,1)S(1)} %get-tuple-element.27.audio_b_ref, f32[256,1]{1,0:T(8,128)S(1)} %get-tuple-element.28.scale_ref, ...), custom_call_target="tpu_custom_call" | custom-call | flops 1073741824 | bytes 4196360 | tf_op jit(solution)/shard_map/pallas_call | solution.py:34
  49.0 2.4 %collective-permute-start.2 = (bf16[256,512]{1,0:T(8,128)(2,1)S(1)}, bf16[256,512]{1,0:T(8,128)(2,1)S(1)}, u32[]{:S(2)}, u32[]{:S(2)}) collective-permute-start(bf16[256,512]{1,0:T(8,128)(2,1)S(1)} %get-tuple-element.29.grad_ref), channel_id=1, source_target_pairs={{0,64},{64,0},{1,65},{65,1},{2,66},{66,2},{3,67},{67,3},{4,68},{68... | collective-permute-start | bytes 786440 | tf_op jit(solution)/shard_map/ppermute | solution.py:19
  51.4 1.3 shard_map.71
  53.0 1.1 shard_map.70
  54.2 1.4 %shard_map.72 = bf16[4,256,512]{2,1,0:T(8,128)(2,1)} custom-call(bf16[8,256,256]{2,1,0:T(8,128)(2,1)S(1)} %get-tuple-element.33.tiles_ref, bf16[256,512]{1,0:T(8,128)(2,1)S(1)} %get-tuple-element.27.audio_b_ref), custom_call_target="tpu_custom_call" | custom-call | tf_op jit(solution)/shard_map/pallas_call | solution.py:34
  55.6 1.9 %collective-permute-start.3 = (bf16[4,256,512]{2,1,0:T(8,128)(2,1)}, bf16[4,256,512]{2,1,0:T(8,128)(2,1)S(1)}, u32[]{:S(2)}, u32[]{:S(2)}) collective-permute-start(bf16[4,256,512]{2,1,0:T(8,128)(2,1)} %shard_map.72), channel_id=1, source_target_pairs={{0,64},{64,0},{1,65},{65,1},{2,66},{66,2},{3,67},{67,3},{4,68},{68... | collective-permute-start | bytes 3145736 | tf_op jit(solution)/shard_map/ppermute | solution.py:19
  57.5 9.7 %all-to-all-start.1 = ((bf16[32,16,512]{2,1,0:T(8,128)(2,1)}), bf16[32,16,512]{2,1,0:T(8,128)(2,1)S(1)}, u32[]{:S(2)}, u32[]{:S(2)}) async-start(bf16[32,16,512]{2,1,0:T(8,128)(2,1)} %bitcast.3), calls=%async_computation.1 | async-start | bytes 1048576 | tf_op jit(solution)/shard_map/all_to_all | solution.py:23
  67.2 1.0 shard_map.73
  68.3 0.7 copy-done.6
  68.9 0.7 copy-done.8
  69.7 0.7 copy-done.10
  70.4 11.0 %all-to-all-done.1.parts_ref = bf16[32,16,512]{2,1,0:T(8,128)(2,1)S(1)} async-done(((bf16[32,16,512]{2,1,0:T(8,128)(2,1)}), bf16[32,16,512]{2,1,0:T(8,128)(2,1)S(1)}, u32[]{:S(2)}, u32[]{:S(2)}) %all-to-all-start.1) | async-done | bytes 524320 | tf_op jit(solution)/shard_map/all_to_all | solution.py:23
  81.4 12.6 %all_to_all.21.parts_ref = bf16[8,16,512]{2,1,0:T(8,128)(2,1)S(1)} all-to-all(bf16[8,16,512]{2,1,0:T(8,128)(2,1)S(1)} %shard_map.74), channel_id=1, replica_groups=mesh['zh'=4,'core'=2,'zl'=2,'x'=4,'y'=8] {'zh','zl'}, dimensions={0} | all-to-all | bytes 262144 | tf_op jit(solution)/shard_map/all_to_all | solution.py:23
  94.1 0.9 shard_map.75
  94.9 7.8 %all-to-all-start.3 = ((bf16[32,16,512]{2,1,0:T(8,128)(2,1)}), bf16[32,16,512]{2,1,0:T(8,128)(2,1)S(1)}, u32[]{:S(2)}, u32[]{:S(2)}) async-start(bf16[32,16,512]{2,1,0:T(8,128)(2,1)} %shard_map.75), calls=%async_computation.3 | async-start | bytes 1048576 | tf_op jit(solution)/shard_map/all_to_all | solution.py:23
  102.7 1.9 %collective-permute-start.4 = (bf16[256,512]{1,0:T(8,128)(2,1)S(1)}, bf16[256,512]{1,0:T(8,128)(2,1)S(1)}, u32[]{:S(2)}, u32[]{:S(2)}) collective-permute-start(bf16[256,512]{1,0:T(8,128)(2,1)S(1)} %copy-done.11), channel_id=1, source_target_pairs={{0,128},{128,256},{256,384},{384,0},{1,129},{129,257},{257,385},{3... | collective-permute-start | bytes 786440 | tf_op jit(solution)/shard_map/ppermute | solution.py:19
  104.7 4.1 %collective-permute-start.5 = (bf16[256,512]{1,0:T(8,128)(2,1)S(1)}, bf16[256,512]{1,0:T(8,128)(2,1)S(1)}, u32[]{:S(2)}, u32[]{:S(2)}) collective-permute-start(bf16[256,512]{1,0:T(8,128)(2,1)S(1)} %copy-done.9), channel_id=1, source_target_pairs={{0,256},{128,384},{256,0},{384,128},{1,257},{129,385},{257,1},{385... | collective-permute-start | bytes 786440 | tf_op jit(solution)/shard_map/ppermute | solution.py:19
  108.8 3.7 %collective-permute-start.6 = (bf16[256,512]{1,0:T(8,128)(2,1)S(1)}, bf16[256,512]{1,0:T(8,128)(2,1)S(1)}, u32[]{:S(2)}, u32[]{:S(2)}) collective-permute-start(bf16[256,512]{1,0:T(8,128)(2,1)S(1)} %copy-done.7), channel_id=1, source_target_pairs={{0,384},{128,0},{256,128},{384,256},{1,385},{129,1},{257,129},{385... | collective-permute-start | bytes 786440 | tf_op jit(solution)/shard_map/ppermute | solution.py:19
  112.6 4.8 %collective-permute-done.4.refs_0_ = bf16[256,512]{1,0:T(8,128)(2,1)S(1)} collective-permute-done((bf16[256,512]{1,0:T(8,128)(2,1)S(1)}, bf16[256,512]{1,0:T(8,128)(2,1)S(1)}, u32[]{:S(2)}, u32[]{:S(2)}) %collective-permute-start.4) | collective-permute-done | bytes 262176 | tf_op jit(solution)/shard_map/ppermute | solution.py:19
  117.4 7.7 %collective-permute-done.5.refs_1_ = bf16[256,512]{1,0:T(8,128)(2,1)S(1)} collective-permute-done((bf16[256,512]{1,0:T(8,128)(2,1)S(1)}, bf16[256,512]{1,0:T(8,128)(2,1)S(1)}, u32[]{:S(2)}, u32[]{:S(2)}) %collective-permute-start.5) | collective-permute-done | bytes 262176 | tf_op jit(solution)/shard_map/ppermute | solution.py:19
  125.1 10.5 %collective-permute-done.6.refs_2_ = bf16[256,512]{1,0:T(8,128)(2,1)S(1)} collective-permute-done((bf16[256,512]{1,0:T(8,128)(2,1)S(1)}, bf16[256,512]{1,0:T(8,128)(2,1)S(1)}, u32[]{:S(2)}, u32[]{:S(2)}) %collective-permute-start.6) | collective-permute-done | bytes 262176 | tf_op jit(solution)/shard_map/ppermute | solution.py:19
  135.6 2.4 %collective-permute-start.7 = (bf16[512,512]{1,0:T(8,128)(2,1)S(1)}, bf16[512,512]{1,0:T(8,128)(2,1)S(1)}, u32[]{:S(2)}, u32[]{:S(2)}) collective-permute-start(bf16[512,512]{1,0:T(8,128)(2,1)S(1)} %bitcast.6), channel_id=1, source_target_pairs={{0,64},{64,0},{1,65},{65,1},{2,66},{66,2},{3,67},{67,3},{4,68},{68... | collective-permute-start | bytes 1572872 | tf_op jit(solution)/shard_map/ppermute | solution.py:19
  138.0 2.1 %shard_map.76.refs_0_ = f32[1024,512]{1,0:T(8,128)} custom-call(s32[2]{0:T(128)S(1)} %pad_add_fusion.place_ref, bf16[512,512]{1,0:T(8,128)(2,1)S(1)} %bitcast.7), custom_call_target="tpu_custom_call" | custom-call | bytes 1572864 | tf_op jit(solution)/shard_map/pallas_call | solution.py:142
  140.1 1.1 shard_map.78
  141.2 2.1 %shard_map.77 = f32[1024,512]{1,0:T(8,128)} custom-call(s32[2]{0:T(128)S(1)} %pad_add_fusion.place_ref, bf16[512,512]{1,0:T(8,128)(2,1)S(1)} %collective-permute-done.7.half_ref, f32[1024,512]{1,0:T(8,128)} %shard_map.76.refs_0_), custom_call_target="tpu_custom_call", output_to_operand_aliasing={{}: (2, {})} | custom-call | bytes 1572864 | tf_op jit(solution)/shard_map/pallas_call | solution.py:142
  (32 shorter events, 0.8 us)
Async XLA Ops:
  0.6 40.4 %copy-start = (bf16[256,1024]{1,0:T(8,128)(2,1)S(1)}, bf16[256,1024]{1,0:T(8,128)(2,1)}, u32[]{:S(2)}) copy-start(bf16[256,1024]{1,0:T(8,128)(2,1)} %features_ref.1) | copy-start | bytes 1572868
  0.6 1.0 copy-start.4
  1.7 42.0 %copy-start.12 = (s32[256]{0:T(256)S(1)}, s32[256]{0:T(256)}, u32[]{:S(2)}) copy-start(s32[256]{0:T(256)} %param.7) | copy-start | bytes 3076
  1.7 42.1 %copy-start.1 = (bf16[1024,512]{1,0:T(8,128)(2,1)S(1)}, bf16[1024,512]{1,0:T(8,128)(2,1)}, u32[]{:S(2)}) copy-start(bf16[1024,512]{1,0:T(8,128)(2,1)} %weight_ref.3) | copy-start | bytes 3145732
  34.1 10.3 %copy-start.2 = (bf16[4,256,512]{2,1,0:T(8,128)(2,1)}, bf16[4,256,512]{2,1,0:T(8,128)(2,1)S(1)}, u32[]{:S(2)}) copy-start(bf16[4,256,512]{2,1,0:T(8,128)(2,1)S(1)} %all_to_all.20.own_ref) | copy-start | bytes 3145732
  34.1 10.3 %collective-permute-start.1 = (bf16[4,256,512]{2,1,0:T(8,128)(2,1)S(1)}, bf16[4,256,512]{2,1,0:T(8,128)(2,1)}, u32[]{:S(2)}, u32[]{:S(2)}) collective-permute-start(bf16[4,256,512]{2,1,0:T(8,128)(2,1)S(1)} %all_to_all.20.own_ref), channel_id=1, source_target_pairs={{0,64},{64,0},{1,65},{65,1},{2,66},{66,2},{3,67},{67,3},{4,68},{68... | collective-permute-start | bytes 3145736 | tf_op jit(solution)/shard_map/ppermute | solution.py:19
  41.7 11.3 %collective-permute-start = (bf16[256,512]{1,0:T(8,128)(2,1)}, bf16[256,512]{1,0:T(8,128)(2,1)S(1)}, u32[]{:S(2)}, u32[]{:S(2)}) collective-permute-start(bf16[256,512]{1,0:T(8,128)(2,1)} %constant_dynamic-slice_fusion), channel_id=1, source_target_pairs={{0,64},{64,0},{1,65},{65,1},{2,66},{66,2},{3,67},{67,3},{4,68},{68... | collective-permute-start | bytes 786440 | tf_op jit(solution)/shard_map/ppermute | solution.py:19
  44.4 1.2 copy-start.3
  49.0 4.0 %collective-permute-start.2 = (bf16[256,512]{1,0:T(8,128)(2,1)S(1)}, bf16[256,512]{1,0:T(8,128)(2,1)S(1)}, u32[]{:S(2)}, u32[]{:S(2)}) collective-permute-start(bf16[256,512]{1,0:T(8,128)(2,1)S(1)} %get-tuple-element.29.grad_ref), channel_id=1, source_target_pairs={{0,64},{64,0},{1,65},{65,1},{2,66},{66,2},{3,67},{67,3},{4,68},{68... | collective-permute-start | bytes 786440 | tf_op jit(solution)/shard_map/ppermute | solution.py:19
  55.6 11.6 %collective-permute-start.3 = (bf16[4,256,512]{2,1,0:T(8,128)(2,1)}, bf16[4,256,512]{2,1,0:T(8,128)(2,1)S(1)}, u32[]{:S(2)}, u32[]{:S(2)}) collective-permute-start(bf16[4,256,512]{2,1,0:T(8,128)(2,1)} %shard_map.72), channel_id=1, source_target_pairs={{0,64},{64,0},{1,65},{65,1},{2,66},{66,2},{3,67},{67,3},{4,68},{68... | collective-permute-start | bytes 3145736 | tf_op jit(solution)/shard_map/ppermute | solution.py:19
  57.5 23.8 %all-to-all-start.1 = ((bf16[32,16,512]{2,1,0:T(8,128)(2,1)}), bf16[32,16,512]{2,1,0:T(8,128)(2,1)S(1)}, u32[]{:S(2)}, u32[]{:S(2)}) async-start(bf16[32,16,512]{2,1,0:T(8,128)(2,1)} %bitcast.3), calls=%async_computation.1 | async-start | bytes 1048576 | tf_op jit(solution)/shard_map/all_to_all | solution.py:23
  68.2 0.7 copy-start.6
  68.9 0.7 copy-start.8
  69.6 0.7 copy-start.10
  81.3 21.4 %copy-start.11 = (bf16[256,512]{1,0:T(8,128)(2,1)S(1)}, bf16[256,512]{1,0:T(8,128)(2,1)}, u32[]{:S(2)}) copy-start(bf16[256,512]{1,0:T(8,128)(2,1)} %copy-done.10) | copy-start | bytes 786436
  81.3 23.3 %copy-start.9 = (bf16[256,512]{1,0:T(8,128)(2,1)S(1)}, bf16[256,512]{1,0:T(8,128)(2,1)}, u32[]{:S(2)}) copy-start(bf16[256,512]{1,0:T(8,128)(2,1)} %copy-done.8) | copy-start | bytes 786436
  81.3 27.5 %copy-start.7 = (bf16[256,512]{1,0:T(8,128)(2,1)S(1)}, bf16[256,512]{1,0:T(8,128)(2,1)}, u32[]{:S(2)}) copy-start(bf16[256,512]{1,0:T(8,128)(2,1)} %copy-done.6) | copy-start | bytes 786436
  94.1 46.0 %copy-start.5 = (bf16[256,512]{1,0:T(8,128)(2,1)S(1)}, bf16[256,512]{1,0:T(8,128)(2,1)}, u32[]{:S(2)}) copy-start(bf16[256,512]{1,0:T(8,128)(2,1)} %text_ref.3) | copy-start | bytes 786436
  94.9 40.7 %all-to-all-start.3 = ((bf16[32,16,512]{2,1,0:T(8,128)(2,1)}), bf16[32,16,512]{2,1,0:T(8,128)(2,1)S(1)}, u32[]{:S(2)}, u32[]{:S(2)}) async-start(bf16[32,16,512]{2,1,0:T(8,128)(2,1)} %shard_map.75), calls=%async_computation.3 | async-start | bytes 1048576 | tf_op jit(solution)/shard_map/all_to_all | solution.py:23
  102.7 14.6 %collective-permute-start.4 = (bf16[256,512]{1,0:T(8,128)(2,1)S(1)}, bf16[256,512]{1,0:T(8,128)(2,1)S(1)}, u32[]{:S(2)}, u32[]{:S(2)}) collective-permute-start(bf16[256,512]{1,0:T(8,128)(2,1)S(1)} %copy-done.11), channel_id=1, source_target_pairs={{0,128},{128,256},{256,384},{384,0},{1,129},{129,257},{257,385},{3... | collective-permute-start | bytes 786440 | tf_op jit(solution)/shard_map/ppermute | solution.py:19
  104.7 20.4 %collective-permute-start.5 = (bf16[256,512]{1,0:T(8,128)(2,1)S(1)}, bf16[256,512]{1,0:T(8,128)(2,1)S(1)}, u32[]{:S(2)}, u32[]{:S(2)}) collective-permute-start(bf16[256,512]{1,0:T(8,128)(2,1)S(1)} %copy-done.9), channel_id=1, source_target_pairs={{0,256},{128,384},{256,0},{384,128},{1,257},{129,385},{257,1},{385... | collective-permute-start | bytes 786440 | tf_op jit(solution)/shard_map/ppermute | solution.py:19
  108.8 26.8 %collective-permute-start.6 = (bf16[256,512]{1,0:T(8,128)(2,1)S(1)}, bf16[256,512]{1,0:T(8,128)(2,1)S(1)}, u32[]{:S(2)}, u32[]{:S(2)}) collective-permute-start(bf16[256,512]{1,0:T(8,128)(2,1)S(1)} %copy-done.7), channel_id=1, source_target_pairs={{0,384},{128,0},{256,128},{384,256},{1,385},{129,1},{257,129},{385... | collective-permute-start | bytes 786440 | tf_op jit(solution)/shard_map/ppermute | solution.py:19
  135.6 5.6 %collective-permute-start.7 = (bf16[512,512]{1,0:T(8,128)(2,1)S(1)}, bf16[512,512]{1,0:T(8,128)(2,1)S(1)}, u32[]{:S(2)}, u32[]{:S(2)}) collective-permute-start(bf16[512,512]{1,0:T(8,128)(2,1)S(1)} %bitcast.6), channel_id=1, source_target_pairs={{0,64},{64,0},{1,65},{65,1},{2,66},{66,2},{3,67},{67,3},{4,68},{68... | collective-permute-start | bytes 1572872 | tf_op jit(solution)/shard_map/ppermute | solution.py:19

commit v4 on v3

v4 whole, which is shorter than its diff:
```python
import jax
import jax.numpy as jnp
from jax import lax
from jax.experimental import pallas as pl
from jax.experimental.pallas import tpu as pltpu
from jax.sharding import Mesh, PartitionSpec as P

SCALE = 100.0
EPS = 1e-06
FINE = ("zh", "core", "zl", "x", "y")
SPLIT = (4, 2, 2, 4, 8)
PLANE = ("x", "y")
COLUMN = ("zh", "zl")
TAIL = 16
MIB = 1 << 20


def shifted(block, axis, distance):
    count = lax.axis_size(axis)
    return lax.ppermute(block, axis, [(i, (i + distance) % count) for i in range(count)])


def exchanged(block, axes):
    return lax.all_to_all(block, axes, split_axis=0, concat_axis=0, tiled=True)


def dot(a, b, da, db):
    return lax.dot_general(a, b, (((da,), (db,)), ((), ())), preferred_element_type=jnp.float32)


def call(kernel, outs, *args, scratch=(), flops=0, limit=16, light=False):
    whole = pl.BlockSpec(memory_space=pltpu.VMEM)
    scalars = pl.BlockSpec(memory_space=pltpu.SMEM)
    size = 0 if light else sum(a.size * a.dtype.itemsize for a in (*args, *outs))
    return pl.pallas_call(
        kernel,
        out_shape=outs,
        in_specs=[scalars if a.shape == (2,) else whole for a in args],
        out_specs=[whole] * len(outs),
        scratch_shapes=scratch,
        compiler_params=pltpu.CompilerParams(vmem_limit_bytes=limit * MIB),
        cost_estimate=pl.CostEstimate(flops=flops, bytes_accessed=size, transcendentals=0),
    )(*args)


def shape(dims, dtype):
    return jax.ShapeDtypeStruct(dims, dtype)


def text_kernel(text_ref, sent_ref):
    rows = text_ref.shape[0]
    text = text_ref[...].astype(jnp.float32)
    scale = lax.rsqrt(jnp.sum(text * text, axis=1, keepdims=True) + EPS)
    text = (text * scale).astype(jnp.bfloat16).astype(jnp.float32)
    largest = jnp.max(jnp.max(jnp.abs(text), axis=1, keepdims=True), axis=0, keepdims=True)
    power = jnp.floor(jnp.log2(jnp.maximum(largest, 1e-30))) - 13.0
    sent_ref[:rows, :] = (text * jnp.exp2(-power)).astype(jnp.bfloat16)
    tail = (sent_ref.shape[0] - rows, sent_ref.shape[1])
    sent_ref[rows:, :] = jnp.broadcast_to(power, tail).astype(jnp.bfloat16)


def audio_kernel(features_ref, weight_ref, audio_ref, audio_b_ref, scale_ref):
    proj = dot(features_ref[...], weight_ref[...], 1, 0)
    scale = lax.rsqrt(jnp.sum(proj * proj, axis=1, keepdims=True) + EPS)
    audio = proj * scale
    audio_ref[...] = audio
    audio_b_ref[...] = audio.astype(jnp.bfloat16)
    scale_ref[...] = scale


def score_kernel(
    place_ref, audio_ref, audio_b_ref, scale_ref, features_ref, positive_ref, own_ref, other_ref,
    grad_ref, tiles_ref, sent_ref, scores_ref,
):
    core = place_ref[1]
    blocks, rows, _ = tiles_ref.shape
    chips = blocks // 2
    audio_b = audio_b_ref[...]

    def text(n):
        held = own_ref if n < chips else other_ref
        start = n % chips * (rows + TAIL)
        power = held[start + rows : start + rows + TAIL, :128].astype(jnp.float32)
        return held[start : start + rows, :], SCALE * jnp.exp2(power[:1, :1])

    for n in range(blocks):
        block, scale = text(n)
        scores_ref[:, n * rows : (n + 1) * rows] = scale * dot(audio_b, block, 1, 1)
    step = 16
    ids = lax.broadcasted_iota(jnp.int32, (step, rows), 1)
    for r in range(0, rows, step):
        scores = scores_ref[r : r + step, :]
        weights = jnp.exp(scores - jnp.max(scores, axis=1, keepdims=True))
        weights = weights * (1.0 / jnp.sum(weights, axis=1, keepdims=True))
        positive = positive_ref[r : r + step, :]
        for n in range(blocks):
            column = core if n < chips else 1 - core
            first = ((n % chips) * 2 + column) * rows
            match = jnp.where(positive - first == ids, 1.0, 0.0)
            part = weights[:, n * rows : (n + 1) * rows] - match
            tiles_ref[n, r : r + step, :] = part.astype(jnp.bfloat16)
    total = jnp.zeros(audio_ref.shape, jnp.float32)
    for n in range(blocks):
        block, scale = text(n)
        total = total + scale * dot(tiles_ref[n], block, 1, 0)
    audio = audio_ref[...]
    along = jnp.sum(audio * total, axis=1, keepdims=True)
    grad = ((total - audio * along) * scale_ref[...]).astype(jnp.bfloat16)
    grad_ref[...] = grad
    half = features_ref.shape[1] // 2
    features = features_ref[:, pl.ds(pl.multiple_of((1 - core) * half, half), half)]
    sent_ref[:half, :] = dot(features, grad, 0, 0).astype(jnp.bfloat16)
    for n in range(chips):
        part = SCALE * dot(tiles_ref[chips + n], audio_b, 0, 0)
        sent_ref[half + n * rows : half + (n + 1) * rows, :] = part.astype(jnp.bfloat16)


def own_kernel(place_ref, features_ref, grad_ref, weight_ref):
    half = features_ref.shape[1] // 2
    features = features_ref[:, pl.ds(pl.multiple_of(place_ref[1] * half, half), half)]
    weight_ref[...] = dot(features, grad_ref[...], 0, 0)


def half_kernel(weight_ref, got_ref, half_ref):
    parts, rows, width = half_ref.shape
    total = weight_ref[...] + got_ref[: parts * rows, :].astype(jnp.float32)
    half_ref[...] = total.astype(jnp.bfloat16).reshape(parts, rows, width)


def features_kernel(grad_ref, weight_ref, out_ref):
    out_ref[...] = dot(grad_ref[...], weight_ref[...], 1, 1).astype(jnp.bfloat16)


def text_sums_kernel(
    place_ref, tiles_ref, audio_b_ref, got_ref,
    home_ref, next_ref, last_ref, forward_ref, backward_ref,
):
    rows = home_ref.shape[0]
    chips = tiles_ref.shape[0] // 2
    half = got_ref.shape[0] - chips * rows

    def sums(distance):
        to = lax.rem(place_ref[0] + distance, chips)
        start = pl.multiple_of(half + to * rows, rows)
        part = SCALE * dot(tiles_ref[to], audio_b_ref[...], 0, 0)
        return part + got_ref[pl.ds(start, rows), :].astype(jnp.float32)

    home_ref[...] = sums(0)
    next_ref[...] = sums(1)
    last_ref[...] = sums(chips - 1)
    across = sums(2).astype(jnp.bfloat16)
    forward_ref[...] = across[: rows // 2]
    backward_ref[...] = across[rows // 2 :]


def relay_kernel(next_ref, last_ref, forward_ref, backward_ref, to_next_ref, to_last_ref):
    cut = next_ref.shape[0] // 2
    ahead = next_ref[:cut, :] + forward_ref[...].astype(jnp.float32)
    behind = last_ref[cut:, :] + backward_ref[...].astype(jnp.float32)
    to_next_ref[:cut, :] = ahead.astype(jnp.bfloat16)
    to_next_ref[cut:, :] = next_ref[cut:, :].astype(jnp.bfloat16)
    to_last_ref[:cut, :] = last_ref[:cut, :].astype(jnp.bfloat16)
    to_last_ref[cut:, :] = behind.astype(jnp.bfloat16)


def fold_kernel(parts_ref, copies_ref):
    total = jnp.sum(parts_ref[...].astype(jnp.float32), axis=0).astype(jnp.bfloat16)
    for n in range(copies_ref.shape[0]):
        copies_ref[n] = total


def place_kernel(place_ref, half_ref, *refs):
    refs[-1][...] = half_ref[...].astype(jnp.float32)


def placed(place, half, side, whole):
    rows, width = half.shape
    given = [] if whole is None else [whole]
    return pl.pallas_call(
        place_kernel,
        out_shape=shape((2 * rows, width), jnp.float32),
        grid_spec=pltpu.PrefetchScalarGridSpec(
            num_scalar_prefetch=1,
            grid=(1,),
            in_specs=[pl.BlockSpec((rows, width), lambda i, at: (0, 0))]
            + [pl.BlockSpec(memory_space=pl.ANY)] * len(given),
            out_specs=pl.BlockSpec((rows, width), lambda i, at: ((at[1] + side) % 2, 0)),
        ),
        input_output_aliases={2: 0} if given else {},
        compiler_params=pltpu.CompilerParams(vmem_limit_bytes=8 * MIB),
        cost_estimate=pl.CostEstimate(
            flops=0, bytes_accessed=6 * rows * width, transcendentals=0
        ),
    )(place, half, *given)


def text_grad_kernel(text_ref, home_ref, *refs):
    grad = home_ref[...]
    for ref in refs[:-1]:
        grad = grad + ref[...].astype(jnp.float32)
    text = text_ref[...].astype(jnp.float32)
    scale = lax.rsqrt(jnp.sum(text * text, axis=1, keepdims=True) + EPS)
    text = text * scale
    along = jnp.sum(text * grad, axis=1, keepdims=True)
    refs[-1][...] = (grad - text * along) * scale


def body(audio_features, proj_weight, text_raw, positive):
    rows, channels = audio_features.shape
    width = text_raw.shape[1]
    chips = lax.axis_size("zh")
    blocks = chips * lax.axis_size("core")
    place = jnp.stack([lax.axis_index("zh"), lax.axis_index("core")]).astype(jnp.int32)
    bf16, f32 = jnp.bfloat16, jnp.float32
    pair_flops = 2 * rows * rows * blocks * width
    half = channels // 2
    block = shape((rows, width), f32)
    block_b = shape((rows, width), bf16)
    cut_b = shape((rows // 2, width), bf16)

    (sent,) = call(text_kernel, (shape((rows + TAIL, width), bf16),), text_raw)
    own = lax.all_gather(sent.astype(jnp.float16), "zh", axis=0, tiled=True).astype(bf16)
    own, audio_features = lax.optimization_barrier((own, audio_features))
    other = shifted(own, "core", 1)
    audio, audio_b, scale = call(
        audio_kernel,
        (block, block_b, shape((rows, 1), f32)),
        audio_features,
        proj_weight,
        flops=2 * rows * channels * width,
    )
    proj_grad, tiles, sent = call(
        score_kernel,
        (block_b, shape((blocks, rows, rows), bf16), shape((half + chips * rows, width), bf16)),
        place,
        audio,
        audio_b,
        scale,
        audio_features,
        positive.reshape(rows, 1),
        own,
        other,
        scratch=[pltpu.VMEM((rows, blocks * rows), f32)],
        flops=3 * pair_flops,
        limit=20,
    )
    got = shifted(sent, "core", 1)
    (weight,) = call(
        own_kernel, (shape((half, width), f32),), place, audio_features, proj_grad, light=True
    )
    (grad_features,) = call(
        features_kernel, (shape((rows, channels), bf16),), proj_grad, proj_weight, light=True
    )
    got, weight, grad_features = lax.optimization_barrier((got, weight, grad_features))
    plane = lax.axis_size(PLANE)
    column = lax.axis_size(COLUMN)
    part = half // plane
    (parts,) = call(half_kernel, (shape((plane, part, width), bf16),), weight, got)
    parts, got = lax.optimization_barrier((parts, got))
    parts = exchanged(parts, PLANE)
    home, following, last, forward, backward = call(
        text_sums_kernel,
        (block, block, block, cut_b, cut_b),
        place,
        tiles,
        audio_b,
        got,
        flops=pair_flops,
    )
    forward = shifted(forward, "zh", 1)
    backward = shifted(backward, "zh", -1)
    parts, forward, backward = lax.optimization_barrier((parts, forward, backward))
    (parts,) = call(fold_kernel, (shape((column, part, width), bf16),), parts)
    parts = exchanged(parts, COLUMN)
    to_next, to_last = call(
        relay_kernel, (block_b, block_b), following, last, forward, backward, light=True
    )
    (parts,) = call(fold_kernel, (shape((plane, part, width), bf16),), parts)
    parts, to_next, to_last = lax.optimization_barrier((parts, to_next, to_last))
    weight_half = exchanged(parts, PLANE).reshape(half, width)
    arrived = [shifted(to_next, "zh", 1), shifted(to_last, "zh", -1)]
    weight_half, arrived = lax.optimization_barrier((weight_half, arrived))
    there = shifted(weight_half, "core", 1)
    grad_weight = placed(place, weight_half, 0, None)
    grad_weight = placed(place, there, 1, grad_weight)
    (grad_text,) = call(text_grad_kernel, (block,), text_raw, home, *arrived)
    return (grad_weight, grad_features, grad_text)


def solution(mesh):
    fine = Mesh(mesh.devices.reshape(SPLIT), FINE)
    rows = P(FINE, None)
    return jax.shard_map(
        body,
        mesh=fine,
        in_specs=(rows, P(), rows, P(FINE)),
        out_specs=(P(), rows, rows),
        check_vma=False,
    )
```

time: 144 us -> 125 us (0.87)
  blocking collectives: 44.9 us -> 28.3 us
  waiting for transfers between devices: 34.1 us -> 24.6 us
  starting transfers between devices: 42.7 us -> 50.1 us
    all_to_all x2 -> x0, blocking collectives: 44.9 us -> none  [exchanged(): return lax.all_to_all(block, axes, split_axis=0, concat_axis=0, tiled=True)]
    all_gather x0 -> x1, blocking collectives: none -> 28.3 us  [body(): lax.all_gather(sent.astype(jnp.float16), 'zh', axis=0, tiled=True)]
    all_to_all x2 -> x3, starting transfers between devices: 17.5 us -> 23.3 us  [exchanged(): return lax.all_to_all(block, axes, split_axis=0, concat_axis=0, tiled=True)]
    all_to_all x2 -> x3, waiting for transfers between devices: 11 us -> 5.62 us  [exchanged(): return lax.all_to_all(block, axes, split_axis=0, concat_axis=0, tiled=True)]
    ppermute x8 -> x7, waiting for transfers between devices: 23.1 us -> 19 us  [shifted(): lax.ppermute(block, axis, [(i, (i + distance) % count) for i in range(cou...]
    ppermute x8 -> x7, starting transfers between devices: 25.2 us -> 26.8 us  [shifted(): lax.ppermute(block, axis, [(i, (i + distance) % count) for i in range(cou...]
    pallas_call x10 -> x11, Pallas kernels: 10.9 us -> 11.6 us  [call(): pl.pallas_call(kernel, out_shape=outs, in_specs=[scalars if a.shape == (2...]
  transfers between devices with their start and end apart: 10 -> 10, of which waited for: 4 -> 7; matrix products, arithmetic and copies ran while one was open for 1% -> 0% of each run, Pallas kernels for 7% -> 5%
where the time goes in v4:
time: 125 us
  starting transfers between devices  50.1 us (40%)
  blocking collectives  28.3 us (23%)
  waiting for transfers between devices  24.6 us (20%)
  Pallas kernels  14.8 us (12%)
  local copies, waits for them, and re-layouts  5.6 us (4%)
    all_gather x1, blocking collectives, body(): lax.all_gather(sent.astype(jnp.float16), 'zh', axis=0, tiled=True)  28.3 us
    ppermute x7, starting transfers between devices, shifted(): lax.ppermute(block, axis, [(i, (i + distance) % count) for i in range(cou...  26.8 us
    all_to_all x3, starting transfers between devices, exchanged(): return lax.all_to_all(block, axes, split_axis=0, concat_axis=0, tiled=True)  23.3 us
    ppermute x7, waiting for transfers between devices, shifted(): lax.ppermute(block, axis, [(i, (i + distance) % count) for i in range(cou...  19 us
    pallas_call x11, Pallas kernels, call(): pl.pallas_call(kernel, out_shape=outs, in_specs=[scalars if a.shape == (2...  11.6 us
    all_to_all x3, waiting for transfers between devices, exchanged(): return lax.all_to_all(block, axes, split_axis=0, concat_axis=0, tiled=True)  5.62 us
    unnamed x26, local copies, waits for them, and re-layouts  5.47 us
    pallas_call x2, Pallas kernels, placed(): pl.pallas_call(place_kernel, out_shape=shape((2 * rows, width), jnp.float...  3.16 us
  transfers between devices with their start and end apart: 10, of which 7 were waited for; matrix products, arithmetic and copies ran while one was open for 0% of the time, Pallas kernels for 5%

profile of v4, /device:TPU:1, one launch (start us, length us, event | category | flops | bytes accessed | tf_op | source)
XLA Modules:
  0.0 124.5 jit_solution(16040761097589083443)
XLA Ops:
  0.6 0.9 copy-done.4
  2.0 28.3 %all-gather.1 = f16[1088,512]{1,0:T(8,128)(2,1)S(1)} all-gather(f16[272,512]{1,0:T(8,128)(2,1)S(1)} %convert_element_type.6), channel_id=1, replica_groups=mesh['zh'=4,'core'=2,'zl'=2,'x'=4,'y'=8] {'zh'}, dimensions={0}, use_global_device_ids=true | all-gather | bytes 1392640 | tf_op jit(solution)/shard_map/all_gather | solution.py:222
  30.5 6.1 %collective-permute-start = (bf16[1088,512]{1,0:T(8,128)(2,1)S(1)}, bf16[1088,512]{1,0:T(8,128)(2,1)}, u32[]{:S(2)}, u32[]{:S(2)}) collective-permute-start(bf16[1088,512]{1,0:T(8,128)(2,1)S(1)} %convert_element_type.7.own_ref), channel_id=1, source_target_pairs={{0,64},{64,0},{1,65},{65,1},{2,66},{66,2},{3,67},{67,3},{4,68},{68... | collective-permute-start | bytes 3342344 | tf_op jit(solution)/shard_map/ppermute | solution.py:20
  37.3 1.7 %collective-permute-done.other_ref = bf16[1088,512]{1,0:T(8,128)(2,1)} collective-permute-done((bf16[1088,512]{1,0:T(8,128)(2,1)S(1)}, bf16[1088,512]{1,0:T(8,128)(2,1)}, u32[]{:S(2)}, u32[]{:S(2)}) %collective-permute-start) | collective-permute-done | bytes 1114144 | tf_op jit(solution)/shard_map/ppermute | solution.py:20
  39.0 4.0 %shard_map.69 = (bf16[256,512]{1,0:T(8,128)(2,1)S(1)}, bf16[8,256,256]{2,1,0:T(8,128)(2,1)S(1)}, bf16[1536,512]{1,0:T(8,128)(2,1)S(1)}) custom-call(s32[2]{0:T(128)S(1)} %pad_add_fusion.place_ref, f32[256,512]{1,0:T(8,128)S(1)} %get-tuple-element.33.audio_ref, bf16[256,512]{1,0:T(8,128)(2,1)S(1)} %get-tuple-element.34.audio_b_ref, ...), custom_call_target="tpu_custom_call" | custom-call | flops 1610612736 | bytes 6424584 | tf_op jit(solution)/shard_map/pallas_call | solution.py:35
  43.0 2.3 %collective-permute-start.1 = (bf16[1536,512]{1,0:T(8,128)(2,1)S(1)}, bf16[1536,512]{1,0:T(8,128)(2,1)S(1)}, u32[]{:S(2)}, u32[]{:S(2)}) collective-permute-start(bf16[1536,512]{1,0:T(8,128)(2,1)S(1)} %get-tuple-element.37), channel_id=1, source_target_pairs={{0,64},{64,0},{1,65},{65,1},{2,66},{66,2},{3,67},{67,3},{4,68},{68... | collective-permute-start | bytes 4718600 | tf_op jit(solution)/shard_map/ppermute | solution.py:20
  45.3 1.3 %shard_map.71 = bf16[256,1024]{1,0:T(8,128)(2,1)} custom-call(bf16[256,512]{1,0:T(8,128)(2,1)S(1)} %get-tuple-element.38.grad_ref, bf16[1024,512]{1,0:T(8,128)(2,1)S(1)} %copy-done), custom_call_target="tpu_custom_call" | custom-call | tf_op jit(solution)/shard_map/pallas_call | solution.py:35
  46.6 0.9 shard_map.70.weight_ref
  47.5 0.8 collective-permute-done.1.got_ref
  48.3 0.9 shard_map.72
  49.3 9.7 %all-to-all-start = ((bf16[32,16,512]{2,1,0:T(8,128)(2,1)}), bf16[32,16,512]{2,1,0:T(8,128)(2,1)S(1)}, u32[]{:S(2)}, u32[]{:S(2)}) async-start(bf16[32,16,512]{2,1,0:T(8,128)(2,1)} %shard_map.72), calls=%async_computation | async-start | bytes 1048576 | tf_op jit(solution)/shard_map/all_to_all | solution.py:24
  58.9 1.0 shard_map.73
  60.0 0.8 copy-done.6
  61.6 0.8 copy-done.10
  62.4 3.0 %collective-permute-start.2 = (bf16[128,512]{1,0:T(8,128)(2,1)S(1)}, bf16[128,512]{1,0:T(8,128)(2,1)S(1)}, u32[]{:S(2)}, u32[]{:S(2)}) collective-permute-start(bf16[128,512]{1,0:T(8,128)(2,1)S(1)} %get-tuple-element.44), channel_id=1, source_target_pairs={{0,128},{128,256},{256,384},{384,0},{1,129},{129,257},{257,385},{3... | collective-permute-start | bytes 393224 | tf_op jit(solution)/shard_map/ppermute | solution.py:20
  65.4 4.4 %collective-permute-start.3 = (bf16[128,512]{1,0:T(8,128)(2,1)S(1)}, bf16[128,512]{1,0:T(8,128)(2,1)S(1)}, u32[]{:S(2)}, u32[]{:S(2)}) collective-permute-start(bf16[128,512]{1,0:T(8,128)(2,1)S(1)} %get-tuple-element.45), channel_id=1, source_target_pairs={{0,384},{128,0},{256,128},{384,256},{1,385},{129,1},{257,129},{385... | collective-permute-start | bytes 393224 | tf_op jit(solution)/shard_map/ppermute | solution.py:20
  69.8 2.9 %collective-permute-done.2.forward_ref = bf16[128,512]{1,0:T(8,128)(2,1)S(1)} collective-permute-done((bf16[128,512]{1,0:T(8,128)(2,1)S(1)}, bf16[128,512]{1,0:T(8,128)(2,1)S(1)}, u32[]{:S(2)}, u32[]{:S(2)}) %collective-permute-start.2) | collective-permute-done | bytes 131104 | tf_op jit(solution)/shard_map/ppermute | solution.py:20
  72.7 3.5 %collective-permute-done.3.backward_ref = bf16[128,512]{1,0:T(8,128)(2,1)S(1)} collective-permute-done((bf16[128,512]{1,0:T(8,128)(2,1)S(1)}, bf16[128,512]{1,0:T(8,128)(2,1)S(1)}, u32[]{:S(2)}, u32[]{:S(2)}) %collective-permute-start.3) | collective-permute-done | bytes 131104 | tf_op jit(solution)/shard_map/ppermute | solution.py:20
  76.9 4.6 %all-to-all-start.1 = ((bf16[8,16,512]{2,1,0:T(8,128)(2,1)}), bf16[8,16,512]{2,1,0:T(8,128)(2,1)S(1)}, u32[]{:S(2)}, u32[]{:S(2)}) async-start(bf16[8,16,512]{2,1,0:T(8,128)(2,1)} %shard_map.74), calls=%async_computation.1 | async-start | bytes 262144 | tf_op jit(solution)/shard_map/all_to_all | solution.py:24
  81.5 1.0 copy-done.9
  82.5 1.0 copy-done.11
  83.6 5.6 %all-to-all-done.1.parts_ref = bf16[8,16,512]{2,1,0:T(8,128)(2,1)S(1)} async-done(((bf16[8,16,512]{2,1,0:T(8,128)(2,1)}), bf16[8,16,512]{2,1,0:T(8,128)(2,1)S(1)}, u32[]{:S(2)}, u32[]{:S(2)}) %all-to-all-start.1) | async-done | bytes 131104 | tf_op jit(solution)/shard_map/all_to_all | solution.py:24
  89.3 0.9 shard_map.75
  90.1 9.0 %all-to-all-start.2 = ((bf16[32,16,512]{2,1,0:T(8,128)(2,1)}), bf16[32,16,512]{2,1,0:T(8,128)(2,1)S(1)}, u32[]{:S(2)}, u32[]{:S(2)}) async-start(bf16[32,16,512]{2,1,0:T(8,128)(2,1)} %shard_map.75), calls=%async_computation.2 | async-start | bytes 1048576 | tf_op jit(solution)/shard_map/all_to_all | solution.py:24
  99.2 2.1 %collective-permute-start.4 = (bf16[256,512]{1,0:T(8,128)(2,1)S(1)}, bf16[256,512]{1,0:T(8,128)(2,1)S(1)}, u32[]{:S(2)}, u32[]{:S(2)}) collective-permute-start(bf16[256,512]{1,0:T(8,128)(2,1)S(1)} %get-tuple-element.54), channel_id=1, source_target_pairs={{0,128},{128,256},{256,384},{384,0},{1,129},{129,257},{257,385},{3... | collective-permute-start | bytes 786440 | tf_op jit(solution)/shard_map/ppermute | solution.py:20
  101.3 5.4 %collective-permute-start.5 = (bf16[256,512]{1,0:T(8,128)(2,1)S(1)}, bf16[256,512]{1,0:T(8,128)(2,1)S(1)}, u32[]{:S(2)}, u32[]{:S(2)}) collective-permute-start(bf16[256,512]{1,0:T(8,128)(2,1)S(1)} %get-tuple-element.55), channel_id=1, source_target_pairs={{0,384},{128,0},{256,128},{384,256},{1,385},{129,1},{257,129},{385... | collective-permute-start | bytes 786440 | tf_op jit(solution)/shard_map/ppermute | solution.py:20
  106.7 3.7 %collective-permute-done.4.refs_0_ = bf16[256,512]{1,0:T(8,128)(2,1)S(1)} collective-permute-done((bf16[256,512]{1,0:T(8,128)(2,1)S(1)}, bf16[256,512]{1,0:T(8,128)(2,1)S(1)}, u32[]{:S(2)}, u32[]{:S(2)}) %collective-permute-start.4) | collective-permute-done | bytes 262176 | tf_op jit(solution)/shard_map/ppermute | solution.py:20
  110.5 6.3 %collective-permute-done.5.refs_1_ = bf16[256,512]{1,0:T(8,128)(2,1)S(1)} collective-permute-done((bf16[256,512]{1,0:T(8,128)(2,1)S(1)}, bf16[256,512]{1,0:T(8,128)(2,1)S(1)}, u32[]{:S(2)}, u32[]{:S(2)}) %collective-permute-start.5) | collective-permute-done | bytes 262176 | tf_op jit(solution)/shard_map/ppermute | solution.py:20
  116.8 3.6 %collective-permute-start.6 = (bf16[512,512]{1,0:T(8,128)(2,1)S(1)}, bf16[512,512]{1,0:T(8,128)(2,1)S(1)}, u32[]{:S(2)}, u32[]{:S(2)}) collective-permute-start(bf16[512,512]{1,0:T(8,128)(2,1)S(1)} %bitcast.4), channel_id=1, source_target_pairs={{0,64},{64,0},{1,65},{65,1},{2,66},{66,2},{3,67},{67,3},{4,68},{68... | collective-permute-start | bytes 1572872 | tf_op jit(solution)/shard_map/ppermute | solution.py:20
  120.3 1.6 %shard_map.77.refs_0_ = f32[1024,512]{1,0:T(8,128)} custom-call(s32[2]{0:T(128)S(1)} %pad_add_fusion.place_ref, bf16[512,512]{1,0:T(8,128)(2,1)S(1)} %bitcast.5), custom_call_target="tpu_custom_call" | custom-call | bytes 1572864 | tf_op jit(solution)/shard_map/pallas_call | solution.py:179
  121.9 1.0 shard_map.79
  123.0 1.6 %shard_map.78 = f32[1024,512]{1,0:T(8,128)} custom-call(s32[2]{0:T(128)S(1)} %pad_add_fusion.place_ref, bf16[512,512]{1,0:T(8,128)(2,1)S(1)} %collective-permute-done.6.half_ref, f32[1024,512]{1,0:T(8,128)} %shard_map.77.refs_0_), custom_call_target="tpu_custom_call", output_to_operand_aliasing={{}: (2, {})} | custom-call | bytes 1572864 | tf_op jit(solution)/shard_map/pallas_call | solution.py:179
  (32 shorter events, 3.0 us)
Async XLA Ops:
  0.6 1.0 copy-start.4
  2.0 34.6 %copy-start.12 = (s32[256]{0:T(256)S(1)}, s32[256]{0:T(256)}, u32[]{:S(2)}) copy-start(s32[256]{0:T(256)} %param.7) | copy-start | bytes 3076
  2.0 34.7 %copy-start = (bf16[1024,512]{1,0:T(8,128)(2,1)S(1)}, bf16[1024,512]{1,0:T(8,128)(2,1)}, u32[]{:S(2)}) copy-start(bf16[1024,512]{1,0:T(8,128)(2,1)} %weight_ref.3) | copy-start | bytes 3145732
  2.0 34.7 %copy-start.1 = (bf16[256,1024]{1,0:T(8,128)(2,1)S(1)}, bf16[256,1024]{1,0:T(8,128)(2,1)}, u32[]{:S(2)}) copy-start(bf16[256,1024]{1,0:T(8,128)(2,1)} %features_ref.2) | copy-start | bytes 1572868
  30.5 8.6 %collective-permute-start = (bf16[1088,512]{1,0:T(8,128)(2,1)S(1)}, bf16[1088,512]{1,0:T(8,128)(2,1)}, u32[]{:S(2)}, u32[]{:S(2)}) collective-permute-start(bf16[1088,512]{1,0:T(8,128)(2,1)S(1)} %convert_element_type.7.own_ref), channel_id=1, source_target_pairs={{0,64},{64,0},{1,65},{65,1},{2,66},{66,2},{3,67},{67,3},{4,68},{68... | collective-permute-start | bytes 3342344 | tf_op jit(solution)/shard_map/ppermute | solution.py:20
  43.0 4.5 %copy-start.2 = (bf16[8,256,256]{2,1,0:T(8,128)(2,1)}, bf16[8,256,256]{2,1,0:T(8,128)(2,1)S(1)}, u32[]{:S(2)}) copy-start(bf16[8,256,256]{2,1,0:T(8,128)(2,1)S(1)} %get-tuple-element.42.tiles_ref) | copy-start | bytes 3145732
  43.0 5.3 %collective-permute-start.1 = (bf16[1536,512]{1,0:T(8,128)(2,1)S(1)}, bf16[1536,512]{1,0:T(8,128)(2,1)S(1)}, u32[]{:S(2)}, u32[]{:S(2)}) collective-permute-start(bf16[1536,512]{1,0:T(8,128)(2,1)S(1)} %get-tuple-element.37), channel_id=1, source_target_pairs={{0,64},{64,0},{1,65},{65,1},{2,66},{66,2},{3,67},{67,3},{4,68},{68... | collective-permute-start | bytes 4718600 | tf_op jit(solution)/shard_map/ppermute | solution.py:20
  48.3 10.6 %copy-start.3 = (bf16[8,256,256]{2,1,0:T(8,128)(2,1)S(1)}, bf16[8,256,256]{2,1,0:T(8,128)(2,1)}, u32[]{:S(2)}) copy-start(bf16[8,256,256]{2,1,0:T(8,128)(2,1)} %copy-done.2) | copy-start | bytes 3145732
  49.3 26.9 %all-to-all-start = ((bf16[32,16,512]{2,1,0:T(8,128)(2,1)}), bf16[32,16,512]{2,1,0:T(8,128)(2,1)S(1)}, u32[]{:S(2)}, u32[]{:S(2)}) async-start(bf16[32,16,512]{2,1,0:T(8,128)(2,1)} %shard_map.72), calls=%async_computation | async-start | bytes 1048576 | tf_op jit(solution)/shard_map/all_to_all | solution.py:24
  60.0 0.8 copy-start.6
  60.8 0.8 copy-start.8
  61.6 0.8 copy-start.10
  62.4 10.3 %collective-permute-start.2 = (bf16[128,512]{1,0:T(8,128)(2,1)S(1)}, bf16[128,512]{1,0:T(8,128)(2,1)S(1)}, u32[]{:S(2)}, u32[]{:S(2)}) collective-permute-start(bf16[128,512]{1,0:T(8,128)(2,1)S(1)} %get-tuple-element.44), channel_id=1, source_target_pairs={{0,128},{128,256},{256,384},{384,0},{1,129},{129,257},{257,385},{3... | collective-permute-start | bytes 393224 | tf_op jit(solution)/shard_map/ppermute | solution.py:20
  65.4 10.8 %collective-permute-start.3 = (bf16[128,512]{1,0:T(8,128)(2,1)S(1)}, bf16[128,512]{1,0:T(8,128)(2,1)S(1)}, u32[]{:S(2)}, u32[]{:S(2)}) collective-permute-start(bf16[128,512]{1,0:T(8,128)(2,1)S(1)} %get-tuple-element.45), channel_id=1, source_target_pairs={{0,384},{128,0},{256,128},{384,256},{1,385},{129,1},{257,129},{385... | collective-permute-start | bytes 393224 | tf_op jit(solution)/shard_map/ppermute | solution.py:20
  76.9 12.3 %all-to-all-start.1 = ((bf16[8,16,512]{2,1,0:T(8,128)(2,1)}), bf16[8,16,512]{2,1,0:T(8,128)(2,1)S(1)}, u32[]{:S(2)}, u32[]{:S(2)}) async-start(bf16[8,16,512]{2,1,0:T(8,128)(2,1)} %shard_map.74), calls=%async_computation.1 | async-start | bytes 262144 | tf_op jit(solution)/shard_map/all_to_all | solution.py:24
  81.5 1.0 copy-start.9
  82.5 1.0 copy-start.11
  90.1 26.6 %all-to-all-start.2 = ((bf16[32,16,512]{2,1,0:T(8,128)(2,1)}), bf16[32,16,512]{2,1,0:T(8,128)(2,1)S(1)}, u32[]{:S(2)}, u32[]{:S(2)}) async-start(bf16[32,16,512]{2,1,0:T(8,128)(2,1)} %shard_map.75), calls=%async_computation.2 | async-start | bytes 1048576 | tf_op jit(solution)/shard_map/all_to_all | solution.py:24
  99.2 22.7 %copy-start.5 = (bf16[256,512]{1,0:T(8,128)(2,1)S(1)}, bf16[256,512]{1,0:T(8,128)(2,1)}, u32[]{:S(2)}) copy-start(bf16[256,512]{1,0:T(8,128)(2,1)} %text_ref.3) | copy-start | bytes 786436
  99.2 22.7 %copy-start.7 = (f32[256,512]{1,0:T(8,128)S(1)}, f32[256,512]{1,0:T(8,128)}, u32[]{:S(2)}) copy-start(f32[256,512]{1,0:T(8,128)} %copy-done.6) | copy-start | bytes 1572868
  99.2 11.3 %collective-permute-start.4 = (bf16[256,512]{1,0:T(8,128)(2,1)S(1)}, bf16[256,512]{1,0:T(8,128)(2,1)S(1)}, u32[]{:S(2)}, u32[]{:S(2)}) collective-permute-start(bf16[256,512]{1,0:T(8,128)(2,1)S(1)} %get-tuple-element.54), channel_id=1, source_target_pairs={{0,128},{128,256},{256,384},{384,0},{1,129},{129,257},{257,385},{3... | collective-permute-start | bytes 786440 | tf_op jit(solution)/shard_map/ppermute | solution.py:20
  101.3 15.5 %collective-permute-start.5 = (bf16[256,512]{1,0:T(8,128)(2,1)S(1)}, bf16[256,512]{1,0:T(8,128)(2,1)S(1)}, u32[]{:S(2)}, u32[]{:S(2)}) collective-permute-start(bf16[256,512]{1,0:T(8,128)(2,1)S(1)} %get-tuple-element.55), channel_id=1, source_target_pairs={{0,384},{128,0},{256,128},{384,256},{1,385},{129,1},{257,129},{385... | collective-permute-start | bytes 786440 | tf_op jit(solution)/shard_map/ppermute | solution.py:20
  116.8 6.2 %collective-permute-start.6 = (bf16[512,512]{1,0:T(8,128)(2,1)S(1)}, bf16[512,512]{1,0:T(8,128)(2,1)S(1)}, u32[]{:S(2)}, u32[]{:S(2)}) collective-permute-start(bf16[512,512]{1,0:T(8,128)(2,1)S(1)} %bitcast.4), channel_id=1, source_target_pairs={{0,64},{64,0},{1,65},{65,1},{2,66},{66,2},{3,67},{67,3},{4,68},{68... | collective-permute-start | bytes 1572872 | tf_op jit(solution)/shard_map/ppermute | solution.py:20

commit v5 on v4

--- a/solution.py
+++ b/solution.py
@@ -131,36 +131,14 @@
     out_ref[...] = dot(grad_ref[...], weight_ref[...], 1, 1).astype(jnp.bfloat16)
 
 
-def text_sums_kernel(
-    place_ref, tiles_ref, audio_b_ref, got_ref,
-    home_ref, next_ref, last_ref, forward_ref, backward_ref,
-):
-    rows = home_ref.shape[0]
+def text_sums_kernel(tiles_ref, audio_b_ref, got_ref, sums_ref):
     chips = tiles_ref.shape[0] // 2
+    rows = sums_ref.shape[0] // chips
     half = got_ref.shape[0] - chips * rows
-
-    def sums(distance):
-        to = lax.rem(place_ref[0] + distance, chips)
-        start = pl.multiple_of(half + to * rows, rows)
-        part = SCALE * dot(tiles_ref[to], audio_b_ref[...], 0, 0)
-        return part + got_ref[pl.ds(start, rows), :].astype(jnp.float32)
-
-    home_ref[...] = sums(0)
-    next_ref[...] = sums(1)
-    last_ref[...] = sums(chips - 1)
-    across = sums(2).astype(jnp.bfloat16)
-    forward_ref[...] = across[: rows // 2]
-    backward_ref[...] = across[rows // 2 :]
-
-
-def relay_kernel(next_ref, last_ref, forward_ref, backward_ref, to_next_ref, to_last_ref):
-    cut = next_ref.shape[0] // 2
-    ahead = next_ref[:cut, :] + forward_ref[...].astype(jnp.float32)
-    behind = last_ref[cut:, :] + backward_ref[...].astype(jnp.float32)
-    to_next_ref[:cut, :] = ahead.astype(jnp.bfloat16)
-    to_next_ref[cut:, :] = next_ref[cut:, :].astype(jnp.bfloat16)
-    to_last_ref[:cut, :] = last_ref[:cut, :].astype(jnp.bfloat16)
-    to_last_ref[cut:, :] = behind.astype(jnp.bfloat16)
+    for n in range(chips):
+        part = SCALE * dot(tiles_ref[n], audio_b_ref[...], 0, 0)
+        part = part + got_ref[half + n * rows : half + (n + 1) * rows, :].astype(jnp.float32)
+        sums_ref[n * rows : (n + 1) * rows, :] = part.astype(jnp.bfloat16)
 
 
 def fold_kernel(parts_ref, copies_ref):
@@ -194,15 +172,13 @@
     )(place, half, *given)
 
 
-def text_grad_kernel(text_ref, home_ref, *refs):
-    grad = home_ref[...]
-    for ref in refs[:-1]:
-        grad = grad + ref[...].astype(jnp.float32)
+def text_grad_kernel(text_ref, sum_ref, grad_ref):
+    grad = sum_ref[...].astype(jnp.float32)
     text = text_ref[...].astype(jnp.float32)
     scale = lax.rsqrt(jnp.sum(text * text, axis=1, keepdims=True) + EPS)
     text = text * scale
     along = jnp.sum(text * grad, axis=1, keepdims=True)
-    refs[-1][...] = (grad - text * along) * scale
+    grad_ref[...] = (grad - text * along) * scale
 
 
 def body(audio_features, proj_weight, text_raw, positive):
@@ -216,7 +192,6 @@
     half = channels // 2
     block = shape((rows, width), f32)
     block_b = shape((rows, width), bf16)
-    cut_b = shape((rows // 2, width), bf16)
 
     (sent,) = call(text_kernel, (shape((rows + TAIL, width), bf16),), text_raw)
     own = lax.all_gather(sent.astype(jnp.float16), "zh", axis=0, tiled=True).astype(bf16)
@@ -258,32 +233,18 @@
     (parts,) = call(half_kernel, (shape((plane, part, width), bf16),), weight, got)
     parts, got = lax.optimization_barrier((parts, got))
     parts = exchanged(parts, PLANE)
-    home, following, last, forward, backward = call(
-        text_sums_kernel,
-        (block, block, block, cut_b, cut_b),
-        place,
-        tiles,
-        audio_b,
-        got,
-        flops=pair_flops,
-    )
-    forward = shifted(forward, "zh", 1)
-    backward = shifted(backward, "zh", -1)
-    parts, forward, backward = lax.optimization_barrier((parts, forward, backward))
+    (sums,) = call(
+        text_sums_kernel, (shape((chips * rows, width), bf16),), tiles, audio_b, got, light=True
+    )
+    text_grad = lax.psum_scatter(sums, "zh", scatter_dimension=0, tiled=True)
     (parts,) = call(fold_kernel, (shape((column, part, width), bf16),), parts)
     parts = exchanged(parts, COLUMN)
-    to_next, to_last = call(
-        relay_kernel, (block_b, block_b), following, last, forward, backward, light=True
-    )
     (parts,) = call(fold_kernel, (shape((plane, part, width), bf16),), parts)
-    parts, to_next, to_last = lax.optimization_barrier((parts, to_next, to_last))
     weight_half = exchanged(parts, PLANE).reshape(half, width)
-    arrived = [shifted(to_next, "zh", 1), shifted(to_last, "zh", -1)]
-    weight_half, arrived = lax.optimization_barrier((weight_half, arrived))
     there = shifted(weight_half, "core", 1)
     grad_weight = placed(place, weight_half, 0, None)
     grad_weight = placed(place, there, 1, grad_weight)
-    (grad_text,) = call(text_grad_kernel, (block,), text_raw, home, *arrived)
+    (grad_text,) = call(text_grad_kernel, (block,), text_raw, text_grad)
     return (grad_weight, grad_features, grad_text)
 
 

time: 125 us -> 137 us (1.096)
  blocking collectives: 28.3 us -> 65.2 us
  starting transfers between devices: 50.1 us -> 25.3 us
  between operations: 0.88 us -> 14.2 us
  waiting for transfers between devices: 24.6 us -> 15.2 us
  local copies, waits for them, and re-layouts: 5.6 us -> 2.06 us
    all_to_all x0 -> x2, blocking collectives: none -> 37 us  [exchanged(): return lax.all_to_all(block, axes, split_axis=0, concat_axis=0, tiled=True)]
    ppermute x7 -> x3, waiting for transfers between devices: 19 us -> 2.55 us  [shifted(): lax.ppermute(block, axis, [(i, (i + distance) % count) for i in range(cou...]
    all_to_all x3 -> x1, starting transfers between devices: 23.3 us -> 9.67 us  [exchanged(): return lax.all_to_all(block, axes, split_axis=0, concat_axis=0, tiled=True)]
    ppermute x7 -> x3, starting transfers between devices: 26.8 us -> 15.6 us  [shifted(): lax.ppermute(block, axis, [(i, (i + distance) % count) for i in range(cou...]
    all_to_all x3 -> x1, waiting for transfers between devices: 5.62 us -> 12.6 us  [exchanged(): return lax.all_to_all(block, axes, split_axis=0, concat_axis=0, tiled=True)]
    unnamed x26 -> x16, local copies, waits for them, and re-layouts: 5.47 us -> 1.92 us
    pallas_call x11 -> x10, Pallas kernels: 11.6 us -> 10.5 us  [call(): pl.pallas_call(kernel, out_shape=outs, in_specs=[scalars if a.shape == (2...]
  transfers between devices with their start and end apart: 10 -> 5, of which waited for: 7 -> 3; matrix products, arithmetic and copies ran while one was open for 0% -> 0% of each run, Pallas kernels for 5% -> 5%
where the time goes in v5:
time: 137 us; the launch traced here: 136 us
  blocking collectives  65.2 us (48%)
  starting transfers between devices  25.3 us (18%)
  waiting for transfers between devices  15.2 us (11%)
  between operations  14.2 us (10%)
  Pallas kernels  13.6 us (10%)
  local copies, waits for them, and re-layouts  2.06 us (2%)
    all_to_all x2, blocking collectives, exchanged(): return lax.all_to_all(block, axes, split_axis=0, concat_axis=0, tiled=True)  37 us
    all_gather x1, blocking collectives, body(): lax.all_gather(sent.astype(jnp.float16), 'zh', axis=0, tiled=True)  28.3 us
    ppermute x3, starting transfers between devices, shifted(): lax.ppermute(block, axis, [(i, (i + distance) % count) for i in range(cou...  15.6 us
    all_to_all x1, waiting for transfers between devices, exchanged(): return lax.all_to_all(block, axes, split_axis=0, concat_axis=0, tiled=True)  12.6 us
    pallas_call x10, Pallas kernels, call(): pl.pallas_call(kernel, out_shape=outs, in_specs=[scalars if a.shape == (2...  10.5 us
    all_to_all x1, starting transfers between devices, exchanged(): return lax.all_to_all(block, axes, split_axis=0, concat_axis=0, tiled=True)  9.67 us
    pallas_call x2, Pallas kernels, placed(): pl.pallas_call(place_kernel, out_shape=shape((2 * rows, width), jnp.float...  3.15 us
  transfers between devices with their start and end apart: 5, of which 3 were waited for; matrix products, arithmetic and copies ran while one was open for 0% of the time, Pallas kernels for 5%

profile of v5, /device:TPU:1, one launch (start us, length us, event | category | flops | bytes accessed | tf_op | source)
XLA Modules:
  0.0 136.0 jit_solution(1431991865110545474)
XLA Ops:
  7.2 0.0 copy-start.2
  7.2 0.9 copy-done.2
  8.1 0.3 shard_map.67
  8.5 0.0 copy-start.7
  8.5 28.3 %all-gather.1 = f16[1088,512]{1,0:T(8,128)(2,1)S(1)} all-gather(f16[272,512]{1,0:T(8,128)(2,1)S(1)} %convert_element_type.6), channel_id=1, replica_groups=mesh['zh'=4,'core'=2,'zl'=2,'x'=4,'y'=8] {'zh'}, dimensions={0}, use_global_device_ids=true | all-gather | bytes 1392640 | tf_op jit(solution)/shard_map/all_gather | solution.py:197
  36.8 0.2 convert_element_type.7.own_ref
  37.0 6.1 %collective-permute-start = (bf16[1088,512]{1,0:T(8,128)(2,1)S(1)}, bf16[1088,512]{1,0:T(8,128)(2,1)}, u32[]{:S(2)}, u32[]{:S(2)}) collective-permute-start(bf16[1088,512]{1,0:T(8,128)(2,1)S(1)} %convert_element_type.7.own_ref), channel_id=1, source_target_pairs={{0,64},{64,0},{1,65},{65,1},{2,66},{66,2},{3,67},{67,3},{4,68},{68... | collective-permute-start | bytes 3342344 | tf_op jit(solution)/shard_map/ppermute | solution.py:20
  43.1 0.1 copy.8.positive_ref
  43.3 0.5 shard_map.68
  43.8 0.1 pad_add_fusion.place_ref
  43.9 1.7 %collective-permute-done.other_ref = bf16[1088,512]{1,0:T(8,128)(2,1)} collective-permute-done((bf16[1088,512]{1,0:T(8,128)(2,1)S(1)}, bf16[1088,512]{1,0:T(8,128)(2,1)}, u32[]{:S(2)}, u32[]{:S(2)}) %collective-permute-start) | collective-permute-done | bytes 1114144 | tf_op jit(solution)/shard_map/ppermute | solution.py:20
  45.6 4.0 %shard_map.69 = (bf16[256,512]{1,0:T(8,128)(2,1)S(1)}, bf16[8,256,256]{2,1,0:T(8,128)(2,1)S(1)}, bf16[1536,512]{1,0:T(8,128)(2,1)S(1)}) custom-call(s32[2]{0:T(128)S(1)} %pad_add_fusion.place_ref, f32[256,512]{1,0:T(8,128)S(1)} %get-tuple-element.17.audio_ref, bf16[256,512]{1,0:T(8,128)(2,1)S(1)} %get-tuple-element.18.audio_b_ref, ...), custom_call_target="tpu_custom_call" | custom-call | flops 1610612736 | bytes 6424584 | tf_op jit(solution)/shard_map/pallas_call | solution.py:35
  49.6 2.3 %collective-permute-start.1 = (bf16[1536,512]{1,0:T(8,128)(2,1)S(1)}, bf16[1536,512]{1,0:T(8,128)(2,1)S(1)}, u32[]{:S(2)}, u32[]{:S(2)}) collective-permute-start(bf16[1536,512]{1,0:T(8,128)(2,1)S(1)} %get-tuple-element.21), channel_id=1, source_target_pairs={{0,64},{64,0},{1,65},{65,1},{2,66},{66,2},{3,67},{67,3},{4,68},{68... | collective-permute-start | bytes 4718600 | tf_op jit(solution)/shard_map/ppermute | solution.py:20
  51.9 1.3 shard_map.71
  53.1 0.9 shard_map.70.weight_ref
  54.0 0.8 collective-permute-done.1.got_ref
  54.9 0.9 shard_map.72
  55.8 9.7 %all-to-all-start = ((bf16[32,16,512]{2,1,0:T(8,128)(2,1)}), bf16[32,16,512]{2,1,0:T(8,128)(2,1)S(1)}, u32[]{:S(2)}, u32[]{:S(2)}) async-start(bf16[32,16,512]{2,1,0:T(8,128)(2,1)} %shard_map.72), calls=%async_computation | async-start | bytes 1048576 | tf_op jit(solution)/shard_map/all_to_all | solution.py:24
  65.5 0.0 reduce-scatter.2.cloned.1.call-start
  65.5 1.4 %shard_map.77 = bf16[1024,512]{1,0:T(8,128)(2,1)} custom-call(bf16[8,256,256]{2,1,0:T(8,128)(2,1)S(1)} %copy-done.5, bf16[256,512]{1,0:T(8,128)(2,1)S(1)} %get-tuple-element.18.audio_b_ref, bf16[1536,512]{1,0:T(8,128)(2,1)S(1)} %collective-permute-done.1.got_ref), custom_call_target="tpu_custom_call" | custom-call | tf_op jit(solution)/shard_map/pallas_call | solution.py:35
  67.0 0.0 reduce-scatter.2.cloned.1.call-update
  67.0 12.6 %all-to-all-done.parts_ref = bf16[32,16,512]{2,1,0:T(8,128)(2,1)S(1)} async-done(((bf16[32,16,512]{2,1,0:T(8,128)(2,1)}), bf16[32,16,512]{2,1,0:T(8,128)(2,1)S(1)}, u32[]{:S(2)}, u32[]{:S(2)}) %all-to-all-start) | async-done | bytes 524320 | tf_op jit(solution)/shard_map/all_to_all | solution.py:24
  79.6 0.1 shard_map.73
  79.7 14.9 %all_to_all.15.parts_ref = bf16[8,16,512]{2,1,0:T(8,128)(2,1)S(1)} all-to-all(bf16[8,16,512]{2,1,0:T(8,128)(2,1)S(1)} %shard_map.73), channel_id=1, replica_groups=mesh['zh'=4,'core'=2,'zl'=2,'x'=4,'y'=8] {'zh','zl'}, dimensions={0} | all-to-all | bytes 262144 | tf_op jit(solution)/shard_map/all_to_all | solution.py:24
  94.5 0.1 shard_map.74
  94.6 22.1 %all_to_all.16 = bf16[32,16,512]{2,1,0:T(8,128)(2,1)S(1)} all-to-all(bf16[32,16,512]{2,1,0:T(8,128)(2,1)S(1)} %shard_map.74), channel_id=1, replica_groups=mesh['zh'=4,'core'=2,'zl'=2,'x'=4,'y'=8] {'x','y'}, dimensions={0} | all-to-all | bytes 1048576 | tf_op jit(solution)/shard_map/all_to_all | solution.py:24
  116.7 7.2 %collective-permute-start.2 = (bf16[512,512]{1,0:T(8,128)(2,1)S(1)}, bf16[512,512]{1,0:T(8,128)(2,1)S(1)}, u32[]{:S(2)}, u32[]{:S(2)}) collective-permute-start(bf16[512,512]{1,0:T(8,128)(2,1)S(1)} %bitcast.4), channel_id=1, source_target_pairs={{0,64},{64,0},{1,65},{65,1},{2,66},{66,2},{3,67},{67,3},{4,68},{68... | collective-permute-start | bytes 1572872 | tf_op jit(solution)/shard_map/ppermute | solution.py:20
  123.9 0.0 reduce-scatter.2.cloned.1.call-done.sum_ref
  124.0 0.9 copy-done.6
  124.9 1.0 shard_map.78
  126.0 1.6 %shard_map.75.refs_0_ = f32[1024,512]{1,0:T(8,128)} custom-call(s32[2]{0:T(128)S(1)} %pad_add_fusion.place_ref, bf16[512,512]{1,0:T(8,128)(2,1)S(1)} %bitcast.5), custom_call_target="tpu_custom_call" | custom-call | bytes 1572864 | tf_op jit(solution)/shard_map/pallas_call | solution.py:157
  127.5 1.6 %shard_map.76 = f32[1024,512]{1,0:T(8,128)} custom-call(s32[2]{0:T(128)S(1)} %pad_add_fusion.place_ref, bf16[512,512]{1,0:T(8,128)(2,1)S(1)} %collective-permute-done.2.half_ref, f32[1024,512]{1,0:T(8,128)} %shard_map.75.refs_0_), custom_call_target="tpu_custom_call", output_to_operand_aliasing={{}: (2, {})} | custom-call | bytes 1572864 | tf_op jit(solution)/shard_map/pallas_call | solution.py:157
  (14 shorter events, 0.1 us)
Async XLA Ops:
  7.2 1.0 copy-start.2
  8.5 34.6 %copy-start.7 = (s32[256]{0:T(256)S(1)}, s32[256]{0:T(256)}, u32[]{:S(2)}) copy-start(s32[256]{0:T(256)} %param.7) | copy-start | bytes 3076
  8.5 34.7 %copy-start = (bf16[1024,512]{1,0:T(8,128)(2,1)S(1)}, bf16[1024,512]{1,0:T(8,128)(2,1)}, u32[]{:S(2)}) copy-start(bf16[1024,512]{1,0:T(8,128)(2,1)} %weight_ref.3) | copy-start | bytes 3145732
  8.5 34.7 %copy-start.1 = (bf16[256,1024]{1,0:T(8,128)(2,1)S(1)}, bf16[256,1024]{1,0:T(8,128)(2,1)}, u32[]{:S(2)}) copy-start(bf16[256,1024]{1,0:T(8,128)(2,1)} %features_ref.2) | copy-start | bytes 1572868
  37.0 8.6 %collective-permute-start = (bf16[1088,512]{1,0:T(8,128)(2,1)S(1)}, bf16[1088,512]{1,0:T(8,128)(2,1)}, u32[]{:S(2)}, u32[]{:S(2)}) collective-permute-start(bf16[1088,512]{1,0:T(8,128)(2,1)S(1)} %convert_element_type.7.own_ref), channel_id=1, source_target_pairs={{0,64},{64,0},{1,65},{65,1},{2,66},{66,2},{3,67},{67,3},{4,68},{68... | collective-permute-start | bytes 3342344 | tf_op jit(solution)/shard_map/ppermute | solution.py:20
  49.6 4.5 %copy-start.4 = (bf16[8,256,256]{2,1,0:T(8,128)(2,1)}, bf16[8,256,256]{2,1,0:T(8,128)(2,1)S(1)}, u32[]{:S(2)}) copy-start(bf16[8,256,256]{2,1,0:T(8,128)(2,1)S(1)} %get-tuple-element.27.tiles_ref) | copy-start | bytes 3145732
  49.6 5.3 %collective-permute-start.1 = (bf16[1536,512]{1,0:T(8,128)(2,1)S(1)}, bf16[1536,512]{1,0:T(8,128)(2,1)S(1)}, u32[]{:S(2)}, u32[]{:S(2)}) collective-permute-start(bf16[1536,512]{1,0:T(8,128)(2,1)S(1)} %get-tuple-element.21), channel_id=1, source_target_pairs={{0,64},{64,0},{1,65},{65,1},{2,66},{66,2},{3,67},{67,3},{4,68},{68... | collective-permute-start | bytes 4718600 | tf_op jit(solution)/shard_map/ppermute | solution.py:20
  54.9 10.6 %copy-start.5 = (bf16[8,256,256]{2,1,0:T(8,128)(2,1)S(1)}, bf16[8,256,256]{2,1,0:T(8,128)(2,1)}, u32[]{:S(2)}) copy-start(bf16[8,256,256]{2,1,0:T(8,128)(2,1)} %copy-done.4) | copy-start | bytes 3145732
  55.8 23.8 %all-to-all-start = ((bf16[32,16,512]{2,1,0:T(8,128)(2,1)}), bf16[32,16,512]{2,1,0:T(8,128)(2,1)S(1)}, u32[]{:S(2)}, u32[]{:S(2)}) async-start(bf16[32,16,512]{2,1,0:T(8,128)(2,1)} %shard_map.72), calls=%async_computation | async-start | bytes 1048576 | tf_op jit(solution)/shard_map/all_to_all | solution.py:24
  65.5 58.5 %reduce-scatter.2.cloned.1.call-start = ((), (), s32[]{:S(2)}) async-start(), calls=%async_computation.4 | async-start | bytes 1310720 | tf_op jit(solution)/shard_map/reduce_scatter | solution.py:239
  67.0 57.0 %copy-start.3 = (bf16[256,512]{1,0:T(8,128)(2,1)S(1)}, bf16[256,512]{1,0:T(8,128)(2,1)}, u32[]{:S(2)}) copy-start(bf16[256,512]{1,0:T(8,128)(2,1)} %text_ref.3) | copy-start | bytes 786436
  116.7 10.8 %collective-permute-start.2 = (bf16[512,512]{1,0:T(8,128)(2,1)S(1)}, bf16[512,512]{1,0:T(8,128)(2,1)S(1)}, u32[]{:S(2)}, u32[]{:S(2)}) collective-permute-start(bf16[512,512]{1,0:T(8,128)(2,1)S(1)} %bitcast.4), channel_id=1, source_target_pairs={{0,64},{64,0},{1,65},{65,1},{2,66},{66,2},{3,67},{67,3},{4,68},{68... | collective-permute-start | bytes 1572872 | tf_op jit(solution)/shard_map/ppermute | solution.py:20
  124.0 1.0 copy-start.6
Sparse Core Ops, SparseCore 0:
  69.7 38.1 reduce-scatter.1

commit v6 on v5

--- a/solution.py
+++ b/solution.py
@@ -28,16 +28,53 @@
     return lax.dot_general(a, b, (((da,), (db,)), ((), ())), preferred_element_type=jnp.float32)
 
 
-def call(kernel, outs, *args, scratch=(), flops=0, limit=16, light=False):
+def call(kernel, outs, *args, scratch=(), flops=0, limit=16, light=False, far=(), far_outs=False):
     whole = pl.BlockSpec(memory_space=pltpu.VMEM)
     scalars = pl.BlockSpec(memory_space=pltpu.SMEM)
+    hbm = pl.BlockSpec(memory_space=pltpu.HBM)
     size = 0 if light else sum(a.size * a.dtype.itemsize for a in (*args, *outs))
+    args = [
+        pltpu.with_memory_space_constraint(a, pltpu.HBM) if n in far else a
+        for n, a in enumerate(args)
+    ]
+    staged = [args[n] for n in far] + (list(outs) if far_outs else [])
+
+    def staging(*refs):
+        refs = list(refs)
+        sems = refs.pop() if staged else None
+        count = len(refs) - len(staged)
+        refs, buffers = refs[:count], refs[count:]
+        moves = []
+        for n, at in enumerate(far):
+            moves.append(pltpu.make_async_copy(refs[at], buffers[n], sems.at[n]))
+            refs[at] = buffers[n]
+        for move in moves:
+            move.start()
+        for move in moves:
+            move.wait()
+        moves = []
+        if far_outs:
+            for n in range(len(far), len(staged)):
+                at = len(args) + n - len(far)
+                moves.append(pltpu.make_async_copy(buffers[n], refs[at], sems.at[n]))
+                refs[at] = buffers[n]
+        kernel(*refs)
+        for move in moves:
+            move.start()
+        for move in moves:
+            move.wait()
+
+    buffers = [pltpu.VMEM(a.shape, a.dtype) for a in staged]
+    if staged:
+        buffers.append(pltpu.SemaphoreType.DMA((len(staged),)))
     return pl.pallas_call(
-        kernel,
-        out_shape=outs,
-        in_specs=[scalars if a.shape == (2,) else whole for a in args],
-        out_specs=[whole] * len(outs),
-        scratch_shapes=scratch,
+        staging,
+        out_shape=[pltpu.HBM(a.shape, a.dtype) for a in outs] if far_outs else outs,
+        in_specs=[
+            scalars if a.shape == (2,) else hbm if n in far else whole for n, a in enumerate(args)
+        ],
+        out_specs=[hbm if far_outs else whole] * len(outs),
+        scratch_shapes=[*scratch, *buffers],
         compiler_params=pltpu.CompilerParams(vmem_limit_bytes=limit * MIB),
         cost_estimate=pl.CostEstimate(flops=flops, bytes_accessed=size, transcendentals=0),
     )(*args)
@@ -131,14 +168,27 @@
     out_ref[...] = dot(grad_ref[...], weight_ref[...], 1, 1).astype(jnp.bfloat16)
 
 
-def text_sums_kernel(tiles_ref, audio_b_ref, got_ref, sums_ref):
-    chips = tiles_ref.shape[0] // 2
-    rows = sums_ref.shape[0] // chips
-    half = got_ref.shape[0] - chips * rows
-    for n in range(chips):
-        part = SCALE * dot(tiles_ref[n], audio_b_ref[...], 0, 0)
-        part = part + got_ref[half + n * rows : half + (n + 1) * rows, :].astype(jnp.float32)
-        sums_ref[n * rows : (n + 1) * rows, :] = part.astype(jnp.bfloat16)
+def summed(place_ref, tiles_ref, audio_b_ref, got_ref, distance):
+    chips, rows = tiles_ref.shape[0] // 2, tiles_ref.shape[2]
+    to = lax.rem(place_ref[0] + distance, chips)
+    start = pl.multiple_of(got_ref.shape[0] - chips * rows + to * rows, rows)
+    part = SCALE * dot(tiles_ref[to], audio_b_ref[...], 0, 0)
+    return part + got_ref[pl.ds(start, rows), :].astype(jnp.float32)
+
+
+def text_sums_kernel(place_ref, tiles_ref, audio_b_ref, got_ref, across_ref, last_ref):
+    refs = (place_ref, tiles_ref, audio_b_ref, got_ref)
+    across_ref[...] = summed(*refs, 2).astype(jnp.bfloat16)
+    last_ref[...] = summed(*refs, 3).astype(jnp.bfloat16)
+
+
+def relay_kernel(
+    place_ref, tiles_ref, audio_b_ref, got_ref, across_ref, last_ref, to_next_ref, home_ref
+):
+    refs = (place_ref, tiles_ref, audio_b_ref, got_ref)
+    ahead = summed(*refs, 1) + across_ref[...].astype(jnp.float32)
+    to_next_ref[...] = ahead.astype(jnp.bfloat16)
+    home_ref[...] = summed(*refs, 0) + last_ref[...].astype(jnp.float32)
 
 
 def fold_kernel(parts_ref, copies_ref):
@@ -172,8 +222,8 @@
     )(place, half, *given)
 
 
-def text_grad_kernel(text_ref, sum_ref, grad_ref):
-    grad = sum_ref[...].astype(jnp.float32)
+def text_grad_kernel(text_ref, home_ref, arrived_ref, grad_ref):
+    grad = home_ref[...] + arrived_ref[...].astype(jnp.float32)
     text = text_ref[...].astype(jnp.float32)
     scale = lax.rsqrt(jnp.sum(text * text, axis=1, keepdims=True) + EPS)
     text = text * scale
@@ -230,21 +280,39 @@
     plane = lax.axis_size(PLANE)
     column = lax.axis_size(COLUMN)
     part = half // plane
-    (parts,) = call(half_kernel, (shape((plane, part, width), bf16),), weight, got)
+    (parts,) = call(half_kernel, (shape((plane, part, width), bf16),), weight, got, far_outs=True)
     parts, got = lax.optimization_barrier((parts, got))
     parts = exchanged(parts, PLANE)
-    (sums,) = call(
-        text_sums_kernel, (shape((chips * rows, width), bf16),), tiles, audio_b, got, light=True
-    )
-    text_grad = lax.psum_scatter(sums, "zh", scatter_dimension=0, tiled=True)
-    (parts,) = call(fold_kernel, (shape((column, part, width), bf16),), parts)
+    across, last = call(
+        text_sums_kernel, (block_b, block_b), place, tiles, audio_b, got, flops=pair_flops // 2
+    )
+    across = shifted(across, "zh", 1)
+    last = shifted(last, "zh", -1)
+    parts, across, last = lax.optimization_barrier((parts, across, last))
+    (parts,) = call(fold_kernel, (shape((column, part, width), bf16),), parts, far_outs=True)
     parts = exchanged(parts, COLUMN)
-    (parts,) = call(fold_kernel, (shape((plane, part, width), bf16),), parts)
+    to_next, home = call(
+        relay_kernel,
+        (block_b, block),
+        place,
+        tiles,
+        audio_b,
+        got,
+        across,
+        last,
+        light=True,
+        far=(1, 2, 3, 4, 5),
+        far_outs=True,
+    )
+    (parts,) = call(fold_kernel, (shape((plane, part, width), bf16),), parts, far_outs=True)
+    parts, to_next, home = lax.optimization_barrier((parts, to_next, home))
     weight_half = exchanged(parts, PLANE).reshape(half, width)
+    arrived = shifted(to_next, "zh", 1)
+    weight_half, arrived = lax.optimization_barrier((weight_half, arrived))
     there = shifted(weight_half, "core", 1)
     grad_weight = placed(place, weight_half, 0, None)
     grad_weight = placed(place, there, 1, grad_weight)
-    (grad_text,) = call(text_grad_kernel, (block,), text_raw, text_grad)
+    (grad_text,) = call(text_grad_kernel, (block,), text_raw, home, arrived)
     return (grad_weight, grad_features, grad_text)
 
 

time: 137 us -> 127 us (0.927)
  blocking collectives: 65.2 us -> 28.3 us
  starting transfers between devices: 25.3 us -> 46.8 us
  waiting for transfers between devices: 15.2 us -> 30.8 us
  between operations: 14.2 us -> 0.94 us
  Pallas kernels: 13.6 us -> 18.2 us
    all_to_all x2 -> x0, blocking collectives: 37 us -> none  [exchanged(): return lax.all_to_all(block, axes, split_axis=0, concat_axis=0, tiled=True)]
    ppermute x3 -> x6, waiting for transfers between devices: 2.55 us -> 26.8 us  [shifted(): lax.ppermute(block, axis, [(i, (i + distance) % count) for i in range(cou...]
    all_to_all x1 -> x3, starting transfers between devices: 9.67 us -> 23.6 us  [exchanged(): return lax.all_to_all(block, axes, split_axis=0, concat_axis=0, tiled=True)]
    all_to_all x1 -> x3, waiting for transfers between devices: 12.6 us -> 4.06 us  [exchanged(): return lax.all_to_all(block, axes, split_axis=0, concat_axis=0, tiled=True)]
    ppermute x3 -> x6, starting transfers between devices: 15.6 us -> 23.1 us  [shifted(): lax.ppermute(block, axis, [(i, (i + distance) % count) for i in range(cou...]
    pallas_call x10 -> x11, Pallas kernels: 10.5 us -> 15.1 us  [call(): pl.pallas_call(staging, out_shape=[pltpu.HBM(a.shape, a.dtype) for a in o...]
  transfers between devices with their start and end apart: 5 -> 9, of which waited for: 3 -> 6; matrix products, arithmetic and copies ran while one was open for 0% -> 0% of each run, Pallas kernels for 5% -> 8%
where the time goes in v6:
time: 127 us; the launch traced here: 126 us
  starting transfers between devices  46.8 us (37%)
  waiting for transfers between devices  30.8 us (24%)
  blocking collectives  28.3 us (22%)
  Pallas kernels  18.2 us (14%)
    all_gather x1, blocking collectives, body(): lax.all_gather(sent.astype(jnp.float16), 'zh', axis=0, tiled=True)  28.3 us
    ppermute x6, waiting for transfers between devices, shifted(): lax.ppermute(block, axis, [(i, (i + distance) % count) for i in range(cou...  26.8 us
    all_to_all x3, starting transfers between devices, exchanged(): return lax.all_to_all(block, axes, split_axis=0, concat_axis=0, tiled=True)  23.6 us
    ppermute x6, starting transfers between devices, shifted(): lax.ppermute(block, axis, [(i, (i + distance) % count) for i in range(cou...  23.1 us
    pallas_call x11, Pallas kernels, call(): pl.pallas_call(staging, out_shape=[pltpu.HBM(a.shape, a.dtype) for a in o...  15.1 us
    all_to_all x3, waiting for transfers between devices, exchanged(): return lax.all_to_all(block, axes, split_axis=0, concat_axis=0, tiled=True)  4.06 us
    pallas_call x2, Pallas kernels, placed(): pl.pallas_call(place_kernel, out_shape=shape((2 * rows, width), jnp.float...  3.16 us
  transfers between devices with their start and end apart: 9, of which 6 were waited for; matrix products, arithmetic and copies ran while one was open for 0% of the time, Pallas kernels for 8%

profile of v6, /device:TPU:1, one launch (start us, length us, event | category | flops | bytes accessed | tf_op | source)
XLA Modules:
  0.0 126.5 jit_solution(12481578450486080312)
XLA Ops:
  0.6 0.9 copy-done.6
  1.6 0.3 shard_map.67
  2.0 28.3 %all-gather.1 = f16[1088,512]{1,0:T(8,128)(2,1)S(1)} all-gather(f16[272,512]{1,0:T(8,128)(2,1)S(1)} %convert_element_type.6), channel_id=1, replica_groups=mesh['zh'=4,'core'=2,'zl'=2,'x'=4,'y'=8] {'zh'}, dimensions={0}, use_global_device_ids=true | all-gather | bytes 1392640 | tf_op jit(solution)/shard_map/all_gather | solution.py:247
  30.2 0.2 convert_element_type.7.refs_6_
  30.5 6.1 %collective-permute-start = (bf16[1088,512]{1,0:T(8,128)(2,1)S(1)}, bf16[1088,512]{1,0:T(8,128)(2,1)}, u32[]{:S(2)}, u32[]{:S(2)}) collective-permute-start(bf16[1088,512]{1,0:T(8,128)(2,1)S(1)} %convert_element_type.7.refs_6_), channel_id=1, source_target_pairs={{0,64},{64,0},{1,65},{65,1},{2,66},{66,2},{3,67},{67,3},{4,68},{68... | collective-permute-start | bytes 3342344 | tf_op jit(solution)/shard_map/ppermute | solution.py:20
  36.6 0.1 copy.8.refs_5_
  36.7 0.5 shard_map.68
  37.3 1.7 %collective-permute-done.refs_7_ = bf16[1088,512]{1,0:T(8,128)(2,1)} collective-permute-done((bf16[1088,512]{1,0:T(8,128)(2,1)S(1)}, bf16[1088,512]{1,0:T(8,128)(2,1)}, u32[]{:S(2)}, u32[]{:S(2)}) %collective-permute-start) | collective-permute-done | bytes 1114144 | tf_op jit(solution)/shard_map/ppermute | solution.py:20
  39.0 4.0 %shard_map.69 = (bf16[256,512]{1,0:T(8,128)(2,1)S(1)}, bf16[8,256,256]{2,1,0:T(8,128)(2,1)S(1)}, bf16[1536,512]{1,0:T(8,128)(2,1)S(1)}) custom-call(s32[2]{0:T(128)S(1)} %pad_add_fusion.refs_0_.place_ref, f32[256,512]{1,0:T(8,128)S(1)} %get-tuple-element.29.refs_1_, bf16[256,512]{1,0:T(8,128)(2,1)S(1)} %get-tuple-element.30.refs_2_, ...), custom_call_target="tpu_custom_call" | custom-call | flops 1610612736 | bytes 6424584 | tf_op jit(solution)/shard_map/pallas_call | solution.py:70
  43.0 2.3 %collective-permute-start.1 = (bf16[1536,512]{1,0:T(8,128)(2,1)S(1)}, bf16[1536,512]{1,0:T(8,128)(2,1)S(1)}, u32[]{:S(2)}, u32[]{:S(2)}) collective-permute-start(bf16[1536,512]{1,0:T(8,128)(2,1)S(1)} %get-tuple-element.33), channel_id=1, source_target_pairs={{0,64},{64,0},{1,65},{65,1},{2,66},{66,2},{3,67},{67,3},{4,68},{68... | collective-permute-start | bytes 4718600 | tf_op jit(solution)/shard_map/ppermute | solution.py:20
  45.3 1.3 shard_map.71
  46.6 0.9 shard_map.70.refs_0_
  47.5 0.9 collective-permute-done.1.refs_1_.refs_3_
  48.3 0.9 shard_map.72
  49.3 9.8 %all-to-all-start = ((bf16[32,16,512]{2,1,0:T(8,128)(2,1)}), bf16[32,16,512]{2,1,0:T(8,128)(2,1)S(1)}, u32[]{:S(2)}, u32[]{:S(2)}) async-start(bf16[32,16,512]{2,1,0:T(8,128)(2,1)} %shard_map.72), calls=%async_computation | async-start | bytes 1048576 | tf_op jit(solution)/shard_map/all_to_all | solution.py:24
  59.1 0.9 shard_map.73
  60.0 3.0 %collective-permute-start.2 = (bf16[256,512]{1,0:T(8,128)(2,1)S(1)}, bf16[256,512]{1,0:T(8,128)(2,1)S(1)}, u32[]{:S(2)}, u32[]{:S(2)}) collective-permute-start(bf16[256,512]{1,0:T(8,128)(2,1)S(1)} %get-tuple-element.40), channel_id=1, source_target_pairs={{0,128},{128,256},{256,384},{384,0},{1,129},{129,257},{257,385},{3... | collective-permute-start | bytes 786440 | tf_op jit(solution)/shard_map/ppermute | solution.py:20
  63.0 4.4 %collective-permute-start.3 = (bf16[256,512]{1,0:T(8,128)(2,1)S(1)}, bf16[256,512]{1,0:T(8,128)(2,1)S(1)}, u32[]{:S(2)}, u32[]{:S(2)}) collective-permute-start(bf16[256,512]{1,0:T(8,128)(2,1)S(1)} %get-tuple-element.41), channel_id=1, source_target_pairs={{0,384},{128,0},{256,128},{384,256},{1,385},{129,1},{257,129},{385... | collective-permute-start | bytes 786440 | tf_op jit(solution)/shard_map/ppermute | solution.py:20
  67.4 8.5 %collective-permute-done.2.refs_4_ = bf16[256,512]{1,0:T(8,128)(2,1)S(1)} collective-permute-done((bf16[256,512]{1,0:T(8,128)(2,1)S(1)}, bf16[256,512]{1,0:T(8,128)(2,1)S(1)}, u32[]{:S(2)}, u32[]{:S(2)}) %collective-permute-start.2) | collective-permute-done | bytes 262176 | tf_op jit(solution)/shard_map/ppermute | solution.py:20
  75.9 3.5 %collective-permute-done.3.refs_5_ = bf16[256,512]{1,0:T(8,128)(2,1)S(1)} collective-permute-done((bf16[256,512]{1,0:T(8,128)(2,1)S(1)}, bf16[256,512]{1,0:T(8,128)(2,1)S(1)}, u32[]{:S(2)}, u32[]{:S(2)}) %collective-permute-start.3) | collective-permute-done | bytes 262176 | tf_op jit(solution)/shard_map/ppermute | solution.py:20
  79.4 0.8 shard_map.74
  80.2 4.6 %all-to-all-start.1 = ((bf16[8,16,512]{2,1,0:T(8,128)(2,1)}), bf16[8,16,512]{2,1,0:T(8,128)(2,1)S(1)}, u32[]{:S(2)}, u32[]{:S(2)}) async-start(bf16[8,16,512]{2,1,0:T(8,128)(2,1)} %shard_map.74), calls=%async_computation.1 | async-start | bytes 262144 | tf_op jit(solution)/shard_map/all_to_all | solution.py:24
  84.8 3.7 %shard_map.76 = (bf16[256,512]{1,0:T(8,128)(2,1)}, f32[256,512]{1,0:T(8,128)}) custom-call(s32[2]{0:T(128)S(1)} %pad_add_fusion.refs_0_.place_ref, bf16[8,256,256]{2,1,0:T(8,128)(2,1)} %copy-done.2, bf16[256,512]{1,0:T(8,128)(2,1)} %copy-done.5, bf16[1536,512]{1,0:T(8,128)(2,1)} %copy-done, bf16[256,512]{1,0:T(8,128)(2,1)} %copy-done.9, ...), custom_call_target="tpu_custom_call" | custom-call | tf_op jit(solution)/shard_map/pallas_call | solution.py:70
  88.5 4.1 %all-to-all-done.1.refs_0_ = bf16[8,16,512]{2,1,0:T(8,128)(2,1)S(1)} async-done(((bf16[8,16,512]{2,1,0:T(8,128)(2,1)}), bf16[8,16,512]{2,1,0:T(8,128)(2,1)S(1)}, u32[]{:S(2)}, u32[]{:S(2)}) %all-to-all-start.1) | async-done | bytes 131104 | tf_op jit(solution)/shard_map/all_to_all | solution.py:24
  92.6 0.9 shard_map.75
  93.4 9.2 %all-to-all-start.2 = ((bf16[32,16,512]{2,1,0:T(8,128)(2,1)}), bf16[32,16,512]{2,1,0:T(8,128)(2,1)S(1)}, u32[]{:S(2)}, u32[]{:S(2)}) async-start(bf16[32,16,512]{2,1,0:T(8,128)(2,1)} %shard_map.75), calls=%async_computation.2 | async-start | bytes 1048576 | tf_op jit(solution)/shard_map/all_to_all | solution.py:24
  102.7 2.1 %collective-permute-start.4 = (bf16[256,512]{1,0:T(8,128)(2,1)S(1)}, bf16[256,512]{1,0:T(8,128)(2,1)S(1)}, u32[]{:S(2)}, u32[]{:S(2)}) collective-permute-start(bf16[256,512]{1,0:T(8,128)(2,1)S(1)} %copy-done.12), channel_id=1, source_target_pairs={{0,128},{128,256},{256,384},{384,0},{1,129},{129,257},{257,385},{3... | collective-permute-start | bytes 786440 | tf_op jit(solution)/shard_map/ppermute | solution.py:20
  104.8 12.2 %collective-permute-done.4.refs_2_ = bf16[256,512]{1,0:T(8,128)(2,1)S(1)} collective-permute-done((bf16[256,512]{1,0:T(8,128)(2,1)S(1)}, bf16[256,512]{1,0:T(8,128)(2,1)S(1)}, u32[]{:S(2)}, u32[]{:S(2)}) %collective-permute-start.4) | collective-permute-done | bytes 262176 | tf_op jit(solution)/shard_map/ppermute | solution.py:20
  117.0 5.3 %collective-permute-start.5 = (bf16[512,512]{1,0:T(8,128)(2,1)S(1)}, bf16[512,512]{1,0:T(8,128)(2,1)S(1)}, u32[]{:S(2)}, u32[]{:S(2)}) collective-permute-start(bf16[512,512]{1,0:T(8,128)(2,1)S(1)} %bitcast.4), channel_id=1, source_target_pairs={{0,64},{64,0},{1,65},{65,1},{2,66},{66,2},{3,67},{67,3},{4,68},{68... | collective-permute-start | bytes 1572872 | tf_op jit(solution)/shard_map/ppermute | solution.py:20
  122.3 1.6 %shard_map.77.refs_0_ = f32[1024,512]{1,0:T(8,128)} custom-call(s32[2]{0:T(128)S(1)} %pad_add_fusion.refs_0_.place_ref, bf16[512,512]{1,0:T(8,128)(2,1)S(1)} %bitcast.5), custom_call_target="tpu_custom_call" | custom-call | bytes 1572864 | tf_op jit(solution)/shard_map/pallas_call | solution.py:207
  123.9 1.0 shard_map.79
  124.9 1.6 %shard_map.78 = f32[1024,512]{1,0:T(8,128)} custom-call(s32[2]{0:T(128)S(1)} %pad_add_fusion.refs_0_.place_ref, bf16[512,512]{1,0:T(8,128)(2,1)S(1)} %collective-permute-done.5.half_ref, f32[1024,512]{1,0:T(8,128)} %shard_map.77.refs_0_), custom_call_target="tpu_custom_call", output_to_operand_aliasing={{}: (2, {})} | custom-call | bytes 1572864 | tf_op jit(solution)/shard_map/pallas_call | solution.py:207
  (30 shorter events, 0.2 us)
Async XLA Ops:
  0.6 1.0 copy-start.6
  2.0 34.6 %copy-start.11 = (s32[256]{0:T(256)S(1)}, s32[256]{0:T(256)}, u32[]{:S(2)}) copy-start(s32[256]{0:T(256)} %param.7) | copy-start | bytes 3076
  2.0 34.7 %copy-start.1 = (bf16[1024,512]{1,0:T(8,128)(2,1)S(1)}, bf16[1024,512]{1,0:T(8,128)(2,1)}, u32[]{:S(2)}) copy-start(bf16[1024,512]{1,0:T(8,128)(2,1)} %refs_1_.4) | copy-start | bytes 3145732
  2.0 34.7 %copy-start.4 = (bf16[256,1024]{1,0:T(8,128)(2,1)S(1)}, bf16[256,1024]{1,0:T(8,128)(2,1)}, u32[]{:S(2)}) copy-start(bf16[256,1024]{1,0:T(8,128)(2,1)} %refs_1_.3) | copy-start | bytes 1572868
  30.5 8.6 %collective-permute-start = (bf16[1088,512]{1,0:T(8,128)(2,1)S(1)}, bf16[1088,512]{1,0:T(8,128)(2,1)}, u32[]{:S(2)}, u32[]{:S(2)}) collective-permute-start(bf16[1088,512]{1,0:T(8,128)(2,1)S(1)} %convert_element_type.7.refs_6_), channel_id=1, source_target_pairs={{0,64},{64,0},{1,65},{65,1},{2,66},{66,2},{3,67},{67,3},{4,68},{68... | collective-permute-start | bytes 3342344 | tf_op jit(solution)/shard_map/ppermute | solution.py:20
  37.3 21.8 %copy-start.5 = (bf16[256,512]{1,0:T(8,128)(2,1)}, bf16[256,512]{1,0:T(8,128)(2,1)S(1)}, u32[]{:S(2)}) copy-start(bf16[256,512]{1,0:T(8,128)(2,1)S(1)} %get-tuple-element.30.refs_2_) | copy-start | bytes 786436
  43.0 4.4 %copy-start.2 = (bf16[8,256,256]{2,1,0:T(8,128)(2,1)}, bf16[8,256,256]{2,1,0:T(8,128)(2,1)S(1)}, u32[]{:S(2)}) copy-start(bf16[8,256,256]{2,1,0:T(8,128)(2,1)S(1)} %get-tuple-element.38.refs_1_) | copy-start | bytes 3145732
  43.0 5.3 %collective-permute-start.1 = (bf16[1536,512]{1,0:T(8,128)(2,1)S(1)}, bf16[1536,512]{1,0:T(8,128)(2,1)S(1)}, u32[]{:S(2)}, u32[]{:S(2)}) collective-permute-start(bf16[1536,512]{1,0:T(8,128)(2,1)S(1)} %get-tuple-element.33), channel_id=1, source_target_pairs={{0,64},{64,0},{1,65},{65,1},{2,66},{66,2},{3,67},{67,3},{4,68},{68... | collective-permute-start | bytes 4718600 | tf_op jit(solution)/shard_map/ppermute | solution.py:20
  48.3 10.8 %copy-start = (bf16[1536,512]{1,0:T(8,128)(2,1)}, bf16[1536,512]{1,0:T(8,128)(2,1)S(1)}, u32[]{:S(2)}) copy-start(bf16[1536,512]{1,0:T(8,128)(2,1)S(1)} %collective-permute-done.1.refs_1_.refs_3_) | copy-start | bytes 4718596
  48.3 10.8 %copy-start.3 = (bf16[8,256,256]{2,1,0:T(8,128)(2,1)S(1)}, bf16[8,256,256]{2,1,0:T(8,128)(2,1)}, u32[]{:S(2)}) copy-start(bf16[8,256,256]{2,1,0:T(8,128)(2,1)} %copy-done.2) | copy-start | bytes 3145732
  49.3 30.2 %all-to-all-start = ((bf16[32,16,512]{2,1,0:T(8,128)(2,1)}), bf16[32,16,512]{2,1,0:T(8,128)(2,1)S(1)}, u32[]{:S(2)}, u32[]{:S(2)}) async-start(bf16[32,16,512]{2,1,0:T(8,128)(2,1)} %shard_map.72), calls=%async_computation | async-start | bytes 1048576 | tf_op jit(solution)/shard_map/all_to_all | solution.py:24
  60.0 15.9 %collective-permute-start.2 = (bf16[256,512]{1,0:T(8,128)(2,1)S(1)}, bf16[256,512]{1,0:T(8,128)(2,1)S(1)}, u32[]{:S(2)}, u32[]{:S(2)}) collective-permute-start(bf16[256,512]{1,0:T(8,128)(2,1)S(1)} %get-tuple-element.40), channel_id=1, source_target_pairs={{0,128},{128,256},{256,384},{384,0},{1,129},{129,257},{257,385},{3... | collective-permute-start | bytes 786440 | tf_op jit(solution)/shard_map/ppermute | solution.py:20
  63.0 16.4 %collective-permute-start.3 = (bf16[256,512]{1,0:T(8,128)(2,1)S(1)}, bf16[256,512]{1,0:T(8,128)(2,1)S(1)}, u32[]{:S(2)}, u32[]{:S(2)}) collective-permute-start(bf16[256,512]{1,0:T(8,128)(2,1)S(1)} %get-tuple-element.41), channel_id=1, source_target_pairs={{0,384},{128,0},{256,128},{384,256},{1,385},{129,1},{257,129},{385... | collective-permute-start | bytes 786440 | tf_op jit(solution)/shard_map/ppermute | solution.py:20
  75.9 8.9 %copy-start.9 = (bf16[256,512]{1,0:T(8,128)(2,1)}, bf16[256,512]{1,0:T(8,128)(2,1)S(1)}, u32[]{:S(2)}) copy-start(bf16[256,512]{1,0:T(8,128)(2,1)S(1)} %collective-permute-done.2.refs_4_) | copy-start | bytes 786436
  79.4 5.4 %copy-start.10 = (bf16[256,512]{1,0:T(8,128)(2,1)}, bf16[256,512]{1,0:T(8,128)(2,1)S(1)}, u32[]{:S(2)}) copy-start(bf16[256,512]{1,0:T(8,128)(2,1)S(1)} %collective-permute-done.3.refs_5_) | copy-start | bytes 786436
  80.2 12.3 %all-to-all-start.1 = ((bf16[8,16,512]{2,1,0:T(8,128)(2,1)}), bf16[8,16,512]{2,1,0:T(8,128)(2,1)S(1)}, u32[]{:S(2)}, u32[]{:S(2)}) async-start(bf16[8,16,512]{2,1,0:T(8,128)(2,1)} %shard_map.74), calls=%async_computation.1 | async-start | bytes 262144 | tf_op jit(solution)/shard_map/all_to_all | solution.py:24
  88.5 14.2 %copy-start.12 = (bf16[256,512]{1,0:T(8,128)(2,1)S(1)}, bf16[256,512]{1,0:T(8,128)(2,1)}, u32[]{:S(2)}) copy-start(bf16[256,512]{1,0:T(8,128)(2,1)} %get-tuple-element.48) | copy-start | bytes 786436
  93.4 23.5 %all-to-all-start.2 = ((bf16[32,16,512]{2,1,0:T(8,128)(2,1)}), bf16[32,16,512]{2,1,0:T(8,128)(2,1)S(1)}, u32[]{:S(2)}, u32[]{:S(2)}) async-start(bf16[32,16,512]{2,1,0:T(8,128)(2,1)} %shard_map.75), calls=%async_computation.2 | async-start | bytes 1048576 | tf_op jit(solution)/shard_map/all_to_all | solution.py:24
  102.7 21.2 %copy-start.7 = (bf16[256,512]{1,0:T(8,128)(2,1)S(1)}, bf16[256,512]{1,0:T(8,128)(2,1)}, u32[]{:S(2)}) copy-start(bf16[256,512]{1,0:T(8,128)(2,1)} %refs_0_.4) | copy-start | bytes 786436
  102.7 21.2 %copy-start.8 = (f32[256,512]{1,0:T(8,128)S(1)}, f32[256,512]{1,0:T(8,128)}, u32[]{:S(2)}) copy-start(f32[256,512]{1,0:T(8,128)} %get-tuple-element.51.refs_1_) | copy-start | bytes 1572868
  102.7 14.2 %collective-permute-start.4 = (bf16[256,512]{1,0:T(8,128)(2,1)S(1)}, bf16[256,512]{1,0:T(8,128)(2,1)S(1)}, u32[]{:S(2)}, u32[]{:S(2)}) collective-permute-start(bf16[256,512]{1,0:T(8,128)(2,1)S(1)} %copy-done.12), channel_id=1, source_target_pairs={{0,128},{128,256},{256,384},{384,0},{1,129},{129,257},{257,385},{3... | collective-permute-start | bytes 786440 | tf_op jit(solution)/shard_map/ppermute | solution.py:20
  117.0 7.9 %collective-permute-start.5 = (bf16[512,512]{1,0:T(8,128)(2,1)S(1)}, bf16[512,512]{1,0:T(8,128)(2,1)S(1)}, u32[]{:S(2)}, u32[]{:S(2)}) collective-permute-start(bf16[512,512]{1,0:T(8,128)(2,1)S(1)} %bitcast.4), channel_id=1, source_target_pairs={{0,64},{64,0},{1,65},{65,1},{2,66},{66,2},{3,67},{67,3},{4,68},{68... | collective-permute-start | bytes 1572872 | tf_op jit(solution)/shard_map/ppermute | solution.py:20

commit v7 on v6

--- a/solution.py
+++ b/solution.py
@@ -176,19 +176,27 @@
     return part + got_ref[pl.ds(start, rows), :].astype(jnp.float32)
 
 
-def text_sums_kernel(place_ref, tiles_ref, audio_b_ref, got_ref, across_ref, last_ref):
-    refs = (place_ref, tiles_ref, audio_b_ref, got_ref)
-    across_ref[...] = summed(*refs, 2).astype(jnp.bfloat16)
-    last_ref[...] = summed(*refs, 3).astype(jnp.bfloat16)
+def text_sums_kernel(place_ref, tiles_ref, audio_b_ref, got_ref, forward_ref, backward_ref):
+    across = summed(place_ref, tiles_ref, audio_b_ref, got_ref, 2).astype(jnp.bfloat16)
+    cut = forward_ref.shape[0]
+    forward_ref[...] = across[:cut]
+    backward_ref[...] = across[cut:]
 
 
 def relay_kernel(
-    place_ref, tiles_ref, audio_b_ref, got_ref, across_ref, last_ref, to_next_ref, home_ref
+    place_ref, tiles_ref, audio_b_ref, got_ref, forward_ref, backward_ref, to_next_ref, to_last_ref
 ):
     refs = (place_ref, tiles_ref, audio_b_ref, got_ref)
-    ahead = summed(*refs, 1) + across_ref[...].astype(jnp.float32)
-    to_next_ref[...] = ahead.astype(jnp.bfloat16)
-    home_ref[...] = summed(*refs, 0) + last_ref[...].astype(jnp.float32)
+    cut = forward_ref.shape[0]
+    ahead, behind = summed(*refs, 1), summed(*refs, 3)
+    to_next_ref[:cut, :] = (ahead[:cut] + forward_ref[...].astype(jnp.float32)).astype(jnp.bfloat16)
+    to_next_ref[cut:, :] = ahead[cut:].astype(jnp.bfloat16)
+    to_last_ref[:cut, :] = behind[:cut].astype(jnp.bfloat16)
+    to_last_ref[cut:, :] = (behind[cut:] + backward_ref[...].astype(jnp.float32)).astype(jnp.bfloat16)
+
+
+def home_kernel(place_ref, tiles_ref, audio_b_ref, got_ref, home_ref):
+    home_ref[...] = summed(place_ref, tiles_ref, audio_b_ref, got_ref, 0)
 
 
 def fold_kernel(parts_ref, copies_ref):
@@ -222,8 +230,8 @@
     )(place, half, *given)
 
 
-def text_grad_kernel(text_ref, home_ref, arrived_ref, grad_ref):
-    grad = home_ref[...] + arrived_ref[...].astype(jnp.float32)
+def text_grad_kernel(text_ref, home_ref, next_ref, last_ref, grad_ref):
+    grad = home_ref[...] + (next_ref[...].astype(jnp.float32) + last_ref[...].astype(jnp.float32))
     text = text_ref[...].astype(jnp.float32)
     scale = lax.rsqrt(jnp.sum(text * text, axis=1, keepdims=True) + EPS)
     text = text * scale
@@ -242,6 +250,7 @@
     half = channels // 2
     block = shape((rows, width), f32)
     block_b = shape((rows, width), bf16)
+    cut_b = shape((rows // 2, width), bf16)
 
     (sent,) = call(text_kernel, (shape((rows + TAIL, width), bf16),), text_raw)
     own = lax.all_gather(sent.astype(jnp.float16), "zh", axis=0, tiled=True).astype(bf16)
@@ -283,36 +292,47 @@
     (parts,) = call(half_kernel, (shape((plane, part, width), bf16),), weight, got, far_outs=True)
     parts, got = lax.optimization_barrier((parts, got))
     parts = exchanged(parts, PLANE)
-    across, last = call(
-        text_sums_kernel, (block_b, block_b), place, tiles, audio_b, got, flops=pair_flops // 2
-    )
-    across = shifted(across, "zh", 1)
-    last = shifted(last, "zh", -1)
-    parts, across, last = lax.optimization_barrier((parts, across, last))
+    forward, backward = call(
+        text_sums_kernel, (cut_b, cut_b), place, tiles, audio_b, got, flops=pair_flops // 4
+    )
+    forward = shifted(forward, "zh", 1)
+    backward = shifted(backward, "zh", -1)
+    parts, forward, backward = lax.optimization_barrier((parts, forward, backward))
     (parts,) = call(fold_kernel, (shape((column, part, width), bf16),), parts, far_outs=True)
     parts = exchanged(parts, COLUMN)
-    to_next, home = call(
+    to_next, to_last = call(
         relay_kernel,
-        (block_b, block),
+        (block_b, block_b),
         place,
         tiles,
         audio_b,
         got,
-        across,
-        last,
+        forward,
+        backward,
         light=True,
         far=(1, 2, 3, 4, 5),
         far_outs=True,
     )
     (parts,) = call(fold_kernel, (shape((plane, part, width), bf16),), parts, far_outs=True)
-    parts, to_next, home = lax.optimization_barrier((parts, to_next, home))
+    parts, to_next, to_last, tiles = lax.optimization_barrier((parts, to_next, to_last, tiles))
     weight_half = exchanged(parts, PLANE).reshape(half, width)
-    arrived = shifted(to_next, "zh", 1)
-    weight_half, arrived = lax.optimization_barrier((weight_half, arrived))
+    arrived = [shifted(to_next, "zh", 1), shifted(to_last, "zh", -1)]
+    (home,) = call(
+        home_kernel,
+        (block,),
+        place,
+        tiles,
+        audio_b,
+        got,
+        light=True,
+        far=(1, 2, 3),
+        far_outs=True,
+    )
+    weight_half, arrived, home = lax.optimization_barrier((weight_half, arrived, home))
     there = shifted(weight_half, "core", 1)
     grad_weight = placed(place, weight_half, 0, None)
     grad_weight = placed(place, there, 1, grad_weight)
-    (grad_text,) = call(text_grad_kernel, (block,), text_raw, home, arrived)
+    (grad_text,) = call(text_grad_kernel, (block,), text_raw, home, *arrived)
     return (grad_weight, grad_features, grad_text)
 
 

time: 127 us -> 124 us (0.976)
  waiting for transfers between devices: 30.8 us -> 20.7 us
  Pallas kernels: 18.2 us -> 21.7 us
  starting transfers between devices: 46.8 us -> 49.2 us
    ppermute x6 -> x7, waiting for transfers between devices: 26.8 us -> 16.2 us  [shifted(): lax.ppermute(block, axis, [(i, (i + distance) % count) for i in range(cou...]
    pallas_call x11 -> x12, Pallas kernels: 15.1 us -> 18.5 us  [call(): pl.pallas_call(staging, out_shape=[pltpu.HBM(a.shape, a.dtype) for a in o...]
    ppermute x6 -> x7, starting transfers between devices: 23.1 us -> 26.1 us  [shifted(): lax.ppermute(block, axis, [(i, (i + distance) % count) for i in range(cou...]
  transfers between devices with their start and end apart: 9 -> 10, of which waited for: 6 -> 7; matrix products, arithmetic and copies ran while one was open for 0% -> 0% of each run, Pallas kernels for 8% -> 11%
where the time goes in v7:
time: 124 us; the launch traced here: 123 us
  starting transfers between devices  49.2 us (40%)
  blocking collectives  28.3 us (23%)
  Pallas kernels  21.7 us (18%)
  waiting for transfers between devices  20.7 us (17%)
  local copies, waits for them, and re-layouts  2.39 us (2%)
    all_gather x1, blocking collectives, body(): lax.all_gather(sent.astype(jnp.float16), 'zh', axis=0, tiled=True)  28.3 us
    ppermute x7, starting transfers between devices, shifted(): lax.ppermute(block, axis, [(i, (i + distance) % count) for i in range(cou...  26.1 us
    all_to_all x3, starting transfers between devices, exchanged(): return lax.all_to_all(block, axes, split_axis=0, concat_axis=0, tiled=True)  23.1 us
    pallas_call x12, Pallas kernels, call(): pl.pallas_call(staging, out_shape=[pltpu.HBM(a.shape, a.dtype) for a in o...  18.5 us
    ppermute x7, waiting for transfers between devices, shifted(): lax.ppermute(block, axis, [(i, (i + distance) % count) for i in range(cou...  16.2 us
    all_to_all x3, waiting for transfers between devices, exchanged(): return lax.all_to_all(block, axes, split_axis=0, concat_axis=0, tiled=True)  4.5 us
    pallas_call x2, Pallas kernels, placed(): pl.pallas_call(place_kernel, out_shape=shape((2 * rows, width), jnp.float...  3.16 us
  transfers between devices with their start and end apart: 10, of which 7 were waited for; matrix products, arithmetic and copies ran while one was open for 0% of the time, Pallas kernels for 11%

profile of v7, /device:TPU:1, one launch (start us, length us, event | category | flops | bytes accessed | tf_op | source)
XLA Modules:
  0.0 123.5 jit_solution(3711854349101119951)
XLA Ops:
  0.6 0.9 copy-done.9
  2.0 28.3 %all-gather.1 = f16[1088,512]{1,0:T(8,128)(2,1)S(1)} all-gather(f16[272,512]{1,0:T(8,128)(2,1)S(1)} %convert_element_type.6), channel_id=1, replica_groups=mesh['zh'=4,'core'=2,'zl'=2,'x'=4,'y'=8] {'zh'}, dimensions={0}, use_global_device_ids=true | all-gather | bytes 1392640 | tf_op jit(solution)/shard_map/all_gather | solution.py:256
  30.4 6.1 %collective-permute-start = (bf16[1088,512]{1,0:T(8,128)(2,1)S(1)}, bf16[1088,512]{1,0:T(8,128)(2,1)}, u32[]{:S(2)}, u32[]{:S(2)}) collective-permute-start(bf16[1088,512]{1,0:T(8,128)(2,1)S(1)} %convert_element_type.7.refs_6_), channel_id=1, source_target_pairs={{0,64},{64,0},{1,65},{65,1},{2,66},{66,2},{3,67},{67,3},{4,68},{68... | collective-permute-start | bytes 3342344 | tf_op jit(solution)/shard_map/ppermute | solution.py:20
  37.3 1.7 %collective-permute-done.refs_7_ = bf16[1088,512]{1,0:T(8,128)(2,1)} collective-permute-done((bf16[1088,512]{1,0:T(8,128)(2,1)S(1)}, bf16[1088,512]{1,0:T(8,128)(2,1)}, u32[]{:S(2)}, u32[]{:S(2)}) %collective-permute-start) | collective-permute-done | bytes 1114144 | tf_op jit(solution)/shard_map/ppermute | solution.py:20
  39.0 1.2 %copy-done.8 = bf16[1088,512]{1,0:T(8,128)(2,1)S(1)} copy-done((bf16[1088,512]{1,0:T(8,128)(2,1)S(1)}, bf16[1088,512]{1,0:T(8,128)(2,1)}, u32[]{:S(2)}) %copy-start.8) | copy-done | bytes 1114136
  40.3 4.1 %shard_map.69 = (bf16[256,512]{1,0:T(8,128)(2,1)S(1)}, bf16[8,256,256]{2,1,0:T(8,128)(2,1)S(1)}, bf16[1536,512]{1,0:T(8,128)(2,1)S(1)}) custom-call(s32[2]{0:T(128)S(1)} %pad_add_fusion.refs_0_.place_ref, f32[256,512]{1,0:T(8,128)S(1)} %get-tuple-element.32.refs_1_, bf16[256,512]{1,0:T(8,128)(2,1)S(1)} %get-tuple-element.33.refs_2_, ...), custom_call_target="tpu_custom_call" | custom-call | flops 1610612736 | bytes 6424584 | tf_op jit(solution)/shard_map/pallas_call | solution.py:70
  44.4 2.3 %collective-permute-start.1 = (bf16[1536,512]{1,0:T(8,128)(2,1)S(1)}, bf16[1536,512]{1,0:T(8,128)(2,1)S(1)}, u32[]{:S(2)}, u32[]{:S(2)}) collective-permute-start(bf16[1536,512]{1,0:T(8,128)(2,1)S(1)} %get-tuple-element.36), channel_id=1, source_target_pairs={{0,64},{64,0},{1,65},{65,1},{2,66},{66,2},{3,67},{67,3},{4,68},{68... | collective-permute-start | bytes 4718600 | tf_op jit(solution)/shard_map/ppermute | solution.py:20
  46.7 1.3 %shard_map.71 = bf16[256,1024]{1,0:T(8,128)(2,1)} custom-call(bf16[256,512]{1,0:T(8,128)(2,1)S(1)} %get-tuple-element.37.refs_2_.refs_0_, bf16[1024,512]{1,0:T(8,128)(2,1)S(1)} %copy-done.3), custom_call_target="tpu_custom_call" | custom-call | tf_op jit(solution)/shard_map/pallas_call | solution.py:70
  48.0 0.9 shard_map.70.refs_0_
  48.9 0.9 collective-permute-done.1.refs_1_.refs_3_
  49.8 1.0 shard_map.72
  50.8 9.7 %all-to-all-start = ((bf16[32,16,512]{2,1,0:T(8,128)(2,1)}), bf16[32,16,512]{2,1,0:T(8,128)(2,1)S(1)}, u32[]{:S(2)}, u32[]{:S(2)}) async-start(bf16[32,16,512]{2,1,0:T(8,128)(2,1)} %shard_map.72), calls=%async_computation | async-start | bytes 1048576 | tf_op jit(solution)/shard_map/all_to_all | solution.py:24
  60.5 0.8 shard_map.73
  61.3 3.0 %collective-permute-start.2 = (bf16[128,512]{1,0:T(8,128)(2,1)S(1)}, bf16[128,512]{1,0:T(8,128)(2,1)S(1)}, u32[]{:S(2)}, u32[]{:S(2)}) collective-permute-start(bf16[128,512]{1,0:T(8,128)(2,1)S(1)} %get-tuple-element.43), channel_id=1, source_target_pairs={{0,128},{128,256},{256,384},{384,0},{1,129},{129,257},{257,385},{3... | collective-permute-start | bytes 393224 | tf_op jit(solution)/shard_map/ppermute | solution.py:20
  64.3 4.4 %collective-permute-start.3 = (bf16[128,512]{1,0:T(8,128)(2,1)S(1)}, bf16[128,512]{1,0:T(8,128)(2,1)S(1)}, u32[]{:S(2)}, u32[]{:S(2)}) collective-permute-start(bf16[128,512]{1,0:T(8,128)(2,1)S(1)} %get-tuple-element.44), channel_id=1, source_target_pairs={{0,384},{128,0},{256,128},{384,256},{1,385},{129,1},{257,129},{385... | collective-permute-start | bytes 393224 | tf_op jit(solution)/shard_map/ppermute | solution.py:20
  68.7 2.9 %collective-permute-done.2.refs_4_ = bf16[128,512]{1,0:T(8,128)(2,1)S(1)} collective-permute-done((bf16[128,512]{1,0:T(8,128)(2,1)S(1)}, bf16[128,512]{1,0:T(8,128)(2,1)S(1)}, u32[]{:S(2)}, u32[]{:S(2)}) %collective-permute-start.2) | collective-permute-done | bytes 131104 | tf_op jit(solution)/shard_map/ppermute | solution.py:20
  71.6 3.5 %collective-permute-done.3.refs_5_ = bf16[128,512]{1,0:T(8,128)(2,1)S(1)} collective-permute-done((bf16[128,512]{1,0:T(8,128)(2,1)S(1)}, bf16[128,512]{1,0:T(8,128)(2,1)S(1)}, u32[]{:S(2)}, u32[]{:S(2)}) %collective-permute-start.3) | collective-permute-done | bytes 131104 | tf_op jit(solution)/shard_map/ppermute | solution.py:20
  75.1 0.7 shard_map.74
  75.9 4.6 %all-to-all-start.1 = ((bf16[8,16,512]{2,1,0:T(8,128)(2,1)}), bf16[8,16,512]{2,1,0:T(8,128)(2,1)S(1)}, u32[]{:S(2)}, u32[]{:S(2)}) async-start(bf16[8,16,512]{2,1,0:T(8,128)(2,1)} %shard_map.74), calls=%async_computation.1 | async-start | bytes 262144 | tf_op jit(solution)/shard_map/all_to_all | solution.py:24
  80.4 3.5 %shard_map.76 = (bf16[256,512]{1,0:T(8,128)(2,1)}, bf16[256,512]{1,0:T(8,128)(2,1)}) custom-call(s32[2]{0:T(128)S(1)} %pad_add_fusion.refs_0_.place_ref, bf16[8,256,256]{2,1,0:T(8,128)(2,1)} %copy-done.1, bf16[256,512]{1,0:T(8,128)(2,1)} %copy-done.4, bf16[1536,512]{1,0:T(8,128)(2,1)} %copy-done, bf16[128,512]{1,0:T(8,128)(2,1)} %copy-done.11, ...), custom_call_target="tpu_custom_call" | custom-call | tf_op jit(solution)/shard_map/pallas_call | solution.py:70
  84.0 4.5 %all-to-all-done.1.refs_0_ = bf16[8,16,512]{2,1,0:T(8,128)(2,1)S(1)} async-done(((bf16[8,16,512]{2,1,0:T(8,128)(2,1)}), bf16[8,16,512]{2,1,0:T(8,128)(2,1)S(1)}, u32[]{:S(2)}, u32[]{:S(2)}) %all-to-all-start.1) | async-done | bytes 131104 | tf_op jit(solution)/shard_map/all_to_all | solution.py:24
  88.5 0.9 shard_map.75
  89.3 8.8 %all-to-all-start.2 = ((bf16[32,16,512]{2,1,0:T(8,128)(2,1)}), bf16[32,16,512]{2,1,0:T(8,128)(2,1)S(1)}, u32[]{:S(2)}, u32[]{:S(2)}) async-start(bf16[32,16,512]{2,1,0:T(8,128)(2,1)} %shard_map.75), calls=%async_computation.2 | async-start | bytes 1048576 | tf_op jit(solution)/shard_map/all_to_all | solution.py:24
  98.2 1.9 %collective-permute-start.4 = (bf16[256,512]{1,0:T(8,128)(2,1)S(1)}, bf16[256,512]{1,0:T(8,128)(2,1)S(1)}, u32[]{:S(2)}, u32[]{:S(2)}) collective-permute-start(bf16[256,512]{1,0:T(8,128)(2,1)S(1)} %copy-done.15), channel_id=1, source_target_pairs={{0,128},{128,256},{256,384},{384,0},{1,129},{129,257},{257,385},{3... | collective-permute-start | bytes 786440 | tf_op jit(solution)/shard_map/ppermute | solution.py:20
  100.1 5.4 %collective-permute-start.5 = (bf16[256,512]{1,0:T(8,128)(2,1)S(1)}, bf16[256,512]{1,0:T(8,128)(2,1)S(1)}, u32[]{:S(2)}, u32[]{:S(2)}) collective-permute-start(bf16[256,512]{1,0:T(8,128)(2,1)S(1)} %copy-done.14), channel_id=1, source_target_pairs={{0,384},{128,0},{256,128},{384,256},{1,385},{129,1},{257,129},{385... | collective-permute-start | bytes 786440 | tf_op jit(solution)/shard_map/ppermute | solution.py:20
  105.6 3.4 %shard_map.77.refs_1_ = f32[256,512]{1,0:T(8,128)} custom-call(s32[2]{0:T(128)S(1)} %pad_add_fusion.refs_0_.place_ref, bf16[8,256,256]{2,1,0:T(8,128)(2,1)} %copy-done.1, bf16[256,512]{1,0:T(8,128)(2,1)} %copy-done.4, bf16[1536,512]{1,0:T(8,128)(2,1)} %copy-done), custom_call_target="tpu_custom_call" | custom-call | tf_op jit(solution)/shard_map/pallas_call | solution.py:70
  109.1 3.7 %collective-permute-done.4.refs_2_ = bf16[256,512]{1,0:T(8,128)(2,1)S(1)} collective-permute-done((bf16[256,512]{1,0:T(8,128)(2,1)S(1)}, bf16[256,512]{1,0:T(8,128)(2,1)S(1)}, u32[]{:S(2)}, u32[]{:S(2)}) %collective-permute-start.4) | collective-permute-done | bytes 262176 | tf_op jit(solution)/shard_map/ppermute | solution.py:20
  112.8 3.5 %collective-permute-done.5.refs_3_ = bf16[256,512]{1,0:T(8,128)(2,1)S(1)} collective-permute-done((bf16[256,512]{1,0:T(8,128)(2,1)S(1)}, bf16[256,512]{1,0:T(8,128)(2,1)S(1)}, u32[]{:S(2)}, u32[]{:S(2)}) %collective-permute-start.5) | collective-permute-done | bytes 262176 | tf_op jit(solution)/shard_map/ppermute | solution.py:20
  116.3 2.9 %collective-permute-start.6 = (bf16[512,512]{1,0:T(8,128)(2,1)S(1)}, bf16[512,512]{1,0:T(8,128)(2,1)S(1)}, u32[]{:S(2)}, u32[]{:S(2)}) collective-permute-start(bf16[512,512]{1,0:T(8,128)(2,1)S(1)} %bitcast.4), channel_id=1, source_target_pairs={{0,64},{64,0},{1,65},{65,1},{2,66},{66,2},{3,67},{67,3},{4,68},{68... | collective-permute-start | bytes 1572872 | tf_op jit(solution)/shard_map/ppermute | solution.py:20
  119.3 1.6 %shard_map.78.refs_0_ = f32[1024,512]{1,0:T(8,128)} custom-call(s32[2]{0:T(128)S(1)} %pad_add_fusion.refs_0_.place_ref, bf16[512,512]{1,0:T(8,128)(2,1)S(1)} %bitcast.5), custom_call_target="tpu_custom_call" | custom-call | bytes 1572864 | tf_op jit(solution)/shard_map/pallas_call | solution.py:215
  120.9 1.1 shard_map.80
  121.9 1.6 %shard_map.79 = f32[1024,512]{1,0:T(8,128)} custom-call(s32[2]{0:T(128)S(1)} %pad_add_fusion.refs_0_.place_ref, bf16[512,512]{1,0:T(8,128)(2,1)S(1)} %collective-permute-done.6.half_ref, f32[1024,512]{1,0:T(8,128)} %shard_map.78.refs_0_), custom_call_target="tpu_custom_call", output_to_operand_aliasing={{}: (2, {})} | custom-call | bytes 1572864 | tf_op jit(solution)/shard_map/pallas_call | solution.py:215
  (39 shorter events, 1.3 us)
Async XLA Ops:
  0.6 1.0 copy-start.9
  2.0 34.6 %copy-start.13 = (s32[256]{0:T(256)S(1)}, s32[256]{0:T(256)}, u32[]{:S(2)}) copy-start(s32[256]{0:T(256)} %param.7) | copy-start | bytes 3076
  2.0 34.7 %copy-start.2 = (bf16[1024,512]{1,0:T(8,128)(2,1)S(1)}, bf16[1024,512]{1,0:T(8,128)(2,1)}, u32[]{:S(2)}) copy-start(bf16[1024,512]{1,0:T(8,128)(2,1)} %refs_1_.4) | copy-start | bytes 3145732
  2.0 34.7 %copy-start.5 = (bf16[256,1024]{1,0:T(8,128)(2,1)S(1)}, bf16[256,1024]{1,0:T(8,128)(2,1)}, u32[]{:S(2)}) copy-start(bf16[256,1024]{1,0:T(8,128)(2,1)} %refs_1_.3) | copy-start | bytes 1572868
  30.4 8.6 %copy-start.7 = (bf16[1088,512]{1,0:T(8,128)(2,1)}, bf16[1088,512]{1,0:T(8,128)(2,1)S(1)}, u32[]{:S(2)}) copy-start(bf16[1088,512]{1,0:T(8,128)(2,1)S(1)} %convert_element_type.7.refs_6_) | copy-start | bytes 3342340
  30.4 8.6 %collective-permute-start = (bf16[1088,512]{1,0:T(8,128)(2,1)S(1)}, bf16[1088,512]{1,0:T(8,128)(2,1)}, u32[]{:S(2)}, u32[]{:S(2)}) collective-permute-start(bf16[1088,512]{1,0:T(8,128)(2,1)S(1)} %convert_element_type.7.refs_6_), channel_id=1, source_target_pairs={{0,64},{64,0},{1,65},{65,1},{2,66},{66,2},{3,67},{67,3},{4,68},{68... | collective-permute-start | bytes 3342344 | tf_op jit(solution)/shard_map/ppermute | solution.py:20
  37.2 23.2 %copy-start.4 = (bf16[256,512]{1,0:T(8,128)(2,1)}, bf16[256,512]{1,0:T(8,128)(2,1)S(1)}, u32[]{:S(2)}) copy-start(bf16[256,512]{1,0:T(8,128)(2,1)S(1)} %get-tuple-element.33.refs_2_) | copy-start | bytes 786436
  39.0 1.2 %copy-start.8 = (bf16[1088,512]{1,0:T(8,128)(2,1)S(1)}, bf16[1088,512]{1,0:T(8,128)(2,1)}, u32[]{:S(2)}) copy-start(bf16[1088,512]{1,0:T(8,128)(2,1)} %copy-done.7) | copy-start | bytes 3342340
  40.3 6.5 %copy-start.3 = (bf16[1024,512]{1,0:T(8,128)(2,1)S(1)}, bf16[1024,512]{1,0:T(8,128)(2,1)}, u32[]{:S(2)}) copy-start(bf16[1024,512]{1,0:T(8,128)(2,1)} %refs_1_.4) | copy-start | bytes 3145732
  44.4 16.0 %copy-start.1 = (bf16[8,256,256]{2,1,0:T(8,128)(2,1)}, bf16[8,256,256]{2,1,0:T(8,128)(2,1)S(1)}, u32[]{:S(2)}) copy-start(bf16[8,256,256]{2,1,0:T(8,128)(2,1)S(1)} %get-tuple-element.53.refs_1_) | copy-start | bytes 3145732
  44.4 5.3 %collective-permute-start.1 = (bf16[1536,512]{1,0:T(8,128)(2,1)S(1)}, bf16[1536,512]{1,0:T(8,128)(2,1)S(1)}, u32[]{:S(2)}, u32[]{:S(2)}) collective-permute-start(bf16[1536,512]{1,0:T(8,128)(2,1)S(1)} %get-tuple-element.36), channel_id=1, source_target_pairs={{0,64},{64,0},{1,65},{65,1},{2,66},{66,2},{3,67},{67,3},{4,68},{68... | collective-permute-start | bytes 4718600 | tf_op jit(solution)/shard_map/ppermute | solution.py:20
  49.7 10.7 %copy-start = (bf16[1536,512]{1,0:T(8,128)(2,1)}, bf16[1536,512]{1,0:T(8,128)(2,1)S(1)}, u32[]{:S(2)}) copy-start(bf16[1536,512]{1,0:T(8,128)(2,1)S(1)} %collective-permute-done.1.refs_1_.refs_3_) | copy-start | bytes 4718596
  50.8 24.3 %all-to-all-start = ((bf16[32,16,512]{2,1,0:T(8,128)(2,1)}), bf16[32,16,512]{2,1,0:T(8,128)(2,1)S(1)}, u32[]{:S(2)}, u32[]{:S(2)}) async-start(bf16[32,16,512]{2,1,0:T(8,128)(2,1)} %shard_map.72), calls=%async_computation | async-start | bytes 1048576 | tf_op jit(solution)/shard_map/all_to_all | solution.py:24
  61.3 10.3 %collective-permute-start.2 = (bf16[128,512]{1,0:T(8,128)(2,1)S(1)}, bf16[128,512]{1,0:T(8,128)(2,1)S(1)}, u32[]{:S(2)}, u32[]{:S(2)}) collective-permute-start(bf16[128,512]{1,0:T(8,128)(2,1)S(1)} %get-tuple-element.43), channel_id=1, source_target_pairs={{0,128},{128,256},{256,384},{384,0},{1,129},{129,257},{257,385},{3... | collective-permute-start | bytes 393224 | tf_op jit(solution)/shard_map/ppermute | solution.py:20
  64.3 10.8 %collective-permute-start.3 = (bf16[128,512]{1,0:T(8,128)(2,1)S(1)}, bf16[128,512]{1,0:T(8,128)(2,1)S(1)}, u32[]{:S(2)}, u32[]{:S(2)}) collective-permute-start(bf16[128,512]{1,0:T(8,128)(2,1)S(1)} %get-tuple-element.44), channel_id=1, source_target_pairs={{0,384},{128,0},{256,128},{384,256},{1,385},{129,1},{257,129},{385... | collective-permute-start | bytes 393224 | tf_op jit(solution)/shard_map/ppermute | solution.py:20
  71.6 8.8 %copy-start.11 = (bf16[128,512]{1,0:T(8,128)(2,1)}, bf16[128,512]{1,0:T(8,128)(2,1)S(1)}, u32[]{:S(2)}) copy-start(bf16[128,512]{1,0:T(8,128)(2,1)S(1)} %collective-permute-done.2.refs_4_) | copy-start | bytes 393220
  75.1 5.3 %copy-start.12 = (bf16[128,512]{1,0:T(8,128)(2,1)}, bf16[128,512]{1,0:T(8,128)(2,1)S(1)}, u32[]{:S(2)}) copy-start(bf16[128,512]{1,0:T(8,128)(2,1)S(1)} %collective-permute-done.3.refs_5_) | copy-start | bytes 393220
  75.9 12.6 %all-to-all-start.1 = ((bf16[8,16,512]{2,1,0:T(8,128)(2,1)}), bf16[8,16,512]{2,1,0:T(8,128)(2,1)S(1)}, u32[]{:S(2)}, u32[]{:S(2)}) async-start(bf16[8,16,512]{2,1,0:T(8,128)(2,1)} %shard_map.74), calls=%async_computation.1 | async-start | bytes 262144 | tf_op jit(solution)/shard_map/all_to_all | solution.py:24
  83.9 14.2 %copy-start.15 = (bf16[256,512]{1,0:T(8,128)(2,1)S(1)}, bf16[256,512]{1,0:T(8,128)(2,1)}, u32[]{:S(2)}) copy-start(bf16[256,512]{1,0:T(8,128)(2,1)} %get-tuple-element.51) | copy-start | bytes 786436
  84.0 16.2 %copy-start.14 = (bf16[256,512]{1,0:T(8,128)(2,1)S(1)}, bf16[256,512]{1,0:T(8,128)(2,1)}, u32[]{:S(2)}) copy-start(bf16[256,512]{1,0:T(8,128)(2,1)} %get-tuple-element.52) | copy-start | bytes 786436
  89.3 27.0 %all-to-all-start.2 = ((bf16[32,16,512]{2,1,0:T(8,128)(2,1)}), bf16[32,16,512]{2,1,0:T(8,128)(2,1)S(1)}, u32[]{:S(2)}, u32[]{:S(2)}) async-start(bf16[32,16,512]{2,1,0:T(8,128)(2,1)} %shard_map.75), calls=%async_computation.2 | async-start | bytes 1048576 | tf_op jit(solution)/shard_map/all_to_all | solution.py:24
  98.2 14.6 %collective-permute-start.4 = (bf16[256,512]{1,0:T(8,128)(2,1)S(1)}, bf16[256,512]{1,0:T(8,128)(2,1)S(1)}, u32[]{:S(2)}, u32[]{:S(2)}) collective-permute-start(bf16[256,512]{1,0:T(8,128)(2,1)S(1)} %copy-done.15), channel_id=1, source_target_pairs={{0,128},{128,256},{256,384},{384,0},{1,129},{129,257},{257,385},{3... | collective-permute-start | bytes 786440 | tf_op jit(solution)/shard_map/ppermute | solution.py:20
  100.1 16.2 %collective-permute-start.5 = (bf16[256,512]{1,0:T(8,128)(2,1)S(1)}, bf16[256,512]{1,0:T(8,128)(2,1)S(1)}, u32[]{:S(2)}, u32[]{:S(2)}) collective-permute-start(bf16[256,512]{1,0:T(8,128)(2,1)S(1)} %copy-done.14), channel_id=1, source_target_pairs={{0,384},{128,0},{256,128},{384,256},{1,385},{129,1},{257,129},{385... | collective-permute-start | bytes 786440 | tf_op jit(solution)/shard_map/ppermute | solution.py:20
  109.0 11.8 %copy-start.6 = (f32[256,512]{1,0:T(8,128)S(1)}, f32[256,512]{1,0:T(8,128)}, u32[]{:S(2)}) copy-start(f32[256,512]{1,0:T(8,128)} %shard_map.77.refs_1_) | copy-start | bytes 1572868
  109.1 11.8 %copy-start.10 = (bf16[256,512]{1,0:T(8,128)(2,1)S(1)}, bf16[256,512]{1,0:T(8,128)(2,1)}, u32[]{:S(2)}) copy-start(bf16[256,512]{1,0:T(8,128)(2,1)} %refs_0_.4) | copy-start | bytes 786436
  116.3 5.6 %collective-permute-start.6 = (bf16[512,512]{1,0:T(8,128)(2,1)S(1)}, bf16[512,512]{1,0:T(8,128)(2,1)S(1)}, u32[]{:S(2)}, u32[]{:S(2)}) collective-permute-start(bf16[512,512]{1,0:T(8,128)(2,1)S(1)} %bitcast.4), channel_id=1, source_target_pairs={{0,64},{64,0},{1,65},{65,1},{2,66},{66,2},{3,67},{67,3},{4,68},{68... | collective-permute-start | bytes 1572872 | tf_op jit(solution)/shard_map/ppermute | solution.py:20

commit v8 on v7

--- a/solution.py
+++ b/solution.py
@@ -1,3 +1,5 @@
+import functools
+
 import jax
 import jax.numpy as jnp
 from jax import lax
@@ -12,6 +14,7 @@
 PLANE = ("x", "y")
 COLUMN = ("zh", "zl")
 TAIL = 16
+EARLY = 64
 MIB = 1 << 20
 
 
@@ -96,50 +99,58 @@
     sent_ref[rows:, :] = jnp.broadcast_to(power, tail).astype(jnp.bfloat16)
 
 
-def audio_kernel(features_ref, weight_ref, audio_ref, audio_b_ref, scale_ref):
+def text_block(held_ref, n, rows):
+    start = n * (rows + TAIL)
+    power = held_ref[start + rows : start + rows + TAIL, :128].astype(jnp.float32)
+    return held_ref[start : start + rows, :], SCALE * jnp.exp2(power[:1, :1])
+
+
+def audio_kernel(
+    features_ref, weight_ref, own_ref, audio_ref, audio_b_ref, scale_ref, scores_ref
+):
+    rows = audio_ref.shape[0]
     proj = dot(features_ref[...], weight_ref[...], 1, 0)
     scale = lax.rsqrt(jnp.sum(proj * proj, axis=1, keepdims=True) + EPS)
     audio = proj * scale
+    audio_b = audio.astype(jnp.bfloat16)
     audio_ref[...] = audio
-    audio_b_ref[...] = audio.astype(jnp.bfloat16)
+    audio_b_ref[...] = audio_b
     scale_ref[...] = scale
+    for n in range(scores_ref.shape[1] // rows):
+        block, factor = text_block(own_ref, n, rows)
+        scores_ref[:, n * rows : (n + 1) * rows] = factor * dot(audio_b, block, 1, 1)
 
 
 def score_kernel(
     place_ref, audio_ref, audio_b_ref, scale_ref, features_ref, positive_ref, own_ref, other_ref,
-    grad_ref, tiles_ref, sent_ref, scores_ref,
+    own_scores_ref, grad_ref, tiles_ref, sent_ref, scores_ref,
 ):
     core = place_ref[1]
     blocks, rows, _ = tiles_ref.shape
     chips = blocks // 2
     audio_b = audio_b_ref[...]
-
-    def text(n):
-        held = own_ref if n < chips else other_ref
-        start = n % chips * (rows + TAIL)
-        power = held[start + rows : start + rows + TAIL, :128].astype(jnp.float32)
-        return held[start : start + rows, :], SCALE * jnp.exp2(power[:1, :1])
-
-    for n in range(blocks):
-        block, scale = text(n)
-        scores_ref[:, n * rows : (n + 1) * rows] = scale * dot(audio_b, block, 1, 1)
+    for n in range(chips):
+        block, factor = text_block(other_ref, n, rows)
+        scores_ref[:, n * rows : (n + 1) * rows] = factor * dot(audio_b, block, 1, 1)
     step = 16
     ids = lax.broadcasted_iota(jnp.int32, (step, rows), 1)
     for r in range(0, rows, step):
-        scores = scores_ref[r : r + step, :]
-        weights = jnp.exp(scores - jnp.max(scores, axis=1, keepdims=True))
-        weights = weights * (1.0 / jnp.sum(weights, axis=1, keepdims=True))
+        both = [own_scores_ref[r : r + step, :], scores_ref[r : r + step, :]]
+        peak = jnp.maximum(*(jnp.max(scores, axis=1, keepdims=True) for scores in both))
+        both = [jnp.exp(scores - peak) for scores in both]
+        share = 1.0 / sum(jnp.sum(weights, axis=1, keepdims=True) for weights in both)
         positive = positive_ref[r : r + step, :]
         for n in range(blocks):
             column = core if n < chips else 1 - core
             first = ((n % chips) * 2 + column) * rows
             match = jnp.where(positive - first == ids, 1.0, 0.0)
-            part = weights[:, n * rows : (n + 1) * rows] - match
+            lanes = slice(n % chips * rows, (n % chips + 1) * rows)
+            part = both[n // chips][:, lanes] * share - match
             tiles_ref[n, r : r + step, :] = part.astype(jnp.bfloat16)
     total = jnp.zeros(audio_ref.shape, jnp.float32)
     for n in range(blocks):
-        block, scale = text(n)
-        total = total + scale * dot(tiles_ref[n], block, 1, 0)
+        block, factor = text_block(own_ref if n < chips else other_ref, n % chips, rows)
+        total = total + factor * dot(tiles_ref[n], block, 1, 0)
     audio = audio_ref[...]
     along = jnp.sum(audio * total, axis=1, keepdims=True)
     grad = ((total - audio * along) * scale_ref[...]).astype(jnp.bfloat16)
@@ -177,26 +188,41 @@
 
 
 def text_sums_kernel(place_ref, tiles_ref, audio_b_ref, got_ref, forward_ref, backward_ref):
-    across = summed(place_ref, tiles_ref, audio_b_ref, got_ref, 2).astype(jnp.bfloat16)
-    cut = forward_ref.shape[0]
-    forward_ref[...] = across[:cut]
-    backward_ref[...] = across[cut:]
+    refs = (place_ref, tiles_ref, audio_b_ref, got_ref)
+    rows = tiles_ref.shape[2]
+    cut = rows // 2
+    across = summed(*refs, 2).astype(jnp.bfloat16)
+    forward_ref[:cut, :] = across[:cut]
+    backward_ref[:cut, :] = across[cut:]
+    forward_ref[cut:, :] = summed(*refs, 1)[rows - EARLY :].astype(jnp.bfloat16)
+    backward_ref[cut:, :] = summed(*refs, 3)[:EARLY].astype(jnp.bfloat16)
 
 
 def relay_kernel(
     place_ref, tiles_ref, audio_b_ref, got_ref, forward_ref, backward_ref, to_next_ref, to_last_ref
 ):
     refs = (place_ref, tiles_ref, audio_b_ref, got_ref)
-    cut = forward_ref.shape[0]
+    rows = tiles_ref.shape[2]
+    cut = rows // 2
+    forward = forward_ref[:cut, :].astype(jnp.float32)
+    backward = backward_ref[:cut, :].astype(jnp.float32)
     ahead, behind = summed(*refs, 1), summed(*refs, 3)
-    to_next_ref[:cut, :] = (ahead[:cut] + forward_ref[...].astype(jnp.float32)).astype(jnp.bfloat16)
-    to_next_ref[cut:, :] = ahead[cut:].astype(jnp.bfloat16)
-    to_last_ref[:cut, :] = behind[:cut].astype(jnp.bfloat16)
-    to_last_ref[cut:, :] = (behind[cut:] + backward_ref[...].astype(jnp.float32)).astype(jnp.bfloat16)
-
-
-def home_kernel(place_ref, tiles_ref, audio_b_ref, got_ref, home_ref):
-    home_ref[...] = summed(place_ref, tiles_ref, audio_b_ref, got_ref, 0)
+    to_next_ref[:cut, :] = (ahead[:cut] + forward).astype(jnp.bfloat16)
+    to_next_ref[cut:, :] = ahead[cut : rows - EARLY].astype(jnp.bfloat16)
+    to_last_ref[: cut - EARLY, :] = behind[EARLY:cut].astype(jnp.bfloat16)
+    to_last_ref[cut - EARLY :, :] = (behind[cut:] + backward).astype(jnp.bfloat16)
+
+
+def home_kernel(
+    place_ref, tiles_ref, audio_b_ref, got_ref, forward_ref, backward_ref, home_ref
+):
+    home = summed(place_ref, tiles_ref, audio_b_ref, got_ref, 0)
+    rows = home.shape[0]
+    forward = forward_ref[rows // 2 :, :].astype(jnp.float32)
+    backward = backward_ref[rows // 2 :, :].astype(jnp.float32)
+    home_ref[:EARLY, :] = home[:EARLY] + backward
+    home_ref[EARLY : rows - EARLY, :] = home[EARLY : rows - EARLY]
+    home_ref[rows - EARLY :, :] = home[rows - EARLY :] + forward
 
 
 def fold_kernel(parts_ref, copies_ref):
@@ -205,23 +231,36 @@
         copies_ref[n] = total
 
 
-def place_kernel(place_ref, half_ref, *refs):
-    refs[-1][...] = half_ref[...].astype(jnp.float32)
+def place_kernel(side, place_ref, half_ref, *refs):
+    whole_ref, buffer, sems = refs[-3:]
+    pieces = sems.shape[0]
+    rows = half_ref.shape[0]
+    step = rows // pieces
+    first = lax.rem(place_ref[1] + side, 2) * rows
+    moves = []
+    for n in range(pieces):
+        part = pl.ds(n * step, step)
+        buffer[part, :] = half_ref[part, :].astype(jnp.float32)
+        to = pl.ds(pl.multiple_of(first + n * step, step), step)
+        moves.append(pltpu.make_async_copy(buffer.at[part, :], whole_ref.at[to, :], sems.at[n]))
+        moves[-1].start()
+    for move in moves:
+        move.wait()
 
 
 def placed(place, half, side, whole):
     rows, width = half.shape
     given = [] if whole is None else [whole]
     return pl.pallas_call(
-        place_kernel,
+        functools.partial(place_kernel, side),
         out_shape=shape((2 * rows, width), jnp.float32),
-        grid_spec=pltpu.PrefetchScalarGridSpec(
-            num_scalar_prefetch=1,
-            grid=(1,),
-            in_specs=[pl.BlockSpec((rows, width), lambda i, at: (0, 0))]
-            + [pl.BlockSpec(memory_space=pl.ANY)] * len(given),
-            out_specs=pl.BlockSpec((rows, width), lambda i, at: ((at[1] + side) % 2, 0)),
-        ),
+        in_specs=[
+            pl.BlockSpec(memory_space=pltpu.SMEM),
+            pl.BlockSpec(memory_space=pltpu.VMEM),
+            *[pl.BlockSpec(memory_space=pl.ANY)] * len(given),
+        ],
+        out_specs=pl.BlockSpec(memory_space=pl.ANY),
+        scratch_shapes=[pltpu.VMEM((rows, width), jnp.float32), pltpu.SemaphoreType.DMA((4,))],
         input_output_aliases={2: 0} if given else {},
         compiler_params=pltpu.CompilerParams(vmem_limit_bytes=8 * MIB),
         cost_estimate=pl.CostEstimate(
@@ -231,7 +270,12 @@
 
 
 def text_grad_kernel(text_ref, home_ref, next_ref, last_ref, grad_ref):
-    grad = home_ref[...] + (next_ref[...].astype(jnp.float32) + last_ref[...].astype(jnp.float32))
+    rows, late = home_ref.shape[0], next_ref.shape[0]
+    home = home_ref[...]
+    ahead, behind = next_ref[...].astype(jnp.float32), last_ref[...].astype(jnp.float32)
+    middle = home[rows - late : late] + ahead[rows - late :] + behind[: 2 * late - rows]
+    first, final = home[: rows - late] + ahead[: rows - late], home[late:] + behind[2 * late - rows :]
+    grad = jnp.concatenate([first, middle, final])
     text = text_ref[...].astype(jnp.float32)
     scale = lax.rsqrt(jnp.sum(text * text, axis=1, keepdims=True) + EPS)
     text = text * scale
@@ -250,17 +294,19 @@
     half = channels // 2
     block = shape((rows, width), f32)
     block_b = shape((rows, width), bf16)
-    cut_b = shape((rows // 2, width), bf16)
+    early_b = shape((rows // 2 + EARLY, width), bf16)
+    late_b = shape((rows - EARLY, width), bf16)
 
     (sent,) = call(text_kernel, (shape((rows + TAIL, width), bf16),), text_raw)
     own = lax.all_gather(sent.astype(jnp.float16), "zh", axis=0, tiled=True).astype(bf16)
     own, audio_features = lax.optimization_barrier((own, audio_features))
     other = shifted(own, "core", 1)
-    audio, audio_b, scale = call(
+    audio, audio_b, scale, own_scores = call(
         audio_kernel,
-        (block, block_b, shape((rows, 1), f32)),
+        (block, block_b, shape((rows, 1), f32), shape((rows, chips * rows), f32)),
         audio_features,
         proj_weight,
+        own,
         flops=2 * rows * channels * width,
     )
     proj_grad, tiles, sent = call(
@@ -274,7 +320,8 @@
         positive.reshape(rows, 1),
         own,
         other,
-        scratch=[pltpu.VMEM((rows, blocks * rows), f32)],
+        own_scores,
+        scratch=[pltpu.VMEM((rows, chips * rows), f32)],
         flops=3 * pair_flops,
         limit=20,
     )
@@ -293,7 +340,7 @@
     parts, got = lax.optimization_barrier((parts, got))
     parts = exchanged(parts, PLANE)
     forward, backward = call(
-        text_sums_kernel, (cut_b, cut_b), place, tiles, audio_b, got, flops=pair_flops // 4
+        text_sums_kernel, (early_b, early_b), place, tiles, audio_b, got, flops=pair_flops // 4
     )
     forward = shifted(forward, "zh", 1)
     backward = shifted(backward, "zh", -1)
@@ -302,7 +349,7 @@
     parts = exchanged(parts, COLUMN)
     to_next, to_last = call(
         relay_kernel,
-        (block_b, block_b),
+        (late_b, late_b),
         place,
         tiles,
         audio_b,
@@ -324,8 +371,10 @@
         tiles,
         audio_b,
         got,
+        forward,
+        backward,
         light=True,
-        far=(1, 2, 3),
+        far=(1, 2, 3, 4, 5),
         far_outs=True,
     )
     weight_half, arrived, home = lax.optimization_barrier((weight_half, arrived, home))

time: 124 us -> 124 us (level)
  starting transfers between devices: 49.2 us -> 51.3 us
  local copies, waits for them, and re-layouts: 2.39 us -> 1.14 us
    ppermute x7, starting transfers between devices: 26.1 us -> 27.8 us  [shifted(): lax.ppermute(block, axis, [(i, (i + distance) % count) for i in range(cou...]
    unnamed x32 -> x28, local copies, waits for them, and re-layouts: 2.26 us -> 1.01 us
  transfers between devices with their start and end apart: 10 -> 10, of which waited for: 7 -> 6; matrix products, arithmetic and copies ran while one was open for 0% -> 0% of each run, Pallas kernels for 11% -> 11%
where the time goes in v8:
time: 124 us; the launch traced here: 123 us
  starting transfers between devices  51.3 us (41%)
  blocking collectives  28.3 us (23%)
  Pallas kernels  21.8 us (18%)
  waiting for transfers between devices  19.6 us (16%)
    all_gather x1, blocking collectives, body(): lax.all_gather(sent.astype(jnp.float16), 'zh', axis=0, tiled=True)  28.3 us
    ppermute x7, starting transfers between devices, shifted(): lax.ppermute(block, axis, [(i, (i + distance) % count) for i in range(cou...  27.8 us
    all_to_all x3, starting transfers between devices, exchanged(): return lax.all_to_all(block, axes, split_axis=0, concat_axis=0, tiled=True)  23.5 us
    pallas_call x12, Pallas kernels, call(): pl.pallas_call(staging, out_shape=[pltpu.HBM(a.shape, a.dtype) for a in o...  18.7 us
    ppermute x7, waiting for transfers between devices, shifted(): lax.ppermute(block, axis, [(i, (i + distance) % count) for i in range(cou...  15.3 us
    all_to_all x3, waiting for transfers between devices, exchanged(): return lax.all_to_all(block, axes, split_axis=0, concat_axis=0, tiled=True)  4.28 us
    pallas_call x2, Pallas kernels, placed(): pl.pallas_call(functools.partial(place_kernel, side), out_shape=shape((2...  3.11 us
  transfers between devices with their start and end apart: 10, of which 6 were waited for; matrix products, arithmetic and copies ran while one was open for 0% of the time, Pallas kernels for 11%

profile of v8, /device:TPU:1, one launch (start us, length us, event | category | flops | bytes accessed | tf_op | source)
XLA Modules:
  0.0 123.4 jit_solution(10709279187560772091)
XLA Ops:
  0.6 0.9 copy-done.7
  1.6 0.3 shard_map.67
  2.0 28.3 %all-gather.1 = f16[1088,512]{1,0:T(8,128)(2,1)S(1)} all-gather(f16[272,512]{1,0:T(8,128)(2,1)S(1)} %convert_element_type.6), channel_id=1, replica_groups=mesh['zh'=4,'core'=2,'zl'=2,'x'=4,'y'=8] {'zh'}, dimensions={0}, use_global_device_ids=true | all-gather | bytes 1392640 | tf_op jit(solution)/shard_map/all_gather | solution.py:301
  30.5 6.1 %collective-permute-start = (bf16[1088,512]{1,0:T(8,128)(2,1)S(1)}, bf16[1088,512]{1,0:T(8,128)(2,1)}, u32[]{:S(2)}, u32[]{:S(2)}) collective-permute-start(bf16[1088,512]{1,0:T(8,128)(2,1)S(1)} %convert_element_type.7.refs_2_.refs_6_), channel_id=1, source_target_pairs={{0,64},{64,0},{1,65},{65,1},{2,66},{66,2},{3,67},{67,3},{4,68},{68... | collective-permute-start | bytes 3342344 | tf_op jit(solution)/shard_map/ppermute | solution.py:23
  36.7 0.9 shard_map.68
  37.7 1.3 %collective-permute-done.refs_7_ = bf16[1088,512]{1,0:T(8,128)(2,1)} collective-permute-done((bf16[1088,512]{1,0:T(8,128)(2,1)S(1)}, bf16[1088,512]{1,0:T(8,128)(2,1)}, u32[]{:S(2)}, u32[]{:S(2)}) %collective-permute-start) | collective-permute-done | bytes 1114144 | tf_op jit(solution)/shard_map/ppermute | solution.py:23
  39.0 3.8 %shard_map.69 = (bf16[256,512]{1,0:T(8,128)(2,1)S(1)}, bf16[8,256,256]{2,1,0:T(8,128)(2,1)S(1)}, bf16[1536,512]{1,0:T(8,128)(2,1)S(1)}) custom-call(s32[2]{0:T(128)S(1)} %pad_add_fusion.refs_0_.place_ref, f32[256,512]{1,0:T(8,128)S(1)} %get-tuple-element.34.refs_1_, bf16[256,512]{1,0:T(8,128)(2,1)S(1)} %get-tuple-element.35.refs_2_, ...), custom_call_target="tpu_custom_call" | custom-call | flops 1610612736 | bytes 7473160 | tf_op jit(solution)/shard_map/pallas_call | solution.py:73
  42.8 2.3 %collective-permute-start.1 = (bf16[1536,512]{1,0:T(8,128)(2,1)S(1)}, bf16[1536,512]{1,0:T(8,128)(2,1)S(1)}, u32[]{:S(2)}, u32[]{:S(2)}) collective-permute-start(bf16[1536,512]{1,0:T(8,128)(2,1)S(1)} %get-tuple-element.38), channel_id=1, source_target_pairs={{0,64},{64,0},{1,65},{65,1},{2,66},{66,2},{3,67},{67,3},{4,68},{68... | collective-permute-start | bytes 4718600 | tf_op jit(solution)/shard_map/ppermute | solution.py:23
  45.1 1.3 %shard_map.71 = bf16[256,1024]{1,0:T(8,128)(2,1)} custom-call(bf16[256,512]{1,0:T(8,128)(2,1)S(1)} %get-tuple-element.39.refs_2_.refs_0_, bf16[1024,512]{1,0:T(8,128)(2,1)S(1)} %copy-done.3), custom_call_target="tpu_custom_call" | custom-call | tf_op jit(solution)/shard_map/pallas_call | solution.py:73
  46.4 0.9 shard_map.70.refs_0_
  47.3 0.9 collective-permute-done.1.refs_1_.refs_3_
  48.1 1.0 shard_map.72
  49.2 9.7 %all-to-all-start = ((bf16[32,16,512]{2,1,0:T(8,128)(2,1)}), bf16[32,16,512]{2,1,0:T(8,128)(2,1)S(1)}, u32[]{:S(2)}, u32[]{:S(2)}) async-start(bf16[32,16,512]{2,1,0:T(8,128)(2,1)} %shard_map.72), calls=%async_computation | async-start | bytes 1048576 | tf_op jit(solution)/shard_map/all_to_all | solution.py:27
  58.9 0.9 shard_map.73
  59.8 3.0 %collective-permute-start.2 = (bf16[192,512]{1,0:T(8,128)(2,1)S(1)}, bf16[192,512]{1,0:T(8,128)(2,1)S(1)}, u32[]{:S(2)}, u32[]{:S(2)}) collective-permute-start(bf16[192,512]{1,0:T(8,128)(2,1)S(1)} %get-tuple-element.45), channel_id=1, source_target_pairs={{0,128},{128,256},{256,384},{384,0},{1,129},{129,257},{257,385},{3... | collective-permute-start | bytes 589832 | tf_op jit(solution)/shard_map/ppermute | solution.py:23
  62.8 4.4 %collective-permute-start.3 = (bf16[192,512]{1,0:T(8,128)(2,1)S(1)}, bf16[192,512]{1,0:T(8,128)(2,1)S(1)}, u32[]{:S(2)}, u32[]{:S(2)}) collective-permute-start(bf16[192,512]{1,0:T(8,128)(2,1)S(1)} %get-tuple-element.46), channel_id=1, source_target_pairs={{0,384},{128,0},{256,128},{384,256},{1,385},{129,1},{257,129},{385... | collective-permute-start | bytes 589832 | tf_op jit(solution)/shard_map/ppermute | solution.py:23
  67.2 5.7 %collective-permute-done.2.refs_4_ = bf16[192,512]{1,0:T(8,128)(2,1)S(1)} collective-permute-done((bf16[192,512]{1,0:T(8,128)(2,1)S(1)}, bf16[192,512]{1,0:T(8,128)(2,1)S(1)}, u32[]{:S(2)}, u32[]{:S(2)}) %collective-permute-start.2) | collective-permute-done | bytes 196640 | tf_op jit(solution)/shard_map/ppermute | solution.py:23
  72.9 3.5 %collective-permute-done.3.refs_5_ = bf16[192,512]{1,0:T(8,128)(2,1)S(1)} collective-permute-done((bf16[192,512]{1,0:T(8,128)(2,1)S(1)}, bf16[192,512]{1,0:T(8,128)(2,1)S(1)}, u32[]{:S(2)}, u32[]{:S(2)}) %collective-permute-start.3) | collective-permute-done | bytes 196640 | tf_op jit(solution)/shard_map/ppermute | solution.py:23
  76.4 0.7 shard_map.74
  77.2 4.6 %all-to-all-start.1 = ((bf16[8,16,512]{2,1,0:T(8,128)(2,1)}), bf16[8,16,512]{2,1,0:T(8,128)(2,1)S(1)}, u32[]{:S(2)}, u32[]{:S(2)}) async-start(bf16[8,16,512]{2,1,0:T(8,128)(2,1)} %shard_map.74), calls=%async_computation.1 | async-start | bytes 262144 | tf_op jit(solution)/shard_map/all_to_all | solution.py:27
  81.8 3.5 %shard_map.76 = (bf16[192,512]{1,0:T(8,128)(2,1)}, bf16[192,512]{1,0:T(8,128)(2,1)}) custom-call(s32[2]{0:T(128)S(1)} %pad_add_fusion.refs_0_.place_ref, bf16[8,256,256]{2,1,0:T(8,128)(2,1)} %copy-done.1, bf16[256,512]{1,0:T(8,128)(2,1)} %copy-done.4, bf16[1536,512]{1,0:T(8,128)(2,1)} %copy-done, bf16[192,512]{1,0:T(8,128)(2,1)} %copy-done.9, ...), custom_call_target="tpu_custom_call" | custom-call | tf_op jit(solution)/shard_map/pallas_call | solution.py:73
  85.3 4.3 %all-to-all-done.1.refs_0_ = bf16[8,16,512]{2,1,0:T(8,128)(2,1)S(1)} async-done(((bf16[8,16,512]{2,1,0:T(8,128)(2,1)}), bf16[8,16,512]{2,1,0:T(8,128)(2,1)S(1)}, u32[]{:S(2)}, u32[]{:S(2)}) %all-to-all-start.1) | async-done | bytes 131104 | tf_op jit(solution)/shard_map/all_to_all | solution.py:27
  89.6 0.9 shard_map.75
  90.4 9.2 %all-to-all-start.2 = ((bf16[32,16,512]{2,1,0:T(8,128)(2,1)}), bf16[32,16,512]{2,1,0:T(8,128)(2,1)S(1)}, u32[]{:S(2)}, u32[]{:S(2)}) async-start(bf16[32,16,512]{2,1,0:T(8,128)(2,1)} %shard_map.75), calls=%async_computation.2 | async-start | bytes 1048576 | tf_op jit(solution)/shard_map/all_to_all | solution.py:27
  99.7 1.9 %collective-permute-start.4 = (bf16[192,512]{1,0:T(8,128)(2,1)S(1)}, bf16[192,512]{1,0:T(8,128)(2,1)S(1)}, u32[]{:S(2)}, u32[]{:S(2)}) collective-permute-start(bf16[192,512]{1,0:T(8,128)(2,1)S(1)} %copy-done.13), channel_id=1, source_target_pairs={{0,128},{128,256},{256,384},{384,0},{1,129},{129,257},{257,385},{3... | collective-permute-start | bytes 589832 | tf_op jit(solution)/shard_map/ppermute | solution.py:23
  101.6 5.5 %collective-permute-start.5 = (bf16[192,512]{1,0:T(8,128)(2,1)S(1)}, bf16[192,512]{1,0:T(8,128)(2,1)S(1)}, u32[]{:S(2)}, u32[]{:S(2)}) collective-permute-start(bf16[192,512]{1,0:T(8,128)(2,1)S(1)} %copy-done.12), channel_id=1, source_target_pairs={{0,384},{128,0},{256,128},{384,256},{1,385},{129,1},{257,129},{385... | collective-permute-start | bytes 589832 | tf_op jit(solution)/shard_map/ppermute | solution.py:23
  107.1 3.5 %shard_map.77.refs_1_ = f32[256,512]{1,0:T(8,128)} custom-call(s32[2]{0:T(128)S(1)} %pad_add_fusion.refs_0_.place_ref, bf16[8,256,256]{2,1,0:T(8,128)(2,1)} %copy-done.1, bf16[256,512]{1,0:T(8,128)(2,1)} %copy-done.4, bf16[1536,512]{1,0:T(8,128)(2,1)} %copy-done, bf16[192,512]{1,0:T(8,128)(2,1)} %copy-done.9, bf16[192,512]{1,0:T(8,128)(2,1)} %copy-done.10), custom_call_target="tpu_custom_call" | custom-call | tf_op jit(solution)/shard_map/pallas_call | solution.py:73
  110.7 3.9 %collective-permute-done.5.refs_3_ = bf16[192,512]{1,0:T(8,128)(2,1)S(1)} collective-permute-done((bf16[192,512]{1,0:T(8,128)(2,1)S(1)}, bf16[192,512]{1,0:T(8,128)(2,1)S(1)}, u32[]{:S(2)}, u32[]{:S(2)}) %collective-permute-start.5) | collective-permute-done | bytes 196640 | tf_op jit(solution)/shard_map/ppermute | solution.py:23
  114.6 4.7 %collective-permute-start.6 = (bf16[512,512]{1,0:T(8,128)(2,1)S(1)}, bf16[512,512]{1,0:T(8,128)(2,1)S(1)}, u32[]{:S(2)}, u32[]{:S(2)}) collective-permute-start(bf16[512,512]{1,0:T(8,128)(2,1)S(1)} %bitcast.4), channel_id=1, source_target_pairs={{0,64},{64,0},{1,65},{65,1},{2,66},{66,2},{3,67},{67,3},{4,68},{68... | collective-permute-start | bytes 1572872 | tf_op jit(solution)/shard_map/ppermute | solution.py:23
  119.3 1.6 %shard_map.78.refs_0_ = f32[1024,512]{1,0:T(8,128)} custom-call(s32[2]{0:T(128)S(1)} %pad_add_fusion.refs_0_.place_ref, bf16[512,512]{1,0:T(8,128)(2,1)S(1)} %bitcast.5), custom_call_target="tpu_custom_call" | custom-call | bytes 1572864 | tf_op jit(solution)/shard_map/pallas_call | solution.py:254
  120.9 1.0 shard_map.80
  121.9 1.6 %shard_map.79 = f32[1024,512]{1,0:T(8,128)} custom-call(s32[2]{0:T(128)S(1)} %pad_add_fusion.refs_0_.place_ref, bf16[512,512]{1,0:T(8,128)(2,1)S(1)} %collective-permute-done.6.half_ref, f32[1024,512]{1,0:T(8,128)} %shard_map.78.refs_0_), custom_call_target="tpu_custom_call", output_to_operand_aliasing={{}: (2, {})} | custom-call | bytes 1572864 | tf_op jit(solution)/shard_map/pallas_call | solution.py:254
  (35 shorter events, 0.5 us)
Async XLA Ops:
  0.6 1.0 copy-start.7
  2.0 34.6 %copy-start.11 = (s32[256]{0:T(256)S(1)}, s32[256]{0:T(256)}, u32[]{:S(2)}) copy-start(s32[256]{0:T(256)} %param.7) | copy-start | bytes 3076
  2.0 34.7 %copy-start.2 = (bf16[1024,512]{1,0:T(8,128)(2,1)S(1)}, bf16[1024,512]{1,0:T(8,128)(2,1)}, u32[]{:S(2)}) copy-start(bf16[1024,512]{1,0:T(8,128)(2,1)} %refs_1_.4) | copy-start | bytes 3145732
  2.0 34.7 %copy-start.6 = (bf16[256,1024]{1,0:T(8,128)(2,1)S(1)}, bf16[256,1024]{1,0:T(8,128)(2,1)}, u32[]{:S(2)}) copy-start(bf16[256,1024]{1,0:T(8,128)(2,1)} %refs_1_.3) | copy-start | bytes 1572868
  30.5 8.6 %collective-permute-start = (bf16[1088,512]{1,0:T(8,128)(2,1)S(1)}, bf16[1088,512]{1,0:T(8,128)(2,1)}, u32[]{:S(2)}, u32[]{:S(2)}) collective-permute-start(bf16[1088,512]{1,0:T(8,128)(2,1)S(1)} %convert_element_type.7.refs_2_.refs_6_), channel_id=1, source_target_pairs={{0,64},{64,0},{1,65},{65,1},{2,66},{66,2},{3,67},{67,3},{4,68},{68... | collective-permute-start | bytes 3342344 | tf_op jit(solution)/shard_map/ppermute | solution.py:23
  37.6 21.2 %copy-start.4 = (bf16[256,512]{1,0:T(8,128)(2,1)}, bf16[256,512]{1,0:T(8,128)(2,1)S(1)}, u32[]{:S(2)}) copy-start(bf16[256,512]{1,0:T(8,128)(2,1)S(1)} %get-tuple-element.35.refs_2_) | copy-start | bytes 786436
  39.0 6.1 %copy-start.3 = (bf16[1024,512]{1,0:T(8,128)(2,1)S(1)}, bf16[1024,512]{1,0:T(8,128)(2,1)}, u32[]{:S(2)}) copy-start(bf16[1024,512]{1,0:T(8,128)(2,1)} %refs_1_.4) | copy-start | bytes 3145732
  42.8 16.1 %copy-start.1 = (bf16[8,256,256]{2,1,0:T(8,128)(2,1)}, bf16[8,256,256]{2,1,0:T(8,128)(2,1)S(1)}, u32[]{:S(2)}) copy-start(bf16[8,256,256]{2,1,0:T(8,128)(2,1)S(1)} %get-tuple-element.55.refs_1_) | copy-start | bytes 3145732
  42.8 5.3 %collective-permute-start.1 = (bf16[1536,512]{1,0:T(8,128)(2,1)S(1)}, bf16[1536,512]{1,0:T(8,128)(2,1)S(1)}, u32[]{:S(2)}, u32[]{:S(2)}) collective-permute-start(bf16[1536,512]{1,0:T(8,128)(2,1)S(1)} %get-tuple-element.38), channel_id=1, source_target_pairs={{0,64},{64,0},{1,65},{65,1},{2,66},{66,2},{3,67},{67,3},{4,68},{68... | collective-permute-start | bytes 4718600 | tf_op jit(solution)/shard_map/ppermute | solution.py:23
  48.1 10.8 %copy-start = (bf16[1536,512]{1,0:T(8,128)(2,1)}, bf16[1536,512]{1,0:T(8,128)(2,1)S(1)}, u32[]{:S(2)}) copy-start(bf16[1536,512]{1,0:T(8,128)(2,1)S(1)} %collective-permute-done.1.refs_1_.refs_3_) | copy-start | bytes 4718596
  49.2 27.3 %all-to-all-start = ((bf16[32,16,512]{2,1,0:T(8,128)(2,1)}), bf16[32,16,512]{2,1,0:T(8,128)(2,1)S(1)}, u32[]{:S(2)}, u32[]{:S(2)}) async-start(bf16[32,16,512]{2,1,0:T(8,128)(2,1)} %shard_map.72), calls=%async_computation | async-start | bytes 1048576 | tf_op jit(solution)/shard_map/all_to_all | solution.py:27
  59.8 13.1 %collective-permute-start.2 = (bf16[192,512]{1,0:T(8,128)(2,1)S(1)}, bf16[192,512]{1,0:T(8,128)(2,1)S(1)}, u32[]{:S(2)}, u32[]{:S(2)}) collective-permute-start(bf16[192,512]{1,0:T(8,128)(2,1)S(1)} %get-tuple-element.45), channel_id=1, source_target_pairs={{0,128},{128,256},{256,384},{384,0},{1,129},{129,257},{257,385},{3... | collective-permute-start | bytes 589832 | tf_op jit(solution)/shard_map/ppermute | solution.py:23
  62.8 13.6 %collective-permute-start.3 = (bf16[192,512]{1,0:T(8,128)(2,1)S(1)}, bf16[192,512]{1,0:T(8,128)(2,1)S(1)}, u32[]{:S(2)}, u32[]{:S(2)}) collective-permute-start(bf16[192,512]{1,0:T(8,128)(2,1)S(1)} %get-tuple-element.46), channel_id=1, source_target_pairs={{0,384},{128,0},{256,128},{384,256},{1,385},{129,1},{257,129},{385... | collective-permute-start | bytes 589832 | tf_op jit(solution)/shard_map/ppermute | solution.py:23
  72.9 8.9 %copy-start.9 = (bf16[192,512]{1,0:T(8,128)(2,1)}, bf16[192,512]{1,0:T(8,128)(2,1)S(1)}, u32[]{:S(2)}) copy-start(bf16[192,512]{1,0:T(8,128)(2,1)S(1)} %collective-permute-done.2.refs_4_) | copy-start | bytes 589828
  76.4 5.4 %copy-start.10 = (bf16[192,512]{1,0:T(8,128)(2,1)}, bf16[192,512]{1,0:T(8,128)(2,1)S(1)}, u32[]{:S(2)}) copy-start(bf16[192,512]{1,0:T(8,128)(2,1)S(1)} %collective-permute-done.3.refs_5_) | copy-start | bytes 589828
  77.2 12.4 %all-to-all-start.1 = ((bf16[8,16,512]{2,1,0:T(8,128)(2,1)}), bf16[8,16,512]{2,1,0:T(8,128)(2,1)S(1)}, u32[]{:S(2)}, u32[]{:S(2)}) async-start(bf16[8,16,512]{2,1,0:T(8,128)(2,1)} %shard_map.74), calls=%async_computation.1 | async-start | bytes 262144 | tf_op jit(solution)/shard_map/all_to_all | solution.py:27
  85.3 14.4 %copy-start.13 = (bf16[192,512]{1,0:T(8,128)(2,1)S(1)}, bf16[192,512]{1,0:T(8,128)(2,1)}, u32[]{:S(2)}) copy-start(bf16[192,512]{1,0:T(8,128)(2,1)} %get-tuple-element.53) | copy-start | bytes 589828
  85.3 16.3 %copy-start.12 = (bf16[192,512]{1,0:T(8,128)(2,1)S(1)}, bf16[192,512]{1,0:T(8,128)(2,1)}, u32[]{:S(2)}) copy-start(bf16[192,512]{1,0:T(8,128)(2,1)} %get-tuple-element.54) | copy-start | bytes 589828
  90.4 24.2 %all-to-all-start.2 = ((bf16[32,16,512]{2,1,0:T(8,128)(2,1)}), bf16[32,16,512]{2,1,0:T(8,128)(2,1)S(1)}, u32[]{:S(2)}, u32[]{:S(2)}) async-start(bf16[32,16,512]{2,1,0:T(8,128)(2,1)} %shard_map.75), calls=%async_computation.2 | async-start | bytes 1048576 | tf_op jit(solution)/shard_map/all_to_all | solution.py:27
  99.7 11.0 %collective-permute-start.4 = (bf16[192,512]{1,0:T(8,128)(2,1)S(1)}, bf16[192,512]{1,0:T(8,128)(2,1)S(1)}, u32[]{:S(2)}, u32[]{:S(2)}) collective-permute-start(bf16[192,512]{1,0:T(8,128)(2,1)S(1)} %copy-done.13), channel_id=1, source_target_pairs={{0,128},{128,256},{256,384},{384,0},{1,129},{129,257},{257,385},{3... | collective-permute-start | bytes 589832 | tf_op jit(solution)/shard_map/ppermute | solution.py:23
  101.6 13.0 %collective-permute-start.5 = (bf16[192,512]{1,0:T(8,128)(2,1)S(1)}, bf16[192,512]{1,0:T(8,128)(2,1)S(1)}, u32[]{:S(2)}, u32[]{:S(2)}) collective-permute-start(bf16[192,512]{1,0:T(8,128)(2,1)S(1)} %copy-done.12), channel_id=1, source_target_pairs={{0,384},{128,0},{256,128},{384,256},{1,385},{129,1},{257,129},{385... | collective-permute-start | bytes 589832 | tf_op jit(solution)/shard_map/ppermute | solution.py:23
  110.6 10.2 %copy-start.5 = (f32[256,512]{1,0:T(8,128)S(1)}, f32[256,512]{1,0:T(8,128)}, u32[]{:S(2)}) copy-start(f32[256,512]{1,0:T(8,128)} %shard_map.77.refs_1_) | copy-start | bytes 1572868
  110.7 10.2 %copy-start.8 = (bf16[256,512]{1,0:T(8,128)(2,1)S(1)}, bf16[256,512]{1,0:T(8,128)(2,1)}, u32[]{:S(2)}) copy-start(bf16[256,512]{1,0:T(8,128)(2,1)} %refs_0_.4) | copy-start | bytes 786436
  114.6 7.3 %collective-permute-start.6 = (bf16[512,512]{1,0:T(8,128)(2,1)S(1)}, bf16[512,512]{1,0:T(8,128)(2,1)S(1)}, u32[]{:S(2)}, u32[]{:S(2)}) collective-permute-start(bf16[512,512]{1,0:T(8,128)(2,1)S(1)} %bitcast.4), channel_id=1, source_target_pairs={{0,64},{64,0},{1,65},{65,1},{2,66},{66,2},{3,67},{67,3},{4,68},{68... | collective-permute-start | bytes 1572872 | tf_op jit(solution)/shard_map/ppermute | solution.py:23

commit v9 on v8

--- a/solution.py
+++ b/solution.py
@@ -187,7 +187,7 @@
     return part + got_ref[pl.ds(start, rows), :].astype(jnp.float32)
 
 
-def text_sums_kernel(place_ref, tiles_ref, audio_b_ref, got_ref, forward_ref, backward_ref):
+def early_kernel(place_ref, tiles_ref, audio_b_ref, got_ref, forward_ref, backward_ref):
     refs = (place_ref, tiles_ref, audio_b_ref, got_ref)
     rows = tiles_ref.shape[2]
     cut = rows // 2
@@ -198,31 +198,23 @@
     backward_ref[cut:, :] = summed(*refs, 3)[:EARLY].astype(jnp.bfloat16)
 
 
-def relay_kernel(
-    place_ref, tiles_ref, audio_b_ref, got_ref, forward_ref, backward_ref, to_next_ref, to_last_ref
-):
+def late_kernel(place_ref, tiles_ref, audio_b_ref, got_ref, ahead_ref, behind_ref, home_ref):
     refs = (place_ref, tiles_ref, audio_b_ref, got_ref)
     rows = tiles_ref.shape[2]
-    cut = rows // 2
+    ahead_ref[...] = summed(*refs, 1)[: rows - EARLY]
+    behind_ref[...] = summed(*refs, 3)[EARLY:]
+    home_ref[...] = summed(*refs, 0)
+
+
+def relay_kernel(ahead_ref, behind_ref, forward_ref, backward_ref, to_next_ref, to_last_ref):
+    late = ahead_ref.shape[0]
+    cut = (late + EARLY) // 2
     forward = forward_ref[:cut, :].astype(jnp.float32)
     backward = backward_ref[:cut, :].astype(jnp.float32)
-    ahead, behind = summed(*refs, 1), summed(*refs, 3)
-    to_next_ref[:cut, :] = (ahead[:cut] + forward).astype(jnp.bfloat16)
-    to_next_ref[cut:, :] = ahead[cut : rows - EARLY].astype(jnp.bfloat16)
-    to_last_ref[: cut - EARLY, :] = behind[EARLY:cut].astype(jnp.bfloat16)
-    to_last_ref[cut - EARLY :, :] = (behind[cut:] + backward).astype(jnp.bfloat16)
-
-
-def home_kernel(
-    place_ref, tiles_ref, audio_b_ref, got_ref, forward_ref, backward_ref, home_ref
-):
-    home = summed(place_ref, tiles_ref, audio_b_ref, got_ref, 0)
-    rows = home.shape[0]
-    forward = forward_ref[rows // 2 :, :].astype(jnp.float32)
-    backward = backward_ref[rows // 2 :, :].astype(jnp.float32)
-    home_ref[:EARLY, :] = home[:EARLY] + backward
-    home_ref[EARLY : rows - EARLY, :] = home[EARLY : rows - EARLY]
-    home_ref[rows - EARLY :, :] = home[rows - EARLY :] + forward
+    to_next_ref[:cut, :] = (ahead_ref[:cut, :] + forward).astype(jnp.bfloat16)
+    to_next_ref[cut:, :] = ahead_ref[cut:, :].astype(jnp.bfloat16)
+    to_last_ref[: late - cut, :] = behind_ref[: late - cut, :].astype(jnp.bfloat16)
+    to_last_ref[late - cut :, :] = (behind_ref[late - cut :, :] + backward).astype(jnp.bfloat16)
 
 
 def fold_kernel(parts_ref, copies_ref):
@@ -269,12 +261,17 @@
     )(place, half, *given)
 
 
-def text_grad_kernel(text_ref, home_ref, next_ref, last_ref, grad_ref):
+def text_grad_kernel(
+    text_ref, home_ref, forward_ref, backward_ref, next_ref, last_ref, grad_ref
+):
     rows, late = home_ref.shape[0], next_ref.shape[0]
     home = home_ref[...]
+    forward = forward_ref[rows // 2 :, :].astype(jnp.float32)
+    backward = backward_ref[rows // 2 :, :].astype(jnp.float32)
     ahead, behind = next_ref[...].astype(jnp.float32), last_ref[...].astype(jnp.float32)
-    middle = home[rows - late : late] + ahead[rows - late :] + behind[: 2 * late - rows]
-    first, final = home[: rows - late] + ahead[: rows - late], home[late:] + behind[2 * late - rows :]
+    first = home[:EARLY] + ahead[:EARLY] + backward
+    middle = home[EARLY:late] + ahead[EARLY:] + behind[: late - EARLY]
+    final = home[late:] + forward + behind[late - EARLY :]
     grad = jnp.concatenate([first, middle, final])
     text = text_ref[...].astype(jnp.float32)
     scale = lax.rsqrt(jnp.sum(text * text, axis=1, keepdims=True) + EPS)
@@ -295,7 +292,7 @@
     block = shape((rows, width), f32)
     block_b = shape((rows, width), bf16)
     early_b = shape((rows // 2 + EARLY, width), bf16)
-    late_b = shape((rows - EARLY, width), bf16)
+    late, late_b = (shape((rows - EARLY, width), dtype) for dtype in (f32, bf16))
 
     (sent,) = call(text_kernel, (shape((rows + TAIL, width), bf16),), text_raw)
     own = lax.all_gather(sent.astype(jnp.float16), "zh", axis=0, tiled=True).astype(bf16)
@@ -340,48 +337,47 @@
     parts, got = lax.optimization_barrier((parts, got))
     parts = exchanged(parts, PLANE)
     forward, backward = call(
-        text_sums_kernel, (early_b, early_b), place, tiles, audio_b, got, flops=pair_flops // 4
+        early_kernel, (early_b, early_b), place, tiles, audio_b, got, flops=pair_flops // 4
     )
     forward = shifted(forward, "zh", 1)
     backward = shifted(backward, "zh", -1)
-    parts, forward, backward = lax.optimization_barrier((parts, forward, backward))
+    ahead, behind, home = call(
+        late_kernel,
+        (late, late, block),
+        place,
+        tiles,
+        audio_b,
+        got,
+        flops=pair_flops,
+        far_outs=True,
+    )
+    parts, forward, backward, ahead, behind, home = lax.optimization_barrier(
+        (parts, forward, backward, ahead, behind, home)
+    )
     (parts,) = call(fold_kernel, (shape((column, part, width), bf16),), parts, far_outs=True)
     parts = exchanged(parts, COLUMN)
     to_next, to_last = call(
         relay_kernel,
         (late_b, late_b),
-        place,
-        tiles,
-        audio_b,
-        got,
+        ahead,
+        behind,
         forward,
         backward,
         light=True,
-        far=(1, 2, 3, 4, 5),
+        far=(0, 1, 2, 3),
         far_outs=True,
     )
     (parts,) = call(fold_kernel, (shape((plane, part, width), bf16),), parts, far_outs=True)
-    parts, to_next, to_last, tiles = lax.optimization_barrier((parts, to_next, to_last, tiles))
+    parts, to_next, to_last = lax.optimization_barrier((parts, to_next, to_last))
     weight_half = exchanged(parts, PLANE).reshape(half, width)
     arrived = [shifted(to_next, "zh", 1), shifted(to_last, "zh", -1)]
-    (home,) = call(
-        home_kernel,
-        (block,),
-        place,
-        tiles,
-        audio_b,
-        got,
-        forward,
-        backward,
-        light=True,
-        far=(1, 2, 3, 4, 5),
-        far_outs=True,
-    )
-    weight_half, arrived, home = lax.optimization_barrier((weight_half, arrived, home))
+    weight_half, arrived = lax.optimization_barrier((weight_half, arrived))
     there = shifted(weight_half, "core", 1)
     grad_weight = placed(place, weight_half, 0, None)
     grad_weight = placed(place, there, 1, grad_weight)
-    (grad_text,) = call(text_grad_kernel, (block,), text_raw, home, *arrived)
+    (grad_text,) = call(
+        text_grad_kernel, (block,), text_raw, home, forward, backward, *arrived, far=(1, 2, 3)
+    )
     return (grad_weight, grad_features, grad_text)
 
 

time: 124 us -> 126 us (1.016)
  waiting for transfers between devices: 19.6 us -> 22 us
  Pallas kernels: 21.8 us -> 19.8 us
    pallas_call x12, Pallas kernels: 18.7 us -> 16.7 us  [call(): pl.pallas_call(staging, out_shape=[pltpu.HBM(a.shape, a.dtype) for a in o...]
    all_to_all x3, waiting for transfers between devices: 4.28 us -> 5.71 us  [exchanged(): return lax.all_to_all(block, axes, split_axis=0, concat_axis=0, tiled=True)]
  transfers between devices with their start and end apart: 10 -> 10, of which waited for: 6 -> 7; matrix products, arithmetic and copies ran while one was open for 0% -> 0% of each run, Pallas kernels for 11% -> 9%
where the time goes in v9:
time: 126 us; the launch traced here: 125 us
  starting transfers between devices  51.4 us (41%)
  blocking collectives  28.3 us (22%)
  waiting for transfers between devices  22 us (17%)
  Pallas kernels  19.8 us (16%)
  local copies, waits for them, and re-layouts  1.79 us (1%)
    all_gather x1, blocking collectives, body(): lax.all_gather(sent.astype(jnp.float16), 'zh', axis=0, tiled=True)  28.3 us
    ppermute x7, starting transfers between devices, shifted(): lax.ppermute(block, axis, [(i, (i + distance) % count) for i in range(cou...  27.9 us
    all_to_all x3, starting transfers between devices, exchanged(): return lax.all_to_all(block, axes, split_axis=0, concat_axis=0, tiled=True)  23.5 us
    pallas_call x12, Pallas kernels, call(): pl.pallas_call(staging, out_shape=[pltpu.HBM(a.shape, a.dtype) for a in o...  16.7 us
    ppermute x7, waiting for transfers between devices, shifted(): lax.ppermute(block, axis, [(i, (i + distance) % count) for i in range(cou...  16.3 us
    all_to_all x3, waiting for transfers between devices, exchanged(): return lax.all_to_all(block, axes, split_axis=0, concat_axis=0, tiled=True)  5.71 us
    pallas_call x2, Pallas kernels, placed(): pl.pallas_call(functools.partial(place_kernel, side), out_shape=shape((2...  3.11 us
  transfers between devices with their start and end apart: 10, of which 7 were waited for; matrix products, arithmetic and copies ran while one was open for 0% of the time, Pallas kernels for 9%

profile of v9, /device:TPU:1, one launch (start us, length us, event | category | flops | bytes accessed | tf_op | source)
XLA Modules:
  0.0 124.6 jit_solution(8749575947209942504)
XLA Ops:
  0.6 0.9 copy-done.3
  2.0 28.3 %all-gather.1 = f16[1088,512]{1,0:T(8,128)(2,1)S(1)} all-gather(f16[272,512]{1,0:T(8,128)(2,1)S(1)} %convert_element_type.6), channel_id=1, replica_groups=mesh['zh'=4,'core'=2,'zl'=2,'x'=4,'y'=8] {'zh'}, dimensions={0}, use_global_device_ids=true | all-gather | bytes 1392640 | tf_op jit(solution)/shard_map/all_gather | solution.py:298
  30.5 6.1 %collective-permute-start = (bf16[1088,512]{1,0:T(8,128)(2,1)S(1)}, bf16[1088,512]{1,0:T(8,128)(2,1)}, u32[]{:S(2)}, u32[]{:S(2)}) collective-permute-start(bf16[1088,512]{1,0:T(8,128)(2,1)S(1)} %convert_element_type.7.refs_2_.refs_6_), channel_id=1, source_target_pairs={{0,64},{64,0},{1,65},{65,1},{2,66},{66,2},{3,67},{67,3},{4,68},{68... | collective-permute-start | bytes 3342344 | tf_op jit(solution)/shard_map/ppermute | solution.py:23
  36.7 0.9 shard_map.68
  37.7 1.3 %collective-permute-done.refs_7_ = bf16[1088,512]{1,0:T(8,128)(2,1)} collective-permute-done((bf16[1088,512]{1,0:T(8,128)(2,1)S(1)}, bf16[1088,512]{1,0:T(8,128)(2,1)}, u32[]{:S(2)}, u32[]{:S(2)}) %collective-permute-start) | collective-permute-done | bytes 1114144 | tf_op jit(solution)/shard_map/ppermute | solution.py:23
  39.0 3.8 %shard_map.69 = (bf16[256,512]{1,0:T(8,128)(2,1)S(1)}, bf16[8,256,256]{2,1,0:T(8,128)(2,1)S(1)}, bf16[1536,512]{1,0:T(8,128)(2,1)S(1)}) custom-call(s32[2]{0:T(128)S(1)} %pad_add_fusion.refs_0_.place_ref, f32[256,512]{1,0:T(8,128)S(1)} %get-tuple-element.38.refs_1_, bf16[256,512]{1,0:T(8,128)(2,1)S(1)} %get-tuple-element.39.refs_2_, ...), custom_call_target="tpu_custom_call" | custom-call | flops 1610612736 | bytes 7473160 | tf_op jit(solution)/shard_map/pallas_call | solution.py:73
  42.8 2.3 %collective-permute-start.1 = (bf16[1536,512]{1,0:T(8,128)(2,1)S(1)}, bf16[1536,512]{1,0:T(8,128)(2,1)S(1)}, u32[]{:S(2)}, u32[]{:S(2)}) collective-permute-start(bf16[1536,512]{1,0:T(8,128)(2,1)S(1)} %get-tuple-element.42), channel_id=1, source_target_pairs={{0,64},{64,0},{1,65},{65,1},{2,66},{66,2},{3,67},{67,3},{4,68},{68... | collective-permute-start | bytes 4718600 | tf_op jit(solution)/shard_map/ppermute | solution.py:23
  45.1 1.3 %shard_map.71 = bf16[256,1024]{1,0:T(8,128)(2,1)} custom-call(bf16[256,512]{1,0:T(8,128)(2,1)S(1)} %get-tuple-element.43.refs_2_.refs_0_, bf16[1024,512]{1,0:T(8,128)(2,1)S(1)} %copy-done.1), custom_call_target="tpu_custom_call" | custom-call | tf_op jit(solution)/shard_map/pallas_call | solution.py:73
  46.4 0.9 shard_map.70.refs_0_
  47.3 0.9 collective-permute-done.1.refs_1_.refs_3_
  48.1 0.9 shard_map.72
  49.0 9.7 %all-to-all-start = ((bf16[32,16,512]{2,1,0:T(8,128)(2,1)}), bf16[32,16,512]{2,1,0:T(8,128)(2,1)S(1)}, u32[]{:S(2)}, u32[]{:S(2)}) async-start(bf16[32,16,512]{2,1,0:T(8,128)(2,1)} %shard_map.72), calls=%async_computation | async-start | bytes 1048576 | tf_op jit(solution)/shard_map/all_to_all | solution.py:27
  58.7 0.9 shard_map.73
  59.7 3.0 %collective-permute-start.2 = (bf16[192,512]{1,0:T(8,128)(2,1)S(1)}, bf16[192,512]{1,0:T(8,128)(2,1)S(1)}, u32[]{:S(2)}, u32[]{:S(2)}) collective-permute-start(bf16[192,512]{1,0:T(8,128)(2,1)S(1)} %get-tuple-element.49), channel_id=1, source_target_pairs={{0,128},{128,256},{256,384},{384,0},{1,129},{129,257},{257,385},{3... | collective-permute-start | bytes 589832 | tf_op jit(solution)/shard_map/ppermute | solution.py:23
  62.7 4.4 %collective-permute-start.3 = (bf16[192,512]{1,0:T(8,128)(2,1)S(1)}, bf16[192,512]{1,0:T(8,128)(2,1)}, u32[]{:S(2)}, u32[]{:S(2)}) collective-permute-start(bf16[192,512]{1,0:T(8,128)(2,1)S(1)} %get-tuple-element.50), channel_id=1, source_target_pairs={{0,384},{128,0},{256,128},{384,256},{1,385},{129,1},{257,129},{385... | collective-permute-start | bytes 589832 | tf_op jit(solution)/shard_map/ppermute | solution.py:23
  67.1 1.9 %shard_map.74 = (f32[192,512]{1,0:T(8,128)}, f32[192,512]{1,0:T(8,128)}, f32[256,512]{1,0:T(8,128)}) custom-call(s32[2]{0:T(128)S(1)} %pad_add_fusion.refs_0_.place_ref, bf16[8,256,256]{2,1,0:T(8,128)(2,1)S(1)} %get-tuple-element.47.refs_1_, bf16[256,512]{1,0:T(8,128)(2,1)S(1)} %get-tuple-element.39.refs_2_, ...), custom_call_target="tpu_custom_call" | custom-call | flops 536870912 | bytes 4194312 | tf_op jit(solution)/shard_map/pallas_call | solution.py:73
  69.0 3.8 %collective-permute-done.2.refs_2_ = bf16[192,512]{1,0:T(8,128)(2,1)S(1)} collective-permute-done((bf16[192,512]{1,0:T(8,128)(2,1)S(1)}, bf16[192,512]{1,0:T(8,128)(2,1)S(1)}, u32[]{:S(2)}, u32[]{:S(2)}) %collective-permute-start.2) | collective-permute-done | bytes 196640 | tf_op jit(solution)/shard_map/ppermute | solution.py:23
  73.4 2.9 %collective-permute-done.3.refs_3_ = bf16[192,512]{1,0:T(8,128)(2,1)} collective-permute-done((bf16[192,512]{1,0:T(8,128)(2,1)S(1)}, bf16[192,512]{1,0:T(8,128)(2,1)}, u32[]{:S(2)}, u32[]{:S(2)}) %collective-permute-start.3) | collective-permute-done | bytes 196640 | tf_op jit(solution)/shard_map/ppermute | solution.py:23
  76.4 0.7 shard_map.75
  77.1 4.6 %all-to-all-start.1 = ((bf16[8,16,512]{2,1,0:T(8,128)(2,1)}), bf16[8,16,512]{2,1,0:T(8,128)(2,1)S(1)}, u32[]{:S(2)}, u32[]{:S(2)}) async-start(bf16[8,16,512]{2,1,0:T(8,128)(2,1)} %shard_map.75), calls=%async_computation.1 | async-start | bytes 262144 | tf_op jit(solution)/shard_map/all_to_all | solution.py:27
  81.7 2.0 %shard_map.77 = (bf16[192,512]{1,0:T(8,128)(2,1)}, bf16[192,512]{1,0:T(8,128)(2,1)}) custom-call(f32[192,512]{1,0:T(8,128)} %get-tuple-element.55.refs_0_, f32[192,512]{1,0:T(8,128)} %get-tuple-element.56.refs_1_, bf16[192,512]{1,0:T(8,128)(2,1)} %copy-done.5, bf16[192,512]{1,0:T(8,128)(2,1)} %collective-permute-done.3.refs_3_), custom_call_target="tpu_custom_call" | custom-call | tf_op jit(solution)/shard_map/pallas_call | solution.py:73
  83.8 5.7 %all-to-all-done.1.refs_0_ = bf16[8,16,512]{2,1,0:T(8,128)(2,1)S(1)} async-done(((bf16[8,16,512]{2,1,0:T(8,128)(2,1)}), bf16[8,16,512]{2,1,0:T(8,128)(2,1)S(1)}, u32[]{:S(2)}, u32[]{:S(2)}) %all-to-all-start.1) | async-done | bytes 131104 | tf_op jit(solution)/shard_map/all_to_all | solution.py:27
  89.5 0.9 shard_map.76
  90.4 9.2 %all-to-all-start.2 = ((bf16[32,16,512]{2,1,0:T(8,128)(2,1)}), bf16[32,16,512]{2,1,0:T(8,128)(2,1)S(1)}, u32[]{:S(2)}, u32[]{:S(2)}) async-start(bf16[32,16,512]{2,1,0:T(8,128)(2,1)} %shard_map.76), calls=%async_computation.2 | async-start | bytes 1048576 | tf_op jit(solution)/shard_map/all_to_all | solution.py:27
  99.6 2.1 %collective-permute-start.4 = (bf16[192,512]{1,0:T(8,128)(2,1)S(1)}, bf16[192,512]{1,0:T(8,128)(2,1)S(1)}, u32[]{:S(2)}, u32[]{:S(2)}) collective-permute-start(bf16[192,512]{1,0:T(8,128)(2,1)S(1)} %copy-done.8), channel_id=1, source_target_pairs={{0,128},{128,256},{256,384},{384,0},{1,129},{129,257},{257,385},{3... | collective-permute-start | bytes 589832 | tf_op jit(solution)/shard_map/ppermute | solution.py:23
  101.7 5.5 %collective-permute-start.5 = (bf16[192,512]{1,0:T(8,128)(2,1)S(1)}, bf16[192,512]{1,0:T(8,128)(2,1)S(1)}, u32[]{:S(2)}, u32[]{:S(2)}) collective-permute-start(bf16[192,512]{1,0:T(8,128)(2,1)S(1)} %copy-done.7), channel_id=1, source_target_pairs={{0,384},{128,0},{256,128},{384,256},{1,385},{129,1},{257,129},{385... | collective-permute-start | bytes 589832 | tf_op jit(solution)/shard_map/ppermute | solution.py:23
  107.2 2.3 %collective-permute-done.4.refs_4_ = bf16[192,512]{1,0:T(8,128)(2,1)S(1)} collective-permute-done((bf16[192,512]{1,0:T(8,128)(2,1)S(1)}, bf16[192,512]{1,0:T(8,128)(2,1)S(1)}, u32[]{:S(2)}, u32[]{:S(2)}) %collective-permute-start.4) | collective-permute-done | bytes 196640 | tf_op jit(solution)/shard_map/ppermute | solution.py:23
  109.5 5.0 %collective-permute-done.5.refs_5_ = bf16[192,512]{1,0:T(8,128)(2,1)S(1)} collective-permute-done((bf16[192,512]{1,0:T(8,128)(2,1)S(1)}, bf16[192,512]{1,0:T(8,128)(2,1)S(1)}, u32[]{:S(2)}, u32[]{:S(2)}) %collective-permute-start.5) | collective-permute-done | bytes 196640 | tf_op jit(solution)/shard_map/ppermute | solution.py:23
  114.5 4.7 %collective-permute-start.6 = (bf16[512,512]{1,0:T(8,128)(2,1)S(1)}, bf16[512,512]{1,0:T(8,128)(2,1)S(1)}, u32[]{:S(2)}, u32[]{:S(2)}) collective-permute-start(bf16[512,512]{1,0:T(8,128)(2,1)S(1)} %bitcast.4), channel_id=1, source_target_pairs={{0,64},{64,0},{1,65},{65,1},{2,66},{66,2},{3,67},{67,3},{4,68},{68... | collective-permute-start | bytes 1572872 | tf_op jit(solution)/shard_map/ppermute | solution.py:23
  119.2 1.6 %shard_map.78.refs_0_ = f32[1024,512]{1,0:T(8,128)} custom-call(s32[2]{0:T(128)S(1)} %pad_add_fusion.refs_0_.place_ref, bf16[512,512]{1,0:T(8,128)(2,1)S(1)} %bitcast.5), custom_call_target="tpu_custom_call" | custom-call | bytes 1572864 | tf_op jit(solution)/shard_map/pallas_call | solution.py:246
  120.8 2.2 %shard_map.80 = f32[256,512]{1,0:T(8,128)} custom-call(bf16[256,512]{1,0:T(8,128)(2,1)S(1)} %copy-done.4, f32[256,512]{1,0:T(8,128)} %get-tuple-element.66.refs_1_, bf16[192,512]{1,0:T(8,128)(2,1)} %copy-done.5, bf16[192,512]{1,0:T(8,128)(2,1)} %collective-permute-done.3.refs_3_, bf16[192,512]{1,0:T(8,128)(2,1)S(1)} %collective-permute-done.4.refs_4_, ...), custom_call_target="tpu_custom_call" | custom-call | bytes 2097152 | tf_op jit(solution)/shard_map/pallas_call | solution.py:73
  123.0 1.6 %shard_map.79 = f32[1024,512]{1,0:T(8,128)} custom-call(s32[2]{0:T(128)S(1)} %pad_add_fusion.refs_0_.place_ref, bf16[512,512]{1,0:T(8,128)(2,1)S(1)} %collective-permute-done.6.half_ref, f32[1024,512]{1,0:T(8,128)} %shard_map.78.refs_0_), custom_call_target="tpu_custom_call", output_to_operand_aliasing={{}: (2, {})} | custom-call | bytes 1572864 | tf_op jit(solution)/shard_map/pallas_call | solution.py:246
  (25 shorter events, 1.5 us)
Async XLA Ops:
  0.6 1.0 copy-start.3
  2.0 34.6 %copy-start.6 = (s32[256]{0:T(256)S(1)}, s32[256]{0:T(256)}, u32[]{:S(2)}) copy-start(s32[256]{0:T(256)} %param.7) | copy-start | bytes 3076
  2.0 34.7 %copy-start = (bf16[1024,512]{1,0:T(8,128)(2,1)S(1)}, bf16[1024,512]{1,0:T(8,128)(2,1)}, u32[]{:S(2)}) copy-start(bf16[1024,512]{1,0:T(8,128)(2,1)} %refs_1_.4) | copy-start | bytes 3145732
  2.0 34.7 %copy-start.2 = (bf16[256,1024]{1,0:T(8,128)(2,1)S(1)}, bf16[256,1024]{1,0:T(8,128)(2,1)}, u32[]{:S(2)}) copy-start(bf16[256,1024]{1,0:T(8,128)(2,1)} %refs_1_.3) | copy-start | bytes 1572868
  30.5 8.6 %collective-permute-start = (bf16[1088,512]{1,0:T(8,128)(2,1)S(1)}, bf16[1088,512]{1,0:T(8,128)(2,1)}, u32[]{:S(2)}, u32[]{:S(2)}) collective-permute-start(bf16[1088,512]{1,0:T(8,128)(2,1)S(1)} %convert_element_type.7.refs_2_.refs_6_), channel_id=1, source_target_pairs={{0,64},{64,0},{1,65},{65,1},{2,66},{66,2},{3,67},{67,3},{4,68},{68... | collective-permute-start | bytes 3342344 | tf_op jit(solution)/shard_map/ppermute | solution.py:23
  39.0 6.1 %copy-start.1 = (bf16[1024,512]{1,0:T(8,128)(2,1)S(1)}, bf16[1024,512]{1,0:T(8,128)(2,1)}, u32[]{:S(2)}) copy-start(bf16[1024,512]{1,0:T(8,128)(2,1)} %refs_1_.4) | copy-start | bytes 3145732
  42.8 5.3 %collective-permute-start.1 = (bf16[1536,512]{1,0:T(8,128)(2,1)S(1)}, bf16[1536,512]{1,0:T(8,128)(2,1)S(1)}, u32[]{:S(2)}, u32[]{:S(2)}) collective-permute-start(bf16[1536,512]{1,0:T(8,128)(2,1)S(1)} %get-tuple-element.42), channel_id=1, source_target_pairs={{0,64},{64,0},{1,65},{65,1},{2,66},{66,2},{3,67},{67,3},{4,68},{68... | collective-permute-start | bytes 4718600 | tf_op jit(solution)/shard_map/ppermute | solution.py:23
  49.0 27.4 %all-to-all-start = ((bf16[32,16,512]{2,1,0:T(8,128)(2,1)}), bf16[32,16,512]{2,1,0:T(8,128)(2,1)S(1)}, u32[]{:S(2)}, u32[]{:S(2)}) async-start(bf16[32,16,512]{2,1,0:T(8,128)(2,1)} %shard_map.72), calls=%async_computation | async-start | bytes 1048576 | tf_op jit(solution)/shard_map/all_to_all | solution.py:27
  59.7 13.1 %collective-permute-start.2 = (bf16[192,512]{1,0:T(8,128)(2,1)S(1)}, bf16[192,512]{1,0:T(8,128)(2,1)S(1)}, u32[]{:S(2)}, u32[]{:S(2)}) collective-permute-start(bf16[192,512]{1,0:T(8,128)(2,1)S(1)} %get-tuple-element.49), channel_id=1, source_target_pairs={{0,128},{128,256},{256,384},{384,0},{1,129},{129,257},{257,385},{3... | collective-permute-start | bytes 589832 | tf_op jit(solution)/shard_map/ppermute | solution.py:23
  62.7 13.7 %collective-permute-start.3 = (bf16[192,512]{1,0:T(8,128)(2,1)S(1)}, bf16[192,512]{1,0:T(8,128)(2,1)}, u32[]{:S(2)}, u32[]{:S(2)}) collective-permute-start(bf16[192,512]{1,0:T(8,128)(2,1)S(1)} %get-tuple-element.50), channel_id=1, source_target_pairs={{0,384},{128,0},{256,128},{384,256},{1,385},{129,1},{257,129},{385... | collective-permute-start | bytes 589832 | tf_op jit(solution)/shard_map/ppermute | solution.py:23
  72.8 0.7 copy-start.5
  77.1 12.4 %all-to-all-start.1 = ((bf16[8,16,512]{2,1,0:T(8,128)(2,1)}), bf16[8,16,512]{2,1,0:T(8,128)(2,1)S(1)}, u32[]{:S(2)}, u32[]{:S(2)}) async-start(bf16[8,16,512]{2,1,0:T(8,128)(2,1)} %shard_map.75), calls=%async_computation.1 | async-start | bytes 262144 | tf_op jit(solution)/shard_map/all_to_all | solution.py:27
  83.8 15.8 %copy-start.8 = (bf16[192,512]{1,0:T(8,128)(2,1)S(1)}, bf16[192,512]{1,0:T(8,128)(2,1)}, u32[]{:S(2)}) copy-start(bf16[192,512]{1,0:T(8,128)(2,1)} %get-tuple-element.62) | copy-start | bytes 589828
  83.8 17.9 %copy-start.7 = (bf16[192,512]{1,0:T(8,128)(2,1)S(1)}, bf16[192,512]{1,0:T(8,128)(2,1)}, u32[]{:S(2)}) copy-start(bf16[192,512]{1,0:T(8,128)(2,1)} %get-tuple-element.63) | copy-start | bytes 589828
  90.4 24.2 %all-to-all-start.2 = ((bf16[32,16,512]{2,1,0:T(8,128)(2,1)}), bf16[32,16,512]{2,1,0:T(8,128)(2,1)S(1)}, u32[]{:S(2)}, u32[]{:S(2)}) async-start(bf16[32,16,512]{2,1,0:T(8,128)(2,1)} %shard_map.76), calls=%async_computation.2 | async-start | bytes 1048576 | tf_op jit(solution)/shard_map/all_to_all | solution.py:27
  99.6 21.1 %copy-start.4 = (bf16[256,512]{1,0:T(8,128)(2,1)S(1)}, bf16[256,512]{1,0:T(8,128)(2,1)}, u32[]{:S(2)}) copy-start(bf16[256,512]{1,0:T(8,128)(2,1)} %refs_0_.4) | copy-start | bytes 786436
  99.6 9.9 %collective-permute-start.4 = (bf16[192,512]{1,0:T(8,128)(2,1)S(1)}, bf16[192,512]{1,0:T(8,128)(2,1)S(1)}, u32[]{:S(2)}, u32[]{:S(2)}) collective-permute-start(bf16[192,512]{1,0:T(8,128)(2,1)S(1)} %copy-done.8), channel_id=1, source_target_pairs={{0,128},{128,256},{256,384},{384,0},{1,129},{129,257},{257,385},{3... | collective-permute-start | bytes 589832 | tf_op jit(solution)/shard_map/ppermute | solution.py:23
  101.7 12.8 %collective-permute-start.5 = (bf16[192,512]{1,0:T(8,128)(2,1)S(1)}, bf16[192,512]{1,0:T(8,128)(2,1)S(1)}, u32[]{:S(2)}, u32[]{:S(2)}) collective-permute-start(bf16[192,512]{1,0:T(8,128)(2,1)S(1)} %copy-done.7), channel_id=1, source_target_pairs={{0,384},{128,0},{256,128},{384,256},{1,385},{129,1},{257,129},{385... | collective-permute-start | bytes 589832 | tf_op jit(solution)/shard_map/ppermute | solution.py:23
  114.5 8.5 %collective-permute-start.6 = (bf16[512,512]{1,0:T(8,128)(2,1)S(1)}, bf16[512,512]{1,0:T(8,128)(2,1)S(1)}, u32[]{:S(2)}, u32[]{:S(2)}) collective-permute-start(bf16[512,512]{1,0:T(8,128)(2,1)S(1)} %bitcast.4), channel_id=1, source_target_pairs={{0,64},{64,0},{1,65},{65,1},{2,66},{66,2},{3,67},{67,3},{4,68},{68... | collective-permute-start | bytes 1572872 | tf_op jit(solution)/shard_map/ppermute | solution.py:23

commit v10 on v9

--- a/solution.py
+++ b/solution.py
@@ -16,6 +16,7 @@
 TAIL = 16
 EARLY = 64
 MIB = 1 << 20
+HEAVY = 1 << 36
 
 
 def shifted(block, axis, distance):
@@ -351,9 +352,7 @@
         flops=pair_flops,
         far_outs=True,
     )
-    parts, forward, backward, ahead, behind, home = lax.optimization_barrier(
-        (parts, forward, backward, ahead, behind, home)
-    )
+    parts, ahead, behind, home = lax.optimization_barrier((parts, ahead, behind, home))
     (parts,) = call(fold_kernel, (shape((column, part, width), bf16),), parts, far_outs=True)
     parts = exchanged(parts, COLUMN)
     to_next, to_last = call(
@@ -368,16 +367,23 @@
         far_outs=True,
     )
     (parts,) = call(fold_kernel, (shape((plane, part, width), bf16),), parts, far_outs=True)
-    parts, to_next, to_last = lax.optimization_barrier((parts, to_next, to_last))
     weight_half = exchanged(parts, PLANE).reshape(half, width)
     arrived = [shifted(to_next, "zh", 1), shifted(to_last, "zh", -1)]
-    weight_half, arrived = lax.optimization_barrier((weight_half, arrived))
+    (grad_text,) = call(
+        text_grad_kernel,
+        (block,),
+        text_raw,
+        home,
+        forward,
+        backward,
+        *arrived,
+        flops=HEAVY,
+        far=(1, 2, 3),
+    )
+    weight_half, grad_text = lax.optimization_barrier((weight_half, grad_text))
     there = shifted(weight_half, "core", 1)
     grad_weight = placed(place, weight_half, 0, None)
     grad_weight = placed(place, there, 1, grad_weight)
-    (grad_text,) = call(
-        text_grad_kernel, (block,), text_raw, home, forward, backward, *arrived, far=(1, 2, 3)
-    )
     return (grad_weight, grad_features, grad_text)
 
 

time: 126 us -> 121 us (0.960)
  waiting for transfers between devices: 22 us -> 17.2 us
    ppermute x7, waiting for transfers between devices: 16.3 us -> 2.2 us  [shifted(): lax.ppermute(block, axis, [(i, (i + distance) % count) for i in range(cou...]
    all_to_all x3, waiting for transfers between devices: 5.71 us -> 15 us  [exchanged(): return lax.all_to_all(block, axes, split_axis=0, concat_axis=0, tiled=True)]
    ppermute x7, starting transfers between devices: 27.9 us -> 29.4 us  [shifted(): lax.ppermute(block, axis, [(i, (i + distance) % count) for i in range(cou...]
  transfers between devices with their start and end apart: 10 -> 10, of which waited for: 7 -> 4; matrix products, arithmetic and copies ran while one was open for 0% -> 0% of each run, Pallas kernels for 9% -> 12%
where the time goes in v10:
time: 121 us; the launch traced here: 120 us
  starting transfers between devices  51.9 us (43%)
  blocking collectives  28.3 us (23%)
  Pallas kernels  20.5 us (17%)
  waiting for transfers between devices  17.2 us (14%)
    ppermute x7, starting transfers between devices, shifted(): lax.ppermute(block, axis, [(i, (i + distance) % count) for i in range(cou...  29.4 us
    all_gather x1, blocking collectives, body(): lax.all_gather(sent.astype(jnp.float16), 'zh', axis=0, tiled=True)  28.3 us
    all_to_all x3, starting transfers between devices, exchanged(): return lax.all_to_all(block, axes, split_axis=0, concat_axis=0, tiled=True)  22.5 us
    pallas_call x12, Pallas kernels, call(): pl.pallas_call(staging, out_shape=[pltpu.HBM(a.shape, a.dtype) for a in o...  17.4 us
    all_to_all x3, waiting for transfers between devices, exchanged(): return lax.all_to_all(block, axes, split_axis=0, concat_axis=0, tiled=True)  15 us
    pallas_call x2, Pallas kernels, placed(): pl.pallas_call(functools.partial(place_kernel, side), out_shape=shape((2...  3.11 us
  transfers between devices with their start and end apart: 10, of which 4 were waited for; matrix products, arithmetic and copies ran while one was open for 0% of the time, Pallas kernels for 12%

profile of v10, /device:TPU:1, one launch (start us, length us, event | category | flops | bytes accessed | tf_op | source)
XLA Modules:
  0.0 120.2 jit_solution(7670189019606745179)
XLA Ops:
  0.6 0.9 copy-done.3
  1.6 0.3 shard_map.67
  2.0 28.3 %all-gather.1 = f16[1088,512]{1,0:T(8,128)(2,1)S(1)} all-gather(f16[272,512]{1,0:T(8,128)(2,1)S(1)} %convert_element_type.6), channel_id=1, replica_groups=mesh['zh'=4,'core'=2,'zl'=2,'x'=4,'y'=8] {'zh'}, dimensions={0}, use_global_device_ids=true | all-gather | bytes 1392640 | tf_op jit(solution)/shard_map/all_gather | solution.py:299
  30.2 0.2 convert_element_type.7.refs_2_.refs_6_
  30.5 6.1 %collective-permute-start = (bf16[1088,512]{1,0:T(8,128)(2,1)S(1)}, bf16[1088,512]{1,0:T(8,128)(2,1)}, u32[]{:S(2)}, u32[]{:S(2)}) collective-permute-start(bf16[1088,512]{1,0:T(8,128)(2,1)S(1)} %convert_element_type.7.refs_2_.refs_6_), channel_id=1, source_target_pairs={{0,64},{64,0},{1,65},{65,1},{2,66},{66,2},{3,67},{67,3},{4,68},{68... | collective-permute-start | bytes 3342344 | tf_op jit(solution)/shard_map/ppermute | solution.py:24
  36.6 0.1 copy.8.refs_5_
  36.7 0.9 shard_map.68
  37.7 1.3 %collective-permute-done.refs_7_ = bf16[1088,512]{1,0:T(8,128)(2,1)} collective-permute-done((bf16[1088,512]{1,0:T(8,128)(2,1)S(1)}, bf16[1088,512]{1,0:T(8,128)(2,1)}, u32[]{:S(2)}, u32[]{:S(2)}) %collective-permute-start) | collective-permute-done | bytes 1114144 | tf_op jit(solution)/shard_map/ppermute | solution.py:24
  39.0 3.8 %shard_map.69 = (bf16[256,512]{1,0:T(8,128)(2,1)S(1)}, bf16[8,256,256]{2,1,0:T(8,128)(2,1)S(1)}, bf16[1536,512]{1,0:T(8,128)(2,1)S(1)}) custom-call(s32[2]{0:T(128)S(1)} %pad_add_fusion.refs_0_.place_ref, f32[256,512]{1,0:T(8,128)S(1)} %get-tuple-element.32.refs_1_, bf16[256,512]{1,0:T(8,128)(2,1)S(1)} %get-tuple-element.33.refs_2_, ...), custom_call_target="tpu_custom_call" | custom-call | flops 1610612736 | bytes 7473160 | tf_op jit(solution)/shard_map/pallas_call | solution.py:74
  42.8 2.3 %collective-permute-start.1 = (bf16[1536,512]{1,0:T(8,128)(2,1)S(1)}, bf16[1536,512]{1,0:T(8,128)(2,1)S(1)}, u32[]{:S(2)}, u32[]{:S(2)}) collective-permute-start(bf16[1536,512]{1,0:T(8,128)(2,1)S(1)} %get-tuple-element.36), channel_id=1, source_target_pairs={{0,64},{64,0},{1,65},{65,1},{2,66},{66,2},{3,67},{67,3},{4,68},{68... | collective-permute-start | bytes 4718600 | tf_op jit(solution)/shard_map/ppermute | solution.py:24
  45.1 1.3 %shard_map.71 = bf16[256,1024]{1,0:T(8,128)(2,1)} custom-call(bf16[256,512]{1,0:T(8,128)(2,1)S(1)} %get-tuple-element.37.refs_2_.refs_0_, bf16[1024,512]{1,0:T(8,128)(2,1)S(1)} %copy-done.1), custom_call_target="tpu_custom_call" | custom-call | tf_op jit(solution)/shard_map/pallas_call | solution.py:74
  46.4 0.9 shard_map.70.refs_0_
  47.3 0.9 collective-permute-done.1.refs_1_.refs_3_
  48.1 0.9 shard_map.72
  49.0 9.7 %all-to-all-start = ((bf16[32,16,512]{2,1,0:T(8,128)(2,1)}), bf16[32,16,512]{2,1,0:T(8,128)(2,1)S(1)}, u32[]{:S(2)}, u32[]{:S(2)}) async-start(bf16[32,16,512]{2,1,0:T(8,128)(2,1)} %shard_map.72), calls=%async_computation | async-start | bytes 1048576 | tf_op jit(solution)/shard_map/all_to_all | solution.py:28
  58.7 1.6 %shard_map.76 = (bf16[192,512]{1,0:T(8,128)(2,1)}, bf16[192,512]{1,0:T(8,128)(2,1)}) custom-call(s32[2]{0:T(128)S(1)} %pad_add_fusion.refs_0_.place_ref, bf16[8,256,256]{2,1,0:T(8,128)(2,1)S(1)} %get-tuple-element.41.refs_1_, bf16[256,512]{1,0:T(8,128)(2,1)S(1)} %get-tuple-element.33.refs_2_, bf16[1536,512]{1,0:T(8,128)(2,1)S(1)} %collective-permute-done.1.refs_1_.refs_3_), custom_call_target="tpu_custom_call" | custom-call | flops 134217728 | bytes 3276808 | tf_op jit(solution)/shard_map/pallas_call | solution.py:74
  60.4 3.0 %collective-permute-start.2 = (bf16[192,512]{1,0:T(8,128)(2,1)}, bf16[192,512]{1,0:T(8,128)(2,1)}, u32[]{:S(2)}, u32[]{:S(2)}) collective-permute-start(bf16[192,512]{1,0:T(8,128)(2,1)} %get-tuple-element.48), channel_id=1, source_target_pairs={{0,128},{128,256},{256,384},{384,0},{1,129},{129,257},{257,385},{3... | collective-permute-start | bytes 589832 | tf_op jit(solution)/shard_map/ppermute | solution.py:24
  63.3 4.4 %collective-permute-start.3 = (bf16[192,512]{1,0:T(8,128)(2,1)}, bf16[192,512]{1,0:T(8,128)(2,1)}, u32[]{:S(2)}, u32[]{:S(2)}) collective-permute-start(bf16[192,512]{1,0:T(8,128)(2,1)} %get-tuple-element.49), channel_id=1, source_target_pairs={{0,384},{128,0},{256,128},{384,256},{1,385},{129,1},{257,129},{385... | collective-permute-start | bytes 589832 | tf_op jit(solution)/shard_map/ppermute | solution.py:24
  67.8 1.9 %shard_map.73 = (f32[192,512]{1,0:T(8,128)}, f32[192,512]{1,0:T(8,128)}, f32[256,512]{1,0:T(8,128)}) custom-call(s32[2]{0:T(128)S(1)} %pad_add_fusion.refs_0_.place_ref, bf16[8,256,256]{2,1,0:T(8,128)(2,1)S(1)} %get-tuple-element.41.refs_1_, bf16[256,512]{1,0:T(8,128)(2,1)S(1)} %get-tuple-element.33.refs_2_, ...), custom_call_target="tpu_custom_call" | custom-call | flops 536870912 | bytes 4194312 | tf_op jit(solution)/shard_map/pallas_call | solution.py:74
  69.6 3.2 %all-to-all-done.refs_0_ = bf16[32,16,512]{2,1,0:T(8,128)(2,1)S(1)} async-done(((bf16[32,16,512]{2,1,0:T(8,128)(2,1)}), bf16[32,16,512]{2,1,0:T(8,128)(2,1)S(1)}, u32[]{:S(2)}, u32[]{:S(2)}) %all-to-all-start) | async-done | bytes 524320 | tf_op jit(solution)/shard_map/all_to_all | solution.py:28
  72.9 0.7 shard_map.74
  73.6 3.9 %all-to-all-start.1 = ((bf16[8,16,512]{2,1,0:T(8,128)(2,1)}), bf16[8,16,512]{2,1,0:T(8,128)(2,1)S(1)}, u32[]{:S(2)}, u32[]{:S(2)}) async-start(bf16[8,16,512]{2,1,0:T(8,128)(2,1)} %shard_map.74), calls=%async_computation.1 | async-start | bytes 262144 | tf_op jit(solution)/shard_map/all_to_all | solution.py:28
  77.5 2.1 %shard_map.77 = (bf16[192,512]{1,0:T(8,128)(2,1)}, bf16[192,512]{1,0:T(8,128)(2,1)}) custom-call(f32[192,512]{1,0:T(8,128)} %get-tuple-element.50.refs_0_, f32[192,512]{1,0:T(8,128)} %get-tuple-element.51.refs_1_, bf16[192,512]{1,0:T(8,128)(2,1)} %collective-permute-done.2.refs_2_, bf16[192,512]{1,0:T(8,128)(2,1)} %collective-permute-done.3.refs_3_), custom_call_target="tpu_custom_call" | custom-call | tf_op jit(solution)/shard_map/pallas_call | solution.py:74
  79.6 4.3 %collective-permute-start.4 = (bf16[192,512]{1,0:T(8,128)(2,1)}, bf16[192,512]{1,0:T(8,128)(2,1)S(1)}, u32[]{:S(2)}, u32[]{:S(2)}) collective-permute-start(bf16[192,512]{1,0:T(8,128)(2,1)} %get-tuple-element.52), channel_id=1, source_target_pairs={{0,128},{128,256},{256,384},{384,0},{1,129},{129,257},{257,385},{3... | collective-permute-start | bytes 589832 | tf_op jit(solution)/shard_map/ppermute | solution.py:24
  83.9 3.1 %collective-permute-start.5 = (bf16[192,512]{1,0:T(8,128)(2,1)}, bf16[192,512]{1,0:T(8,128)(2,1)S(1)}, u32[]{:S(2)}, u32[]{:S(2)}) collective-permute-start(bf16[192,512]{1,0:T(8,128)(2,1)} %get-tuple-element.53), channel_id=1, source_target_pairs={{0,384},{128,0},{256,128},{384,256},{1,385},{129,1},{257,129},{385... | collective-permute-start | bytes 589832 | tf_op jit(solution)/shard_map/ppermute | solution.py:24
  87.0 0.9 shard_map.75
  87.9 9.0 %all-to-all-start.2 = ((bf16[32,16,512]{2,1,0:T(8,128)(2,1)}), bf16[32,16,512]{2,1,0:T(8,128)(2,1)S(1)}, u32[]{:S(2)}, u32[]{:S(2)}) async-start(bf16[32,16,512]{2,1,0:T(8,128)(2,1)} %shard_map.75), calls=%async_computation.2 | async-start | bytes 1048576 | tf_op jit(solution)/shard_map/all_to_all | solution.py:28
  96.9 2.2 %shard_map.78 = f32[256,512]{1,0:T(8,128)} custom-call(bf16[256,512]{1,0:T(8,128)(2,1)S(1)} %copy-done.4, f32[256,512]{1,0:T(8,128)} %get-tuple-element.47.refs_1_, bf16[192,512]{1,0:T(8,128)(2,1)} %collective-permute-done.2.refs_2_, bf16[192,512]{1,0:T(8,128)(2,1)} %collective-permute-done.3.refs_3_, bf16[192,512]{1,0:T(8,128)(2,1)S(1)} %collective-permute-done.4.refs_4_, ...), custom_call_target="tpu_custom_call" | custom-call | flops 68719476736 | bytes 2097152 | tf_op jit(solution)/shard_map/pallas_call | solution.py:74
  99.1 11.7 %all-to-all-done.2 = bf16[32,16,512]{2,1,0:T(8,128)(2,1)S(1)} async-done(((bf16[32,16,512]{2,1,0:T(8,128)(2,1)}), bf16[32,16,512]{2,1,0:T(8,128)(2,1)S(1)}, u32[]{:S(2)}, u32[]{:S(2)}) %all-to-all-start.2) | async-done | bytes 524320 | tf_op jit(solution)/shard_map/all_to_all | solution.py:28
  110.9 6.2 %collective-permute-start.6 = (bf16[512,512]{1,0:T(8,128)(2,1)S(1)}, bf16[512,512]{1,0:T(8,128)(2,1)S(1)}, u32[]{:S(2)}, u32[]{:S(2)}) collective-permute-start(bf16[512,512]{1,0:T(8,128)(2,1)S(1)} %bitcast.4), channel_id=1, source_target_pairs={{0,64},{64,0},{1,65},{65,1},{2,66},{66,2},{3,67},{67,3},{4,68},{68... | collective-permute-start | bytes 1572872 | tf_op jit(solution)/shard_map/ppermute | solution.py:24
  117.1 1.6 %shard_map.79.refs_0_ = f32[1024,512]{1,0:T(8,128)} custom-call(s32[2]{0:T(128)S(1)} %pad_add_fusion.refs_0_.place_ref, bf16[512,512]{1,0:T(8,128)(2,1)S(1)} %bitcast.5), custom_call_target="tpu_custom_call" | custom-call | bytes 1572864 | tf_op jit(solution)/shard_map/pallas_call | solution.py:247
  118.7 1.6 %shard_map.80 = f32[1024,512]{1,0:T(8,128)} custom-call(s32[2]{0:T(128)S(1)} %pad_add_fusion.refs_0_.place_ref, bf16[512,512]{1,0:T(8,128)(2,1)S(1)} %collective-permute-done.6.half_ref, f32[1024,512]{1,0:T(8,128)} %shard_map.79.refs_0_), custom_call_target="tpu_custom_call", output_to_operand_aliasing={{}: (2, {})} | custom-call | bytes 1572864 | tf_op jit(solution)/shard_map/pallas_call | solution.py:247
  (19 shorter events, 0.2 us)
Async XLA Ops:
  0.6 1.0 copy-start.3
  2.0 34.6 %copy-start.5 = (s32[256]{0:T(256)S(1)}, s32[256]{0:T(256)}, u32[]{:S(2)}) copy-start(s32[256]{0:T(256)} %param.7) | copy-start | bytes 3076
  2.0 34.7 %copy-start = (bf16[1024,512]{1,0:T(8,128)(2,1)S(1)}, bf16[1024,512]{1,0:T(8,128)(2,1)}, u32[]{:S(2)}) copy-start(bf16[1024,512]{1,0:T(8,128)(2,1)} %refs_1_.4) | copy-start | bytes 3145732
  2.0 34.7 %copy-start.2 = (bf16[256,1024]{1,0:T(8,128)(2,1)S(1)}, bf16[256,1024]{1,0:T(8,128)(2,1)}, u32[]{:S(2)}) copy-start(bf16[256,1024]{1,0:T(8,128)(2,1)} %refs_1_.3) | copy-start | bytes 1572868
  30.5 8.6 %collective-permute-start = (bf16[1088,512]{1,0:T(8,128)(2,1)S(1)}, bf16[1088,512]{1,0:T(8,128)(2,1)}, u32[]{:S(2)}, u32[]{:S(2)}) collective-permute-start(bf16[1088,512]{1,0:T(8,128)(2,1)S(1)} %convert_element_type.7.refs_2_.refs_6_), channel_id=1, source_target_pairs={{0,64},{64,0},{1,65},{65,1},{2,66},{66,2},{3,67},{67,3},{4,68},{68... | collective-permute-start | bytes 3342344 | tf_op jit(solution)/shard_map/ppermute | solution.py:24
  39.0 6.1 %copy-start.1 = (bf16[1024,512]{1,0:T(8,128)(2,1)S(1)}, bf16[1024,512]{1,0:T(8,128)(2,1)}, u32[]{:S(2)}) copy-start(bf16[1024,512]{1,0:T(8,128)(2,1)} %refs_1_.4) | copy-start | bytes 3145732
  42.8 5.3 %collective-permute-start.1 = (bf16[1536,512]{1,0:T(8,128)(2,1)S(1)}, bf16[1536,512]{1,0:T(8,128)(2,1)S(1)}, u32[]{:S(2)}, u32[]{:S(2)}) collective-permute-start(bf16[1536,512]{1,0:T(8,128)(2,1)S(1)} %get-tuple-element.36), channel_id=1, source_target_pairs={{0,64},{64,0},{1,65},{65,1},{2,66},{66,2},{3,67},{67,3},{4,68},{68... | collective-permute-start | bytes 4718600 | tf_op jit(solution)/shard_map/ppermute | solution.py:24
  49.0 23.8 %all-to-all-start = ((bf16[32,16,512]{2,1,0:T(8,128)(2,1)}), bf16[32,16,512]{2,1,0:T(8,128)(2,1)S(1)}, u32[]{:S(2)}, u32[]{:S(2)}) async-start(bf16[32,16,512]{2,1,0:T(8,128)(2,1)} %shard_map.72), calls=%async_computation | async-start | bytes 1048576 | tf_op jit(solution)/shard_map/all_to_all | solution.py:28
  60.4 17.2 %collective-permute-start.2 = (bf16[192,512]{1,0:T(8,128)(2,1)}, bf16[192,512]{1,0:T(8,128)(2,1)}, u32[]{:S(2)}, u32[]{:S(2)}) collective-permute-start(bf16[192,512]{1,0:T(8,128)(2,1)} %get-tuple-element.48), channel_id=1, source_target_pairs={{0,128},{128,256},{256,384},{384,0},{1,129},{129,257},{257,385},{3... | collective-permute-start | bytes 589832 | tf_op jit(solution)/shard_map/ppermute | solution.py:24
  63.3 14.2 %collective-permute-start.3 = (bf16[192,512]{1,0:T(8,128)(2,1)}, bf16[192,512]{1,0:T(8,128)(2,1)}, u32[]{:S(2)}, u32[]{:S(2)}) collective-permute-start(bf16[192,512]{1,0:T(8,128)(2,1)} %get-tuple-element.49), channel_id=1, source_target_pairs={{0,384},{128,0},{256,128},{384,256},{1,385},{129,1},{257,129},{385... | collective-permute-start | bytes 589832 | tf_op jit(solution)/shard_map/ppermute | solution.py:24
  73.6 23.3 %copy-start.4 = (bf16[256,512]{1,0:T(8,128)(2,1)S(1)}, bf16[256,512]{1,0:T(8,128)(2,1)}, u32[]{:S(2)}) copy-start(bf16[256,512]{1,0:T(8,128)(2,1)} %refs_0_.4) | copy-start | bytes 786436
  73.6 13.4 %all-to-all-start.1 = ((bf16[8,16,512]{2,1,0:T(8,128)(2,1)}), bf16[8,16,512]{2,1,0:T(8,128)(2,1)S(1)}, u32[]{:S(2)}, u32[]{:S(2)}) async-start(bf16[8,16,512]{2,1,0:T(8,128)(2,1)} %shard_map.74), calls=%async_computation.1 | async-start | bytes 262144 | tf_op jit(solution)/shard_map/all_to_all | solution.py:28
  79.6 17.3 %collective-permute-start.4 = (bf16[192,512]{1,0:T(8,128)(2,1)}, bf16[192,512]{1,0:T(8,128)(2,1)S(1)}, u32[]{:S(2)}, u32[]{:S(2)}) collective-permute-start(bf16[192,512]{1,0:T(8,128)(2,1)} %get-tuple-element.52), channel_id=1, source_target_pairs={{0,128},{128,256},{256,384},{384,0},{1,129},{129,257},{257,385},{3... | collective-permute-start | bytes 589832 | tf_op jit(solution)/shard_map/ppermute | solution.py:24
  83.9 13.0 %collective-permute-start.5 = (bf16[192,512]{1,0:T(8,128)(2,1)}, bf16[192,512]{1,0:T(8,128)(2,1)S(1)}, u32[]{:S(2)}, u32[]{:S(2)}) collective-permute-start(bf16[192,512]{1,0:T(8,128)(2,1)} %get-tuple-element.53), channel_id=1, source_target_pairs={{0,384},{128,0},{256,128},{384,256},{1,385},{129,1},{257,129},{385... | collective-permute-start | bytes 589832 | tf_op jit(solution)/shard_map/ppermute | solution.py:24
  87.9 23.0 %all-to-all-start.2 = ((bf16[32,16,512]{2,1,0:T(8,128)(2,1)}), bf16[32,16,512]{2,1,0:T(8,128)(2,1)S(1)}, u32[]{:S(2)}, u32[]{:S(2)}) async-start(bf16[32,16,512]{2,1,0:T(8,128)(2,1)} %shard_map.75), calls=%async_computation.2 | async-start | bytes 1048576 | tf_op jit(solution)/shard_map/all_to_all | solution.py:28
  110.9 7.8 %collective-permute-start.6 = (bf16[512,512]{1,0:T(8,128)(2,1)S(1)}, bf16[512,512]{1,0:T(8,128)(2,1)S(1)}, u32[]{:S(2)}, u32[]{:S(2)}) collective-permute-start(bf16[512,512]{1,0:T(8,128)(2,1)S(1)} %bitcast.4), channel_id=1, source_target_pairs={{0,64},{64,0},{1,65},{65,1},{2,66},{66,2},{3,67},{67,3},{4,68},{68... | collective-permute-start | bytes 1572872 | tf_op jit(solution)/shard_map/ppermute | solution.py:24

commit v11 on v10

--- a/solution.py
+++ b/solution.py
@@ -14,7 +14,6 @@
 PLANE = ("x", "y")
 COLUMN = ("zh", "zl")
 TAIL = 16
-EARLY = 64
 MIB = 1 << 20
 HEAVY = 1 << 36
 
@@ -188,34 +187,20 @@
     return part + got_ref[pl.ds(start, rows), :].astype(jnp.float32)
 
 
-def early_kernel(place_ref, tiles_ref, audio_b_ref, got_ref, forward_ref, backward_ref):
+def early_kernel(place_ref, tiles_ref, audio_b_ref, got_ref, across_ref, last_ref):
     refs = (place_ref, tiles_ref, audio_b_ref, got_ref)
-    rows = tiles_ref.shape[2]
-    cut = rows // 2
-    across = summed(*refs, 2).astype(jnp.bfloat16)
-    forward_ref[:cut, :] = across[:cut]
-    backward_ref[:cut, :] = across[cut:]
-    forward_ref[cut:, :] = summed(*refs, 1)[rows - EARLY :].astype(jnp.bfloat16)
-    backward_ref[cut:, :] = summed(*refs, 3)[:EARLY].astype(jnp.bfloat16)
-
-
-def late_kernel(place_ref, tiles_ref, audio_b_ref, got_ref, ahead_ref, behind_ref, home_ref):
+    across_ref[...] = summed(*refs, 2).astype(jnp.bfloat16)
+    last_ref[...] = summed(*refs, 3).astype(jnp.bfloat16)
+
+
+def late_kernel(place_ref, tiles_ref, audio_b_ref, got_ref, ahead_ref, home_ref):
     refs = (place_ref, tiles_ref, audio_b_ref, got_ref)
-    rows = tiles_ref.shape[2]
-    ahead_ref[...] = summed(*refs, 1)[: rows - EARLY]
-    behind_ref[...] = summed(*refs, 3)[EARLY:]
+    ahead_ref[...] = summed(*refs, 1)
     home_ref[...] = summed(*refs, 0)
 
 
-def relay_kernel(ahead_ref, behind_ref, forward_ref, backward_ref, to_next_ref, to_last_ref):
-    late = ahead_ref.shape[0]
-    cut = (late + EARLY) // 2
-    forward = forward_ref[:cut, :].astype(jnp.float32)
-    backward = backward_ref[:cut, :].astype(jnp.float32)
-    to_next_ref[:cut, :] = (ahead_ref[:cut, :] + forward).astype(jnp.bfloat16)
-    to_next_ref[cut:, :] = ahead_ref[cut:, :].astype(jnp.bfloat16)
-    to_last_ref[: late - cut, :] = behind_ref[: late - cut, :].astype(jnp.bfloat16)
-    to_last_ref[late - cut :, :] = (behind_ref[late - cut :, :] + backward).astype(jnp.bfloat16)
+def relay_kernel(ahead_ref, across_ref, to_next_ref):
+    to_next_ref[...] = (ahead_ref[...] + across_ref[...].astype(jnp.float32)).astype(jnp.bfloat16)
 
 
 def fold_kernel(parts_ref, copies_ref):
@@ -262,18 +247,8 @@
     )(place, half, *given)
 
 
-def text_grad_kernel(
-    text_ref, home_ref, forward_ref, backward_ref, next_ref, last_ref, grad_ref
-):
-    rows, late = home_ref.shape[0], next_ref.shape[0]
-    home = home_ref[...]
-    forward = forward_ref[rows // 2 :, :].astype(jnp.float32)
-    backward = backward_ref[rows // 2 :, :].astype(jnp.float32)
-    ahead, behind = next_ref[...].astype(jnp.float32), last_ref[...].astype(jnp.float32)
-    first = home[:EARLY] + ahead[:EARLY] + backward
-    middle = home[EARLY:late] + ahead[EARLY:] + behind[: late - EARLY]
-    final = home[late:] + forward + behind[late - EARLY :]
-    grad = jnp.concatenate([first, middle, final])
+def text_grad_kernel(text_ref, home_ref, last_ref, next_ref, grad_ref):
+    grad = home_ref[...] + (last_ref[...].astype(jnp.float32) + next_ref[...].astype(jnp.float32))
     text = text_ref[...].astype(jnp.float32)
     scale = lax.rsqrt(jnp.sum(text * text, axis=1, keepdims=True) + EPS)
     text = text * scale
@@ -292,8 +267,6 @@
     half = channels // 2
     block = shape((rows, width), f32)
     block_b = shape((rows, width), bf16)
-    early_b = shape((rows // 2 + EARLY, width), bf16)
-    late, late_b = (shape((rows - EARLY, width), dtype) for dtype in (f32, bf16))
 
     (sent,) = call(text_kernel, (shape((rows + TAIL, width), bf16),), text_raw)
     own = lax.all_gather(sent.astype(jnp.float16), "zh", axis=0, tiled=True).astype(bf16)
@@ -337,48 +310,28 @@
     (parts,) = call(half_kernel, (shape((plane, part, width), bf16),), weight, got, far_outs=True)
     parts, got = lax.optimization_barrier((parts, got))
     parts = exchanged(parts, PLANE)
-    forward, backward = call(
-        early_kernel, (early_b, early_b), place, tiles, audio_b, got, flops=pair_flops // 4
-    )
-    forward = shifted(forward, "zh", 1)
-    backward = shifted(backward, "zh", -1)
-    ahead, behind, home = call(
-        late_kernel,
-        (late, late, block),
-        place,
-        tiles,
-        audio_b,
-        got,
-        flops=pair_flops,
-        far_outs=True,
-    )
-    parts, ahead, behind, home = lax.optimization_barrier((parts, ahead, behind, home))
+    across, last = call(
+        early_kernel, (block_b, block_b), place, tiles, audio_b, got, flops=pair_flops // 4
+    )
+    across = shifted(across, "zh", 1)
+    last = shifted(last, "zh", -1)
+    ahead, home = call(
+        late_kernel, (block, block), place, tiles, audio_b, got, flops=pair_flops, far_outs=True
+    )
+    parts, ahead, home = lax.optimization_barrier((parts, ahead, home))
     (parts,) = call(fold_kernel, (shape((column, part, width), bf16),), parts, far_outs=True)
+    parts, ahead = lax.optimization_barrier((parts, ahead))
     parts = exchanged(parts, COLUMN)
-    to_next, to_last = call(
-        relay_kernel,
-        (late_b, late_b),
-        ahead,
-        behind,
-        forward,
-        backward,
-        light=True,
-        far=(0, 1, 2, 3),
-        far_outs=True,
-    )
-    (parts,) = call(fold_kernel, (shape((plane, part, width), bf16),), parts, far_outs=True)
+    (to_next,) = call(
+        relay_kernel, (block_b,), ahead, across, flops=HEAVY, far=(0, 1), far_outs=True
+    )
+    (parts,) = call(
+        fold_kernel, (shape((plane, part, width), bf16),), parts, flops=HEAVY, far_outs=True
+    )
     weight_half = exchanged(parts, PLANE).reshape(half, width)
-    arrived = [shifted(to_next, "zh", 1), shifted(to_last, "zh", -1)]
+    arrived = shifted(to_next, "zh", 1)
     (grad_text,) = call(
-        text_grad_kernel,
-        (block,),
-        text_raw,
-        home,
-        forward,
-        backward,
-        *arrived,
-        flops=HEAVY,
-        far=(1, 2, 3),
+        text_grad_kernel, (block,), text_raw, home, last, arrived, flops=HEAVY, far=(1, 2)
     )
     weight_half, grad_text = lax.optimization_barrier((weight_half, grad_text))
     there = shifted(weight_half, "core", 1)

time: 121 us -> 118 us (0.975)
  starting transfers between devices: 51.9 us -> 49 us
    ppermute x7 -> x6, starting transfers between devices: 29.4 us -> 27.6 us  [shifted(): lax.ppermute(block, axis, [(i, (i + distance) % count) for i in range(cou...]
    ppermute x7 -> x6, waiting for transfers between devices: 2.2 us -> 2.58 us  [shifted(): lax.ppermute(block, axis, [(i, (i + distance) % count) for i in range(cou...]
  transfers between devices with their start and end apart: 10 -> 9, of which waited for: 4 -> 6; matrix products, arithmetic and copies ran while one was open for 0% -> 0% of each run, Pallas kernels for 12% -> 12%
where the time goes in v11:
time: 118 us; the launch traced here: 117 us
  starting transfers between devices  49 us (42%)
  blocking collectives  28.3 us (24%)
  Pallas kernels  20.2 us (17%)
  waiting for transfers between devices  17.1 us (14%)
    all_gather x1, blocking collectives, body(): lax.all_gather(sent.astype(jnp.float16), 'zh', axis=0, tiled=True)  28.3 us
    ppermute x6, starting transfers between devices, shifted(): lax.ppermute(block, axis, [(i, (i + distance) % count) for i in range(cou...  27.6 us
    all_to_all x3, starting transfers between devices, exchanged(): return lax.all_to_all(block, axes, split_axis=0, concat_axis=0, tiled=True)  21.4 us
    pallas_call x12, Pallas kernels, call(): pl.pallas_call(staging, out_shape=[pltpu.HBM(a.shape, a.dtype) for a in o...  17.1 us
    all_to_all x3, waiting for transfers between devices, exchanged(): return lax.all_to_all(block, axes, split_axis=0, concat_axis=0, tiled=True)  14.5 us
    pallas_call x2, Pallas kernels, placed(): pl.pallas_call(functools.partial(place_kernel, side), out_shape=shape((2...  3.11 us
    ppermute x6, waiting for transfers between devices, shifted(): lax.ppermute(block, axis, [(i, (i + distance) % count) for i in range(cou...  2.58 us
  transfers between devices with their start and end apart: 9, of which 6 were waited for; matrix products, arithmetic and copies ran while one was open for 0% of the time, Pallas kernels for 12%

profile of v11, /device:TPU:1, one launch (start us, length us, event | category | flops | bytes accessed | tf_op | source)
XLA Modules:
  0.0 116.8 jit_solution(15993343953920462720)
XLA Ops:
  0.6 0.9 copy-done.3
  1.6 0.3 shard_map.67
  2.0 28.3 %all-gather.1 = f16[1088,512]{1,0:T(8,128)(2,1)S(1)} all-gather(f16[272,512]{1,0:T(8,128)(2,1)S(1)} %convert_element_type.6), channel_id=1, replica_groups=mesh['zh'=4,'core'=2,'zl'=2,'x'=4,'y'=8] {'zh'}, dimensions={0}, use_global_device_ids=true | all-gather | bytes 1392640 | tf_op jit(solution)/shard_map/all_gather | solution.py:272
  30.2 0.2 convert_element_type.7.refs_2_.refs_6_
  30.5 6.1 %collective-permute-start = (bf16[1088,512]{1,0:T(8,128)(2,1)S(1)}, bf16[1088,512]{1,0:T(8,128)(2,1)}, u32[]{:S(2)}, u32[]{:S(2)}) collective-permute-start(bf16[1088,512]{1,0:T(8,128)(2,1)S(1)} %convert_element_type.7.refs_2_.refs_6_), channel_id=1, source_target_pairs={{0,64},{64,0},{1,65},{65,1},{2,66},{66,2},{3,67},{67,3},{4,68},{68... | collective-permute-start | bytes 3342344 | tf_op jit(solution)/shard_map/ppermute | solution.py:23
  36.7 0.9 shard_map.68
  37.7 1.3 %collective-permute-done.refs_7_ = bf16[1088,512]{1,0:T(8,128)(2,1)} collective-permute-done((bf16[1088,512]{1,0:T(8,128)(2,1)S(1)}, bf16[1088,512]{1,0:T(8,128)(2,1)}, u32[]{:S(2)}, u32[]{:S(2)}) %collective-permute-start) | collective-permute-done | bytes 1114144 | tf_op jit(solution)/shard_map/ppermute | solution.py:23
  39.0 3.8 %shard_map.69 = (bf16[256,512]{1,0:T(8,128)(2,1)S(1)}, bf16[8,256,256]{2,1,0:T(8,128)(2,1)S(1)}, bf16[1536,512]{1,0:T(8,128)(2,1)S(1)}) custom-call(s32[2]{0:T(128)S(1)} %pad_add_fusion.refs_0_.place_ref, f32[256,512]{1,0:T(8,128)S(1)} %get-tuple-element.30.refs_1_, bf16[256,512]{1,0:T(8,128)(2,1)S(1)} %get-tuple-element.31.refs_2_, ...), custom_call_target="tpu_custom_call" | custom-call | flops 1610612736 | bytes 7473160 | tf_op jit(solution)/shard_map/pallas_call | solution.py:73
  42.8 2.3 %collective-permute-start.1 = (bf16[1536,512]{1,0:T(8,128)(2,1)S(1)}, bf16[1536,512]{1,0:T(8,128)(2,1)S(1)}, u32[]{:S(2)}, u32[]{:S(2)}) collective-permute-start(bf16[1536,512]{1,0:T(8,128)(2,1)S(1)} %get-tuple-element.34), channel_id=1, source_target_pairs={{0,64},{64,0},{1,65},{65,1},{2,66},{66,2},{3,67},{67,3},{4,68},{68... | collective-permute-start | bytes 4718600 | tf_op jit(solution)/shard_map/ppermute | solution.py:23
  45.1 1.3 %shard_map.71 = bf16[256,1024]{1,0:T(8,128)(2,1)} custom-call(bf16[256,512]{1,0:T(8,128)(2,1)S(1)} %get-tuple-element.35.refs_2_.refs_0_, bf16[1024,512]{1,0:T(8,128)(2,1)S(1)} %copy-done.1), custom_call_target="tpu_custom_call" | custom-call | tf_op jit(solution)/shard_map/pallas_call | solution.py:73
  46.4 0.9 shard_map.70.refs_0_
  47.3 0.9 collective-permute-done.1.refs_1_.refs_3_
  48.1 0.9 shard_map.72
  49.0 9.7 %all-to-all-start = ((bf16[32,16,512]{2,1,0:T(8,128)(2,1)}), bf16[32,16,512]{2,1,0:T(8,128)(2,1)S(1)}, u32[]{:S(2)}, u32[]{:S(2)}) async-start(bf16[32,16,512]{2,1,0:T(8,128)(2,1)} %shard_map.72), calls=%async_computation | async-start | bytes 1048576 | tf_op jit(solution)/shard_map/all_to_all | solution.py:27
  58.7 1.6 %shard_map.76 = (bf16[256,512]{1,0:T(8,128)(2,1)}, bf16[256,512]{1,0:T(8,128)(2,1)}) custom-call(s32[2]{0:T(128)S(1)} %pad_add_fusion.refs_0_.place_ref, bf16[8,256,256]{2,1,0:T(8,128)(2,1)S(1)} %get-tuple-element.39.refs_1_, bf16[256,512]{1,0:T(8,128)(2,1)S(1)} %get-tuple-element.31.refs_2_, bf16[1536,512]{1,0:T(8,128)(2,1)S(1)} %collective-permute-done.1.refs_1_.refs_3_), custom_call_target="tpu_custom_call" | custom-call | flops 134217728 | bytes 3407880 | tf_op jit(solution)/shard_map/pallas_call | solution.py:73
  60.3 3.0 %collective-permute-start.3 = (bf16[256,512]{1,0:T(8,128)(2,1)}, bf16[256,512]{1,0:T(8,128)(2,1)}, u32[]{:S(2)}, u32[]{:S(2)}) collective-permute-start(bf16[256,512]{1,0:T(8,128)(2,1)} %get-tuple-element.49), channel_id=1, source_target_pairs={{0,128},{128,256},{256,384},{384,0},{1,129},{129,257},{257,385},{3... | collective-permute-start | bytes 786440 | tf_op jit(solution)/shard_map/ppermute | solution.py:23
  63.3 4.4 %collective-permute-start.2 = (bf16[256,512]{1,0:T(8,128)(2,1)}, bf16[256,512]{1,0:T(8,128)(2,1)}, u32[]{:S(2)}, u32[]{:S(2)}) collective-permute-start(bf16[256,512]{1,0:T(8,128)(2,1)} %get-tuple-element.47), channel_id=1, source_target_pairs={{0,384},{128,0},{256,128},{384,256},{1,385},{129,1},{257,129},{385... | collective-permute-start | bytes 786440 | tf_op jit(solution)/shard_map/ppermute | solution.py:23
  67.7 1.8 %shard_map.73 = (f32[256,512]{1,0:T(8,128)}, f32[256,512]{1,0:T(8,128)}) custom-call(s32[2]{0:T(128)S(1)} %pad_add_fusion.refs_0_.place_ref, bf16[8,256,256]{2,1,0:T(8,128)(2,1)S(1)} %get-tuple-element.39.refs_1_, bf16[256,512]{1,0:T(8,128)(2,1)S(1)} %get-tuple-element.31.refs_2_, bf16[1536,512]{1,0:T(8,128)(2,1)S(1)} %collective-permute-done.1.refs_1_.refs_3_), custom_call_target="tpu_custom_call" | custom-call | flops 536870912 | bytes 3932168 | tf_op jit(solution)/shard_map/pallas_call | solution.py:73
  69.5 3.3 %all-to-all-done.refs_0_ = bf16[32,16,512]{2,1,0:T(8,128)(2,1)S(1)} async-done(((bf16[32,16,512]{2,1,0:T(8,128)(2,1)}), bf16[32,16,512]{2,1,0:T(8,128)(2,1)S(1)}, u32[]{:S(2)}, u32[]{:S(2)}) %all-to-all-start) | async-done | bytes 524320 | tf_op jit(solution)/shard_map/all_to_all | solution.py:27
  72.9 0.7 shard_map.74
  73.6 3.8 %all-to-all-start.1 = ((bf16[8,16,512]{2,1,0:T(8,128)(2,1)}), bf16[8,16,512]{2,1,0:T(8,128)(2,1)S(1)}, u32[]{:S(2)}, u32[]{:S(2)}) async-start(bf16[8,16,512]{2,1,0:T(8,128)(2,1)} %shard_map.74), calls=%async_computation.1 | async-start | bytes 262144 | tf_op jit(solution)/shard_map/all_to_all | solution.py:27
  77.4 1.9 %shard_map.77 = bf16[256,512]{1,0:T(8,128)(2,1)} custom-call(f32[256,512]{1,0:T(8,128)} %get-tuple-element.48.refs_0_, bf16[256,512]{1,0:T(8,128)(2,1)} %collective-permute-done.3.refs_1_), custom_call_target="tpu_custom_call" | custom-call | flops 68719476736 | bytes 1048576 | tf_op jit(solution)/shard_map/pallas_call | solution.py:73
  79.3 4.4 %collective-permute-start.4 = (bf16[256,512]{1,0:T(8,128)(2,1)}, bf16[256,512]{1,0:T(8,128)(2,1)S(1)}, u32[]{:S(2)}, u32[]{:S(2)}) collective-permute-start(bf16[256,512]{1,0:T(8,128)(2,1)} %shard_map.77), channel_id=1, source_target_pairs={{0,128},{128,256},{256,384},{384,0},{1,129},{129,257},{257,385},{3... | collective-permute-start | bytes 786440 | tf_op jit(solution)/shard_map/ppermute | solution.py:23
  83.7 1.6 %all-to-all-done.1.refs_0_ = bf16[8,16,512]{2,1,0:T(8,128)(2,1)S(1)} async-done(((bf16[8,16,512]{2,1,0:T(8,128)(2,1)}), bf16[8,16,512]{2,1,0:T(8,128)(2,1)S(1)}, u32[]{:S(2)}, u32[]{:S(2)}) %all-to-all-start.1) | async-done | bytes 131104 | tf_op jit(solution)/shard_map/all_to_all | solution.py:27
  85.3 0.9 shard_map.75
  86.2 8.0 %all-to-all-start.2 = ((bf16[32,16,512]{2,1,0:T(8,128)(2,1)}), bf16[32,16,512]{2,1,0:T(8,128)(2,1)S(1)}, u32[]{:S(2)}, u32[]{:S(2)}) async-start(bf16[32,16,512]{2,1,0:T(8,128)(2,1)} %shard_map.75), calls=%async_computation.2 | async-start | bytes 1048576 | tf_op jit(solution)/shard_map/all_to_all | solution.py:27
  94.2 0.4 collective-permute-done.4.refs_3_
  94.5 2.2 %shard_map.78 = f32[256,512]{1,0:T(8,128)} custom-call(bf16[256,512]{1,0:T(8,128)(2,1)S(1)} %copy-done.4, f32[256,512]{1,0:T(8,128)} %get-tuple-element.46.refs_1_, bf16[256,512]{1,0:T(8,128)(2,1)} %collective-permute-done.2.refs_2_, bf16[256,512]{1,0:T(8,128)(2,1)S(1)} %collective-permute-done.4.refs_3_), custom_call_target="tpu_custom_call" | custom-call | flops 68719476736 | bytes 1835008 | tf_op jit(solution)/shard_map/pallas_call | solution.py:73
  96.7 9.6 %all-to-all-done.2 = bf16[32,16,512]{2,1,0:T(8,128)(2,1)S(1)} async-done(((bf16[32,16,512]{2,1,0:T(8,128)(2,1)}), bf16[32,16,512]{2,1,0:T(8,128)(2,1)S(1)}, u32[]{:S(2)}, u32[]{:S(2)}) %all-to-all-start.2) | async-done | bytes 524320 | tf_op jit(solution)/shard_map/all_to_all | solution.py:27
  106.3 7.4 %collective-permute-start.5 = (bf16[512,512]{1,0:T(8,128)(2,1)S(1)}, bf16[512,512]{1,0:T(8,128)(2,1)S(1)}, u32[]{:S(2)}, u32[]{:S(2)}) collective-permute-start(bf16[512,512]{1,0:T(8,128)(2,1)S(1)} %bitcast.4), channel_id=1, source_target_pairs={{0,64},{64,0},{1,65},{65,1},{2,66},{66,2},{3,67},{67,3},{4,68},{68... | collective-permute-start | bytes 1572872 | tf_op jit(solution)/shard_map/ppermute | solution.py:23
  113.7 1.6 %shard_map.79.refs_0_ = f32[1024,512]{1,0:T(8,128)} custom-call(s32[2]{0:T(128)S(1)} %pad_add_fusion.refs_0_.place_ref, bf16[512,512]{1,0:T(8,128)(2,1)S(1)} %bitcast.5), custom_call_target="tpu_custom_call" | custom-call | bytes 1572864 | tf_op jit(solution)/shard_map/pallas_call | solution.py:232
  115.3 1.6 %shard_map.80 = f32[1024,512]{1,0:T(8,128)} custom-call(s32[2]{0:T(128)S(1)} %pad_add_fusion.refs_0_.place_ref, bf16[512,512]{1,0:T(8,128)(2,1)S(1)} %collective-permute-done.5.half_ref, f32[1024,512]{1,0:T(8,128)} %shard_map.79.refs_0_), custom_call_target="tpu_custom_call", output_to_operand_aliasing={{}: (2, {})} | custom-call | bytes 1572864 | tf_op jit(solution)/shard_map/pallas_call | solution.py:232
  (17 shorter events, 0.3 us)
Async XLA Ops:
  0.6 1.0 copy-start.3
  2.0 34.6 %copy-start.5 = (s32[256]{0:T(256)S(1)}, s32[256]{0:T(256)}, u32[]{:S(2)}) copy-start(s32[256]{0:T(256)} %param.7) | copy-start | bytes 3076
  2.0 34.7 %copy-start = (bf16[1024,512]{1,0:T(8,128)(2,1)S(1)}, bf16[1024,512]{1,0:T(8,128)(2,1)}, u32[]{:S(2)}) copy-start(bf16[1024,512]{1,0:T(8,128)(2,1)} %refs_1_.4) | copy-start | bytes 3145732
  2.0 34.7 %copy-start.2 = (bf16[256,1024]{1,0:T(8,128)(2,1)S(1)}, bf16[256,1024]{1,0:T(8,128)(2,1)}, u32[]{:S(2)}) copy-start(bf16[256,1024]{1,0:T(8,128)(2,1)} %refs_1_.3) | copy-start | bytes 1572868
  30.5 8.6 %collective-permute-start = (bf16[1088,512]{1,0:T(8,128)(2,1)S(1)}, bf16[1088,512]{1,0:T(8,128)(2,1)}, u32[]{:S(2)}, u32[]{:S(2)}) collective-permute-start(bf16[1088,512]{1,0:T(8,128)(2,1)S(1)} %convert_element_type.7.refs_2_.refs_6_), channel_id=1, source_target_pairs={{0,64},{64,0},{1,65},{65,1},{2,66},{66,2},{3,67},{67,3},{4,68},{68... | collective-permute-start | bytes 3342344 | tf_op jit(solution)/shard_map/ppermute | solution.py:23
  39.0 6.1 %copy-start.1 = (bf16[1024,512]{1,0:T(8,128)(2,1)S(1)}, bf16[1024,512]{1,0:T(8,128)(2,1)}, u32[]{:S(2)}) copy-start(bf16[1024,512]{1,0:T(8,128)(2,1)} %refs_1_.4) | copy-start | bytes 3145732
  42.8 5.3 %collective-permute-start.1 = (bf16[1536,512]{1,0:T(8,128)(2,1)S(1)}, bf16[1536,512]{1,0:T(8,128)(2,1)S(1)}, u32[]{:S(2)}, u32[]{:S(2)}) collective-permute-start(bf16[1536,512]{1,0:T(8,128)(2,1)S(1)} %get-tuple-element.34), channel_id=1, source_target_pairs={{0,64},{64,0},{1,65},{65,1},{2,66},{66,2},{3,67},{67,3},{4,68},{68... | collective-permute-start | bytes 4718600 | tf_op jit(solution)/shard_map/ppermute | solution.py:23
  49.0 23.8 %all-to-all-start = ((bf16[32,16,512]{2,1,0:T(8,128)(2,1)}), bf16[32,16,512]{2,1,0:T(8,128)(2,1)S(1)}, u32[]{:S(2)}, u32[]{:S(2)}) async-start(bf16[32,16,512]{2,1,0:T(8,128)(2,1)} %shard_map.72), calls=%async_computation | async-start | bytes 1048576 | tf_op jit(solution)/shard_map/all_to_all | solution.py:27
  60.3 17.1 %collective-permute-start.3 = (bf16[256,512]{1,0:T(8,128)(2,1)}, bf16[256,512]{1,0:T(8,128)(2,1)}, u32[]{:S(2)}, u32[]{:S(2)}) collective-permute-start(bf16[256,512]{1,0:T(8,128)(2,1)} %get-tuple-element.49), channel_id=1, source_target_pairs={{0,128},{128,256},{256,384},{384,0},{1,129},{129,257},{257,385},{3... | collective-permute-start | bytes 786440 | tf_op jit(solution)/shard_map/ppermute | solution.py:23
  63.3 30.9 %collective-permute-start.2 = (bf16[256,512]{1,0:T(8,128)(2,1)}, bf16[256,512]{1,0:T(8,128)(2,1)}, u32[]{:S(2)}, u32[]{:S(2)}) collective-permute-start(bf16[256,512]{1,0:T(8,128)(2,1)} %get-tuple-element.47), channel_id=1, source_target_pairs={{0,384},{128,0},{256,128},{384,256},{1,385},{129,1},{257,129},{385... | collective-permute-start | bytes 786440 | tf_op jit(solution)/shard_map/ppermute | solution.py:23
  73.6 11.7 %all-to-all-start.1 = ((bf16[8,16,512]{2,1,0:T(8,128)(2,1)}), bf16[8,16,512]{2,1,0:T(8,128)(2,1)S(1)}, u32[]{:S(2)}, u32[]{:S(2)}) async-start(bf16[8,16,512]{2,1,0:T(8,128)(2,1)} %shard_map.74), calls=%async_computation.1 | async-start | bytes 262144 | tf_op jit(solution)/shard_map/all_to_all | solution.py:27
  79.3 15.3 %copy-start.4 = (bf16[256,512]{1,0:T(8,128)(2,1)S(1)}, bf16[256,512]{1,0:T(8,128)(2,1)}, u32[]{:S(2)}) copy-start(bf16[256,512]{1,0:T(8,128)(2,1)} %refs_0_.4) | copy-start | bytes 786436
  79.3 15.3 %collective-permute-start.4 = (bf16[256,512]{1,0:T(8,128)(2,1)}, bf16[256,512]{1,0:T(8,128)(2,1)S(1)}, u32[]{:S(2)}, u32[]{:S(2)}) collective-permute-start(bf16[256,512]{1,0:T(8,128)(2,1)} %shard_map.77), channel_id=1, source_target_pairs={{0,128},{128,256},{256,384},{384,0},{1,129},{129,257},{257,385},{3... | collective-permute-start | bytes 786440 | tf_op jit(solution)/shard_map/ppermute | solution.py:23
  86.2 20.1 %all-to-all-start.2 = ((bf16[32,16,512]{2,1,0:T(8,128)(2,1)}), bf16[32,16,512]{2,1,0:T(8,128)(2,1)S(1)}, u32[]{:S(2)}, u32[]{:S(2)}) async-start(bf16[32,16,512]{2,1,0:T(8,128)(2,1)} %shard_map.75), calls=%async_computation.2 | async-start | bytes 1048576 | tf_op jit(solution)/shard_map/all_to_all | solution.py:27
  106.3 9.0 %collective-permute-start.5 = (bf16[512,512]{1,0:T(8,128)(2,1)S(1)}, bf16[512,512]{1,0:T(8,128)(2,1)S(1)}, u32[]{:S(2)}, u32[]{:S(2)}) collective-permute-start(bf16[512,512]{1,0:T(8,128)(2,1)S(1)} %bitcast.4), channel_id=1, source_target_pairs={{0,64},{64,0},{1,65},{65,1},{2,66},{66,2},{3,67},{67,3},{4,68},{68... | collective-permute-start | bytes 1572872 | tf_op jit(solution)/shard_map/ppermute | solution.py:23

commit v12 on v11

--- a/solution.py
+++ b/solution.py
@@ -106,7 +106,8 @@
 
 
 def audio_kernel(
-    features_ref, weight_ref, own_ref, audio_ref, audio_b_ref, scale_ref, scores_ref
+    features_ref, weight_ref, own_ref,
+    audio_ref, audio_b_ref, scale_ref, weights_ref, peak_ref, sum_ref, scores_ref,
 ):
     rows = audio_ref.shape[0]
     proj = dot(features_ref[...], weight_ref[...], 1, 0)
@@ -119,11 +120,19 @@
     for n in range(scores_ref.shape[1] // rows):
         block, factor = text_block(own_ref, n, rows)
         scores_ref[:, n * rows : (n + 1) * rows] = factor * dot(audio_b, block, 1, 1)
+    step = 16
+    for r in range(0, rows, step):
+        scores = scores_ref[r : r + step, :]
+        peak = jnp.max(scores, axis=1, keepdims=True)
+        weights = jnp.exp(scores - peak)
+        weights_ref[r : r + step, :] = weights
+        peak_ref[r : r + step, :] = peak
+        sum_ref[r : r + step, :] = jnp.sum(weights, axis=1, keepdims=True)
 
 
 def score_kernel(
     place_ref, audio_ref, audio_b_ref, scale_ref, features_ref, positive_ref, own_ref, other_ref,
-    own_scores_ref, grad_ref, tiles_ref, sent_ref, scores_ref,
+    own_weights_ref, own_peak_ref, own_sum_ref, grad_ref, tiles_ref, sent_ref, scores_ref,
 ):
     core = place_ref[1]
     blocks, rows, _ = tiles_ref.shape
@@ -135,17 +144,21 @@
     step = 16
     ids = lax.broadcasted_iota(jnp.int32, (step, rows), 1)
     for r in range(0, rows, step):
-        both = [own_scores_ref[r : r + step, :], scores_ref[r : r + step, :]]
-        peak = jnp.maximum(*(jnp.max(scores, axis=1, keepdims=True) for scores in both))
-        both = [jnp.exp(scores - peak) for scores in both]
-        share = 1.0 / sum(jnp.sum(weights, axis=1, keepdims=True) for weights in both)
+        scores = scores_ref[r : r + step, :]
+        own_peak = own_peak_ref[r : r + step, :]
+        peak = jnp.maximum(own_peak, jnp.max(scores, axis=1, keepdims=True))
+        other_weights = jnp.exp(scores - peak)
+        factor = jnp.exp(own_peak - peak)
+        total = factor * own_sum_ref[r : r + step, :] + jnp.sum(other_weights, axis=1, keepdims=True)
+        both = [own_weights_ref[r : r + step, :], other_weights]
+        shares = [factor / total, 1.0 / total]
         positive = positive_ref[r : r + step, :]
         for n in range(blocks):
             column = core if n < chips else 1 - core
             first = ((n % chips) * 2 + column) * rows
             match = jnp.where(positive - first == ids, 1.0, 0.0)
             lanes = slice(n % chips * rows, (n % chips + 1) * rows)
-            part = both[n // chips][:, lanes] * share - match
+            part = both[n // chips][:, lanes] * shares[n // chips] - match
             tiles_ref[n, r : r + step, :] = part.astype(jnp.bfloat16)
     total = jnp.zeros(audio_ref.shape, jnp.float32)
     for n in range(blocks):
@@ -268,16 +281,18 @@
     block = shape((rows, width), f32)
     block_b = shape((rows, width), bf16)
 
-    (sent,) = call(text_kernel, (shape((rows + TAIL, width), bf16),), text_raw)
+    (sent,) = call(text_kernel, (shape((rows + TAIL, width), bf16),), text_raw, far=(0,))
     own = lax.all_gather(sent.astype(jnp.float16), "zh", axis=0, tiled=True).astype(bf16)
     own, audio_features = lax.optimization_barrier((own, audio_features))
     other = shifted(own, "core", 1)
-    audio, audio_b, scale, own_scores = call(
+    row_f = shape((rows, 1), f32)
+    audio, audio_b, scale, *own_terms = call(
         audio_kernel,
-        (block, block_b, shape((rows, 1), f32), shape((rows, chips * rows), f32)),
+        (block, block_b, row_f, shape((rows, chips * rows), f32), row_f, row_f),
         audio_features,
         proj_weight,
         own,
+        scratch=[pltpu.VMEM((rows, chips * rows), f32)],
         flops=2 * rows * channels * width,
     )
     proj_grad, tiles, sent = call(
@@ -291,7 +306,7 @@
         positive.reshape(rows, 1),
         own,
         other,
-        own_scores,
+        *own_terms,
         scratch=[pltpu.VMEM((rows, chips * rows), f32)],
         flops=3 * pair_flops,
         limit=20,

time: 118 us -> 118 us (level)
  Pallas kernels: 20.2 us -> 21.4 us
    pallas_call x12, Pallas kernels: 17.1 us -> 18.3 us  [call(): pl.pallas_call(staging, out_shape=[pltpu.HBM(a.shape, a.dtype) for a in o...]
where the time goes in v12:
time: 118 us; the launch traced here: 117 us
  starting transfers between devices  49 us (42%)
  blocking collectives  28.3 us (24%)
  Pallas kernels  21.4 us (18%)
  waiting for transfers between devices  16.9 us (14%)
    all_gather x1, blocking collectives, body(): lax.all_gather(sent.astype(jnp.float16), 'zh', axis=0, tiled=True)  28.3 us
    ppermute x6, starting transfers between devices, shifted(): lax.ppermute(block, axis, [(i, (i + distance) % count) for i in range(cou...  27.6 us
    all_to_all x3, starting transfers between devices, exchanged(): return lax.all_to_all(block, axes, split_axis=0, concat_axis=0, tiled=True)  21.4 us
    pallas_call x12, Pallas kernels, call(): pl.pallas_call(staging, out_shape=[pltpu.HBM(a.shape, a.dtype) for a in o...  18.3 us
    all_to_all x3, waiting for transfers between devices, exchanged(): return lax.all_to_all(block, axes, split_axis=0, concat_axis=0, tiled=True)  14.5 us
    pallas_call x2, Pallas kernels, placed(): pl.pallas_call(functools.partial(place_kernel, side), out_shape=shape((2...  3.11 us
    ppermute x6, waiting for transfers between devices, shifted(): lax.ppermute(block, axis, [(i, (i + distance) % count) for i in range(cou...  2.36 us
  transfers between devices with their start and end apart: 9, of which 6 were waited for; matrix products, arithmetic and copies ran while one was open for 0% of the time, Pallas kernels for 12%

profile of v12, /device:TPU:1, one launch (start us, length us, event | category | flops | bytes accessed | tf_op | source)
XLA Modules:
  0.0 116.8 jit_solution(9329411421162671348)
XLA Ops:
  0.6 1.3 %shard_map.67 = bf16[272,512]{1,0:T(8,128)(2,1)S(1)} custom-call(bf16[256,512]{1,0:T(8,128)(2,1)} %refs_0_.4), custom_call_target="tpu_custom_call" | custom-call | bytes 540672 | tf_op jit(solution)/shard_map/pallas_call | solution.py:73
  2.0 28.3 %all-gather.1 = f16[1088,512]{1,0:T(8,128)(2,1)S(1)} all-gather(f16[272,512]{1,0:T(8,128)(2,1)S(1)} %convert_element_type.6), channel_id=1, replica_groups=mesh['zh'=4,'core'=2,'zl'=2,'x'=4,'y'=8] {'zh'}, dimensions={0}, use_global_device_ids=true | all-gather | bytes 1392640 | tf_op jit(solution)/shard_map/all_gather | solution.py:285
  30.3 0.2 convert_element_type.7.refs_2_.refs_6_
  30.5 6.1 %collective-permute-start = (bf16[1088,512]{1,0:T(8,128)(2,1)S(1)}, bf16[1088,512]{1,0:T(8,128)(2,1)}, u32[]{:S(2)}, u32[]{:S(2)}) collective-permute-start(bf16[1088,512]{1,0:T(8,128)(2,1)S(1)} %convert_element_type.7.refs_2_.refs_6_), channel_id=1, source_target_pairs={{0,64},{64,0},{1,65},{65,1},{2,66},{66,2},{3,67},{67,3},{4,68},{68... | collective-permute-start | bytes 3342344 | tf_op jit(solution)/shard_map/ppermute | solution.py:23
  36.6 0.1 copy.8.refs_5_
  36.7 1.1 shard_map.68
  37.9 1.1 collective-permute-done.refs_7_
  39.1 3.7 %shard_map.69 = (bf16[256,512]{1,0:T(8,128)(2,1)S(1)}, bf16[8,256,256]{2,1,0:T(8,128)(2,1)S(1)}, bf16[1536,512]{1,0:T(8,128)(2,1)S(1)}) custom-call(s32[2]{0:T(128)S(1)} %pad_add_fusion.refs_0_.place_ref, f32[256,512]{1,0:T(8,128)S(1)} %get-tuple-element.32.refs_1_, bf16[256,512]{1,0:T(8,128)(2,1)S(1)} %get-tuple-element.33.refs_2_, ...), custom_call_target="tpu_custom_call" | custom-call | flops 1610612736 | bytes 7475208 | tf_op jit(solution)/shard_map/pallas_call | solution.py:73
  42.8 2.3 %collective-permute-start.1 = (bf16[1536,512]{1,0:T(8,128)(2,1)S(1)}, bf16[1536,512]{1,0:T(8,128)(2,1)S(1)}, u32[]{:S(2)}, u32[]{:S(2)}) collective-permute-start(bf16[1536,512]{1,0:T(8,128)(2,1)S(1)} %get-tuple-element.38), channel_id=1, source_target_pairs={{0,64},{64,0},{1,65},{65,1},{2,66},{66,2},{3,67},{67,3},{4,68},{68... | collective-permute-start | bytes 4718600 | tf_op jit(solution)/shard_map/ppermute | solution.py:23
  45.1 1.3 %shard_map.71 = bf16[256,1024]{1,0:T(8,128)(2,1)} custom-call(bf16[256,512]{1,0:T(8,128)(2,1)S(1)} %get-tuple-element.39.refs_2_.refs_0_, bf16[1024,512]{1,0:T(8,128)(2,1)S(1)} %copy-done.1), custom_call_target="tpu_custom_call" | custom-call | tf_op jit(solution)/shard_map/pallas_call | solution.py:73
  46.4 0.9 shard_map.70.refs_0_
  47.2 0.9 collective-permute-done.1.refs_1_.refs_3_
  48.1 0.9 shard_map.72
  49.0 9.7 %all-to-all-start = ((bf16[32,16,512]{2,1,0:T(8,128)(2,1)}), bf16[32,16,512]{2,1,0:T(8,128)(2,1)S(1)}, u32[]{:S(2)}, u32[]{:S(2)}) async-start(bf16[32,16,512]{2,1,0:T(8,128)(2,1)} %shard_map.72), calls=%async_computation | async-start | bytes 1048576 | tf_op jit(solution)/shard_map/all_to_all | solution.py:27
  58.7 1.6 %shard_map.76 = (bf16[256,512]{1,0:T(8,128)(2,1)}, bf16[256,512]{1,0:T(8,128)(2,1)}) custom-call(s32[2]{0:T(128)S(1)} %pad_add_fusion.refs_0_.place_ref, bf16[8,256,256]{2,1,0:T(8,128)(2,1)S(1)} %get-tuple-element.43.refs_1_, bf16[256,512]{1,0:T(8,128)(2,1)S(1)} %get-tuple-element.33.refs_2_, bf16[1536,512]{1,0:T(8,128)(2,1)S(1)} %collective-permute-done.1.refs_1_.refs_3_), custom_call_target="tpu_custom_call" | custom-call | flops 134217728 | bytes 3407880 | tf_op jit(solution)/shard_map/pallas_call | solution.py:73
  60.3 3.0 %collective-permute-start.3 = (bf16[256,512]{1,0:T(8,128)(2,1)}, bf16[256,512]{1,0:T(8,128)(2,1)}, u32[]{:S(2)}, u32[]{:S(2)}) collective-permute-start(bf16[256,512]{1,0:T(8,128)(2,1)} %get-tuple-element.53), channel_id=1, source_target_pairs={{0,128},{128,256},{256,384},{384,0},{1,129},{129,257},{257,385},{3... | collective-permute-start | bytes 786440 | tf_op jit(solution)/shard_map/ppermute | solution.py:23
  63.3 4.4 %collective-permute-start.2 = (bf16[256,512]{1,0:T(8,128)(2,1)}, bf16[256,512]{1,0:T(8,128)(2,1)}, u32[]{:S(2)}, u32[]{:S(2)}) collective-permute-start(bf16[256,512]{1,0:T(8,128)(2,1)} %get-tuple-element.51), channel_id=1, source_target_pairs={{0,384},{128,0},{256,128},{384,256},{1,385},{129,1},{257,129},{385... | collective-permute-start | bytes 786440 | tf_op jit(solution)/shard_map/ppermute | solution.py:23
  67.7 1.8 %shard_map.73 = (f32[256,512]{1,0:T(8,128)}, f32[256,512]{1,0:T(8,128)}) custom-call(s32[2]{0:T(128)S(1)} %pad_add_fusion.refs_0_.place_ref, bf16[8,256,256]{2,1,0:T(8,128)(2,1)S(1)} %get-tuple-element.43.refs_1_, bf16[256,512]{1,0:T(8,128)(2,1)S(1)} %get-tuple-element.33.refs_2_, bf16[1536,512]{1,0:T(8,128)(2,1)S(1)} %collective-permute-done.1.refs_1_.refs_3_), custom_call_target="tpu_custom_call" | custom-call | flops 536870912 | bytes 3932168 | tf_op jit(solution)/shard_map/pallas_call | solution.py:73
  69.5 3.3 %all-to-all-done.refs_0_ = bf16[32,16,512]{2,1,0:T(8,128)(2,1)S(1)} async-done(((bf16[32,16,512]{2,1,0:T(8,128)(2,1)}), bf16[32,16,512]{2,1,0:T(8,128)(2,1)S(1)}, u32[]{:S(2)}, u32[]{:S(2)}) %all-to-all-start) | async-done | bytes 524320 | tf_op jit(solution)/shard_map/all_to_all | solution.py:27
  72.8 0.8 shard_map.74
  73.6 3.8 %all-to-all-start.1 = ((bf16[8,16,512]{2,1,0:T(8,128)(2,1)}), bf16[8,16,512]{2,1,0:T(8,128)(2,1)S(1)}, u32[]{:S(2)}, u32[]{:S(2)}) async-start(bf16[8,16,512]{2,1,0:T(8,128)(2,1)} %shard_map.74), calls=%async_computation.1 | async-start | bytes 262144 | tf_op jit(solution)/shard_map/all_to_all | solution.py:27
  77.4 1.9 %shard_map.77 = bf16[256,512]{1,0:T(8,128)(2,1)} custom-call(f32[256,512]{1,0:T(8,128)} %get-tuple-element.52.refs_0_, bf16[256,512]{1,0:T(8,128)(2,1)} %collective-permute-done.3.refs_1_), custom_call_target="tpu_custom_call" | custom-call | flops 68719476736 | bytes 1048576 | tf_op jit(solution)/shard_map/pallas_call | solution.py:73
  79.3 4.4 %collective-permute-start.4 = (bf16[256,512]{1,0:T(8,128)(2,1)}, bf16[256,512]{1,0:T(8,128)(2,1)S(1)}, u32[]{:S(2)}, u32[]{:S(2)}) collective-permute-start(bf16[256,512]{1,0:T(8,128)(2,1)} %shard_map.77), channel_id=1, source_target_pairs={{0,128},{128,256},{256,384},{384,0},{1,129},{129,257},{257,385},{3... | collective-permute-start | bytes 786440 | tf_op jit(solution)/shard_map/ppermute | solution.py:23
  83.7 1.6 %all-to-all-done.1.refs_0_ = bf16[8,16,512]{2,1,0:T(8,128)(2,1)S(1)} async-done(((bf16[8,16,512]{2,1,0:T(8,128)(2,1)}), bf16[8,16,512]{2,1,0:T(8,128)(2,1)S(1)}, u32[]{:S(2)}, u32[]{:S(2)}) %all-to-all-start.1) | async-done | bytes 131104 | tf_op jit(solution)/shard_map/all_to_all | solution.py:27
  85.3 0.9 shard_map.75
  86.2 8.0 %all-to-all-start.2 = ((bf16[32,16,512]{2,1,0:T(8,128)(2,1)}), bf16[32,16,512]{2,1,0:T(8,128)(2,1)S(1)}, u32[]{:S(2)}, u32[]{:S(2)}) async-start(bf16[32,16,512]{2,1,0:T(8,128)(2,1)} %shard_map.75), calls=%async_computation.2 | async-start | bytes 1048576 | tf_op jit(solution)/shard_map/all_to_all | solution.py:27
  94.2 0.4 collective-permute-done.4.refs_3_
  94.5 2.2 %shard_map.78 = f32[256,512]{1,0:T(8,128)} custom-call(bf16[256,512]{1,0:T(8,128)(2,1)S(1)} %copy-done.3, f32[256,512]{1,0:T(8,128)} %get-tuple-element.50.refs_1_, bf16[256,512]{1,0:T(8,128)(2,1)} %collective-permute-done.2.refs_2_, bf16[256,512]{1,0:T(8,128)(2,1)S(1)} %collective-permute-done.4.refs_3_), custom_call_target="tpu_custom_call" | custom-call | flops 68719476736 | bytes 1835008 | tf_op jit(solution)/shard_map/pallas_call | solution.py:73
  96.7 9.6 %all-to-all-done.2 = bf16[32,16,512]{2,1,0:T(8,128)(2,1)S(1)} async-done(((bf16[32,16,512]{2,1,0:T(8,128)(2,1)}), bf16[32,16,512]{2,1,0:T(8,128)(2,1)S(1)}, u32[]{:S(2)}, u32[]{:S(2)}) %all-to-all-start.2) | async-done | bytes 524320 | tf_op jit(solution)/shard_map/all_to_all | solution.py:27
  106.3 7.4 %collective-permute-start.5 = (bf16[512,512]{1,0:T(8,128)(2,1)S(1)}, bf16[512,512]{1,0:T(8,128)(2,1)S(1)}, u32[]{:S(2)}, u32[]{:S(2)}) collective-permute-start(bf16[512,512]{1,0:T(8,128)(2,1)S(1)} %bitcast.4), channel_id=1, source_target_pairs={{0,64},{64,0},{1,65},{65,1},{2,66},{66,2},{3,67},{67,3},{4,68},{68... | collective-permute-start | bytes 1572872 | tf_op jit(solution)/shard_map/ppermute | solution.py:23
  113.7 1.6 %shard_map.79.refs_0_ = f32[1024,512]{1,0:T(8,128)} custom-call(s32[2]{0:T(128)S(1)} %pad_add_fusion.refs_0_.place_ref, bf16[512,512]{1,0:T(8,128)(2,1)S(1)} %bitcast.5), custom_call_target="tpu_custom_call" | custom-call | bytes 1572864 | tf_op jit(solution)/shard_map/pallas_call | solution.py:245
  115.3 1.6 %shard_map.80 = f32[1024,512]{1,0:T(8,128)} custom-call(s32[2]{0:T(128)S(1)} %pad_add_fusion.refs_0_.place_ref, bf16[512,512]{1,0:T(8,128)(2,1)S(1)} %collective-permute-done.5.half_ref, f32[1024,512]{1,0:T(8,128)} %shard_map.79.refs_0_), custom_call_target="tpu_custom_call", output_to_operand_aliasing={{}: (2, {})} | custom-call | bytes 1572864 | tf_op jit(solution)/shard_map/pallas_call | solution.py:245
  (15 shorter events, 0.2 us)
Async XLA Ops:
  2.0 34.6 %copy-start.4 = (s32[256]{0:T(256)S(1)}, s32[256]{0:T(256)}, u32[]{:S(2)}) copy-start(s32[256]{0:T(256)} %param.7) | copy-start | bytes 3076
  2.0 34.7 %copy-start = (bf16[1024,512]{1,0:T(8,128)(2,1)S(1)}, bf16[1024,512]{1,0:T(8,128)(2,1)}, u32[]{:S(2)}) copy-start(bf16[1024,512]{1,0:T(8,128)(2,1)} %refs_1_.4) | copy-start | bytes 3145732
  2.0 34.7 %copy-start.2 = (bf16[256,1024]{1,0:T(8,128)(2,1)S(1)}, bf16[256,1024]{1,0:T(8,128)(2,1)}, u32[]{:S(2)}) copy-start(bf16[256,1024]{1,0:T(8,128)(2,1)} %refs_1_.3) | copy-start | bytes 1572868
  30.5 8.6 %collective-permute-start = (bf16[1088,512]{1,0:T(8,128)(2,1)S(1)}, bf16[1088,512]{1,0:T(8,128)(2,1)}, u32[]{:S(2)}, u32[]{:S(2)}) collective-permute-start(bf16[1088,512]{1,0:T(8,128)(2,1)S(1)} %convert_element_type.7.refs_2_.refs_6_), channel_id=1, source_target_pairs={{0,64},{64,0},{1,65},{65,1},{2,66},{66,2},{3,67},{67,3},{4,68},{68... | collective-permute-start | bytes 3342344 | tf_op jit(solution)/shard_map/ppermute | solution.py:23
  39.0 6.0 %copy-start.1 = (bf16[1024,512]{1,0:T(8,128)(2,1)S(1)}, bf16[1024,512]{1,0:T(8,128)(2,1)}, u32[]{:S(2)}) copy-start(bf16[1024,512]{1,0:T(8,128)(2,1)} %refs_1_.4) | copy-start | bytes 3145732
  42.8 5.3 %collective-permute-start.1 = (bf16[1536,512]{1,0:T(8,128)(2,1)S(1)}, bf16[1536,512]{1,0:T(8,128)(2,1)S(1)}, u32[]{:S(2)}, u32[]{:S(2)}) collective-permute-start(bf16[1536,512]{1,0:T(8,128)(2,1)S(1)} %get-tuple-element.38), channel_id=1, source_target_pairs={{0,64},{64,0},{1,65},{65,1},{2,66},{66,2},{3,67},{67,3},{4,68},{68... | collective-permute-start | bytes 4718600 | tf_op jit(solution)/shard_map/ppermute | solution.py:23
  49.0 23.8 %all-to-all-start = ((bf16[32,16,512]{2,1,0:T(8,128)(2,1)}), bf16[32,16,512]{2,1,0:T(8,128)(2,1)S(1)}, u32[]{:S(2)}, u32[]{:S(2)}) async-start(bf16[32,16,512]{2,1,0:T(8,128)(2,1)} %shard_map.72), calls=%async_computation | async-start | bytes 1048576 | tf_op jit(solution)/shard_map/all_to_all | solution.py:27
  60.3 17.0 %collective-permute-start.3 = (bf16[256,512]{1,0:T(8,128)(2,1)}, bf16[256,512]{1,0:T(8,128)(2,1)}, u32[]{:S(2)}, u32[]{:S(2)}) collective-permute-start(bf16[256,512]{1,0:T(8,128)(2,1)} %get-tuple-element.53), channel_id=1, source_target_pairs={{0,128},{128,256},{256,384},{384,0},{1,129},{129,257},{257,385},{3... | collective-permute-start | bytes 786440 | tf_op jit(solution)/shard_map/ppermute | solution.py:23
  63.3 30.8 %collective-permute-start.2 = (bf16[256,512]{1,0:T(8,128)(2,1)}, bf16[256,512]{1,0:T(8,128)(2,1)}, u32[]{:S(2)}, u32[]{:S(2)}) collective-permute-start(bf16[256,512]{1,0:T(8,128)(2,1)} %get-tuple-element.51), channel_id=1, source_target_pairs={{0,384},{128,0},{256,128},{384,256},{1,385},{129,1},{257,129},{385... | collective-permute-start | bytes 786440 | tf_op jit(solution)/shard_map/ppermute | solution.py:23
  73.6 11.7 %all-to-all-start.1 = ((bf16[8,16,512]{2,1,0:T(8,128)(2,1)}), bf16[8,16,512]{2,1,0:T(8,128)(2,1)S(1)}, u32[]{:S(2)}, u32[]{:S(2)}) async-start(bf16[8,16,512]{2,1,0:T(8,128)(2,1)} %shard_map.74), calls=%async_computation.1 | async-start | bytes 262144 | tf_op jit(solution)/shard_map/all_to_all | solution.py:27
  79.3 15.3 %copy-start.3 = (bf16[256,512]{1,0:T(8,128)(2,1)S(1)}, bf16[256,512]{1,0:T(8,128)(2,1)}, u32[]{:S(2)}) copy-start(bf16[256,512]{1,0:T(8,128)(2,1)} %refs_0_.4) | copy-start | bytes 786436
  79.3 15.3 %collective-permute-start.4 = (bf16[256,512]{1,0:T(8,128)(2,1)}, bf16[256,512]{1,0:T(8,128)(2,1)S(1)}, u32[]{:S(2)}, u32[]{:S(2)}) collective-permute-start(bf16[256,512]{1,0:T(8,128)(2,1)} %shard_map.77), channel_id=1, source_target_pairs={{0,128},{128,256},{256,384},{384,0},{1,129},{129,257},{257,385},{3... | collective-permute-start | bytes 786440 | tf_op jit(solution)/shard_map/ppermute | solution.py:23
  86.2 20.1 %all-to-all-start.2 = ((bf16[32,16,512]{2,1,0:T(8,128)(2,1)}), bf16[32,16,512]{2,1,0:T(8,128)(2,1)S(1)}, u32[]{:S(2)}, u32[]{:S(2)}) async-start(bf16[32,16,512]{2,1,0:T(8,128)(2,1)} %shard_map.75), calls=%async_computation.2 | async-start | bytes 1048576 | tf_op jit(solution)/shard_map/all_to_all | solution.py:27
  106.3 9.0 %collective-permute-start.5 = (bf16[512,512]{1,0:T(8,128)(2,1)S(1)}, bf16[512,512]{1,0:T(8,128)(2,1)S(1)}, u32[]{:S(2)}, u32[]{:S(2)}) collective-permute-start(bf16[512,512]{1,0:T(8,128)(2,1)S(1)} %bitcast.4), channel_id=1, source_target_pairs={{0,64},{64,0},{1,65},{65,1},{2,66},{66,2},{3,67},{67,3},{4,68},{68... | collective-permute-start | bytes 1572872 | tf_op jit(solution)/shard_map/ppermute | solution.py:23

commit v13 on v12

--- a/solution.py
+++ b/solution.py
@@ -31,13 +31,13 @@
     return lax.dot_general(a, b, (((da,), (db,)), ((), ())), preferred_element_type=jnp.float32)
 
 
-def call(kernel, outs, *args, scratch=(), flops=0, limit=16, light=False, far=(), far_outs=False):
+def call(kernel, outs, *args, scratch=(), flops=0, limit=16, light=False, far=(), far_outs=False, raw=()):
     whole = pl.BlockSpec(memory_space=pltpu.VMEM)
     scalars = pl.BlockSpec(memory_space=pltpu.SMEM)
     hbm = pl.BlockSpec(memory_space=pltpu.HBM)
     size = 0 if light else sum(a.size * a.dtype.itemsize for a in (*args, *outs))
     args = [
-        pltpu.with_memory_space_constraint(a, pltpu.HBM) if n in far else a
+        pltpu.with_memory_space_constraint(a, pltpu.HBM) if n in (*far, *raw) else a
         for n, a in enumerate(args)
     ]
     staged = [args[n] for n in far] + (list(outs) if far_outs else [])
@@ -74,7 +74,7 @@
         staging,
         out_shape=[pltpu.HBM(a.shape, a.dtype) for a in outs] if far_outs else outs,
         in_specs=[
-            scalars if a.shape == (2,) else hbm if n in far else whole for n, a in enumerate(args)
+            scalars if a.shape == (2,) else hbm if n in (*far, *raw) else whole for n, a in enumerate(args)
         ],
         out_specs=[hbm if far_outs else whole] * len(outs),
         scratch_shapes=[*scratch, *buffers],
@@ -131,14 +131,23 @@
 
 
 def score_kernel(
-    place_ref, audio_ref, audio_b_ref, scale_ref, features_ref, positive_ref, own_ref, other_ref,
+    place_ref, audio_ref, audio_b_ref, scale_ref, features_ref, positive_ref, own_ref, far_ref,
     own_weights_ref, own_peak_ref, own_sum_ref, grad_ref, tiles_ref, sent_ref, scores_ref,
+    other_ref, sems,
 ):
     core = place_ref[1]
     blocks, rows, _ = tiles_ref.shape
     chips = blocks // 2
+    fetches = []
+    for n in range(chips):
+        part = pl.ds(n * (rows + TAIL), rows + TAIL)
+        fetches.append(
+            pltpu.make_async_copy(far_ref.at[part, :], other_ref.at[part, :], sems.at[n])
+        )
+        fetches[n].start()
     audio_b = audio_b_ref[...]
     for n in range(chips):
+        fetches[n].wait()
         block, factor = text_block(other_ref, n, rows)
         scores_ref[:, n * rows : (n + 1) * rows] = factor * dot(audio_b, block, 1, 1)
     step = 16
@@ -307,9 +316,14 @@
         own,
         other,
         *own_terms,
-        scratch=[pltpu.VMEM((rows, chips * rows), f32)],
+        scratch=[
+            pltpu.VMEM((rows, chips * rows), f32),
+            pltpu.VMEM(other.shape, bf16),
+            pltpu.SemaphoreType.DMA((chips,)),
+        ],
         flops=3 * pair_flops,
         limit=20,
+        raw=(7,),
     )
     got = shifted(sent, "core", 1)
     (weight,) = call(

time: 118 us -> 119 us (level)
  no operation moved by 1% of the time
where the time goes in v13:
time: 119 us; the launch traced here: 118 us
  starting transfers between devices  49 us (41%)
  blocking collectives  28.3 us (24%)
  Pallas kernels  22.4 us (19%)
  waiting for transfers between devices  16.9 us (14%)
    all_gather x1, blocking collectives, body(): lax.all_gather(sent.astype(jnp.float16), 'zh', axis=0, tiled=True)  28.3 us
    ppermute x6, starting transfers between devices, shifted(): lax.ppermute(block, axis, [(i, (i + distance) % count) for i in range(cou...  27.6 us
    all_to_all x3, starting transfers between devices, exchanged(): return lax.all_to_all(block, axes, split_axis=0, concat_axis=0, tiled=True)  21.4 us
    pallas_call x12, Pallas kernels, call(): pl.pallas_call(staging, out_shape=[pltpu.HBM(a.shape, a.dtype) for a in o...  19.3 us
    all_to_all x3, waiting for transfers between devices, exchanged(): return lax.all_to_all(block, axes, split_axis=0, concat_axis=0, tiled=True)  14.5 us
    pallas_call x2, Pallas kernels, placed(): pl.pallas_call(functools.partial(place_kernel, side), out_shape=shape((2...  3.11 us
  transfers between devices with their start and end apart: 9, of which 6 were waited for; matrix products, arithmetic and copies ran while one was open for 0% of the time, Pallas kernels for 12%

profile of v13, /device:TPU:1, one launch (start us, length us, event | category | flops | bytes accessed | tf_op | source)
XLA Modules:
  0.0 117.8 jit_solution(1794732763147824455)
XLA Ops:
  0.6 1.3 %shard_map.67 = bf16[272,512]{1,0:T(8,128)(2,1)S(1)} custom-call(bf16[256,512]{1,0:T(8,128)(2,1)} %refs_0_.4), custom_call_target="tpu_custom_call" | custom-call | bytes 540672 | tf_op jit(solution)/shard_map/pallas_call | solution.py:73
  2.0 28.3 %all-gather.1 = f16[1088,512]{1,0:T(8,128)(2,1)S(1)} all-gather(f16[272,512]{1,0:T(8,128)(2,1)S(1)} %convert_element_type.6), channel_id=1, replica_groups=mesh['zh'=4,'core'=2,'zl'=2,'x'=4,'y'=8] {'zh'}, dimensions={0}, use_global_device_ids=true | all-gather | bytes 1392640 | tf_op jit(solution)/shard_map/all_gather | solution.py:294
  30.3 0.2 convert_element_type.7.refs_2_.refs_6_
  30.5 6.1 %collective-permute-start = (bf16[1088,512]{1,0:T(8,128)(2,1)S(1)}, bf16[1088,512]{1,0:T(8,128)(2,1)}, u32[]{:S(2)}, u32[]{:S(2)}) collective-permute-start(bf16[1088,512]{1,0:T(8,128)(2,1)S(1)} %convert_element_type.7.refs_2_.refs_6_), channel_id=1, source_target_pairs={{0,64},{64,0},{1,65},{65,1},{2,66},{66,2},{3,67},{67,3},{4,68},{68... | collective-permute-start | bytes 3342344 | tf_op jit(solution)/shard_map/ppermute | solution.py:23
  36.6 0.1 copy.8.refs_5_
  36.7 1.1 shard_map.68
  37.9 1.1 collective-permute-done.refs_7_
  39.1 4.7 %shard_map.69 = (bf16[256,512]{1,0:T(8,128)(2,1)S(1)}, bf16[8,256,256]{2,1,0:T(8,128)(2,1)S(1)}, bf16[1536,512]{1,0:T(8,128)(2,1)S(1)}) custom-call(s32[2]{0:T(128)S(1)} %pad_add_fusion.refs_0_.place_ref, f32[256,512]{1,0:T(8,128)S(1)} %get-tuple-element.32.refs_1_, bf16[256,512]{1,0:T(8,128)(2,1)S(1)} %get-tuple-element.33.refs_2_, ...), custom_call_target="tpu_custom_call" | custom-call | flops 1610612736 | bytes 7475208 | tf_op jit(solution)/shard_map/pallas_call | solution.py:73
  43.8 2.3 %collective-permute-start.1 = (bf16[1536,512]{1,0:T(8,128)(2,1)S(1)}, bf16[1536,512]{1,0:T(8,128)(2,1)S(1)}, u32[]{:S(2)}, u32[]{:S(2)}) collective-permute-start(bf16[1536,512]{1,0:T(8,128)(2,1)S(1)} %get-tuple-element.38), channel_id=1, source_target_pairs={{0,64},{64,0},{1,65},{65,1},{2,66},{66,2},{3,67},{67,3},{4,68},{68... | collective-permute-start | bytes 4718600 | tf_op jit(solution)/shard_map/ppermute | solution.py:23
  46.1 1.3 %shard_map.71 = bf16[256,1024]{1,0:T(8,128)(2,1)} custom-call(bf16[256,512]{1,0:T(8,128)(2,1)S(1)} %get-tuple-element.39.refs_2_.refs_0_, bf16[1024,512]{1,0:T(8,128)(2,1)S(1)} %copy-done.1), custom_call_target="tpu_custom_call" | custom-call | tf_op jit(solution)/shard_map/pallas_call | solution.py:73
  47.4 0.9 shard_map.70.refs_0_
  48.2 0.9 collective-permute-done.1.refs_1_.refs_3_
  49.1 0.9 shard_map.72
  50.0 9.7 %all-to-all-start = ((bf16[32,16,512]{2,1,0:T(8,128)(2,1)}), bf16[32,16,512]{2,1,0:T(8,128)(2,1)S(1)}, u32[]{:S(2)}, u32[]{:S(2)}) async-start(bf16[32,16,512]{2,1,0:T(8,128)(2,1)} %shard_map.72), calls=%async_computation | async-start | bytes 1048576 | tf_op jit(solution)/shard_map/all_to_all | solution.py:27
  59.7 1.6 %shard_map.76 = (bf16[256,512]{1,0:T(8,128)(2,1)}, bf16[256,512]{1,0:T(8,128)(2,1)}) custom-call(s32[2]{0:T(128)S(1)} %pad_add_fusion.refs_0_.place_ref, bf16[8,256,256]{2,1,0:T(8,128)(2,1)S(1)} %get-tuple-element.43.refs_1_, bf16[256,512]{1,0:T(8,128)(2,1)S(1)} %get-tuple-element.33.refs_2_, bf16[1536,512]{1,0:T(8,128)(2,1)S(1)} %collective-permute-done.1.refs_1_.refs_3_), custom_call_target="tpu_custom_call" | custom-call | flops 134217728 | bytes 3407880 | tf_op jit(solution)/shard_map/pallas_call | solution.py:73
  61.3 3.0 %collective-permute-start.3 = (bf16[256,512]{1,0:T(8,128)(2,1)}, bf16[256,512]{1,0:T(8,128)(2,1)}, u32[]{:S(2)}, u32[]{:S(2)}) collective-permute-start(bf16[256,512]{1,0:T(8,128)(2,1)} %get-tuple-element.53), channel_id=1, source_target_pairs={{0,128},{128,256},{256,384},{384,0},{1,129},{129,257},{257,385},{3... | collective-permute-start | bytes 786440 | tf_op jit(solution)/shard_map/ppermute | solution.py:23
  64.3 4.4 %collective-permute-start.2 = (bf16[256,512]{1,0:T(8,128)(2,1)}, bf16[256,512]{1,0:T(8,128)(2,1)}, u32[]{:S(2)}, u32[]{:S(2)}) collective-permute-start(bf16[256,512]{1,0:T(8,128)(2,1)} %get-tuple-element.51), channel_id=1, source_target_pairs={{0,384},{128,0},{256,128},{384,256},{1,385},{129,1},{257,129},{385... | collective-permute-start | bytes 786440 | tf_op jit(solution)/shard_map/ppermute | solution.py:23
  68.7 1.8 %shard_map.73 = (f32[256,512]{1,0:T(8,128)}, f32[256,512]{1,0:T(8,128)}) custom-call(s32[2]{0:T(128)S(1)} %pad_add_fusion.refs_0_.place_ref, bf16[8,256,256]{2,1,0:T(8,128)(2,1)S(1)} %get-tuple-element.43.refs_1_, bf16[256,512]{1,0:T(8,128)(2,1)S(1)} %get-tuple-element.33.refs_2_, bf16[1536,512]{1,0:T(8,128)(2,1)S(1)} %collective-permute-done.1.refs_1_.refs_3_), custom_call_target="tpu_custom_call" | custom-call | flops 536870912 | bytes 3932168 | tf_op jit(solution)/shard_map/pallas_call | solution.py:73
  70.5 3.3 %all-to-all-done.refs_0_ = bf16[32,16,512]{2,1,0:T(8,128)(2,1)S(1)} async-done(((bf16[32,16,512]{2,1,0:T(8,128)(2,1)}), bf16[32,16,512]{2,1,0:T(8,128)(2,1)S(1)}, u32[]{:S(2)}, u32[]{:S(2)}) %all-to-all-start) | async-done | bytes 524320 | tf_op jit(solution)/shard_map/all_to_all | solution.py:27
  73.8 0.8 shard_map.74
  74.6 3.8 %all-to-all-start.1 = ((bf16[8,16,512]{2,1,0:T(8,128)(2,1)}), bf16[8,16,512]{2,1,0:T(8,128)(2,1)S(1)}, u32[]{:S(2)}, u32[]{:S(2)}) async-start(bf16[8,16,512]{2,1,0:T(8,128)(2,1)} %shard_map.74), calls=%async_computation.1 | async-start | bytes 262144 | tf_op jit(solution)/shard_map/all_to_all | solution.py:27
  78.4 1.9 %shard_map.77 = bf16[256,512]{1,0:T(8,128)(2,1)} custom-call(f32[256,512]{1,0:T(8,128)} %get-tuple-element.52.refs_0_, bf16[256,512]{1,0:T(8,128)(2,1)} %collective-permute-done.3.refs_1_), custom_call_target="tpu_custom_call" | custom-call | flops 68719476736 | bytes 1048576 | tf_op jit(solution)/shard_map/pallas_call | solution.py:73
  80.3 4.4 %collective-permute-start.4 = (bf16[256,512]{1,0:T(8,128)(2,1)}, bf16[256,512]{1,0:T(8,128)(2,1)S(1)}, u32[]{:S(2)}, u32[]{:S(2)}) collective-permute-start(bf16[256,512]{1,0:T(8,128)(2,1)} %shard_map.77), channel_id=1, source_target_pairs={{0,128},{128,256},{256,384},{384,0},{1,129},{129,257},{257,385},{3... | collective-permute-start | bytes 786440 | tf_op jit(solution)/shard_map/ppermute | solution.py:23
  84.7 1.6 %all-to-all-done.1.refs_0_ = bf16[8,16,512]{2,1,0:T(8,128)(2,1)S(1)} async-done(((bf16[8,16,512]{2,1,0:T(8,128)(2,1)}), bf16[8,16,512]{2,1,0:T(8,128)(2,1)S(1)}, u32[]{:S(2)}, u32[]{:S(2)}) %all-to-all-start.1) | async-done | bytes 131104 | tf_op jit(solution)/shard_map/all_to_all | solution.py:27
  86.3 0.9 shard_map.75
  87.2 8.0 %all-to-all-start.2 = ((bf16[32,16,512]{2,1,0:T(8,128)(2,1)}), bf16[32,16,512]{2,1,0:T(8,128)(2,1)S(1)}, u32[]{:S(2)}, u32[]{:S(2)}) async-start(bf16[32,16,512]{2,1,0:T(8,128)(2,1)} %shard_map.75), calls=%async_computation.2 | async-start | bytes 1048576 | tf_op jit(solution)/shard_map/all_to_all | solution.py:27
  95.2 0.4 collective-permute-done.4.refs_3_
  95.5 2.2 %shard_map.78 = f32[256,512]{1,0:T(8,128)} custom-call(bf16[256,512]{1,0:T(8,128)(2,1)S(1)} %copy-done.3, f32[256,512]{1,0:T(8,128)} %get-tuple-element.50.refs_1_, bf16[256,512]{1,0:T(8,128)(2,1)} %collective-permute-done.2.refs_2_, bf16[256,512]{1,0:T(8,128)(2,1)S(1)} %collective-permute-done.4.refs_3_), custom_call_target="tpu_custom_call" | custom-call | flops 68719476736 | bytes 1835008 | tf_op jit(solution)/shard_map/pallas_call | solution.py:73
  97.7 9.6 %all-to-all-done.2 = bf16[32,16,512]{2,1,0:T(8,128)(2,1)S(1)} async-done(((bf16[32,16,512]{2,1,0:T(8,128)(2,1)}), bf16[32,16,512]{2,1,0:T(8,128)(2,1)S(1)}, u32[]{:S(2)}, u32[]{:S(2)}) %all-to-all-start.2) | async-done | bytes 524320 | tf_op jit(solution)/shard_map/all_to_all | solution.py:27
  107.3 7.4 %collective-permute-start.5 = (bf16[512,512]{1,0:T(8,128)(2,1)S(1)}, bf16[512,512]{1,0:T(8,128)(2,1)S(1)}, u32[]{:S(2)}, u32[]{:S(2)}) collective-permute-start(bf16[512,512]{1,0:T(8,128)(2,1)S(1)} %bitcast.4), channel_id=1, source_target_pairs={{0,64},{64,0},{1,65},{65,1},{2,66},{66,2},{3,67},{67,3},{4,68},{68... | collective-permute-start | bytes 1572872 | tf_op jit(solution)/shard_map/ppermute | solution.py:23
  114.7 1.6 %shard_map.79.refs_0_ = f32[1024,512]{1,0:T(8,128)} custom-call(s32[2]{0:T(128)S(1)} %pad_add_fusion.refs_0_.place_ref, bf16[512,512]{1,0:T(8,128)(2,1)S(1)} %bitcast.5), custom_call_target="tpu_custom_call" | custom-call | bytes 1572864 | tf_op jit(solution)/shard_map/pallas_call | solution.py:254
  116.3 1.6 %shard_map.80 = f32[1024,512]{1,0:T(8,128)} custom-call(s32[2]{0:T(128)S(1)} %pad_add_fusion.refs_0_.place_ref, bf16[512,512]{1,0:T(8,128)(2,1)S(1)} %collective-permute-done.5.half_ref, f32[1024,512]{1,0:T(8,128)} %shard_map.79.refs_0_), custom_call_target="tpu_custom_call", output_to_operand_aliasing={{}: (2, {})} | custom-call | bytes 1572864 | tf_op jit(solution)/shard_map/pallas_call | solution.py:254
  (15 shorter events, 0.2 us)
Async XLA Ops:
  2.0 34.6 %copy-start.4 = (s32[256]{0:T(256)S(1)}, s32[256]{0:T(256)}, u32[]{:S(2)}) copy-start(s32[256]{0:T(256)} %param.7) | copy-start | bytes 3076
  2.0 34.7 %copy-start = (bf16[1024,512]{1,0:T(8,128)(2,1)S(1)}, bf16[1024,512]{1,0:T(8,128)(2,1)}, u32[]{:S(2)}) copy-start(bf16[1024,512]{1,0:T(8,128)(2,1)} %refs_1_.4) | copy-start | bytes 3145732
  2.0 34.7 %copy-start.2 = (bf16[256,1024]{1,0:T(8,128)(2,1)S(1)}, bf16[256,1024]{1,0:T(8,128)(2,1)}, u32[]{:S(2)}) copy-start(bf16[256,1024]{1,0:T(8,128)(2,1)} %refs_1_.3) | copy-start | bytes 1572868
  30.5 8.6 %collective-permute-start = (bf16[1088,512]{1,0:T(8,128)(2,1)S(1)}, bf16[1088,512]{1,0:T(8,128)(2,1)}, u32[]{:S(2)}, u32[]{:S(2)}) collective-permute-start(bf16[1088,512]{1,0:T(8,128)(2,1)S(1)} %convert_element_type.7.refs_2_.refs_6_), channel_id=1, source_target_pairs={{0,64},{64,0},{1,65},{65,1},{2,66},{66,2},{3,67},{67,3},{4,68},{68... | collective-permute-start | bytes 3342344 | tf_op jit(solution)/shard_map/ppermute | solution.py:23
  39.0 7.0 %copy-start.1 = (bf16[1024,512]{1,0:T(8,128)(2,1)S(1)}, bf16[1024,512]{1,0:T(8,128)(2,1)}, u32[]{:S(2)}) copy-start(bf16[1024,512]{1,0:T(8,128)(2,1)} %refs_1_.4) | copy-start | bytes 3145732
  43.8 5.3 %collective-permute-start.1 = (bf16[1536,512]{1,0:T(8,128)(2,1)S(1)}, bf16[1536,512]{1,0:T(8,128)(2,1)S(1)}, u32[]{:S(2)}, u32[]{:S(2)}) collective-permute-start(bf16[1536,512]{1,0:T(8,128)(2,1)S(1)} %get-tuple-element.38), channel_id=1, source_target_pairs={{0,64},{64,0},{1,65},{65,1},{2,66},{66,2},{3,67},{67,3},{4,68},{68... | collective-permute-start | bytes 4718600 | tf_op jit(solution)/shard_map/ppermute | solution.py:23
  50.0 23.8 %all-to-all-start = ((bf16[32,16,512]{2,1,0:T(8,128)(2,1)}), bf16[32,16,512]{2,1,0:T(8,128)(2,1)S(1)}, u32[]{:S(2)}, u32[]{:S(2)}) async-start(bf16[32,16,512]{2,1,0:T(8,128)(2,1)} %shard_map.72), calls=%async_computation | async-start | bytes 1048576 | tf_op jit(solution)/shard_map/all_to_all | solution.py:27
  61.3 17.0 %collective-permute-start.3 = (bf16[256,512]{1,0:T(8,128)(2,1)}, bf16[256,512]{1,0:T(8,128)(2,1)}, u32[]{:S(2)}, u32[]{:S(2)}) collective-permute-start(bf16[256,512]{1,0:T(8,128)(2,1)} %get-tuple-element.53), channel_id=1, source_target_pairs={{0,128},{128,256},{256,384},{384,0},{1,129},{129,257},{257,385},{3... | collective-permute-start | bytes 786440 | tf_op jit(solution)/shard_map/ppermute | solution.py:23
  64.3 30.8 %collective-permute-start.2 = (bf16[256,512]{1,0:T(8,128)(2,1)}, bf16[256,512]{1,0:T(8,128)(2,1)}, u32[]{:S(2)}, u32[]{:S(2)}) collective-permute-start(bf16[256,512]{1,0:T(8,128)(2,1)} %get-tuple-element.51), channel_id=1, source_target_pairs={{0,384},{128,0},{256,128},{384,256},{1,385},{129,1},{257,129},{385... | collective-permute-start | bytes 786440 | tf_op jit(solution)/shard_map/ppermute | solution.py:23
  74.6 11.7 %all-to-all-start.1 = ((bf16[8,16,512]{2,1,0:T(8,128)(2,1)}), bf16[8,16,512]{2,1,0:T(8,128)(2,1)S(1)}, u32[]{:S(2)}, u32[]{:S(2)}) async-start(bf16[8,16,512]{2,1,0:T(8,128)(2,1)} %shard_map.74), calls=%async_computation.1 | async-start | bytes 262144 | tf_op jit(solution)/shard_map/all_to_all | solution.py:27
  80.3 15.3 %copy-start.3 = (bf16[256,512]{1,0:T(8,128)(2,1)S(1)}, bf16[256,512]{1,0:T(8,128)(2,1)}, u32[]{:S(2)}) copy-start(bf16[256,512]{1,0:T(8,128)(2,1)} %refs_0_.4) | copy-start | bytes 786436
  80.3 15.3 %collective-permute-start.4 = (bf16[256,512]{1,0:T(8,128)(2,1)}, bf16[256,512]{1,0:T(8,128)(2,1)S(1)}, u32[]{:S(2)}, u32[]{:S(2)}) collective-permute-start(bf16[256,512]{1,0:T(8,128)(2,1)} %shard_map.77), channel_id=1, source_target_pairs={{0,128},{128,256},{256,384},{384,0},{1,129},{129,257},{257,385},{3... | collective-permute-start | bytes 786440 | tf_op jit(solution)/shard_map/ppermute | solution.py:23
  87.2 20.1 %all-to-all-start.2 = ((bf16[32,16,512]{2,1,0:T(8,128)(2,1)}), bf16[32,16,512]{2,1,0:T(8,128)(2,1)S(1)}, u32[]{:S(2)}, u32[]{:S(2)}) async-start(bf16[32,16,512]{2,1,0:T(8,128)(2,1)} %shard_map.75), calls=%async_computation.2 | async-start | bytes 1048576 | tf_op jit(solution)/shard_map/all_to_all | solution.py:27
  107.3 9.0 %collective-permute-start.5 = (bf16[512,512]{1,0:T(8,128)(2,1)S(1)}, bf16[512,512]{1,0:T(8,128)(2,1)S(1)}, u32[]{:S(2)}, u32[]{:S(2)}) collective-permute-start(bf16[512,512]{1,0:T(8,128)(2,1)S(1)} %bitcast.4), channel_id=1, source_target_pairs={{0,64},{64,0},{1,65},{65,1},{2,66},{66,2},{3,67},{67,3},{4,68},{68... | collective-permute-start | bytes 1572872 | tf_op jit(solution)/shard_map/ppermute | solution.py:23
